TPU v7x, 32 devices: a whole 2x2x4 slice. The times are simulated.
32 devices in a mesh: row: 16 (over z, y, core), col: 2 (over x).
Axes of the slice: x: 2, y: 2, z: 4, core: 2. Of those that a mesh axis runs over, the one named last changes fastest.
Arguments:
- blocks: bfloat16 [160, 72, 128, 128], P('row', 'col')
- slot_cols: int32 [160, 72], P('row', 'col'), may hold values from 0 to 79, as said below
- counts: int32 [160, 2], P('row', 'col'), may hold values from 2 to 36, as said below
- demand: bfloat16 [20480, 128], P('col'), may hold values from 0.1 to 10
- value_added: float32 [20480], P('col'), may hold values from 0.5 to 5
Outputs:
- propagated: bfloat16 [20480, 128], P('row')
Inputs may be any that keep to these rules, and one draw needn't show every extreme that they name: `counts`: some block row has all 36 slots live in every column group; live slots come first in each group. `slot_cols`: within one block row and column group the 36 slots name distinct column blocks.
All inputs are finite; a program needn't handle non-finite values.
Results may differ from a plain program's by a relative error of at most 0.0042.
Values may be sent and summed in bfloat16 or wider, within the bound.
No kernel may reach another device: no remote copies, remote signals or barrier semaphores. Data moves between devices by JAX's collectives and lax.ppermute only.
A program may use at most 128 MiB of HBM per device.

v0:
```python
import jax
import jax.numpy as jnp
from jax import lax
from jax.sharding import PartitionSpec as P


def body(blocks, slot_cols, counts, demand, value_added):
    rows_here = blocks.shape[0]
    slot_count = blocks.shape[1]
    block_size = blocks.shape[2]
    demand_width = demand.shape[1]
    group_blocks = demand.shape[0] // block_size
    live_slots = (jnp.arange(slot_count, dtype=jnp.int32)[None, :] < counts).astype(jnp.float32)
    column_sums = jnp.sum(blocks, axis=2, dtype=jnp.float32) * live_slots[:, :, None]
    onehot = (
        slot_cols.reshape(-1)[:, None] == jnp.arange(group_blocks, dtype=jnp.int32)[None, :]
    ).astype(jnp.float32)
    partial_totals = jnp.einsum(
        "nc,nk->ck", onehot, column_sums.reshape(-1, block_size), precision=lax.Precision.HIGHEST
    )
    totals = lax.psum(partial_totals, "row")
    inverse = 1.0 / (totals.reshape(-1) + value_added)
    inverse = inverse.reshape(group_blocks, block_size)
    scaling = inverse[slot_cols] * live_slots[:, :, None]
    coefficients = (blocks * scaling[:, :, None, :]).astype(jnp.bfloat16)

    def local_layer(source):
        picked = source.reshape(group_blocks, block_size, demand_width)[slot_cols]
        product = jnp.einsum(
            "bsij,bsjk->bik", coefficients, picked, preferred_element_type=jnp.float32
        )
        return product.reshape(rows_here * block_size, demand_width)

    group_index = lax.axis_index("col")
    group_rows = group_blocks * block_size
    part_one = local_layer(demand)
    layer_one = lax.psum(part_one, "col").astype(jnp.bfloat16)
    gathered = lax.all_gather(layer_one, "row", axis=0, tiled=True)
    needed = lax.dynamic_slice_in_dim(gathered, group_index * group_rows, group_rows, 0)
    layer_two = lax.psum(local_layer(needed), "col")
    return (layer_one.astype(jnp.float32) + layer_two).astype(jnp.bfloat16)


def solution(mesh):
    return jax.shard_map(
        body,
        mesh=mesh,
        in_specs=(
            P("row", "col", None, None),
            P("row", "col"),
            P("row", "col"),
            P("col", None),
            P("col"),
        ),
        out_specs=P("row", None),
        check_vma=False,
    )
```

profile of v0, /device:TPU:0, one launch (start us, length us, event | category | flops | bytes accessed | tf_op | source)
XLA Modules:
  0.0 243.4 jit_solution(2818086111009467794)
XLA Ops:
  6.5 0.0 copy-start
  6.5 0.0 copy-start.2
  6.5 0.0 all-gather.2.cloned.1.call-start
  6.5 0.9 eq.15
  7.5 0.7 compare_select_fusion
  8.2 0.7 fusion.8
  8.9 0.1 reshape.60
  9.0 0.1 reshape.63
  9.1 8.6 %convert_reduce_fusion = f32[10,36,128]{2,1,0:T(8,128)S(1)} fusion(bf16[10,36,128,128]{3,2,1,0:T(8,128)(2,1)} %param.5), kind=kLoop, calls=%fused_computation.4 | loop fusion | flops 11750400 | bytes 11980800 | tf_op jit(solution)/shard_map/reduce_sum | solution.py:14
  17.7 0.5 convolution_bitcast_fusion
  18.2 63.0 %psum.21 = f32[10240]{0:T(1024)S(1)} all-reduce(f32[10240]{0:T(1024)S(1)} %convolution_bitcast_fusion), channel_id=1, replica_groups=mesh['row'=16,'col'=2] {'row'}, use_global_device_ids=true, to_apply=%region_1.0 | all-reduce | flops 10240 | bytes 81920 | tf_op jit(solution)/shard_map/psum | solution.py:21
  81.2 0.0 copy-done.2
  81.3 1.1 gather_fusion
  82.4 0.1 broadcast_multiply_fusion
  82.5 0.0 copy-done
  82.5 11.1 %gather_fusion.1 = bf16[360,128,128]{2,1,0:T(8,128)(2,1)} fusion(bf16[80,128,128]{2,1,0:T(8,128)(2,1)S(1)} %bitcast.19, s32[1024]{0:T(1024)S(1)} %pad_clamp_fusion), kind=kCustom, calls=%fused_computation.1 | custom fusion | bytes 23594400 | tf_op jit(solution)/shard_map/gather | solution.py:28
  93.7 10.9 %fusion.3 = f32[10,128,128,1]{2,1,3,0:T(8,128)S(1)} fusion(bf16[10,36,128,128]{3,2,1,0:T(8,128)(2,1)} %bitcast.22, bf16[10,36,128,128]{3,2,1,0:T(8,128)(2,1)} %param.5, f32[10,36,128]{2,1,0:T(8,128)S(1)} %broadcast_multiply_fusion), kind=kOutput, calls=%fused_computation.7 | convolution fusion | flops 1527644160 | bytes 24432640 | tf_op jit(solution)/shard_map/bsij,bsjk->bik/dot_general | solution.py:29
  104.6 19.2 %all-reduce.4 = bf16[1280,128]{1,0:T(8,128)(2,1)} all-reduce(f32[1280,128]{1,0:T(8,128)S(1)} %bitcast.24), channel_id=1, replica_groups=mesh['row'=16,'col'=2] {'col'}, use_global_device_ids=true, to_apply=%region_2.0 | all-reduce | flops 163840 | bytes 983040 | tf_op jit(solution)/shard_map/psum | solution.py:37
  123.8 0.0 all-gather.2.cloned.1.call-update
  123.8 0.2 all-reduce.3.cloned.1.call-start
  124.0 52.8 %all-gather.2.cloned.1.call-done = bf16[20480,128]{1,0:T(8,128)(2,1)} async-done(((bf16[1280,128]{1,0:T(8,128)(2,1)}), bf16[20480,128]{1,0:T(8,128)(2,1)}) %all-gather.2.cloned.1.call-update) | async-done | bytes 5242896 | tf_op jit(solution)/shard_map/all_gather | solution.py:38
  176.8 3.0 %constant_dynamic-slice_fusion = bf16[10240,128]{1,0:T(8,128)(2,1)} fusion(bf16[20480,128]{1,0:T(8,128)(2,1)} %all-gather.2.cloned.1.call-done, s32[]{:T(128)S(6)} %select_n.9), kind=kLoop, calls=%fused_computation.20 | loop fusion | bytes 5242884 | tf_op jit(solution)/shard_map/dynamic_slice | solution.py:39
  179.8 12.9 %gather_fusion.2 = bf16[360,128,128]{2,1,0:T(8,128)(2,1)} fusion(bf16[80,128,128]{2,1,0:T(8,128)(2,1)} %bitcast.20, s32[1024]{0:T(1024)S(1)} %pad_clamp_fusion), kind=kCustom, calls=%fused_computation.2 | custom fusion | bytes 23594400 | tf_op jit(solution)/shard_map/gather | solution.py:28
  192.7 0.0 copy-start.1
  192.7 11.8 %fusion.1 = f32[10,128,128,1]{2,1,3,0:T(8,128)} fusion(bf16[10,36,128,128]{3,2,1,0:T(8,128)(2,1)} %bitcast.21, bf16[10,36,128,128]{3,2,1,0:T(8,128)(2,1)} %param.5, f32[10,36,128]{2,1,0:T(8,128)S(1)} %broadcast_multiply_fusion), kind=kOutput, calls=%fused_computation.6 | convolution fusion | flops 1527644160 | bytes 24432640 | tf_op jit(solution)/shard_map/bsij,bsjk->bik/dot_general | solution.py:29
  204.5 0.0 all-reduce.3.cloned.1.call-update
  204.5 30.2 %all-reduce.3.cloned.1.call-done = f32[1280,128]{1,0:T(8,128)} async-done(((f32[1280,128]{1,0:T(8,128)}), f32[1280,128]{1,0:T(8,128)}) %all-reduce.3.cloned.1.call-update) | async-done | bytes 655376 | tf_op jit(solution)/shard_map/psum | solution.py:40
  234.7 0.0 copy-done.1
  234.7 1.9 add_convert_fusion
  (4 shorter events, 0.1 us)
Async XLA Ops:
  6.5 76.0 %copy-start = (bf16[10240,128]{1,0:T(8,128)(2,1)S(1)}, bf16[10240,128]{1,0:T(8,128)(2,1)}, u32[]{:S(2)}) copy-start(bf16[10240,128]{1,0:T(8,128)(2,1)} %param.8) | copy-start | bytes 7864324
  6.5 74.7 %copy-start.2 = (f32[10240]{0:T(1024)S(1)}, f32[10240]{0:T(1024)}, u32[]{:S(2)}) copy-start(f32[10240]{0:T(1024)} %param.9) | copy-start | bytes 122884
  6.5 170.3 %all-gather.2.cloned.1.call-start = ((), (), s32[]{:S(2)}) async-start(), calls=%async_computation | async-start | bytes 5570560 | tf_op jit(solution)/shard_map/all_gather | solution.py:38
  123.8 110.9 %all-reduce.3.cloned.1.call-start = ((), (), s32[]{:S(2)}) async-start(), calls=%async_computation.1 | async-start | bytes 1310720 | tf_op jit(solution)/shard_map/psum | solution.py:40
  192.7 42.0 %copy-start.1 = (bf16[1280,128]{1,0:T(8,128)(2,1)S(1)}, bf16[1280,128]{1,0:T(8,128)(2,1)}, u32[]{:S(2)}) copy-start(bf16[1280,128]{1,0:T(8,128)(2,1)} %all-reduce.4) | copy-start | bytes 983044
Sparse Core Ops, SparseCore 0:
  123.9 52.8 all-gather.1
  204.6 30.0 all-reduce.2
where the time goes:
time: 244 us; the launch traced here: 243 us
  waiting for transfers between devices  83 us (34%)
  blocking collectives  82.2 us (34%)
  local copies, waits for them, and re-layouts  29.2 us (12%)
  matrix products  23.2 us (10%)
  between operations  13.5 us (6%)
  other arithmetic  12.1 us (5%)
    psum x1, blocking collectives, body(): totals = lax.psum(partial_totals, 'row')  63 us
    all_gather x1, waiting for transfers between devices, body(): gathered = lax.all_gather(layer_one, 'row', axis=0, tiled=True)  52.8 us
    psum x1, waiting for transfers between devices, body(): layer_two = lax.psum(local_layer(needed), 'col')  30.2 us
    gather x2, local copies, waits for them, and re-layouts, local_layer(): picked = source.reshape(group_blocks, block_size, demand_width)[slot_cols]  24 us
    dot_general x2, matrix products, local_layer(): jnp.einsum('bsij,bsjk->bik', coefficients, picked, preferred_element_type...  22.7 us
    psum x1, blocking collectives, body(): layer_one = lax.psum(part_one, 'col').astype(jnp.bfloat16)  19.2 us
    reduce_sum x1, other arithmetic, body(): jnp.sum(blocks, axis=2, dtype=jnp.float32) * live_slots[:, :, None]  8.63 us
  transfers between devices with their start and end apart: 2, of which 2 were waited for; matrix products, arithmetic and copies ran while one was open for 0% of the time, Pallas kernels for 0%

commit v1 on v0

v1 whole, which is shorter than its diff:
```python
import functools

import jax
import jax.numpy as jnp
from jax import lax
from jax.experimental import pallas as pl
from jax.experimental.pallas import tpu as pltpu
from jax.sharding import PartitionSpec as P

VMEM_LIMIT = 40 * 1024 * 1024


def chunk_of(slot_count):
    for size in (4, 3, 2):
        if slot_count % size == 0:
            return size
    return 1


def chunk_total(counts_ref, b, chunk):
    return lax.div(counts_ref[b, 0] + (chunk - 1), chunk)


def sums_kernel(cols_ref, counts_ref, blocks_ref, sums_ref, held_ref, acc_ref, sems):
    rows, slots, size, _ = blocks_ref.shape
    groups = sums_ref.shape[0]
    chunk = chunk_of(slots)

    def fetch(b, k):
        part = pl.ds(k * chunk, chunk)
        return pltpu.make_async_copy(blocks_ref.at[b, part], held_ref.at[b, part], sems.at[b])

    for b in range(rows):

        def start(k, carry, b=b):
            fetch(b, k).start()
            return carry

        lax.fori_loop(0, chunk_total(counts_ref, b, chunk), start, 0)
    acc_ref[...] = jnp.zeros_like(acc_ref)
    for b in range(rows):
        total = chunk_total(counts_ref, b, chunk)

        def finish(k, carry, b=b):
            fetch(b, k).wait()
            return carry

        lax.fori_loop(0, total, finish, 0)

        def add(k, carry, b=b):
            for u in range(chunk):
                slot = k * chunk + u
                col = jnp.where(slot < counts_ref[b, 0], cols_ref[b, slot], groups)
                block = held_ref[b, slot].astype(jnp.float32)
                acc_ref[col] += jnp.sum(block.reshape(size // 8, 8, size), axis=0)
            return carry

        lax.fori_loop(0, total, add, 0)
    sums_ref[...] = jnp.sum(acc_ref[:groups], axis=1)


def first_kernel(cols_ref, counts_ref, sums_ref, added_ref, demand_ref, blocks_ref, out_ref, coef_ref, inverse_ref):
    rows, slots, size, _ = blocks_ref.shape
    chunk = chunk_of(slots)
    inverse_ref[...] = (1.0 / (jnp.sum(sums_ref[...], axis=0) + added_ref[...]))[:, None, :]
    for b in range(rows):

        def add(k, acc, b=b):
            left, right = [], []
            for u in range(chunk):
                slot = k * chunk + u
                col = cols_ref[b, slot]
                live = (slot < counts_ref[b, 0]).astype(jnp.float32)
                scale = inverse_ref[col] * live
                coef = (blocks_ref[b, slot].astype(jnp.float32) * scale).astype(jnp.bfloat16)
                coef_ref[b, slot] = coef
                left.append(coef)
                right.append(demand_ref[col])
            return acc + jnp.dot(
                jnp.concatenate(left, axis=1), jnp.concatenate(right, axis=0), preferred_element_type=jnp.float32
            )

        out_ref[b] = lax.fori_loop(
            0, chunk_total(counts_ref, b, chunk), add, jnp.zeros((size, out_ref.shape[2]), jnp.float32)
        ).astype(out_ref.dtype)


def second_kernel(place, cols_ref, counts_ref, source_ref, coef_ref, out_ref):
    rows, slots, size, _ = coef_ref.shape
    chunk = chunk_of(slots)
    for b in range(rows):

        def add(k, acc, b=b):
            left, right = [], []
            for u in range(chunk):
                slot = k * chunk + u
                left.append(coef_ref[b, slot])
                right.append(source_ref[place(cols_ref[b, slot])])
            return acc + jnp.dot(
                jnp.concatenate(left, axis=1), jnp.concatenate(right, axis=0), preferred_element_type=jnp.float32
            )

        out_ref[b] = lax.fori_loop(
            0, chunk_total(counts_ref, b, chunk), add, jnp.zeros((size, out_ref.shape[2]), jnp.float32)
        ).astype(out_ref.dtype)


SMEM = pl.BlockSpec(memory_space=pltpu.SMEM)
VMEM = pl.BlockSpec(memory_space=pltpu.VMEM)
PARAMS = pltpu.CompilerParams(vmem_limit_bytes=VMEM_LIMIT)


def in_vmem(array):
    return pltpu.with_memory_space_constraint(array, pltpu.VMEM)


def body(n_row, n_col, blocks, slot_cols, counts, demand, value_added):
    rows, slots, size, _ = blocks.shape
    width = demand.shape[1]
    groups = demand.shape[0] // size
    group_devices = n_row // n_col
    paired = n_col == 2 and n_row == 16 and rows % 2 == 0
    group = lax.axis_index("col")
    me = lax.axis_index("row")

    sums, held = pl.pallas_call(
        sums_kernel,
        name="column_sums",
        out_shape=(
            jax.ShapeDtypeStruct((groups, size), jnp.float32),
            pltpu.VMEM(blocks.shape, blocks.dtype),
        ),
        in_specs=[SMEM, SMEM, pl.BlockSpec(memory_space=pl.ANY)],
        out_specs=(VMEM, VMEM),
        scratch_shapes=[pltpu.VMEM((groups + 1, 8, size), jnp.float32), pltpu.SemaphoreType.DMA((rows,))],
        compiler_params=PARAMS,
    )(slot_cols, counts, blocks)

    if paired:
        for masks in ((1, 2, 3), (4, 8, 12)):
            parts = [sums] + [lax.ppermute(sums, "row", [(i, i ^ m) for i in range(n_row)]) for m in masks]
            if masks[0] == 1:
                sums = functools.reduce(jnp.add, parts)
        sums = jnp.stack(parts)
    else:
        sums = lax.psum(sums, "row")[None]

    partial, coefs = pl.pallas_call(
        first_kernel,
        name="first_layer",
        out_shape=(
            jax.ShapeDtypeStruct((rows, size, width), jnp.bfloat16 if paired else jnp.float32),
            pltpu.VMEM(blocks.shape, blocks.dtype),
        ),
        in_specs=[SMEM, SMEM, VMEM, VMEM, VMEM, VMEM],
        out_specs=(VMEM, VMEM),
        scratch_shapes=[pltpu.VMEM((groups, 1, size), jnp.float32)],
        input_output_aliases={5: 1},
        compiler_params=PARAMS,
    )(slot_cols, counts, sums, value_added.reshape(groups, size), demand.reshape(groups, size, width), in_vmem(held))

    def exchange(part):
        if paired:
            other = lax.ppermute(part, "col", [(0, 1), (1, 0)])
            return part.astype(jnp.float32) + other.astype(jnp.float32)
        return lax.psum(part, "col")

    layer_one = exchange(partial).astype(jnp.bfloat16)
    if paired:
        half = rows // 2
        across = [(c * group_devices + i, (1 - c) * group_devices + i) for c in range(2) for i in range(group_devices)]
        pairs = []
        for c in range(2):
            for i in range(group_devices):
                pairs.append(((c * group_devices + i) * 2 + c, ((1 - c) * group_devices + i) * 2 + c))
        arrived = lax.ppermute(layer_one[half:], ("row", "col"), pairs)
        mine = jnp.where(me // group_devices == group, layer_one[:half], arrived)
        source = lax.all_gather(mine, "row", axis=0, tiled=True)

        def place(col, group):
            owner, inside = lax.div(col, rows), lax.rem(col, rows)
            near = inside < half
            holder = jnp.where(near, group, 1 - group) * group_devices + owner
            return holder * half + jnp.where(near, inside, inside - half)

        index = place(slot_cols, group)
    else:
        gathered = lax.all_gather(layer_one, "row", axis=0, tiled=True)
        source = lax.dynamic_slice_in_dim(gathered, group * groups, groups, 0)
        index = slot_cols

    partial = pl.pallas_call(
        functools.partial(second_kernel, lambda col: col),
        name="second_layer",
        out_shape=jax.ShapeDtypeStruct((rows, size, width), jnp.bfloat16 if paired else jnp.float32),
        in_specs=[SMEM, SMEM, VMEM, VMEM],
        out_specs=VMEM,
        compiler_params=PARAMS,
    )(index, counts, source, in_vmem(coefs))
    result = layer_one.astype(jnp.float32) + exchange(partial)
    return result.astype(jnp.bfloat16).reshape(rows * size, width)


def solution(mesh):
    return jax.shard_map(
        functools.partial(body, mesh.shape["row"], mesh.shape["col"]),
        mesh=mesh,
        in_specs=(
            P("row", "col", None, None),
            P("row", "col"),
            P("row", "col"),
            P("col", None),
            P("col"),
        ),
        out_specs=P("row", None),
        check_vma=False,
    )
```

time: 244 us -> 131 us (0.54)
  blocking collectives: 82.2 us -> 0 us
  matrix products: 23.2 us -> 0 us
  Pallas kernels: 0 us -> 20.7 us
  local copies, waits for them, and re-layouts: 29.2 us -> 10.2 us
  starting transfers between devices: 0.22 us -> 12.8 us
  waiting for transfers between devices: 83 us -> 70.5 us
  other arithmetic: 12.1 us -> 1.67 us
    psum x2 -> x0, blocking collectives: 82.2 us -> none  [the longest x1 63 us: body(): totals = lax.psum(partial_totals, 'row')]
    psum x1 -> x0, waiting for transfers between devices: 30.2 us -> none  [body(): layer_two = lax.psum(local_layer(needed), 'col')]
    gather x4 -> x0, local copies, waits for them, and re-layouts: 25.1 us -> none  [the longest x2 24 us: local_layer(): picked = source.reshape(group_blocks, block_size, demand_width)[slot_cols]]
    dot_general x3 -> x0, matrix products: 23.2 us -> none  [the longest x2 22.7 us: local_layer(): jnp.einsum('bsij,bsjk->bik', coefficients, picked, preferred_element_type...]
    ppermute x0 -> x9, waiting for transfers between devices: none -> 22.6 us  [the longest x2 10.5 us: exchange(): other = lax.ppermute(part, 'col', [(0, 1), (1, 0)])]
    pallas_call x0 -> x3, Pallas kernels: none -> 20.7 us  [the longest x1 8.74 us: body(): pl.pallas_call(first_kernel, name='first_layer', out_shape=(jax.ShapeDtyp...]
    ppermute x0 -> x9, starting transfers between devices: none -> 12.8 us  [the longest x6 7.82 us: body(): lax.ppermute(sums, 'row', [(i, i ^ m) for i in range(n_row)])]
    unnamed x6 -> x11, local copies, waits for them, and re-layouts: 0.01 us -> 10.2 us
  transfers between devices with their start and end apart: 2 -> 10, of which waited for: 2 -> 8; matrix products, arithmetic and copies ran while one was open for 0% -> 0% of each run, Pallas kernels for 0% -> 0%
where the time goes in v1:
time: 131 us; the launch traced here: 129 us
  waiting for transfers between devices  70.5 us (54%)
  Pallas kernels  20.7 us (16%)
  between operations  13.5 us (10%)
  starting transfers between devices  12.8 us (10%)
  local copies, waits for them, and re-layouts  10.2 us (8%)
  other arithmetic  1.67 us (1%)
    all_gather x1, waiting for transfers between devices, body(): source = lax.all_gather(mine, 'row', axis=0, tiled=True)  47.9 us
    ppermute x2, waiting for transfers between devices, exchange(): other = lax.ppermute(part, 'col', [(0, 1), (1, 0)])  10.5 us
    unnamed x11, local copies, waits for them, and re-layouts  10.2 us
    ppermute x6, waiting for transfers between devices, body(): lax.ppermute(sums, 'row', [(i, i ^ m) for i in range(n_row)])  9.25 us
    pallas_call x1, Pallas kernels, body(): pl.pallas_call(first_kernel, name='first_layer', out_shape=(jax.ShapeDtyp...  8.74 us
    pallas_call x1, Pallas kernels, body(): pl.pallas_call(functools.partial(second_kernel, lambda col: col), name='s...  8.33 us
    ppermute x6, starting transfers between devices, body(): lax.ppermute(sums, 'row', [(i, i ^ m) for i in range(n_row)])  7.82 us
    ppermute x2, starting transfers between devices, exchange(): other = lax.ppermute(part, 'col', [(0, 1), (1, 0)])  3.71 us
  transfers between devices with their start and end apart: 10, of which 8 were waited for; matrix products, arithmetic and copies ran while one was open for 0% of the time, Pallas kernels for 0%

profile of v1, /device:TPU:0, one launch (start us, length us, event | category | flops | bytes accessed | tf_op | source)
XLA Modules:
  0.0 129.4 jit_solution(9530665904342381257)
XLA Ops:
  6.5 0.0 all-gather.2.cloned.1.call-start
  6.5 0.7 copy.11.counts_ref
  7.3 0.0 copy-start.2
  7.3 0.7 copy-done.2
  8.0 0.0 copy-start.4
  8.0 0.0 copy-start.3
  8.0 3.6 %column_sums.1 = (f32[80,128]{1,0:T(8,128)S(1)}, bf16[10,36,128,128]{3,2,1,0:T(8,128)(2,1)S(1)}) custom-call(s32[10,36]{1,0:T(8,128)S(1)} %copy-done.2, s32[10,1]{1,0:T(8,128)S(1)} %copy.11.counts_ref, bf16[10,36,128,128]{3,2,1,0:T(8,128)(2,1)} %blocks_ref.1), custom_call_target="tpu_custom_call" | custom-call | tf_op jit(solution)/shard_map/column_sums/pallas_call | solution.py:126
  11.6 0.1 collective-permute-start
  11.7 3.1 %collective-permute-start.1 = (f32[80,128]{1,0:T(8,128)S(1)}, f32[80,128]{1,0:T(8,128)S(1)}, u32[]{:S(2)}, u32[]{:S(2)}) collective-permute-start(f32[80,128]{1,0:T(8,128)S(1)} %get-tuple-element.9), channel_id=1, source_target_pairs={{0,4},{2,6},{4,0},{6,2},{8,12},{10,14},{12,8},{14,10},{16,20},{18,... | collective-permute-start | bytes 122888 | tf_op jit(solution)/shard_map/ppermute | solution.py:141
  14.8 0.1 collective-permute-start.2
  14.8 0.0 collective-permute-done
  14.8 2.1 %collective-permute-done.1 = f32[80,128]{1,0:T(8,128)S(1)} collective-permute-done((f32[80,128]{1,0:T(8,128)S(1)}, f32[80,128]{1,0:T(8,128)S(1)}, u32[]{:S(2)}, u32[]{:S(2)}) %collective-permute-start.1) | collective-permute-done | bytes 40992 | tf_op jit(solution)/shard_map/ppermute | solution.py:141
  16.9 1.4 %collective-permute-done.2 = f32[80,128]{1,0:T(8,128)S(1)} collective-permute-done((f32[80,128]{1,0:T(8,128)S(1)}, f32[80,128]{1,0:T(8,128)S(1)}, u32[]{:S(2)}, u32[]{:S(2)}) %collective-permute-start.2) | collective-permute-done | bytes 40992 | tf_op jit(solution)/shard_map/ppermute | solution.py:141
  18.3 1.8 %collective-permute-start.3 = (f32[80,128]{1,0:T(8,128)S(1)}, f32[80,128]{1,0:T(8,128)S(1)}, u32[]{:S(2)}, u32[]{:S(2)}) collective-permute-start(f32[80,128]{1,0:T(8,128)S(1)} %add_add_fusion), channel_id=1, source_target_pairs={{0,8},{2,10},{4,12},{6,14},{8,0},{10,2},{12,4},{14,6},{16,24},{18,... | collective-permute-start | bytes 122888 | tf_op jit(solution)/shard_map/ppermute | solution.py:141
  20.1 2.8 %collective-permute-start.4 = (f32[80,128]{1,0:T(8,128)S(1)}, f32[80,128]{1,0:T(8,128)S(1)}, u32[]{:S(2)}, u32[]{:S(2)}) collective-permute-start(f32[80,128]{1,0:T(8,128)S(1)} %add_add_fusion), channel_id=1, source_target_pairs={{0,16},{2,18},{4,20},{6,22},{8,24},{10,26},{12,28},{14,30},{16,0},... | collective-permute-start | bytes 122888 | tf_op jit(solution)/shard_map/ppermute | solution.py:141
  22.9 0.0 collective-permute-start.5
  22.9 0.0 collective-permute-done.3
  22.9 2.9 %collective-permute-done.4 = f32[80,128]{1,0:T(8,128)S(1)} collective-permute-done((f32[80,128]{1,0:T(8,128)S(1)}, f32[80,128]{1,0:T(8,128)S(1)}, u32[]{:S(2)}, u32[]{:S(2)}) %collective-permute-start.4) | collective-permute-done | bytes 40992 | tf_op jit(solution)/shard_map/ppermute | solution.py:141
  25.8 2.9 %collective-permute-done.5 = f32[80,128]{1,0:T(8,128)S(1)} collective-permute-done((f32[80,128]{1,0:T(8,128)S(1)}, f32[80,128]{1,0:T(8,128)S(1)}, u32[]{:S(2)}, u32[]{:S(2)}) %collective-permute-start.5) | collective-permute-done | bytes 40992 | tf_op jit(solution)/shard_map/ppermute | solution.py:141
  28.7 0.0 copy-done.4
  28.7 8.7 %first_layer.1 = (bf16[10,128,128]{2,1,0:T(8,128)(2,1)S(1)}, bf16[10,36,128,128]{3,2,1,0:T(8,128)(2,1)S(1)}) custom-call(s32[10,36]{1,0:T(8,128)S(1)} %copy-done.2, s32[10,1]{1,0:T(8,128)S(1)} %copy.11.counts_ref, f32[4,80,128]{2,1,0:T(8,128)S(1)} %pad_maximum_fusion.sums_ref, f32[80,128]{1,0:T(8,128)S(1)} %bitcast.7, ...), custom_call_target="tpu_custom_call", output_to_operand_aliasing={{1}: (5, {})} | custom-call | tf_op jit(solution)/shard_map/first_layer/pallas_call | solution.py:148
  37.5 0.0 copy-start
  37.5 4.4 %copy-done = bf16[10,36,128,128]{3,2,1,0:T(8,128)(2,1)} copy-done((bf16[10,36,128,128]{3,2,1,0:T(8,128)(2,1)}, bf16[10,36,128,128]{3,2,1,0:T(8,128)(2,1)S(1)}, u32[]{:S(2)}) %copy-start) | copy-done | bytes 11796504
  41.8 1.8 %collective-permute-start.6 = (bf16[10,128,128]{2,1,0:T(8,128)(2,1)S(1)}, bf16[10,128,128]{2,1,0:T(8,128)(2,1)S(1)}, u32[]{:S(2)}, u32[]{:S(2)}) collective-permute-start(bf16[10,128,128]{2,1,0:T(8,128)(2,1)S(1)} %get-tuple-element.11), channel_id=1, source_target_pairs={{0,1},{1,0},{2,3},{3,2},{4,5},{5,4},{6,7},{7,6},{8,9},{9,8},{10,11... | collective-permute-start | bytes 983048 | tf_op jit(solution)/shard_map/ppermute | solution.py:164
  43.6 5.3 %collective-permute-done.6 = bf16[10,128,128]{2,1,0:T(8,128)(2,1)S(1)} collective-permute-done((bf16[10,128,128]{2,1,0:T(8,128)(2,1)S(1)}, bf16[10,128,128]{2,1,0:T(8,128)(2,1)S(1)}, u32[]{:S(2)}, u32[]{:S(2)}) %collective-permute-start.6) | collective-permute-done | bytes 327712 | tf_op jit(solution)/shard_map/ppermute | solution.py:164
  48.9 0.1 add_convert_fusion.1
  49.0 1.3 %collective-permute-start.7 = (bf16[5,128,128]{2,1,0:T(8,128)(2,1)S(1)}, bf16[5,128,128]{2,1,0:T(8,128)(2,1)S(1)}, u32[]{:S(2)}, u32[]{:S(2)}) collective-permute-start(bf16[5,128,128]{2,1,0:T(8,128)(2,1)S(1)} %slice.9), channel_id=1, source_target_pairs={{0,16},{2,18},{4,20},{6,22},{8,24},{10,26},{12,28},{14,30},{17,1},... | collective-permute-start | bytes 491528 | tf_op jit(solution)/shard_map/ppermute | solution.py:176
  50.4 2.8 %collective-permute-done.7 = bf16[5,128,128]{2,1,0:T(8,128)(2,1)S(1)} collective-permute-done((bf16[5,128,128]{2,1,0:T(8,128)(2,1)S(1)}, bf16[5,128,128]{2,1,0:T(8,128)(2,1)S(1)}, u32[]{:S(2)}, u32[]{:S(2)}) %collective-permute-start.7) | collective-permute-done | bytes 163872 | tf_op jit(solution)/shard_map/ppermute | solution.py:176
  53.2 0.7 slice_select_fusion
  53.9 0.0 all-gather.2.cloned.1.call-update
  53.9 0.0 copy-done.3
  53.9 47.9 %all-gather.2.cloned.1.call-done.source_ref = bf16[80,128,128]{2,1,0:T(8,128)(2,1)} async-done(((bf16[5,128,128]{2,1,0:T(8,128)(2,1)}), bf16[80,128,128]{2,1,0:T(8,128)(2,1)}) %all-gather.2.cloned.1.call-update) | async-done | bytes 2621456 | tf_op jit(solution)/shard_map/all_gather | solution.py:178
  101.8 0.0 copy-start.1
  101.8 4.3 %copy-done.1 = bf16[10,36,128,128]{3,2,1,0:T(8,128)(2,1)S(1)} copy-done((bf16[10,36,128,128]{3,2,1,0:T(8,128)(2,1)S(1)}, bf16[10,36,128,128]{3,2,1,0:T(8,128)(2,1)}, u32[]{:S(2)}) %copy-start.1) | copy-done | bytes 11796504
  106.2 8.3 %second_layer.1 = bf16[10,128,128]{2,1,0:T(8,128)(2,1)S(1)} custom-call(s32[10,36]{1,0:T(8,128)S(1)} %fusion.3.cols_ref, s32[10,1]{1,0:T(8,128)S(1)} %copy.11.counts_ref, bf16[80,128,128]{2,1,0:T(8,128)(2,1)} %all-gather.2.cloned.1.call-done.source_ref, bf16[10,36,128,128]{3,2,1,0:T(8,128)(2,1)S(1)} %copy-done.1), custom_call_target="tpu_custom_call" | custom-call | tf_op jit(solution)/shard_map/second_layer/pallas_call | solution.py:192
  114.5 1.9 %collective-permute-start.8 = (bf16[10,128,128]{2,1,0:T(8,128)(2,1)S(1)}, bf16[10,128,128]{2,1,0:T(8,128)(2,1)S(1)}, u32[]{:S(2)}, u32[]{:S(2)}) collective-permute-start(bf16[10,128,128]{2,1,0:T(8,128)(2,1)S(1)} %second_layer.1), channel_id=1, source_target_pairs={{0,1},{1,0},{2,3},{3,2},{4,5},{5,4},{6,7},{7,6},{8,9},{9,8},{10,11... | collective-permute-start | bytes 983048 | tf_op jit(solution)/shard_map/ppermute | solution.py:164
  116.4 5.2 %collective-permute-done.8 = bf16[10,128,128]{2,1,0:T(8,128)(2,1)S(1)} collective-permute-done((bf16[10,128,128]{2,1,0:T(8,128)(2,1)S(1)}, bf16[10,128,128]{2,1,0:T(8,128)(2,1)S(1)}, u32[]{:S(2)}, u32[]{:S(2)}) %collective-permute-start.8) | collective-permute-done | bytes 327712 | tf_op jit(solution)/shard_map/ppermute | solution.py:164
  121.7 0.9 add_convert_fusion
  (4 shorter events, 0.1 us)
Async XLA Ops:
  6.5 95.3 %all-gather.2.cloned.1.call-start = ((), (), s32[]{:S(2)}) async-start(), calls=%async_computation | async-start | bytes 2785280 | tf_op jit(solution)/shard_map/all_gather | solution.py:178
  7.3 0.7 copy-start.2
  8.0 20.7 %copy-start.4 = (f32[10240]{0:T(1024)S(1)}, f32[10240]{0:T(1024)}, u32[]{:S(2)}) copy-start(f32[10240]{0:T(1024)} %param.9) | copy-start | bytes 122884
  8.0 45.9 %copy-start.3 = (s32[10,36]{1,0:T(8,128)S(1)}, s32[10,36]{1,0:T(8,128)}, u32[]{:S(2)}) copy-start(s32[10,36]{1,0:T(8,128)} %cols_ref.3) | copy-start | bytes 4324
  11.6 3.2 %collective-permute-start = (f32[80,128]{1,0:T(8,128)S(1)}, f32[80,128]{1,0:T(8,128)S(1)}, u32[]{:S(2)}, u32[]{:S(2)}) collective-permute-start(f32[80,128]{1,0:T(8,128)S(1)} %get-tuple-element.9), channel_id=1, source_target_pairs={{0,2},{2,0},{4,6},{6,4},{8,10},{10,8},{12,14},{14,12},{16,18},{18,... | collective-permute-start | bytes 122888 | tf_op jit(solution)/shard_map/ppermute | solution.py:141
  11.7 5.2 %collective-permute-start.1 = (f32[80,128]{1,0:T(8,128)S(1)}, f32[80,128]{1,0:T(8,128)S(1)}, u32[]{:S(2)}, u32[]{:S(2)}) collective-permute-start(f32[80,128]{1,0:T(8,128)S(1)} %get-tuple-element.9), channel_id=1, source_target_pairs={{0,4},{2,6},{4,0},{6,2},{8,12},{10,14},{12,8},{14,10},{16,20},{18,... | collective-permute-start | bytes 122888 | tf_op jit(solution)/shard_map/ppermute | solution.py:141
  14.8 3.5 %collective-permute-start.2 = (f32[80,128]{1,0:T(8,128)S(1)}, f32[80,128]{1,0:T(8,128)S(1)}, u32[]{:S(2)}, u32[]{:S(2)}) collective-permute-start(f32[80,128]{1,0:T(8,128)S(1)} %get-tuple-element.9), channel_id=1, source_target_pairs={{0,6},{2,4},{4,2},{6,0},{8,14},{10,12},{12,10},{14,8},{16,22},{18,... | collective-permute-start | bytes 122888 | tf_op jit(solution)/shard_map/ppermute | solution.py:141
  18.3 4.6 %collective-permute-start.3 = (f32[80,128]{1,0:T(8,128)S(1)}, f32[80,128]{1,0:T(8,128)S(1)}, u32[]{:S(2)}, u32[]{:S(2)}) collective-permute-start(f32[80,128]{1,0:T(8,128)S(1)} %add_add_fusion), channel_id=1, source_target_pairs={{0,8},{2,10},{4,12},{6,14},{8,0},{10,2},{12,4},{14,6},{16,24},{18,... | collective-permute-start | bytes 122888 | tf_op jit(solution)/shard_map/ppermute | solution.py:141
  20.1 5.7 %collective-permute-start.4 = (f32[80,128]{1,0:T(8,128)S(1)}, f32[80,128]{1,0:T(8,128)S(1)}, u32[]{:S(2)}, u32[]{:S(2)}) collective-permute-start(f32[80,128]{1,0:T(8,128)S(1)} %add_add_fusion), channel_id=1, source_target_pairs={{0,16},{2,18},{4,20},{6,22},{8,24},{10,26},{12,28},{14,30},{16,0},... | collective-permute-start | bytes 122888 | tf_op jit(solution)/shard_map/ppermute | solution.py:141
  22.9 5.8 %collective-permute-start.5 = (f32[80,128]{1,0:T(8,128)S(1)}, f32[80,128]{1,0:T(8,128)S(1)}, u32[]{:S(2)}, u32[]{:S(2)}) collective-permute-start(f32[80,128]{1,0:T(8,128)S(1)} %add_add_fusion), channel_id=1, source_target_pairs={{0,24},{2,26},{4,28},{6,30},{8,16},{10,18},{12,20},{14,22},{16,8},... | collective-permute-start | bytes 122888 | tf_op jit(solution)/shard_map/ppermute | solution.py:141
  37.5 4.4 %copy-start = (bf16[10,36,128,128]{3,2,1,0:T(8,128)(2,1)}, bf16[10,36,128,128]{3,2,1,0:T(8,128)(2,1)S(1)}, u32[]{:S(2)}) copy-start(bf16[10,36,128,128]{3,2,1,0:T(8,128)(2,1)S(1)} %get-tuple-element.12.coef_ref) | copy-start | bytes 35389444
  41.8 7.1 %collective-permute-start.6 = (bf16[10,128,128]{2,1,0:T(8,128)(2,1)S(1)}, bf16[10,128,128]{2,1,0:T(8,128)(2,1)S(1)}, u32[]{:S(2)}, u32[]{:S(2)}) collective-permute-start(bf16[10,128,128]{2,1,0:T(8,128)(2,1)S(1)} %get-tuple-element.11), channel_id=1, source_target_pairs={{0,1},{1,0},{2,3},{3,2},{4,5},{5,4},{6,7},{7,6},{8,9},{9,8},{10,11... | collective-permute-start | bytes 983048 | tf_op jit(solution)/shard_map/ppermute | solution.py:164
  49.0 4.2 %collective-permute-start.7 = (bf16[5,128,128]{2,1,0:T(8,128)(2,1)S(1)}, bf16[5,128,128]{2,1,0:T(8,128)(2,1)S(1)}, u32[]{:S(2)}, u32[]{:S(2)}) collective-permute-start(bf16[5,128,128]{2,1,0:T(8,128)(2,1)S(1)} %slice.9), channel_id=1, source_target_pairs={{0,16},{2,18},{4,20},{6,22},{8,24},{10,26},{12,28},{14,30},{17,1},... | collective-permute-start | bytes 491528 | tf_op jit(solution)/shard_map/ppermute | solution.py:176
  101.8 4.4 %copy-start.1 = (bf16[10,36,128,128]{3,2,1,0:T(8,128)(2,1)S(1)}, bf16[10,36,128,128]{3,2,1,0:T(8,128)(2,1)}, u32[]{:S(2)}) copy-start(bf16[10,36,128,128]{3,2,1,0:T(8,128)(2,1)} %copy-done) | copy-start | bytes 35389444
  114.5 7.1 %collective-permute-start.8 = (bf16[10,128,128]{2,1,0:T(8,128)(2,1)S(1)}, bf16[10,128,128]{2,1,0:T(8,128)(2,1)S(1)}, u32[]{:S(2)}, u32[]{:S(2)}) collective-permute-start(bf16[10,128,128]{2,1,0:T(8,128)(2,1)S(1)} %second_layer.1), channel_id=1, source_target_pairs={{0,1},{1,0},{2,3},{3,2},{4,5},{5,4},{6,7},{7,6},{8,9},{9,8},{10,11... | collective-permute-start | bytes 983048 | tf_op jit(solution)/shard_map/ppermute | solution.py:164
Sparse Core Ops, SparseCore 0:
  54.0 47.7 all-gather.1

commit v2 on v1

v2 whole, which is shorter than its diff:
```python
import functools

import jax
import jax.numpy as jnp
from jax import lax
from jax.experimental import pallas as pl
from jax.experimental.pallas import tpu as pltpu
from jax.sharding import PartitionSpec as P

VMEM_LIMIT = 12 * 1024 * 1024


def divisor(slot_count, most):
    return max(size for size in range(1, most + 1) if slot_count % size == 0)


def chunk_total(counts_ref, b, chunk):
    return lax.div(counts_ref[b, 0] + (chunk - 1), chunk)


def sums_kernel(cols_ref, counts_ref, blocks_ref, sums_ref, held_ref, acc_ref, sems):
    rows, slots, size, _ = blocks_ref.shape
    groups = sums_ref.shape[0]
    chunk = divisor(slots, 4)

    def fetch(b, k):
        part = pl.ds(k * chunk, chunk)
        return pltpu.make_async_copy(blocks_ref.at[b, part], held_ref.at[b, part], sems.at[b])

    for b in range(rows):

        def start(k, carry, b=b):
            fetch(b, k).start()
            return carry

        lax.fori_loop(0, chunk_total(counts_ref, b, chunk), start, 0)
    acc_ref[...] = jnp.zeros_like(acc_ref)
    for b in range(rows):
        total = chunk_total(counts_ref, b, chunk)

        def finish(k, carry, b=b):
            fetch(b, k).wait()
            return carry

        lax.fori_loop(0, total, finish, 0)

        def add(k, carry, b=b):
            for u in range(chunk):
                slot = k * chunk + u
                col = jnp.where(slot < counts_ref[b, 0], cols_ref[b, slot], groups)
                block = held_ref[b, slot].astype(jnp.float32)
                acc_ref[col] += jnp.sum(block.reshape(size // 8, 8, size), axis=0)
            return carry

        lax.fori_loop(0, total, add, 0)
    sums_ref[...] = jnp.sum(acc_ref[:groups], axis=1)


def first_kernel(base_ref, cols_ref, counts_ref, sums_ref, added_ref, demand_ref, blocks_ref, out_ref, coef_ref, inverse_ref):
    slots = blocks_ref.shape[1]
    size = blocks_ref.shape[2]
    chunk = divisor(slots, 12)
    inverse_ref[...] = (1.0 / (jnp.sum(sums_ref[...], axis=0) + added_ref[...]))[:, None, :]
    for b in range(out_ref.shape[0]):
        row = base_ref[0] + b

        def add(k, acc, row=row):
            left, right = [], []
            for u in range(chunk):
                slot = k * chunk + u
                col = cols_ref[row, slot]
                live = slot < counts_ref[row, 0]
                block = blocks_ref[row, jnp.where(live, slot, 0)].astype(jnp.float32)
                coef = jnp.where(live, block * inverse_ref[col], 0.0).astype(jnp.bfloat16)
                coef_ref[row, slot] = coef
                left.append(coef)
                right.append(demand_ref[col])
            return acc + jnp.dot(
                jnp.concatenate(left, axis=1), jnp.concatenate(right, axis=0), preferred_element_type=jnp.float32
            )

        out_ref[b] = lax.fori_loop(
            0, chunk_total(counts_ref, row, chunk), add, jnp.zeros((size, out_ref.shape[2]), jnp.float32)
        ).astype(out_ref.dtype)


def second_layer(first_row, index_ref, counts_ref, coef_ref, source_ref, own_ref, flag, out_ref):
    slots = coef_ref.shape[1]
    size = coef_ref.shape[2]
    chunk = divisor(slots, 12)
    for b in range(out_ref.shape[0]):
        row = first_row + b

        def add(k, acc, row=row):
            left, right = [], []
            for u in range(chunk):
                slot = k * chunk + u
                left.append(coef_ref[row, slot])
                right.append(source_ref[index_ref[row, slot]])
            return acc + jnp.dot(
                jnp.concatenate(left, axis=1), jnp.concatenate(right, axis=0), preferred_element_type=jnp.float32
            )

        start = jnp.where(flag, own_ref[b].astype(jnp.float32), 0.0)
        out_ref[b] = lax.fori_loop(0, chunk_total(counts_ref, row, chunk), add, start).astype(out_ref.dtype)


def second_kernel_a(group_ref, index_ref, counts_ref, coef_ref, own_ref, *rest):
    pieces, (out_ref, source_ref) = rest[:-2], rest[-2:]
    part = pieces[0].shape[0]
    for i, piece in enumerate(pieces):
        source_ref[i * part : (i + 1) * part] = piece[...]
    second_layer(0, index_ref, counts_ref, coef_ref, source_ref, own_ref, group_ref[0] == 0, out_ref)


def second_kernel_b(group_ref, index_ref, counts_ref, coef_ref, own_ref, source_ref, out_ref):
    second_layer(
        out_ref.shape[0], index_ref, counts_ref, coef_ref, source_ref, own_ref, group_ref[0] == 1, out_ref
    )


def second_kernel(group_ref, index_ref, counts_ref, coef_ref, own_ref, source_ref, out_ref):
    second_layer(0, index_ref, counts_ref, coef_ref, source_ref, own_ref, group_ref[0] == 0, out_ref)


SMEM = pl.BlockSpec(memory_space=pltpu.SMEM)
VMEM = pl.BlockSpec(memory_space=pltpu.VMEM)
PARAMS = pltpu.CompilerParams(vmem_limit_bytes=VMEM_LIMIT)


def in_vmem(array):
    return pltpu.with_memory_space_constraint(array, pltpu.VMEM)


def body(n_row, n_col, blocks, slot_cols, counts, demand, value_added):
    rows, slots, size, _ = blocks.shape
    width = demand.shape[1]
    groups = demand.shape[0] // size
    group_devices = n_row // n_col
    paired = n_col == 2 and n_row == 16 and rows % 2 == 0
    half = rows // 2
    group = lax.axis_index("col")
    me = lax.axis_index("row")
    group_word = group.astype(jnp.int32).reshape(1)

    sums, held = pl.pallas_call(
        sums_kernel,
        name="column_sums",
        out_shape=(
            jax.ShapeDtypeStruct((groups, size), jnp.float32),
            pltpu.VMEM(blocks.shape, blocks.dtype),
        ),
        in_specs=[SMEM, SMEM, pl.BlockSpec(memory_space=pltpu.HBM)],
        out_specs=(VMEM, VMEM),
        scratch_shapes=[pltpu.VMEM((groups + 1, 8, size), jnp.float32), pltpu.SemaphoreType.DMA((rows,))],
        compiler_params=PARAMS,
    )(slot_cols, counts, pltpu.with_memory_space_constraint(blocks, pltpu.HBM))

    def flip(array, mask):
        return lax.ppermute(array, "row", [(i, i ^ mask) for i in range(n_row)])

    def swap(array):
        return lax.ppermute(array, "col", [(0, 1), (1, 0)])

    if paired:
        sums = functools.reduce(jnp.add, [sums] + [flip(sums, m) for m in (1, 2, 3)])
        sums = jnp.stack([sums] + [flip(sums, m) for m in (4, 8, 12)])
    else:
        sums = lax.psum(sums, "row")[None]

    def first_layer(base, count, dtype, held):
        return pl.pallas_call(
            first_kernel,
            name="first_layer",
            out_shape=(
                jax.ShapeDtypeStruct((count, size, width), dtype),
                pltpu.VMEM(blocks.shape, blocks.dtype),
            ),
            in_specs=[SMEM, SMEM, SMEM, VMEM, VMEM, VMEM, VMEM],
            out_specs=(VMEM, VMEM),
            scratch_shapes=[pltpu.VMEM((groups, 1, size), jnp.float32)],
            input_output_aliases={6: 1},
            compiler_params=PARAMS,
        )(
            base,
            slot_cols,
            counts,
            sums,
            value_added.reshape(groups, size),
            demand.reshape(groups, size, width),
            in_vmem(held),
        )

    def second_call(kernel, name, count, index, coefs, own, sources, keep_sources):
        dtype = jnp.bfloat16 if paired else jnp.float32
        out = jax.ShapeDtypeStruct((count, size, width), dtype)
        return pl.pallas_call(
            kernel,
            name=name,
            out_shape=(out, jax.ShapeDtypeStruct((groups, size, width), jnp.bfloat16)) if keep_sources else out,
            in_specs=[SMEM, SMEM, SMEM] + [VMEM] * (2 + len(sources)),
            out_specs=(VMEM, VMEM) if keep_sources else VMEM,
            compiler_params=PARAMS,
        )(group_word, index, counts, in_vmem(coefs), own, *sources)

    if not paired:
        partial, coefs = first_layer(jnp.zeros((1,), jnp.int32), rows, jnp.float32, held)
        layer_one = lax.psum(partial, "col").astype(jnp.bfloat16)
        gathered = lax.all_gather(layer_one, "row", axis=0, tiled=True)
        source = lax.dynamic_slice_in_dim(gathered, group * groups, groups, 0)
        partial = second_call(second_kernel, "second_layer", rows, slot_cols, coefs, layer_one, [source], False)
        return lax.psum(partial, "col").astype(jnp.bfloat16).reshape(rows * size, width)

    sent, coefs = first_layer((1 - group_word) * half, half, jnp.bfloat16, held)
    arrived = swap(sent)
    kept, coefs = first_layer(group_word * half, half, jnp.float32, coefs)
    own = (kept + arrived.astype(jnp.float32)).astype(jnp.bfloat16)

    crossed = flip(own, group_devices)
    at_home = me // group_devices == group
    home = jnp.where(at_home, own, crossed)
    away = swap(jnp.where(at_home, crossed, own))
    home_y, home_z = flip(home, 2), flip(home, 4)
    away_y, away_z = flip(away, 2), flip(away, 4)
    home_yz, away_yz = flip(home_z, 2), flip(away_y, 4)
    near = [home, home_y, home_z, home_yz, away, away_y, away_z, away_yz]
    pieces = []
    for piece in near:
        pieces += [piece, flip(piece, 1)]

    owner, inside = slot_cols // rows, slot_cols % rows
    position = owner ^ (me % group_devices)
    away_piece = ((inside // half) != group).astype(jnp.int32)
    index = ((away_piece * group_devices + position // 2 * 2 + position % 2) * half) + inside % half

    part_a, source = second_call(second_kernel_a, "second_layer", half, index, coefs, own, pieces, True)
    other_a = swap(part_a)
    part_b = second_call(second_kernel_b, "second_layer", half, index, coefs, own, [source], False)
    other_b = swap(part_b)
    parts = [
        (mine.astype(jnp.float32) + other.astype(jnp.float32)).astype(jnp.bfloat16)
        for mine, other in ((part_a, other_a), (part_b, other_b))
    ]
    return jnp.concatenate(parts, axis=0).reshape(rows * size, width)


def solution(mesh):
    return jax.shard_map(
        functools.partial(body, mesh.shape["row"], mesh.shape["col"]),
        mesh=mesh,
        in_specs=(
            P("row", "col", None, None),
            P("row", "col"),
            P("row", "col"),
            P("col", None),
            P("col"),
        ),
        out_specs=P("row", None),
        check_vma=False,
    )
```

time: 131 us -> 87.3 us (0.67)
  waiting for transfers between devices: 70.5 us -> 33.7 us
  between operations: 13.5 us -> 0.21 us
  local copies, waits for them, and re-layouts: 10.2 us -> 19 us
  Pallas kernels: 20.7 us -> 14 us
  starting transfers between devices: 12.8 us -> 18.1 us
    all_gather x1 -> x0, waiting for transfers between devices: 47.9 us -> none  [body(): source = lax.all_gather(mine, 'row', axis=0, tiled=True)]
    ppermute x9 -> x25, waiting for transfers between devices: 22.6 us -> 33.7 us  [the longest x21 25.8 us: flip(): return lax.ppermute(array, 'row', [(i, i ^ mask) for i in range(n_row)])]
    unnamed x11 -> x17, local copies, waits for them, and re-layouts: 10.2 us -> 19 us
    pallas_call x2 -> x4, Pallas kernels: 17.1 us -> 10.6 us  [the longest x2 5.56 us: first_layer(): pl.pallas_call(first_kernel, name='first_layer', out_shape=(jax.ShapeDtyp...]
    ppermute x9 -> x25, starting transfers between devices: 12.8 us -> 18.1 us  [the longest x21 14.7 us: flip(): return lax.ppermute(array, 'row', [(i, i ^ mask) for i in range(n_row)])]
  transfers between devices with their start and end apart: 10 -> 25, of which waited for: 8 -> 13; matrix products, arithmetic and copies ran while one was open for 0% -> 0% of each run, Pallas kernels for 0% -> 6%
where the time goes in v2:
time: 87.3 us; the launch traced here: 85.9 us
  waiting for transfers between devices  33.7 us (39%)
  local copies, waits for them, and re-layouts  19 us (22%)
  starting transfers between devices  18.1 us (21%)
  Pallas kernels  14 us (16%)
  other arithmetic  0.97 us (1%)
    ppermute x21, waiting for transfers between devices, flip(): return lax.ppermute(array, 'row', [(i, i ^ mask) for i in range(n_row)])  25.8 us
    unnamed x17, local copies, waits for them, and re-layouts  19 us
    ppermute x21, starting transfers between devices, flip(): return lax.ppermute(array, 'row', [(i, i ^ mask) for i in range(n_row)])  14.7 us
    ppermute x4, waiting for transfers between devices, swap(): return lax.ppermute(array, 'col', [(0, 1), (1, 0)])  7.82 us
    pallas_call x2, Pallas kernels, first_layer(): pl.pallas_call(first_kernel, name='first_layer', out_shape=(jax.ShapeDtyp...  5.56 us
    pallas_call x2, Pallas kernels, second_call(): pl.pallas_call(kernel, name=name, out_shape=(out, jax.ShapeDtypeStruct((g...  5.06 us
    ppermute x4, starting transfers between devices, swap(): return lax.ppermute(array, 'col', [(0, 1), (1, 0)])  3.43 us
    pallas_call x1, Pallas kernels, body(): pl.pallas_call(sums_kernel, name='column_sums', out_shape=(jax.ShapeDtype...  3.38 us
  transfers between devices with their start and end apart: 25, of which 13 were waited for; matrix products, arithmetic and copies ran while one was open for 0% of the time, Pallas kernels for 6%

profile of v2, /device:TPU:0, one launch (start us, length us, event | category | flops | bytes accessed | tf_op | source)
XLA Modules:
  0.0 85.9 jit_solution(16109033699998235299)
XLA Ops:
  0.0 0.9 %copy.11.counts_ref = s32[10,1]{1,0:T(8,128)S(1)} copy(s32[10,1]{0,1:T(1,128)} %param.7) | data formatting | bytes 80 | tf_op args[2]
  0.9 0.7 copy-done.6
  1.6 3.4 %column_sums.1 = (f32[80,128]{1,0:T(8,128)S(1)}, bf16[10,36,128,128]{3,2,1,0:T(8,128)(2,1)S(1)}) custom-call(s32[10,36]{1,0:T(8,128)S(1)} %copy-done.6, s32[10,1]{1,0:T(8,128)S(1)} %copy.11.counts_ref, bf16[10,36,128,128]{3,2,1,0:T(8,128)(2,1)} %blocks_ref.1), custom_call_target="tpu_custom_call" | custom-call | tf_op jit(solution)/shard_map/column_sums/pallas_call | solution.py:146
  5.0 0.0 copy-start
  5.0 4.3 %copy-done = bf16[10,36,128,128]{3,2,1,0:T(8,128)(2,1)} copy-done((bf16[10,36,128,128]{3,2,1,0:T(8,128)(2,1)}, bf16[10,36,128,128]{3,2,1,0:T(8,128)(2,1)S(1)}, u32[]{:S(2)}) %copy-start) | copy-done | bytes 11796504
  9.3 0.0 collective-permute-start
  9.3 3.0 %collective-permute-start.1 = (f32[80,128]{1,0:T(8,128)S(1)}, f32[80,128]{1,0:T(8,128)S(1)}, u32[]{:S(2)}, u32[]{:S(2)}) collective-permute-start(f32[80,128]{1,0:T(8,128)S(1)} %get-tuple-element.13), channel_id=1, source_target_pairs={{0,4},{2,6},{4,0},{6,2},{8,12},{10,14},{12,8},{14,10},{16,20},{18,... | collective-permute-start | bytes 122888 | tf_op jit(solution)/shard_map/ppermute | solution.py:160
  12.3 0.0 collective-permute-start.2
  12.3 0.0 collective-permute-done
  12.3 2.0 %collective-permute-done.1 = f32[80,128]{1,0:T(8,128)S(1)} collective-permute-done((f32[80,128]{1,0:T(8,128)S(1)}, f32[80,128]{1,0:T(8,128)S(1)}, u32[]{:S(2)}, u32[]{:S(2)}) %collective-permute-start.1) | collective-permute-done | bytes 40992 | tf_op jit(solution)/shard_map/ppermute | solution.py:160
  14.3 1.8 %collective-permute-done.2 = f32[80,128]{1,0:T(8,128)S(1)} collective-permute-done((f32[80,128]{1,0:T(8,128)S(1)}, f32[80,128]{1,0:T(8,128)S(1)}, u32[]{:S(2)}, u32[]{:S(2)}) %collective-permute-start.2) | collective-permute-done | bytes 40992 | tf_op jit(solution)/shard_map/ppermute | solution.py:160
  16.1 1.8 %collective-permute-start.3 = (f32[80,128]{1,0:T(8,128)S(1)}, f32[80,128]{1,0:T(8,128)S(1)}, u32[]{:S(2)}, u32[]{:S(2)}) collective-permute-start(f32[80,128]{1,0:T(8,128)S(1)} %add_add_fusion), channel_id=1, source_target_pairs={{0,8},{2,10},{4,12},{6,14},{8,0},{10,2},{12,4},{14,6},{16,24},{18,... | collective-permute-start | bytes 122888 | tf_op jit(solution)/shard_map/ppermute | solution.py:160
  17.9 2.7 %collective-permute-start.4 = (f32[80,128]{1,0:T(8,128)S(1)}, f32[80,128]{1,0:T(8,128)S(1)}, u32[]{:S(2)}, u32[]{:S(2)}) collective-permute-start(f32[80,128]{1,0:T(8,128)S(1)} %add_add_fusion), channel_id=1, source_target_pairs={{0,16},{2,18},{4,20},{6,22},{8,24},{10,26},{12,28},{14,30},{16,0},... | collective-permute-start | bytes 122888 | tf_op jit(solution)/shard_map/ppermute | solution.py:160
  20.7 0.0 collective-permute-start.5
  20.7 0.0 collective-permute-done.3
  20.7 3.0 %collective-permute-done.4 = f32[80,128]{1,0:T(8,128)S(1)} collective-permute-done((f32[80,128]{1,0:T(8,128)S(1)}, f32[80,128]{1,0:T(8,128)S(1)}, u32[]{:S(2)}, u32[]{:S(2)}) %collective-permute-start.4) | collective-permute-done | bytes 40992 | tf_op jit(solution)/shard_map/ppermute | solution.py:160
  23.6 2.8 %collective-permute-done.5 = f32[80,128]{1,0:T(8,128)S(1)} collective-permute-done((f32[80,128]{1,0:T(8,128)S(1)}, f32[80,128]{1,0:T(8,128)S(1)}, u32[]{:S(2)}, u32[]{:S(2)}) %collective-permute-start.5) | collective-permute-done | bytes 40992 | tf_op jit(solution)/shard_map/ppermute | solution.py:160
  26.5 4.3 %copy-done.1 = bf16[10,36,128,128]{3,2,1,0:T(8,128)(2,1)S(1)} copy-done((bf16[10,36,128,128]{3,2,1,0:T(8,128)(2,1)S(1)}, bf16[10,36,128,128]{3,2,1,0:T(8,128)(2,1)}, u32[]{:S(2)}) %copy-start.1) | copy-done | bytes 11796504
  30.9 3.1 %first_layer.2 = (bf16[5,128,128]{2,1,0:T(8,128)(2,1)S(1)}, bf16[10,36,128,128]{3,2,1,0:T(8,128)(2,1)S(1)}) custom-call(s32[1]{0:T(128)S(6)} %mul.25.base_ref, s32[10,36]{1,0:T(8,128)S(1)} %copy-done.7, s32[10,1]{1,0:T(8,128)S(1)} %copy.11.counts_ref, f32[4,80,128]{2,1,0:T(8,128)S(1)} %pad_maximum_fusion.1.sums_ref, ...), custom_call_target="tpu_custom_call", output_to_operand_aliasing={{1}: (6, {})} | custom-call | tf_op jit(solution)/shard_map/first_layer/pallas_call | solution.py:172
  34.0 1.0 %collective-permute-start.6 = (bf16[5,128,128]{2,1,0:T(8,128)(2,1)S(1)}, bf16[5,128,128]{2,1,0:T(8,128)(2,1)S(1)}, u32[]{:S(2)}, u32[]{:S(2)}) collective-permute-start(bf16[5,128,128]{2,1,0:T(8,128)(2,1)S(1)} %get-tuple-element.18), channel_id=1, source_target_pairs={{0,1},{1,0},{2,3},{3,2},{4,5},{5,4},{6,7},{7,6},{8,9},{9,8},{10,11... | collective-permute-start | bytes 491528 | tf_op jit(solution)/shard_map/ppermute | solution.py:163
  35.0 2.5 %first_layer.3 = (f32[5,128,128]{2,1,0:T(8,128)S(1)}, bf16[10,36,128,128]{3,2,1,0:T(8,128)(2,1)S(1)}) custom-call(s32[1]{0:T(128)S(6)} %mul.24.base_ref, s32[10,36]{1,0:T(8,128)S(1)} %copy-done.7, s32[10,1]{1,0:T(8,128)S(1)} %copy.11.counts_ref, f32[4,80,128]{2,1,0:T(8,128)S(1)} %pad_maximum_fusion.1.sums_ref, ...), custom_call_target="tpu_custom_call", output_to_operand_aliasing={{1}: (6, {})} | custom-call | tf_op jit(solution)/shard_map/first_layer/pallas_call | solution.py:172
  37.5 0.0 copy-start.2
  37.5 4.3 %copy-done.2 = bf16[10,36,128,128]{3,2,1,0:T(8,128)(2,1)} copy-done((bf16[10,36,128,128]{3,2,1,0:T(8,128)(2,1)}, bf16[10,36,128,128]{3,2,1,0:T(8,128)(2,1)S(1)}, u32[]{:S(2)}) %copy-start.2) | copy-done | bytes 11796504
  41.8 0.0 collective-permute-done.6
  41.9 0.1 collective-permute-start.7
  42.0 8.6 %collective-permute-done.7 = bf16[5,128,128]{2,1,0:T(8,128)(2,1)S(1)} collective-permute-done((bf16[5,128,128]{2,1,0:T(8,128)(2,1)S(1)}, bf16[5,128,128]{2,1,0:T(8,128)(2,1)S(1)}, u32[]{:S(2)}, u32[]{:S(2)}) %collective-permute-start.7) | collective-permute-done | bytes 163872 | tf_op jit(solution)/shard_map/ppermute | solution.py:160
  50.6 0.2 collective-permute-start.15
  50.8 0.0 collective-permute-start.11
  50.8 2.2 %collective-permute-start.9 = (bf16[5,128,128]{2,1,0:T(8,128)(2,1)S(1)}, bf16[5,128,128]{2,1,0:T(8,128)(2,1)S(1)}, u32[]{:S(2)}, u32[]{:S(2)}) collective-permute-start(bf16[5,128,128]{2,1,0:T(8,128)(2,1)S(1)} %get-tuple-element.22.rest_0_), channel_id=1, source_target_pairs={{0,4},{2,6},{4,0},{6,2},{8,12},{10,14},{12,8},{14,10},{16,20},{18,... | collective-permute-start | bytes 491528 | tf_op jit(solution)/shard_map/ppermute | solution.py:160
  53.0 0.0 collective-permute-start.8
  53.0 2.9 %collective-permute-done.15.rest_8_ = bf16[5,128,128]{2,1,0:T(8,128)(2,1)S(1)} collective-permute-done((bf16[5,128,128]{2,1,0:T(8,128)(2,1)S(1)}, bf16[5,128,128]{2,1,0:T(8,128)(2,1)S(1)}, u32[]{:S(2)}, u32[]{:S(2)}) %collective-permute-start.15) | collective-permute-done | bytes 163872 | tf_op jit(solution)/shard_map/ppermute | solution.py:163
  56.0 0.4 collective-permute-start.17
  56.3 0.0 collective-permute-done.11.rest_4_
  56.3 2.0 %collective-permute-start.13 = (bf16[5,128,128]{2,1,0:T(8,128)(2,1)S(1)}, bf16[5,128,128]{2,1,0:T(8,128)(2,1)S(1)}, u32[]{:S(2)}, u32[]{:S(2)}) collective-permute-start(bf16[5,128,128]{2,1,0:T(8,128)(2,1)S(1)} %collective-permute-done.11.rest_4_), channel_id=1, source_target_pairs={{0,4},{2,6},{4,0},{6,2},{8,12},{10,14},{12,8},{14,10},{16,20},{18,... | collective-permute-start | bytes 491528 | tf_op jit(solution)/shard_map/ppermute | solution.py:160
  58.3 0.0 collective-permute-start.19
  58.4 0.0 collective-permute-done.9.rest_2_
  58.4 0.0 collective-permute-start.10
  58.4 0.0 collective-permute-done.8.rest_1_
  58.4 0.5 collective-permute-start.12
  58.9 2.7 %collective-permute-done.17.rest_10_ = bf16[5,128,128]{2,1,0:T(8,128)(2,1)S(1)} collective-permute-done((bf16[5,128,128]{2,1,0:T(8,128)(2,1)S(1)}, bf16[5,128,128]{2,1,0:T(8,128)(2,1)S(1)}, u32[]{:S(2)}, u32[]{:S(2)}) %collective-permute-start.17) | collective-permute-done | bytes 163872 | tf_op jit(solution)/shard_map/ppermute | solution.py:160
  61.6 1.4 %collective-permute-start.21 = (bf16[5,128,128]{2,1,0:T(8,128)(2,1)S(1)}, bf16[5,128,128]{2,1,0:T(8,128)(2,1)S(1)}, u32[]{:S(2)}, u32[]{:S(2)}) collective-permute-start(bf16[5,128,128]{2,1,0:T(8,128)(2,1)S(1)} %collective-permute-done.17.rest_10_), channel_id=1, source_target_pairs={{0,8},{2,10},{4,12},{6,14},{8,0},{10,2},{12,4},{14,6},{16,24},{18,... | collective-permute-start | bytes 491528 | tf_op jit(solution)/shard_map/ppermute | solution.py:160
  63.0 0.4 collective-permute-done.13.rest_6_
  63.3 0.0 collective-permute-start.16
  63.4 1.7 %collective-permute-done.19.rest_12_ = bf16[5,128,128]{2,1,0:T(8,128)(2,1)S(1)} collective-permute-done((bf16[5,128,128]{2,1,0:T(8,128)(2,1)S(1)}, bf16[5,128,128]{2,1,0:T(8,128)(2,1)S(1)}, u32[]{:S(2)}, u32[]{:S(2)}) %collective-permute-start.19) | collective-permute-done | bytes 163872 | tf_op jit(solution)/shard_map/ppermute | solution.py:160
  65.1 0.0 collective-permute-start.18
  65.1 0.0 collective-permute-done.10.rest_3_
  65.1 0.5 collective-permute-start.14
  65.6 0.0 collective-permute-done.12.rest_5_
  65.6 0.1 collective-permute-start.20
  65.7 1.5 %collective-permute-done.21.rest_14_ = bf16[5,128,128]{2,1,0:T(8,128)(2,1)S(1)} collective-permute-done((bf16[5,128,128]{2,1,0:T(8,128)(2,1)S(1)}, bf16[5,128,128]{2,1,0:T(8,128)(2,1)S(1)}, u32[]{:S(2)}, u32[]{:S(2)}) %collective-permute-start.21) | collective-permute-done | bytes 163872 | tf_op jit(solution)/shard_map/ppermute | solution.py:160
  67.2 0.0 collective-permute-start.22
  67.2 0.0 collective-permute-done.16.rest_9_
  67.2 0.0 collective-permute-done.14.rest_7_
  67.2 0.0 collective-permute-done.18.rest_11_
  67.2 0.0 collective-permute-done.20.rest_13_
  67.3 1.3 %collective-permute-done.22.rest_15_ = bf16[5,128,128]{2,1,0:T(8,128)(2,1)S(1)} collective-permute-done((bf16[5,128,128]{2,1,0:T(8,128)(2,1)S(1)}, bf16[5,128,128]{2,1,0:T(8,128)(2,1)S(1)}, u32[]{:S(2)}, u32[]{:S(2)}) %collective-permute-start.22) | collective-permute-done | bytes 163872 | tf_op jit(solution)/shard_map/ppermute | solution.py:160
  68.6 4.3 %copy-done.3 = bf16[10,36,128,128]{3,2,1,0:T(8,128)(2,1)S(1)} copy-done((bf16[10,36,128,128]{3,2,1,0:T(8,128)(2,1)S(1)}, bf16[10,36,128,128]{3,2,1,0:T(8,128)(2,1)}, u32[]{:S(2)}) %copy-start.3) | copy-done | bytes 11796504
  72.9 2.3 %second_layer.2 = (bf16[5,128,128]{2,1,0:T(8,128)(2,1)S(1)}, bf16[80,128,128]{2,1,0:T(8,128)(2,1)S(1)}) custom-call(s32[1]{0:T(128)} %bitcast.group_ref, s32[10,36]{1,0:T(8,128)S(1)} %fusion.6.index_ref, s32[10,1]{1,0:T(8,128)S(1)} %copy.11.counts_ref, bf16[10,36,128,128]{3,2,1,0:T(8,128)(2,1)S(1)} %copy-done.3, ...), custom_call_target="tpu_custom_call" | custom-call | tf_op jit(solution)/shard_map/second_layer/pallas_call | solution.py:197
  75.3 1.5 %collective-permute-start.23 = (bf16[5,128,128]{2,1,0:T(8,128)(2,1)S(1)}, bf16[5,128,128]{2,1,0:T(8,128)(2,1)S(1)}, u32[]{:S(2)}, u32[]{:S(2)}) collective-permute-start(bf16[5,128,128]{2,1,0:T(8,128)(2,1)S(1)} %get-tuple-element.19), channel_id=1, source_target_pairs={{0,1},{1,0},{2,3},{3,2},{4,5},{5,4},{6,7},{7,6},{8,9},{9,8},{10,11... | collective-permute-start | bytes 491528 | tf_op jit(solution)/shard_map/ppermute | solution.py:163
  76.8 2.7 %second_layer.3 = bf16[5,128,128]{2,1,0:T(8,128)(2,1)S(1)} custom-call(s32[1]{0:T(128)} %bitcast.group_ref, s32[10,36]{1,0:T(8,128)S(1)} %fusion.6.index_ref, s32[10,1]{1,0:T(8,128)S(1)} %copy.11.counts_ref, bf16[10,36,128,128]{3,2,1,0:T(8,128)(2,1)S(1)} %copy-done.3, bf16[5,128,128]{2,1,0:T(8,128)(2,1)S(1)} %add_convert_fusion.2.own_ref, ...), custom_call_target="tpu_custom_call" | custom-call | tf_op jit(solution)/shard_map/second_layer/pallas_call | solution.py:197
  79.5 0.7 collective-permute-start.24
  80.2 1.5 %collective-permute-done.23 = bf16[5,128,128]{2,1,0:T(8,128)(2,1)S(1)} collective-permute-done((bf16[5,128,128]{2,1,0:T(8,128)(2,1)S(1)}, bf16[5,128,128]{2,1,0:T(8,128)(2,1)S(1)}, u32[]{:S(2)}, u32[]{:S(2)}) %collective-permute-start.23) | collective-permute-done | bytes 163872 | tf_op jit(solution)/shard_map/ppermute | solution.py:163
  81.7 3.4 %collective-permute-done.24 = bf16[5,128,128]{2,1,0:T(8,128)(2,1)S(1)} collective-permute-done((bf16[5,128,128]{2,1,0:T(8,128)(2,1)S(1)}, bf16[5,128,128]{2,1,0:T(8,128)(2,1)S(1)}, u32[]{:S(2)}, u32[]{:S(2)}) %collective-permute-start.24) | collective-permute-done | bytes 163872 | tf_op jit(solution)/shard_map/ppermute | solution.py:163
  85.1 0.8 pad_maximum_fusion
  (16 shorter events, 0.2 us)
Async XLA Ops:
  0.0 26.5 %copy-start.5 = (f32[10240]{0:T(1024)S(1)}, f32[10240]{0:T(1024)}, u32[]{:S(2)}) copy-start(f32[10240]{0:T(1024)} %param.9) | copy-start | bytes 122884
  0.0 26.5 %copy-start.4 = (bf16[10240,128]{1,0:T(8,128)(2,1)S(1)}, bf16[10240,128]{1,0:T(8,128)(2,1)}, u32[]{:S(2)}) copy-start(bf16[10240,128]{1,0:T(8,128)(2,1)} %param.8) | copy-start | bytes 7864324
  0.9 0.7 copy-start.6
  1.6 24.9 %copy-start.7 = (s32[10,36]{1,0:T(8,128)S(1)}, s32[10,36]{1,0:T(8,128)}, u32[]{:S(2)}) copy-start(s32[10,36]{1,0:T(8,128)} %cols_ref.5) | copy-start | bytes 4324
  5.0 4.3 %copy-start = (bf16[10,36,128,128]{3,2,1,0:T(8,128)(2,1)}, bf16[10,36,128,128]{3,2,1,0:T(8,128)(2,1)S(1)}, u32[]{:S(2)}) copy-start(bf16[10,36,128,128]{3,2,1,0:T(8,128)(2,1)S(1)} %get-tuple-element.14.blocks_ref) | copy-start | bytes 35389444
  9.3 3.0 %collective-permute-start = (f32[80,128]{1,0:T(8,128)S(1)}, f32[80,128]{1,0:T(8,128)S(1)}, u32[]{:S(2)}, u32[]{:S(2)}) collective-permute-start(f32[80,128]{1,0:T(8,128)S(1)} %get-tuple-element.13), channel_id=1, source_target_pairs={{0,2},{2,0},{4,6},{6,4},{8,10},{10,8},{12,14},{14,12},{16,18},{18,... | collective-permute-start | bytes 122888 | tf_op jit(solution)/shard_map/ppermute | solution.py:160
  9.3 5.0 %collective-permute-start.1 = (f32[80,128]{1,0:T(8,128)S(1)}, f32[80,128]{1,0:T(8,128)S(1)}, u32[]{:S(2)}, u32[]{:S(2)}) collective-permute-start(f32[80,128]{1,0:T(8,128)S(1)} %get-tuple-element.13), channel_id=1, source_target_pairs={{0,4},{2,6},{4,0},{6,2},{8,12},{10,14},{12,8},{14,10},{16,20},{18,... | collective-permute-start | bytes 122888 | tf_op jit(solution)/shard_map/ppermute | solution.py:160
  12.3 3.8 %collective-permute-start.2 = (f32[80,128]{1,0:T(8,128)S(1)}, f32[80,128]{1,0:T(8,128)S(1)}, u32[]{:S(2)}, u32[]{:S(2)}) collective-permute-start(f32[80,128]{1,0:T(8,128)S(1)} %get-tuple-element.13), channel_id=1, source_target_pairs={{0,6},{2,4},{4,2},{6,0},{8,14},{10,12},{12,10},{14,8},{16,22},{18,... | collective-permute-start | bytes 122888 | tf_op jit(solution)/shard_map/ppermute | solution.py:160
  16.1 4.6 %collective-permute-start.3 = (f32[80,128]{1,0:T(8,128)S(1)}, f32[80,128]{1,0:T(8,128)S(1)}, u32[]{:S(2)}, u32[]{:S(2)}) collective-permute-start(f32[80,128]{1,0:T(8,128)S(1)} %add_add_fusion), channel_id=1, source_target_pairs={{0,8},{2,10},{4,12},{6,14},{8,0},{10,2},{12,4},{14,6},{16,24},{18,... | collective-permute-start | bytes 122888 | tf_op jit(solution)/shard_map/ppermute | solution.py:160
  17.9 5.7 %collective-permute-start.4 = (f32[80,128]{1,0:T(8,128)S(1)}, f32[80,128]{1,0:T(8,128)S(1)}, u32[]{:S(2)}, u32[]{:S(2)}) collective-permute-start(f32[80,128]{1,0:T(8,128)S(1)} %add_add_fusion), channel_id=1, source_target_pairs={{0,16},{2,18},{4,20},{6,22},{8,24},{10,26},{12,28},{14,30},{16,0},... | collective-permute-start | bytes 122888 | tf_op jit(solution)/shard_map/ppermute | solution.py:160
  20.7 5.8 %collective-permute-start.5 = (f32[80,128]{1,0:T(8,128)S(1)}, f32[80,128]{1,0:T(8,128)S(1)}, u32[]{:S(2)}, u32[]{:S(2)}) collective-permute-start(f32[80,128]{1,0:T(8,128)S(1)} %add_add_fusion), channel_id=1, source_target_pairs={{0,24},{2,26},{4,28},{6,30},{8,16},{10,18},{12,20},{14,22},{16,8},... | collective-permute-start | bytes 122888 | tf_op jit(solution)/shard_map/ppermute | solution.py:160
  26.5 4.4 %copy-start.1 = (bf16[10,36,128,128]{3,2,1,0:T(8,128)(2,1)S(1)}, bf16[10,36,128,128]{3,2,1,0:T(8,128)(2,1)}, u32[]{:S(2)}) copy-start(bf16[10,36,128,128]{3,2,1,0:T(8,128)(2,1)} %copy-done) | copy-start | bytes 35389444
  34.0 7.8 %collective-permute-start.6 = (bf16[5,128,128]{2,1,0:T(8,128)(2,1)S(1)}, bf16[5,128,128]{2,1,0:T(8,128)(2,1)S(1)}, u32[]{:S(2)}, u32[]{:S(2)}) collective-permute-start(bf16[5,128,128]{2,1,0:T(8,128)(2,1)S(1)} %get-tuple-element.18), channel_id=1, source_target_pairs={{0,1},{1,0},{2,3},{3,2},{4,5},{5,4},{6,7},{7,6},{8,9},{9,8},{10,11... | collective-permute-start | bytes 491528 | tf_op jit(solution)/shard_map/ppermute | solution.py:163
  37.5 4.3 %copy-start.2 = (bf16[10,36,128,128]{3,2,1,0:T(8,128)(2,1)}, bf16[10,36,128,128]{3,2,1,0:T(8,128)(2,1)S(1)}, u32[]{:S(2)}) copy-start(bf16[10,36,128,128]{3,2,1,0:T(8,128)(2,1)S(1)} %get-tuple-element.16.coef_ref) | copy-start | bytes 35389444
  41.9 8.7 %collective-permute-start.7 = (bf16[5,128,128]{2,1,0:T(8,128)(2,1)S(1)}, bf16[5,128,128]{2,1,0:T(8,128)(2,1)S(1)}, u32[]{:S(2)}, u32[]{:S(2)}) collective-permute-start(bf16[5,128,128]{2,1,0:T(8,128)(2,1)S(1)} %add_convert_fusion.2.own_ref), channel_id=1, source_target_pairs={{0,16},{2,18},{4,20},{6,22},{8,24},{10,26},{12,28},{14,30},{16,0},... | collective-permute-start | bytes 491528 | tf_op jit(solution)/shard_map/ppermute | solution.py:160
  50.6 5.4 %collective-permute-start.15 = (bf16[5,128,128]{2,1,0:T(8,128)(2,1)S(1)}, bf16[5,128,128]{2,1,0:T(8,128)(2,1)S(1)}, u32[]{:S(2)}, u32[]{:S(2)}) collective-permute-start(bf16[5,128,128]{2,1,0:T(8,128)(2,1)S(1)} %get-tuple-element.21), channel_id=1, source_target_pairs={{0,1},{1,0},{2,3},{3,2},{4,5},{5,4},{6,7},{7,6},{8,9},{9,8},{10,11... | collective-permute-start | bytes 491528 | tf_op jit(solution)/shard_map/ppermute | solution.py:163
  50.8 5.5 %collective-permute-start.11 = (bf16[5,128,128]{2,1,0:T(8,128)(2,1)S(1)}, bf16[5,128,128]{2,1,0:T(8,128)(2,1)S(1)}, u32[]{:S(2)}, u32[]{:S(2)}) collective-permute-start(bf16[5,128,128]{2,1,0:T(8,128)(2,1)S(1)} %get-tuple-element.22.rest_0_), channel_id=1, source_target_pairs={{0,8},{2,10},{4,12},{6,14},{8,0},{10,2},{12,4},{14,6},{16,24},{18,... | collective-permute-start | bytes 491528 | tf_op jit(solution)/shard_map/ppermute | solution.py:160
  50.8 7.5 %collective-permute-start.9 = (bf16[5,128,128]{2,1,0:T(8,128)(2,1)S(1)}, bf16[5,128,128]{2,1,0:T(8,128)(2,1)S(1)}, u32[]{:S(2)}, u32[]{:S(2)}) collective-permute-start(bf16[5,128,128]{2,1,0:T(8,128)(2,1)S(1)} %get-tuple-element.22.rest_0_), channel_id=1, source_target_pairs={{0,4},{2,6},{4,0},{6,2},{8,12},{10,14},{12,8},{14,10},{16,20},{18,... | collective-permute-start | bytes 491528 | tf_op jit(solution)/shard_map/ppermute | solution.py:160
  53.0 5.3 %collective-permute-start.8 = (bf16[5,128,128]{2,1,0:T(8,128)(2,1)S(1)}, bf16[5,128,128]{2,1,0:T(8,128)(2,1)S(1)}, u32[]{:S(2)}, u32[]{:S(2)}) collective-permute-start(bf16[5,128,128]{2,1,0:T(8,128)(2,1)S(1)} %get-tuple-element.22.rest_0_), channel_id=1, source_target_pairs={{0,2},{2,0},{4,6},{6,4},{8,10},{10,8},{12,14},{14,12},{16,18},{18,... | collective-permute-start | bytes 491528 | tf_op jit(solution)/shard_map/ppermute | solution.py:160
  56.0 5.6 %collective-permute-start.17 = (bf16[5,128,128]{2,1,0:T(8,128)(2,1)S(1)}, bf16[5,128,128]{2,1,0:T(8,128)(2,1)S(1)}, u32[]{:S(2)}, u32[]{:S(2)}) collective-permute-start(bf16[5,128,128]{2,1,0:T(8,128)(2,1)S(1)} %collective-permute-done.15.rest_8_), channel_id=1, source_target_pairs={{0,4},{2,6},{4,0},{6,2},{8,12},{10,14},{12,8},{14,10},{16,20},{18,... | collective-permute-start | bytes 491528 | tf_op jit(solution)/shard_map/ppermute | solution.py:160
  56.3 7.0 %collective-permute-start.13 = (bf16[5,128,128]{2,1,0:T(8,128)(2,1)S(1)}, bf16[5,128,128]{2,1,0:T(8,128)(2,1)S(1)}, u32[]{:S(2)}, u32[]{:S(2)}) collective-permute-start(bf16[5,128,128]{2,1,0:T(8,128)(2,1)S(1)} %collective-permute-done.11.rest_4_), channel_id=1, source_target_pairs={{0,4},{2,6},{4,0},{6,2},{8,12},{10,14},{12,8},{14,10},{16,20},{18,... | collective-permute-start | bytes 491528 | tf_op jit(solution)/shard_map/ppermute | solution.py:160
  58.3 6.7 %collective-permute-start.19 = (bf16[5,128,128]{2,1,0:T(8,128)(2,1)S(1)}, bf16[5,128,128]{2,1,0:T(8,128)(2,1)S(1)}, u32[]{:S(2)}, u32[]{:S(2)}) collective-permute-start(bf16[5,128,128]{2,1,0:T(8,128)(2,1)S(1)} %collective-permute-done.15.rest_8_), channel_id=1, source_target_pairs={{0,8},{2,10},{4,12},{6,14},{8,0},{10,2},{12,4},{14,6},{16,24},{18,... | collective-permute-start | bytes 491528 | tf_op jit(solution)/shard_map/ppermute | solution.py:160
  58.4 6.7 %collective-permute-start.10 = (bf16[5,128,128]{2,1,0:T(8,128)(2,1)S(1)}, bf16[5,128,128]{2,1,0:T(8,128)(2,1)S(1)}, u32[]{:S(2)}, u32[]{:S(2)}) collective-permute-start(bf16[5,128,128]{2,1,0:T(8,128)(2,1)S(1)} %collective-permute-done.9.rest_2_), channel_id=1, source_target_pairs={{0,2},{2,0},{4,6},{6,4},{8,10},{10,8},{12,14},{14,12},{16,18},{18,... | collective-permute-start | bytes 491528 | tf_op jit(solution)/shard_map/ppermute | solution.py:160
  58.4 7.2 %collective-permute-start.12 = (bf16[5,128,128]{2,1,0:T(8,128)(2,1)S(1)}, bf16[5,128,128]{2,1,0:T(8,128)(2,1)S(1)}, u32[]{:S(2)}, u32[]{:S(2)}) collective-permute-start(bf16[5,128,128]{2,1,0:T(8,128)(2,1)S(1)} %collective-permute-done.11.rest_4_), channel_id=1, source_target_pairs={{0,2},{2,0},{4,6},{6,4},{8,10},{10,8},{12,14},{14,12},{16,18},{18,... | collective-permute-start | bytes 491528 | tf_op jit(solution)/shard_map/ppermute | solution.py:160
  61.6 5.6 %collective-permute-start.21 = (bf16[5,128,128]{2,1,0:T(8,128)(2,1)S(1)}, bf16[5,128,128]{2,1,0:T(8,128)(2,1)S(1)}, u32[]{:S(2)}, u32[]{:S(2)}) collective-permute-start(bf16[5,128,128]{2,1,0:T(8,128)(2,1)S(1)} %collective-permute-done.17.rest_10_), channel_id=1, source_target_pairs={{0,8},{2,10},{4,12},{6,14},{8,0},{10,2},{12,4},{14,6},{16,24},{18,... | collective-permute-start | bytes 491528 | tf_op jit(solution)/shard_map/ppermute | solution.py:160
  63.3 3.9 %collective-permute-start.16 = (bf16[5,128,128]{2,1,0:T(8,128)(2,1)S(1)}, bf16[5,128,128]{2,1,0:T(8,128)(2,1)S(1)}, u32[]{:S(2)}, u32[]{:S(2)}) collective-permute-start(bf16[5,128,128]{2,1,0:T(8,128)(2,1)S(1)} %collective-permute-done.15.rest_8_), channel_id=1, source_target_pairs={{0,2},{2,0},{4,6},{6,4},{8,10},{10,8},{12,14},{14,12},{16,18},{18,... | collective-permute-start | bytes 491528 | tf_op jit(solution)/shard_map/ppermute | solution.py:160
  65.1 2.2 %collective-permute-start.18 = (bf16[5,128,128]{2,1,0:T(8,128)(2,1)S(1)}, bf16[5,128,128]{2,1,0:T(8,128)(2,1)S(1)}, u32[]{:S(2)}, u32[]{:S(2)}) collective-permute-start(bf16[5,128,128]{2,1,0:T(8,128)(2,1)S(1)} %collective-permute-done.17.rest_10_), channel_id=1, source_target_pairs={{0,2},{2,0},{4,6},{6,4},{8,10},{10,8},{12,14},{14,12},{16,18},{18,... | collective-permute-start | bytes 491528 | tf_op jit(solution)/shard_map/ppermute | solution.py:160
  65.1 2.1 %collective-permute-start.14 = (bf16[5,128,128]{2,1,0:T(8,128)(2,1)S(1)}, bf16[5,128,128]{2,1,0:T(8,128)(2,1)S(1)}, u32[]{:S(2)}, u32[]{:S(2)}) collective-permute-start(bf16[5,128,128]{2,1,0:T(8,128)(2,1)S(1)} %collective-permute-done.13.rest_6_), channel_id=1, source_target_pairs={{0,2},{2,0},{4,6},{6,4},{8,10},{10,8},{12,14},{14,12},{16,18},{18,... | collective-permute-start | bytes 491528 | tf_op jit(solution)/shard_map/ppermute | solution.py:160
  65.6 1.7 %collective-permute-start.20 = (bf16[5,128,128]{2,1,0:T(8,128)(2,1)S(1)}, bf16[5,128,128]{2,1,0:T(8,128)(2,1)S(1)}, u32[]{:S(2)}, u32[]{:S(2)}) collective-permute-start(bf16[5,128,128]{2,1,0:T(8,128)(2,1)S(1)} %collective-permute-done.19.rest_12_), channel_id=1, source_target_pairs={{0,2},{2,0},{4,6},{6,4},{8,10},{10,8},{12,14},{14,12},{16,18},{18,... | collective-permute-start | bytes 491528 | tf_op jit(solution)/shard_map/ppermute | solution.py:160
  67.2 1.4 %collective-permute-start.22 = (bf16[5,128,128]{2,1,0:T(8,128)(2,1)S(1)}, bf16[5,128,128]{2,1,0:T(8,128)(2,1)S(1)}, u32[]{:S(2)}, u32[]{:S(2)}) collective-permute-start(bf16[5,128,128]{2,1,0:T(8,128)(2,1)S(1)} %collective-permute-done.21.rest_14_), channel_id=1, source_target_pairs={{0,2},{2,0},{4,6},{6,4},{8,10},{10,8},{12,14},{14,12},{16,18},{18,... | collective-permute-start | bytes 491528 | tf_op jit(solution)/shard_map/ppermute | solution.py:160
  68.6 4.4 %copy-start.3 = (bf16[10,36,128,128]{3,2,1,0:T(8,128)(2,1)S(1)}, bf16[10,36,128,128]{3,2,1,0:T(8,128)(2,1)}, u32[]{:S(2)}) copy-start(bf16[10,36,128,128]{3,2,1,0:T(8,128)(2,1)} %copy-done.2) | copy-start | bytes 35389444
  75.3 6.4 %collective-permute-start.23 = (bf16[5,128,128]{2,1,0:T(8,128)(2,1)S(1)}, bf16[5,128,128]{2,1,0:T(8,128)(2,1)S(1)}, u32[]{:S(2)}, u32[]{:S(2)}) collective-permute-start(bf16[5,128,128]{2,1,0:T(8,128)(2,1)S(1)} %get-tuple-element.19), channel_id=1, source_target_pairs={{0,1},{1,0},{2,3},{3,2},{4,5},{5,4},{6,7},{7,6},{8,9},{9,8},{10,11... | collective-permute-start | bytes 491528 | tf_op jit(solution)/shard_map/ppermute | solution.py:163
  79.5 5.6 %collective-permute-start.24 = (bf16[5,128,128]{2,1,0:T(8,128)(2,1)S(1)}, bf16[5,128,128]{2,1,0:T(8,128)(2,1)S(1)}, u32[]{:S(2)}, u32[]{:S(2)}) collective-permute-start(bf16[5,128,128]{2,1,0:T(8,128)(2,1)S(1)} %second_layer.3), channel_id=1, source_target_pairs={{0,1},{1,0},{2,3},{3,2},{4,5},{5,4},{6,7},{7,6},{8,9},{9,8},{10,11... | collective-permute-start | bytes 491528 | tf_op jit(solution)/shard_map/ppermute | solution.py:163

commit v3 on v2

v3 whole, which is shorter than its diff:
```python
import functools

import jax
import jax.numpy as jnp
from jax import lax
from jax.experimental import pallas as pl
from jax.experimental.pallas import tpu as pltpu
from jax.sharding import PartitionSpec as P

VMEM_LIMIT = 12 * 1024 * 1024


def divisor(slot_count, most):
    return max(size for size in range(1, most + 1) if slot_count % size == 0)


def chunk_total(counts_ref, b, chunk):
    return lax.div(counts_ref[b] + (chunk - 1), chunk)


def sums_kernel(cols_ref, counts_ref, blocks_ref, sums_ref, held_ref, acc_ref, sems):
    rows, slots, size, _ = blocks_ref.shape
    groups = sums_ref.shape[0]
    chunk = divisor(slots, 4)

    def fetch(b, k):
        part = pl.ds(k * chunk, chunk)
        return pltpu.make_async_copy(blocks_ref.at[b, part], held_ref.at[b, part], sems.at[b])

    for b in range(rows):

        def start(k, carry, b=b):
            fetch(b, k).start()
            return carry

        lax.fori_loop(0, chunk_total(counts_ref, b, chunk), start, 0)
    acc_ref[...] = jnp.zeros_like(acc_ref)
    for b in range(rows):
        total = chunk_total(counts_ref, b, chunk)

        def finish(k, carry, b=b):
            fetch(b, k).wait()
            return carry

        lax.fori_loop(0, total, finish, 0)

        def add(k, carry, b=b):
            for u in range(chunk):
                slot = k * chunk + u
                col = jnp.where(slot < counts_ref[b], cols_ref[b, slot], groups)
                block = held_ref[b, slot].astype(jnp.float32)
                acc_ref[col] += jnp.sum(block.reshape(size // 8, 8, size), axis=0)
            return carry

        lax.fori_loop(0, total, add, 0)
    sums_ref[...] = jnp.sum(acc_ref[:groups], axis=1)


def multiply_rows(rows, counts_ref, chunk, slots, start, gather, acc_ref):
    def product(row, first):
        left, right = zip(*[gather(row, first + u) for u in range(chunk)])
        return jnp.dot(jnp.concatenate(left, axis=1), jnp.concatenate(right, axis=0), preferred_element_type=jnp.float32)

    for b, row in enumerate(rows):
        acc_ref[b] = start(b) + product(row, 0)
    for b, row in enumerate(rows):

        def add(k, carry, b=b, row=row):
            acc_ref[b] += product(row, k * chunk)
            return carry

        lax.fori_loop(1, chunk_total(counts_ref, row, chunk), add, 0)


def first_kernel(sending, cols_ref, counts_ref, sums_ref, added_ref, demand_ref, blocks_ref, out_ref, coef_ref, inverse_ref, acc_ref):
    slots = blocks_ref.shape[1]
    count = out_ref.shape[0]
    inverse_ref[...] = (1.0 / (jnp.sum(sums_ref[...].astype(jnp.float32), axis=0) + added_ref[...]))[:, None, :]
    base = 0
    if sending is not None:
        side = lax.axis_index("col")
        base = (1 - side if sending else side) * count

    def gather(row, slot):
        col = cols_ref[row, slot]
        live = slot < counts_ref[row]
        block = blocks_ref[row, jnp.where(live, slot, 0)].astype(jnp.float32)
        coef = jnp.where(live, block * inverse_ref[col], 0.0).astype(jnp.bfloat16)
        coef_ref[row, slot] = coef
        return coef, demand_ref[col]

    rows = [base + b for b in range(count)]
    multiply_rows(rows, counts_ref, divisor(slots, 12), slots, lambda b: 0.0, gather, acc_ref)
    out_ref[...] = acc_ref[...].astype(out_ref.dtype)


def second_rows(first_row, place, cols_ref, counts_ref, coef_ref, source_ref, start, out_ref, acc_ref):
    slots = coef_ref.shape[1]

    def gather(row, slot):
        return coef_ref[row, slot], source_ref[place(cols_ref[row, slot])]

    rows = [first_row + b for b in range(out_ref.shape[0])]
    multiply_rows(rows, counts_ref, divisor(slots, 12), slots, start, gather, acc_ref)
    out_ref[...] = acc_ref[...].astype(out_ref.dtype)


def exact_scale(count, part):
    scale = -(-(1 << 16) // part)
    assert all((i * scale) >> 16 == i // part for i in range(count))
    return scale


def second_part_kernel(which, cols_ref, counts_ref, coef_ref, own_ref, *rest):
    if which == 0:
        pieces, (out_ref, source_ref, acc_ref) = rest[:-3], rest[-3:]
        part = pieces[0].shape[0]
        for i, piece in enumerate(pieces):
            source_ref[i * part : (i + 1) * part] = piece[...]
    else:
        source_ref, out_ref, acc_ref = rest
    part = out_ref.shape[0]
    side = lax.axis_index("col")
    near = lax.rem(lax.axis_index("row"), 8) * 2 + side
    scale = exact_scale(source_ref.shape[0], part)

    def place(col):
        piece = lax.shift_right_logical(col * scale, 16)
        return col + part * ((piece ^ near) - piece)

    def start(b):
        return jnp.where(side == which, own_ref[b].astype(jnp.float32), 0.0)

    second_rows(which * part, place, cols_ref, counts_ref, coef_ref, source_ref, start, out_ref, acc_ref)


def second_kernel(cols_ref, counts_ref, coef_ref, own_ref, source_ref, out_ref, acc_ref):
    first = lax.axis_index("col") == 0

    def start(b):
        return jnp.where(first, own_ref[b].astype(jnp.float32), 0.0)

    second_rows(0, lambda col: col, cols_ref, counts_ref, coef_ref, source_ref, start, out_ref, acc_ref)


def sort_kernel(own_ref, crossed_ref, home_ref, away_ref):
    at_home = lax.div(lax.axis_index("row"), 8) == lax.axis_index("col")

    @pl.when(at_home)
    def _():
        home_ref[...] = own_ref[...]
        away_ref[...] = crossed_ref[...]

    @pl.when(jnp.logical_not(at_home))
    def _():
        home_ref[...] = crossed_ref[...]
        away_ref[...] = own_ref[...]


SMEM = pl.BlockSpec(memory_space=pltpu.SMEM)
VMEM = pl.BlockSpec(memory_space=pltpu.VMEM)
PARAMS = pltpu.CompilerParams(vmem_limit_bytes=VMEM_LIMIT)


def in_vmem(array):
    return pltpu.with_memory_space_constraint(array, pltpu.VMEM)


def body(n_row, n_col, blocks, slot_cols, counts, demand, value_added):
    rows, slots, size, _ = blocks.shape
    width = demand.shape[1]
    groups = demand.shape[0] // size
    group_devices = n_row // n_col
    paired = n_col == 2 and n_row == 16 and rows % 2 == 0
    half = rows // 2
    counts = counts.reshape(rows)

    sums, held = pl.pallas_call(
        sums_kernel,
        name="column_sums",
        out_shape=(
            jax.ShapeDtypeStruct((groups, size), jnp.float32),
            pltpu.VMEM(blocks.shape, blocks.dtype),
        ),
        in_specs=[SMEM, SMEM, pl.BlockSpec(memory_space=pltpu.HBM)],
        out_specs=(VMEM, VMEM),
        scratch_shapes=[pltpu.VMEM((groups + 1, 8, size), jnp.float32), pltpu.SemaphoreType.DMA((rows,))],
        compiler_params=PARAMS,
    )(slot_cols, counts, pltpu.with_memory_space_constraint(blocks, pltpu.HBM))

    def flip(array, mask):
        return lax.ppermute(array, "row", [(i, i ^ mask) for i in range(n_row)])

    def swap(array):
        return lax.ppermute(array, "col", [(0, 1), (1, 0)])

    if paired:
        for masks in ((1, 2, 3), (4, 8, 12)):
            sums = sums.astype(jnp.bfloat16)
            parts = [sums] + [flip(sums, m) for m in masks]
            sums = functools.reduce(jnp.add, [part.astype(jnp.float32) for part in parts])
    else:
        sums = lax.psum(sums, "row")

    def first_layer(sending, count, dtype, held):
        return pl.pallas_call(
            functools.partial(first_kernel, sending),
            name="first_layer",
            out_shape=(
                jax.ShapeDtypeStruct((count, size, width), dtype),
                pltpu.VMEM(blocks.shape, blocks.dtype),
            ),
            in_specs=[SMEM, SMEM, VMEM, VMEM, VMEM, VMEM],
            out_specs=(VMEM, VMEM),
            scratch_shapes=[
                pltpu.VMEM((groups, 1, size), jnp.float32),
                pltpu.VMEM((count, size, width), jnp.float32),
            ],
            input_output_aliases={5: 1},
            compiler_params=PARAMS,
        )(
            slot_cols,
            counts,
            sums[None],
            value_added.reshape(groups, size),
            demand.reshape(groups, size, width),
            in_vmem(held),
        )

    def second_call(kernel, count, coefs, own, sources, keep_sources):
        dtype = jnp.bfloat16 if paired else jnp.float32
        out = jax.ShapeDtypeStruct((count, size, width), dtype)
        return pl.pallas_call(
            kernel,
            name="second_layer",
            out_shape=(out, jax.ShapeDtypeStruct((groups, size, width), jnp.bfloat16)) if keep_sources else out,
            in_specs=[SMEM, SMEM] + [VMEM] * (2 + len(sources)),
            out_specs=(VMEM, VMEM) if keep_sources else VMEM,
            scratch_shapes=[pltpu.VMEM((count, size, width), jnp.float32)],
            compiler_params=PARAMS,
        )(slot_cols, counts, in_vmem(coefs), own, *sources)

    if not paired:
        group = lax.axis_index("col")
        partial, coefs = first_layer(None, rows, jnp.float32, held)
        layer_one = lax.psum(partial, "col").astype(jnp.bfloat16)
        gathered = lax.all_gather(layer_one, "row", axis=0, tiled=True)
        source = lax.dynamic_slice_in_dim(gathered, group * groups, groups, 0)
        partial = second_call(second_kernel, rows, coefs, layer_one, [source], False)
        return lax.psum(partial, "col").astype(jnp.bfloat16).reshape(rows * size, width)

    sent, coefs = first_layer(True, half, jnp.bfloat16, held)
    arrived = swap(sent)
    kept, coefs = first_layer(False, half, jnp.float32, coefs)
    own = (kept + arrived.astype(jnp.float32)).astype(jnp.bfloat16)

    crossed = flip(own, group_devices)
    piece = jax.ShapeDtypeStruct(own.shape, own.dtype)
    home, away = pl.pallas_call(
        sort_kernel,
        name="home_and_away",
        out_shape=(piece, piece),
        in_specs=[VMEM, VMEM],
        out_specs=(VMEM, VMEM),
        compiler_params=PARAMS,
    )(own, crossed)
    away = swap(away)
    home_y, home_z = flip(home, 2), flip(home, 4)
    away_y, away_z = flip(away, 2), flip(away, 4)
    home_yz, away_yz = flip(home_z, 2), flip(away_y, 4)
    pieces = []
    for pair in ((home, away), (home_y, away_y), (home_z, away_z), (home_yz, away_yz)):
        pieces += [*pair, flip(pair[0], 1), flip(pair[1], 1)]

    part_a, source = second_call(functools.partial(second_part_kernel, 0), half, coefs, own, pieces, True)
    other_a = swap(part_a)
    part_b = second_call(functools.partial(second_part_kernel, 1), half, coefs, own, [source], False)
    other_b = swap(part_b)
    parts = [
        (mine.astype(jnp.float32) + other.astype(jnp.float32)).astype(jnp.bfloat16)
        for mine, other in ((part_a, other_a), (part_b, other_b))
    ]
    return jnp.concatenate(parts, axis=0).reshape(rows * size, width)


def solution(mesh):
    return jax.shard_map(
        functools.partial(body, mesh.shape["row"], mesh.shape["col"]),
        mesh=mesh,
        in_specs=(
            P("row", "col", None, None),
            P("row", "col"),
            P("row", "col"),
            P("col", None),
            P("col"),
        ),
        out_specs=P("row", None),
        check_vma=False,
    )
```

time: 87.3 us -> 69.1 us (0.79)
  local copies, waits for them, and re-layouts: 19 us -> 1.52 us
  starting transfers between devices: 18.1 us -> 24.2 us
  waiting for transfers between devices: 33.7 us -> 29.5 us
  Pallas kernels: 14 us -> 12 us
    unnamed x17 -> x12, local copies, waits for them, and re-layouts: 19 us -> 1.52 us
    ppermute x21, waiting for transfers between devices: 25.8 us -> 18.7 us  [flip(): return lax.ppermute(array, 'row', [(i, i ^ mask) for i in range(n_row)])]
    ppermute x21, starting transfers between devices: 14.7 us -> 21.1 us  [flip(): return lax.ppermute(array, 'row', [(i, i ^ mask) for i in range(n_row)])]
    ppermute x4, waiting for transfers between devices: 7.82 us -> 10.8 us  [swap(): return lax.ppermute(array, 'col', [(0, 1), (1, 0)])]
    pallas_call x4 -> x5, Pallas kernels: 10.6 us -> 8.78 us  [the longest x2 5.21 us: first_layer(): pl.pallas_call(functools.partial(first_kernel, sending), name='first_laye...]
  transfers between devices with their start and end apart: 25 -> 25, of which waited for: 13 -> 14; matrix products, arithmetic and copies ran while one was open for 0% -> 0% of each run, Pallas kernels for 6% -> 3%
where the time goes in v3:
time: 69.1 us; the launch traced here: 68.3 us
  waiting for transfers between devices  29.5 us (43%)
  starting transfers between devices  24.2 us (35%)
  Pallas kernels  12 us (17%)
  local copies, waits for them, and re-layouts  1.52 us (2%)
  other arithmetic  0.93 us (1%)
    ppermute x21, starting transfers between devices, flip(): return lax.ppermute(array, 'row', [(i, i ^ mask) for i in range(n_row)])  21.1 us
    ppermute x21, waiting for transfers between devices, flip(): return lax.ppermute(array, 'row', [(i, i ^ mask) for i in range(n_row)])  18.7 us
    ppermute x4, waiting for transfers between devices, swap(): return lax.ppermute(array, 'col', [(0, 1), (1, 0)])  10.8 us
    pallas_call x2, Pallas kernels, first_layer(): pl.pallas_call(functools.partial(first_kernel, sending), name='first_laye...  5.21 us
    pallas_call x2, Pallas kernels, second_call(): pl.pallas_call(kernel, name='second_layer', out_shape=(out, jax.ShapeDtyp...  3.56 us
    pallas_call x1, Pallas kernels, body(): pl.pallas_call(sums_kernel, name='column_sums', out_shape=(jax.ShapeDtype...  3.19 us
    ppermute x4, starting transfers between devices, swap(): return lax.ppermute(array, 'col', [(0, 1), (1, 0)])  3.17 us
    unnamed x12, local copies, waits for them, and re-layouts  1.52 us
  transfers between devices with their start and end apart: 25, of which 14 were waited for; matrix products, arithmetic and copies ran while one was open for 0% of the time, Pallas kernels for 3%

profile of v3, /device:TPU:0, one launch (start us, length us, event | category | flops | bytes accessed | tf_op | source)
XLA Modules:
  0.0 68.3 jit_solution(2210194707571307207)
XLA Ops:
  0.0 0.8 %copy-done.1 = s32[10,36]{1,0:T(8,128)S(1)} copy-done((s32[10,36]{1,0:T(8,128)S(1)}, s32[10,36]{1,0:T(8,128)}, u32[]{:S(2)}) %copy-start.1) | copy-done | bytes 1464
  0.9 0.7 copy-done.4
  1.5 3.2 %column_sums.1 = (f32[80,128]{1,0:T(8,128)S(1)}, bf16[10,36,128,128]{3,2,1,0:T(8,128)(2,1)S(1)}) custom-call(s32[10,36]{1,0:T(8,128)S(1)} %copy-done.1, s32[10]{0:T(128)S(1)} %bitcast.10, bf16[10,36,128,128]{3,2,1,0:T(8,128)(2,1)} %blocks_ref.1), custom_call_target="tpu_custom_call" | custom-call | tf_op jit(solution)/shard_map/column_sums/pallas_call | solution.py:178
  4.7 3.1 %collective-permute-start.1 = (bf16[80,128]{1,0:T(8,128)(2,1)S(1)}, bf16[80,128]{1,0:T(8,128)(2,1)S(1)}, u32[]{:S(2)}, u32[]{:S(2)}) collective-permute-start(bf16[80,128]{1,0:T(8,128)(2,1)S(1)} %convert_element_type.54), channel_id=1, source_target_pairs={{0,4},{2,6},{4,0},{6,2},{8,12},{10,14},{12,8},{14,10},{16,20},{18,... | collective-permute-start | bytes 61448 | tf_op jit(solution)/shard_map/ppermute | solution.py:192
  7.8 0.0 collective-permute-start
  7.8 0.2 collective-permute-start.2
  8.0 1.6 %collective-permute-done.1 = bf16[80,128]{1,0:T(8,128)(2,1)S(1)} collective-permute-done((bf16[80,128]{1,0:T(8,128)(2,1)S(1)}, bf16[80,128]{1,0:T(8,128)(2,1)S(1)}, u32[]{:S(2)}, u32[]{:S(2)}) %collective-permute-start.1) | collective-permute-done | bytes 20512 | tf_op jit(solution)/shard_map/ppermute | solution.py:192
  9.6 0.0 collective-permute-done
  9.6 1.4 %collective-permute-done.2 = bf16[80,128]{1,0:T(8,128)(2,1)S(1)} collective-permute-done((bf16[80,128]{1,0:T(8,128)(2,1)S(1)}, bf16[80,128]{1,0:T(8,128)(2,1)S(1)}, u32[]{:S(2)}, u32[]{:S(2)}) %collective-permute-start.2) | collective-permute-done | bytes 20512 | tf_op jit(solution)/shard_map/ppermute | solution.py:192
  11.1 3.2 %collective-permute-start.5 = (bf16[80,128]{1,0:T(8,128)(2,1)S(1)}, bf16[80,128]{1,0:T(8,128)(2,1)S(1)}, u32[]{:S(2)}, u32[]{:S(2)}) collective-permute-start(bf16[80,128]{1,0:T(8,128)(2,1)S(1)} %add_convert_fusion.3), channel_id=1, source_target_pairs={{0,24},{2,26},{4,28},{6,30},{8,16},{10,18},{12,20},{14,22},{16,8},... | collective-permute-start | bytes 61448 | tf_op jit(solution)/shard_map/ppermute | solution.py:192
  14.2 0.1 collective-permute-start.4
  14.3 1.2 %collective-permute-start.3 = (bf16[80,128]{1,0:T(8,128)(2,1)S(1)}, bf16[80,128]{1,0:T(8,128)(2,1)S(1)}, u32[]{:S(2)}, u32[]{:S(2)}) collective-permute-start(bf16[80,128]{1,0:T(8,128)(2,1)S(1)} %add_convert_fusion.3), channel_id=1, source_target_pairs={{0,8},{2,10},{4,12},{6,14},{8,0},{10,2},{12,4},{14,6},{16,24},{18,... | collective-permute-start | bytes 61448 | tf_op jit(solution)/shard_map/ppermute | solution.py:192
  15.5 1.2 %collective-permute-done.5 = bf16[80,128]{1,0:T(8,128)(2,1)S(1)} collective-permute-done((bf16[80,128]{1,0:T(8,128)(2,1)S(1)}, bf16[80,128]{1,0:T(8,128)(2,1)S(1)}, u32[]{:S(2)}, u32[]{:S(2)}) %collective-permute-start.5) | collective-permute-done | bytes 20512 | tf_op jit(solution)/shard_map/ppermute | solution.py:192
  16.7 2.2 %collective-permute-done.4 = bf16[80,128]{1,0:T(8,128)(2,1)S(1)} collective-permute-done((bf16[80,128]{1,0:T(8,128)(2,1)S(1)}, bf16[80,128]{1,0:T(8,128)(2,1)S(1)}, u32[]{:S(2)}, u32[]{:S(2)}) %collective-permute-start.4) | collective-permute-done | bytes 20512 | tf_op jit(solution)/shard_map/ppermute | solution.py:192
  18.9 0.0 collective-permute-done.3
  19.0 0.0 copy-done
  19.0 0.0 copy-done.3
  19.0 0.0 copy-start.2
  19.0 0.0 copy-start.5
  19.0 2.9 %first_layer.2 = (bf16[5,128,128]{2,1,0:T(8,128)(2,1)S(1)}, bf16[10,36,128,128]{3,2,1,0:T(8,128)(2,1)S(1)}) custom-call(s32[10,36]{1,0:T(8,128)S(1)} %copy-done.1, s32[10]{0:T(128)S(1)} %bitcast.11, f32[1,80,128]{2,1,0:T(8,128)S(1)} %add_bitcast_fusion.sums_ref, f32[80,128]{1,0:T(8,128)S(1)} %bitcast.8, ...), custom_call_target="tpu_custom_call", output_to_operand_aliasing={{1}: (5, {})} | custom-call | tf_op jit(solution)/shard_map/first_layer/pallas_call | solution.py:206
  21.9 1.0 %collective-permute-start.6 = (bf16[5,128,128]{2,1,0:T(8,128)(2,1)S(1)}, bf16[5,128,128]{2,1,0:T(8,128)(2,1)S(1)}, u32[]{:S(2)}, u32[]{:S(2)}) collective-permute-start(bf16[5,128,128]{2,1,0:T(8,128)(2,1)S(1)} %get-tuple-element.20), channel_id=1, source_target_pairs={{0,1},{1,0},{2,3},{3,2},{4,5},{5,4},{6,7},{7,6},{8,9},{9,8},{10,11... | collective-permute-start | bytes 491528 | tf_op jit(solution)/shard_map/ppermute | solution.py:195
  22.9 2.3 %first_layer.3 = (f32[5,128,128]{2,1,0:T(8,128)S(1)}, bf16[10,36,128,128]{3,2,1,0:T(8,128)(2,1)S(1)}) custom-call(s32[10,36]{1,0:T(8,128)S(1)} %copy-done.1, s32[10]{0:T(128)S(1)} %bitcast.12, f32[1,80,128]{2,1,0:T(8,128)S(1)} %add_bitcast_fusion.sums_ref, f32[80,128]{1,0:T(8,128)S(1)} %bitcast.9, ...), custom_call_target="tpu_custom_call", output_to_operand_aliasing={{1}: (5, {})} | custom-call | tf_op jit(solution)/shard_map/first_layer/pallas_call | solution.py:206
  25.2 2.1 %collective-permute-done.6 = bf16[5,128,128]{2,1,0:T(8,128)(2,1)S(1)} collective-permute-done((bf16[5,128,128]{2,1,0:T(8,128)(2,1)S(1)}, bf16[5,128,128]{2,1,0:T(8,128)(2,1)S(1)}, u32[]{:S(2)}, u32[]{:S(2)}) %collective-permute-start.6) | collective-permute-done | bytes 163872 | tf_op jit(solution)/shard_map/ppermute | solution.py:195
  27.4 1.6 %collective-permute-start.7 = (bf16[5,128,128]{2,1,0:T(8,128)(2,1)S(1)}, bf16[5,128,128]{2,1,0:T(8,128)(2,1)S(1)}, u32[]{:S(2)}, u32[]{:S(2)}) collective-permute-start(bf16[5,128,128]{2,1,0:T(8,128)(2,1)S(1)} %add_convert_fusion.2.own_ref), channel_id=1, source_target_pairs={{0,16},{2,18},{4,20},{6,22},{8,24},{10,26},{12,28},{14,30},{16,0},... | collective-permute-start | bytes 491528 | tf_op jit(solution)/shard_map/ppermute | solution.py:192
  29.0 6.4 %collective-permute-done.7.crossed_ref = bf16[5,128,128]{2,1,0:T(8,128)(2,1)S(1)} collective-permute-done((bf16[5,128,128]{2,1,0:T(8,128)(2,1)S(1)}, bf16[5,128,128]{2,1,0:T(8,128)(2,1)S(1)}, u32[]{:S(2)}, u32[]{:S(2)}) %collective-permute-start.7) | collective-permute-done | bytes 163872 | tf_op jit(solution)/shard_map/ppermute | solution.py:192
  35.5 0.1 collective-permute-start.8
  35.5 2.0 %collective-permute-start.15 = (bf16[5,128,128]{2,1,0:T(8,128)(2,1)S(1)}, bf16[5,128,128]{2,1,0:T(8,128)(2,1)S(1)}, u32[]{:S(2)}, u32[]{:S(2)}) collective-permute-start(bf16[5,128,128]{2,1,0:T(8,128)(2,1)S(1)} %get-tuple-element.21.rest_0_), channel_id=1, source_target_pairs={{0,8},{2,10},{4,12},{6,14},{8,0},{10,2},{12,4},{14,6},{16,24},{18,... | collective-permute-start | bytes 491528 | tf_op jit(solution)/shard_map/ppermute | solution.py:192
  37.5 1.8 %collective-permute-start.11 = (bf16[5,128,128]{2,1,0:T(8,128)(2,1)S(1)}, bf16[5,128,128]{2,1,0:T(8,128)(2,1)S(1)}, u32[]{:S(2)}, u32[]{:S(2)}) collective-permute-start(bf16[5,128,128]{2,1,0:T(8,128)(2,1)S(1)} %get-tuple-element.21.rest_0_), channel_id=1, source_target_pairs={{0,4},{2,6},{4,0},{6,2},{8,12},{10,14},{12,8},{14,10},{16,20},{18,... | collective-permute-start | bytes 491528 | tf_op jit(solution)/shard_map/ppermute | solution.py:192
  39.3 0.0 collective-permute-start.9
  39.3 1.6 %collective-permute-done.8.rest_1_ = bf16[5,128,128]{2,1,0:T(8,128)(2,1)S(1)} collective-permute-done((bf16[5,128,128]{2,1,0:T(8,128)(2,1)S(1)}, bf16[5,128,128]{2,1,0:T(8,128)(2,1)S(1)}, u32[]{:S(2)}, u32[]{:S(2)}) %collective-permute-start.8) | collective-permute-done | bytes 163872 | tf_op jit(solution)/shard_map/ppermute | solution.py:195
  40.8 1.7 %collective-permute-start.12 = (bf16[5,128,128]{2,1,0:T(8,128)(2,1)S(1)}, bf16[5,128,128]{2,1,0:T(8,128)(2,1)S(1)}, u32[]{:S(2)}, u32[]{:S(2)}) collective-permute-start(bf16[5,128,128]{2,1,0:T(8,128)(2,1)S(1)} %collective-permute-done.8.rest_1_), channel_id=1, source_target_pairs={{0,4},{2,6},{4,0},{6,2},{8,12},{10,14},{12,8},{14,10},{16,20},{18,... | collective-permute-start | bytes 491528 | tf_op jit(solution)/shard_map/ppermute | solution.py:192
  42.6 0.0 collective-permute-start.16
  42.6 0.0 collective-permute-done.15.rest_8_
  42.6 0.0 collective-permute-start.10
  42.6 1.1 %collective-permute-done.11.rest_4_ = bf16[5,128,128]{2,1,0:T(8,128)(2,1)S(1)} collective-permute-done((bf16[5,128,128]{2,1,0:T(8,128)(2,1)S(1)}, bf16[5,128,128]{2,1,0:T(8,128)(2,1)S(1)}, u32[]{:S(2)}, u32[]{:S(2)}) %collective-permute-start.11) | collective-permute-done | bytes 163872 | tf_op jit(solution)/shard_map/ppermute | solution.py:192
  43.7 2.5 %collective-permute-start.19 = (bf16[5,128,128]{2,1,0:T(8,128)(2,1)S(1)}, bf16[5,128,128]{2,1,0:T(8,128)(2,1)S(1)}, u32[]{:S(2)}, u32[]{:S(2)}) collective-permute-start(bf16[5,128,128]{2,1,0:T(8,128)(2,1)S(1)} %collective-permute-done.15.rest_8_), channel_id=1, source_target_pairs={{0,4},{2,6},{4,0},{6,2},{8,12},{10,14},{12,8},{14,10},{16,20},{18,... | collective-permute-start | bytes 491528 | tf_op jit(solution)/shard_map/ppermute | solution.py:192
  46.2 0.0 collective-permute-done.9.rest_2_
  46.2 0.0 collective-permute-start.17
  46.2 0.4 collective-permute-done.12.rest_5_
  46.6 2.7 %collective-permute-start.20 = (bf16[5,128,128]{2,1,0:T(8,128)(2,1)S(1)}, bf16[5,128,128]{2,1,0:T(8,128)(2,1)S(1)}, u32[]{:S(2)}, u32[]{:S(2)}) collective-permute-start(bf16[5,128,128]{2,1,0:T(8,128)(2,1)S(1)} %collective-permute-done.12.rest_5_), channel_id=1, source_target_pairs={{0,8},{2,10},{4,12},{6,14},{8,0},{10,2},{12,4},{14,6},{16,24},{18,... | collective-permute-start | bytes 491528 | tf_op jit(solution)/shard_map/ppermute | solution.py:192
  49.2 0.0 collective-permute-done.16.rest_9_
  49.2 0.0 collective-permute-start.13
  49.2 0.0 collective-permute-done.10.rest_3_
  49.2 0.5 collective-permute-start.14
  49.8 0.1 collective-permute-done.19.rest_12_
  49.9 0.0 collective-permute-start.18
  49.9 0.0 collective-permute-done.17.rest_10_
  49.9 0.5 collective-permute-start.21
  50.4 2.9 %collective-permute-done.20.rest_13_ = bf16[5,128,128]{2,1,0:T(8,128)(2,1)S(1)} collective-permute-done((bf16[5,128,128]{2,1,0:T(8,128)(2,1)S(1)}, bf16[5,128,128]{2,1,0:T(8,128)(2,1)S(1)}, u32[]{:S(2)}, u32[]{:S(2)}) %collective-permute-start.20) | collective-permute-done | bytes 163872 | tf_op jit(solution)/shard_map/ppermute | solution.py:192
  53.3 0.0 collective-permute-start.22
  53.3 0.0 collective-permute-done.13.rest_6_
  53.3 0.0 collective-permute-done.18.rest_11_
  53.3 0.0 collective-permute-done.14.rest_7_
  53.3 0.0 collective-permute-done.21.rest_14_
  53.3 1.4 %collective-permute-done.22.rest_15_ = bf16[5,128,128]{2,1,0:T(8,128)(2,1)S(1)} collective-permute-done((bf16[5,128,128]{2,1,0:T(8,128)(2,1)S(1)}, bf16[5,128,128]{2,1,0:T(8,128)(2,1)S(1)}, u32[]{:S(2)}, u32[]{:S(2)}) %collective-permute-start.22) | collective-permute-done | bytes 163872 | tf_op jit(solution)/shard_map/ppermute | solution.py:192
  54.7 0.0 copy-done.2
  54.7 0.0 copy-done.5
  54.7 1.6 %second_layer.2 = (bf16[5,128,128]{2,1,0:T(8,128)(2,1)S(1)}, bf16[80,128,128]{2,1,0:T(8,128)(2,1)S(1)}) custom-call(s32[10,36]{1,0:T(8,128)S(1)} %copy-done.2, s32[10]{0:T(128)S(1)} %bitcast.13, bf16[10,36,128,128]{3,2,1,0:T(8,128)(2,1)S(1)} %get-tuple-element.18.coef_ref, bf16[5,128,128]{2,1,0:T(8,128)(2,1)S(1)} %add_convert_fusion.2.own_ref, ...), custom_call_target="tpu_custom_call" | custom-call | tf_op jit(solution)/shard_map/second_layer/pallas_call | solution.py:233
  56.3 2.0 %second_layer.3 = bf16[5,128,128]{2,1,0:T(8,128)(2,1)S(1)} custom-call(s32[10,36]{1,0:T(8,128)S(1)} %copy-done.2, s32[10]{0:T(128)S(1)} %bitcast.14, bf16[10,36,128,128]{3,2,1,0:T(8,128)(2,1)S(1)} %get-tuple-element.18.coef_ref, bf16[5,128,128]{2,1,0:T(8,128)(2,1)S(1)} %add_convert_fusion.2.own_ref, bf16[80,128,128]{2,1,0:T(8,128)(2,1)S(1)} %get-tuple-element.24.rest_0_), custom_call_target="tpu_custom_call" | custom-call | tf_op jit(solution)/shard_map/second_layer/pallas_call | solution.py:233
  58.2 1.2 %collective-permute-start.24 = (bf16[5,128,128]{2,1,0:T(8,128)(2,1)S(1)}, bf16[5,128,128]{2,1,0:T(8,128)(2,1)S(1)}, u32[]{:S(2)}, u32[]{:S(2)}) collective-permute-start(bf16[5,128,128]{2,1,0:T(8,128)(2,1)S(1)} %second_layer.3), channel_id=1, source_target_pairs={{0,1},{1,0},{2,3},{3,2},{4,5},{5,4},{6,7},{7,6},{8,9},{9,8},{10,11... | collective-permute-start | bytes 491528 | tf_op jit(solution)/shard_map/ppermute | solution.py:195
  59.4 0.9 %collective-permute-start.23 = (bf16[5,128,128]{2,1,0:T(8,128)(2,1)S(1)}, bf16[5,128,128]{2,1,0:T(8,128)(2,1)S(1)}, u32[]{:S(2)}, u32[]{:S(2)}) collective-permute-start(bf16[5,128,128]{2,1,0:T(8,128)(2,1)S(1)} %get-tuple-element.23), channel_id=1, source_target_pairs={{0,1},{1,0},{2,3},{3,2},{4,5},{5,4},{6,7},{7,6},{8,9},{9,8},{10,11... | collective-permute-start | bytes 491528 | tf_op jit(solution)/shard_map/ppermute | solution.py:195
  60.3 5.1 %collective-permute-done.24 = bf16[5,128,128]{2,1,0:T(8,128)(2,1)S(1)} collective-permute-done((bf16[5,128,128]{2,1,0:T(8,128)(2,1)S(1)}, bf16[5,128,128]{2,1,0:T(8,128)(2,1)S(1)}, u32[]{:S(2)}, u32[]{:S(2)}) %collective-permute-start.24) | collective-permute-done | bytes 163872 | tf_op jit(solution)/shard_map/ppermute | solution.py:195
  65.5 2.0 %collective-permute-done.23 = bf16[5,128,128]{2,1,0:T(8,128)(2,1)S(1)} collective-permute-done((bf16[5,128,128]{2,1,0:T(8,128)(2,1)S(1)}, bf16[5,128,128]{2,1,0:T(8,128)(2,1)S(1)}, u32[]{:S(2)}, u32[]{:S(2)}) %collective-permute-start.23) | collective-permute-done | bytes 163872 | tf_op jit(solution)/shard_map/ppermute | solution.py:195
  67.6 0.8 %pad_maximum_fusion = bf16[10,128,128]{2,1,0:T(8,128)(2,1)} fusion(bf16[5,128,128]{2,1,0:T(8,128)(2,1)S(1)} %add_convert_fusion, bf16[5,128,128]{2,1,0:T(8,128)(2,1)S(1)} %add_convert_fusion.1), kind=kLoop, calls=%fused_computation | loop fusion | flops 163840 | bytes 655360 | tf_op jit(solution)/shard_map/concatenate | solution.py:283
  (11 shorter events, 0.2 us)
Async XLA Ops:
  0.0 19.0 %copy-start = (bf16[10240,128]{1,0:T(8,128)(2,1)S(1)}, bf16[10240,128]{1,0:T(8,128)(2,1)}, u32[]{:S(2)}) copy-start(bf16[10240,128]{1,0:T(8,128)(2,1)} %param.8) | copy-start | bytes 7864324
  0.0 0.8 %copy-start.1 = (s32[10,36]{1,0:T(8,128)S(1)}, s32[10,36]{1,0:T(8,128)}, u32[]{:S(2)}) copy-start(s32[10,36]{1,0:T(8,128)} %cols_ref.9) | copy-start | bytes 4324
  0.8 0.7 copy-start.4
  1.5 17.5 %copy-start.3 = (f32[10240]{0:T(1024)S(1)}, f32[10240]{0:T(1024)}, u32[]{:S(2)}) copy-start(f32[10240]{0:T(1024)} %param.9) | copy-start | bytes 122884
  4.7 4.9 %collective-permute-start.1 = (bf16[80,128]{1,0:T(8,128)(2,1)S(1)}, bf16[80,128]{1,0:T(8,128)(2,1)S(1)}, u32[]{:S(2)}, u32[]{:S(2)}) collective-permute-start(bf16[80,128]{1,0:T(8,128)(2,1)S(1)} %convert_element_type.54), channel_id=1, source_target_pairs={{0,4},{2,6},{4,0},{6,2},{8,12},{10,14},{12,8},{14,10},{16,20},{18,... | collective-permute-start | bytes 61448 | tf_op jit(solution)/shard_map/ppermute | solution.py:192
  7.8 1.8 %collective-permute-start = (bf16[80,128]{1,0:T(8,128)(2,1)S(1)}, bf16[80,128]{1,0:T(8,128)(2,1)S(1)}, u32[]{:S(2)}, u32[]{:S(2)}) collective-permute-start(bf16[80,128]{1,0:T(8,128)(2,1)S(1)} %convert_element_type.54), channel_id=1, source_target_pairs={{0,2},{2,0},{4,6},{6,4},{8,10},{10,8},{12,14},{14,12},{16,18},{18,... | collective-permute-start | bytes 61448 | tf_op jit(solution)/shard_map/ppermute | solution.py:192
  7.8 3.2 %collective-permute-start.2 = (bf16[80,128]{1,0:T(8,128)(2,1)S(1)}, bf16[80,128]{1,0:T(8,128)(2,1)S(1)}, u32[]{:S(2)}, u32[]{:S(2)}) collective-permute-start(bf16[80,128]{1,0:T(8,128)(2,1)S(1)} %convert_element_type.54), channel_id=1, source_target_pairs={{0,6},{2,4},{4,2},{6,0},{8,14},{10,12},{12,10},{14,8},{16,22},{18,... | collective-permute-start | bytes 61448 | tf_op jit(solution)/shard_map/ppermute | solution.py:192
  11.1 5.6 %collective-permute-start.5 = (bf16[80,128]{1,0:T(8,128)(2,1)S(1)}, bf16[80,128]{1,0:T(8,128)(2,1)S(1)}, u32[]{:S(2)}, u32[]{:S(2)}) collective-permute-start(bf16[80,128]{1,0:T(8,128)(2,1)S(1)} %add_convert_fusion.3), channel_id=1, source_target_pairs={{0,24},{2,26},{4,28},{6,30},{8,16},{10,18},{12,20},{14,22},{16,8},... | collective-permute-start | bytes 61448 | tf_op jit(solution)/shard_map/ppermute | solution.py:192
  14.2 4.7 %collective-permute-start.4 = (bf16[80,128]{1,0:T(8,128)(2,1)S(1)}, bf16[80,128]{1,0:T(8,128)(2,1)S(1)}, u32[]{:S(2)}, u32[]{:S(2)}) collective-permute-start(bf16[80,128]{1,0:T(8,128)(2,1)S(1)} %add_convert_fusion.3), channel_id=1, source_target_pairs={{0,16},{2,18},{4,20},{6,22},{8,24},{10,26},{12,28},{14,30},{16,0},... | collective-permute-start | bytes 61448 | tf_op jit(solution)/shard_map/ppermute | solution.py:192
  14.3 4.6 %collective-permute-start.3 = (bf16[80,128]{1,0:T(8,128)(2,1)S(1)}, bf16[80,128]{1,0:T(8,128)(2,1)S(1)}, u32[]{:S(2)}, u32[]{:S(2)}) collective-permute-start(bf16[80,128]{1,0:T(8,128)(2,1)S(1)} %add_convert_fusion.3), channel_id=1, source_target_pairs={{0,8},{2,10},{4,12},{6,14},{8,0},{10,2},{12,4},{14,6},{16,24},{18,... | collective-permute-start | bytes 61448 | tf_op jit(solution)/shard_map/ppermute | solution.py:192
  19.0 35.7 %copy-start.2 = (s32[10,36]{1,0:T(8,128)S(1)}, s32[10,36]{1,0:T(8,128)}, u32[]{:S(2)}) copy-start(s32[10,36]{1,0:T(8,128)} %cols_ref.9) | copy-start | bytes 4324
  19.0 35.7 %copy-start.5 = (s32[10,1]{0,1:T(1,128)S(1)}, s32[10,1]{0,1:T(1,128)}, u32[]{:S(2)}) copy-start(s32[10,1]{0,1:T(1,128)} %param.7) | copy-start | bytes 124
  21.9 5.4 %collective-permute-start.6 = (bf16[5,128,128]{2,1,0:T(8,128)(2,1)S(1)}, bf16[5,128,128]{2,1,0:T(8,128)(2,1)S(1)}, u32[]{:S(2)}, u32[]{:S(2)}) collective-permute-start(bf16[5,128,128]{2,1,0:T(8,128)(2,1)S(1)} %get-tuple-element.20), channel_id=1, source_target_pairs={{0,1},{1,0},{2,3},{3,2},{4,5},{5,4},{6,7},{7,6},{8,9},{9,8},{10,11... | collective-permute-start | bytes 491528 | tf_op jit(solution)/shard_map/ppermute | solution.py:195
  27.4 8.1 %collective-permute-start.7 = (bf16[5,128,128]{2,1,0:T(8,128)(2,1)S(1)}, bf16[5,128,128]{2,1,0:T(8,128)(2,1)S(1)}, u32[]{:S(2)}, u32[]{:S(2)}) collective-permute-start(bf16[5,128,128]{2,1,0:T(8,128)(2,1)S(1)} %add_convert_fusion.2.own_ref), channel_id=1, source_target_pairs={{0,16},{2,18},{4,20},{6,22},{8,24},{10,26},{12,28},{14,30},{16,0},... | collective-permute-start | bytes 491528 | tf_op jit(solution)/shard_map/ppermute | solution.py:192
  35.5 5.4 %collective-permute-start.8 = (bf16[5,128,128]{2,1,0:T(8,128)(2,1)S(1)}, bf16[5,128,128]{2,1,0:T(8,128)(2,1)S(1)}, u32[]{:S(2)}, u32[]{:S(2)}) collective-permute-start(bf16[5,128,128]{2,1,0:T(8,128)(2,1)S(1)} %get-tuple-element.22), channel_id=1, source_target_pairs={{0,1},{1,0},{2,3},{3,2},{4,5},{5,4},{6,7},{7,6},{8,9},{9,8},{10,11... | collective-permute-start | bytes 491528 | tf_op jit(solution)/shard_map/ppermute | solution.py:195
  35.5 7.0 %collective-permute-start.15 = (bf16[5,128,128]{2,1,0:T(8,128)(2,1)S(1)}, bf16[5,128,128]{2,1,0:T(8,128)(2,1)S(1)}, u32[]{:S(2)}, u32[]{:S(2)}) collective-permute-start(bf16[5,128,128]{2,1,0:T(8,128)(2,1)S(1)} %get-tuple-element.21.rest_0_), channel_id=1, source_target_pairs={{0,8},{2,10},{4,12},{6,14},{8,0},{10,2},{12,4},{14,6},{16,24},{18,... | collective-permute-start | bytes 491528 | tf_op jit(solution)/shard_map/ppermute | solution.py:192
  37.5 6.2 %collective-permute-start.11 = (bf16[5,128,128]{2,1,0:T(8,128)(2,1)S(1)}, bf16[5,128,128]{2,1,0:T(8,128)(2,1)S(1)}, u32[]{:S(2)}, u32[]{:S(2)}) collective-permute-start(bf16[5,128,128]{2,1,0:T(8,128)(2,1)S(1)} %get-tuple-element.21.rest_0_), channel_id=1, source_target_pairs={{0,4},{2,6},{4,0},{6,2},{8,12},{10,14},{12,8},{14,10},{16,20},{18,... | collective-permute-start | bytes 491528 | tf_op jit(solution)/shard_map/ppermute | solution.py:192
  39.3 6.9 %collective-permute-start.9 = (bf16[5,128,128]{2,1,0:T(8,128)(2,1)S(1)}, bf16[5,128,128]{2,1,0:T(8,128)(2,1)S(1)}, u32[]{:S(2)}, u32[]{:S(2)}) collective-permute-start(bf16[5,128,128]{2,1,0:T(8,128)(2,1)S(1)} %get-tuple-element.21.rest_0_), channel_id=1, source_target_pairs={{0,2},{2,0},{4,6},{6,4},{8,10},{10,8},{12,14},{14,12},{16,18},{18,... | collective-permute-start | bytes 491528 | tf_op jit(solution)/shard_map/ppermute | solution.py:192
  40.8 5.7 %collective-permute-start.12 = (bf16[5,128,128]{2,1,0:T(8,128)(2,1)S(1)}, bf16[5,128,128]{2,1,0:T(8,128)(2,1)S(1)}, u32[]{:S(2)}, u32[]{:S(2)}) collective-permute-start(bf16[5,128,128]{2,1,0:T(8,128)(2,1)S(1)} %collective-permute-done.8.rest_1_), channel_id=1, source_target_pairs={{0,4},{2,6},{4,0},{6,2},{8,12},{10,14},{12,8},{14,10},{16,20},{18,... | collective-permute-start | bytes 491528 | tf_op jit(solution)/shard_map/ppermute | solution.py:192
  42.6 6.7 %collective-permute-start.16 = (bf16[5,128,128]{2,1,0:T(8,128)(2,1)S(1)}, bf16[5,128,128]{2,1,0:T(8,128)(2,1)S(1)}, u32[]{:S(2)}, u32[]{:S(2)}) collective-permute-start(bf16[5,128,128]{2,1,0:T(8,128)(2,1)S(1)} %collective-permute-done.8.rest_1_), channel_id=1, source_target_pairs={{0,8},{2,10},{4,12},{6,14},{8,0},{10,2},{12,4},{14,6},{16,24},{18,... | collective-permute-start | bytes 491528 | tf_op jit(solution)/shard_map/ppermute | solution.py:192
  42.6 6.7 %collective-permute-start.10 = (bf16[5,128,128]{2,1,0:T(8,128)(2,1)S(1)}, bf16[5,128,128]{2,1,0:T(8,128)(2,1)S(1)}, u32[]{:S(2)}, u32[]{:S(2)}) collective-permute-start(bf16[5,128,128]{2,1,0:T(8,128)(2,1)S(1)} %collective-permute-done.8.rest_1_), channel_id=1, source_target_pairs={{0,2},{2,0},{4,6},{6,4},{8,10},{10,8},{12,14},{14,12},{16,18},{18,... | collective-permute-start | bytes 491528 | tf_op jit(solution)/shard_map/ppermute | solution.py:192
  43.7 6.2 %collective-permute-start.19 = (bf16[5,128,128]{2,1,0:T(8,128)(2,1)S(1)}, bf16[5,128,128]{2,1,0:T(8,128)(2,1)S(1)}, u32[]{:S(2)}, u32[]{:S(2)}) collective-permute-start(bf16[5,128,128]{2,1,0:T(8,128)(2,1)S(1)} %collective-permute-done.15.rest_8_), channel_id=1, source_target_pairs={{0,4},{2,6},{4,0},{6,2},{8,12},{10,14},{12,8},{14,10},{16,20},{18,... | collective-permute-start | bytes 491528 | tf_op jit(solution)/shard_map/ppermute | solution.py:192
  46.2 3.7 %collective-permute-start.17 = (bf16[5,128,128]{2,1,0:T(8,128)(2,1)S(1)}, bf16[5,128,128]{2,1,0:T(8,128)(2,1)S(1)}, u32[]{:S(2)}, u32[]{:S(2)}) collective-permute-start(bf16[5,128,128]{2,1,0:T(8,128)(2,1)S(1)} %collective-permute-done.15.rest_8_), channel_id=1, source_target_pairs={{0,2},{2,0},{4,6},{6,4},{8,10},{10,8},{12,14},{14,12},{16,18},{18,... | collective-permute-start | bytes 491528 | tf_op jit(solution)/shard_map/ppermute | solution.py:192
  46.6 6.7 %collective-permute-start.20 = (bf16[5,128,128]{2,1,0:T(8,128)(2,1)S(1)}, bf16[5,128,128]{2,1,0:T(8,128)(2,1)S(1)}, u32[]{:S(2)}, u32[]{:S(2)}) collective-permute-start(bf16[5,128,128]{2,1,0:T(8,128)(2,1)S(1)} %collective-permute-done.12.rest_5_), channel_id=1, source_target_pairs={{0,8},{2,10},{4,12},{6,14},{8,0},{10,2},{12,4},{14,6},{16,24},{18,... | collective-permute-start | bytes 491528 | tf_op jit(solution)/shard_map/ppermute | solution.py:192
  49.2 4.0 %collective-permute-start.13 = (bf16[5,128,128]{2,1,0:T(8,128)(2,1)S(1)}, bf16[5,128,128]{2,1,0:T(8,128)(2,1)S(1)}, u32[]{:S(2)}, u32[]{:S(2)}) collective-permute-start(bf16[5,128,128]{2,1,0:T(8,128)(2,1)S(1)} %collective-permute-done.11.rest_4_), channel_id=1, source_target_pairs={{0,2},{2,0},{4,6},{6,4},{8,10},{10,8},{12,14},{14,12},{16,18},{18,... | collective-permute-start | bytes 491528 | tf_op jit(solution)/shard_map/ppermute | solution.py:192
  49.2 4.0 %collective-permute-start.14 = (bf16[5,128,128]{2,1,0:T(8,128)(2,1)S(1)}, bf16[5,128,128]{2,1,0:T(8,128)(2,1)S(1)}, u32[]{:S(2)}, u32[]{:S(2)}) collective-permute-start(bf16[5,128,128]{2,1,0:T(8,128)(2,1)S(1)} %collective-permute-done.12.rest_5_), channel_id=1, source_target_pairs={{0,2},{2,0},{4,6},{6,4},{8,10},{10,8},{12,14},{14,12},{16,18},{18,... | collective-permute-start | bytes 491528 | tf_op jit(solution)/shard_map/ppermute | solution.py:192
  49.9 3.4 %collective-permute-start.18 = (bf16[5,128,128]{2,1,0:T(8,128)(2,1)S(1)}, bf16[5,128,128]{2,1,0:T(8,128)(2,1)S(1)}, u32[]{:S(2)}, u32[]{:S(2)}) collective-permute-start(bf16[5,128,128]{2,1,0:T(8,128)(2,1)S(1)} %collective-permute-done.16.rest_9_), channel_id=1, source_target_pairs={{0,2},{2,0},{4,6},{6,4},{8,10},{10,8},{12,14},{14,12},{16,18},{18,... | collective-permute-start | bytes 491528 | tf_op jit(solution)/shard_map/ppermute | solution.py:192
  49.9 3.4 %collective-permute-start.21 = (bf16[5,128,128]{2,1,0:T(8,128)(2,1)S(1)}, bf16[5,128,128]{2,1,0:T(8,128)(2,1)S(1)}, u32[]{:S(2)}, u32[]{:S(2)}) collective-permute-start(bf16[5,128,128]{2,1,0:T(8,128)(2,1)S(1)} %collective-permute-done.19.rest_12_), channel_id=1, source_target_pairs={{0,2},{2,0},{4,6},{6,4},{8,10},{10,8},{12,14},{14,12},{16,18},{18,... | collective-permute-start | bytes 491528 | tf_op jit(solution)/shard_map/ppermute | solution.py:192
  53.3 1.4 %collective-permute-start.22 = (bf16[5,128,128]{2,1,0:T(8,128)(2,1)S(1)}, bf16[5,128,128]{2,1,0:T(8,128)(2,1)S(1)}, u32[]{:S(2)}, u32[]{:S(2)}) collective-permute-start(bf16[5,128,128]{2,1,0:T(8,128)(2,1)S(1)} %collective-permute-done.20.rest_13_), channel_id=1, source_target_pairs={{0,2},{2,0},{4,6},{6,4},{8,10},{10,8},{12,14},{14,12},{16,18},{18,... | collective-permute-start | bytes 491528 | tf_op jit(solution)/shard_map/ppermute | solution.py:192
  58.2 7.2 %collective-permute-start.24 = (bf16[5,128,128]{2,1,0:T(8,128)(2,1)S(1)}, bf16[5,128,128]{2,1,0:T(8,128)(2,1)S(1)}, u32[]{:S(2)}, u32[]{:S(2)}) collective-permute-start(bf16[5,128,128]{2,1,0:T(8,128)(2,1)S(1)} %second_layer.3), channel_id=1, source_target_pairs={{0,1},{1,0},{2,3},{3,2},{4,5},{5,4},{6,7},{7,6},{8,9},{9,8},{10,11... | collective-permute-start | bytes 491528 | tf_op jit(solution)/shard_map/ppermute | solution.py:195
  59.4 8.1 %collective-permute-start.23 = (bf16[5,128,128]{2,1,0:T(8,128)(2,1)S(1)}, bf16[5,128,128]{2,1,0:T(8,128)(2,1)S(1)}, u32[]{:S(2)}, u32[]{:S(2)}) collective-permute-start(bf16[5,128,128]{2,1,0:T(8,128)(2,1)S(1)} %get-tuple-element.23), channel_id=1, source_target_pairs={{0,1},{1,0},{2,3},{3,2},{4,5},{5,4},{6,7},{7,6},{8,9},{9,8},{10,11... | collective-permute-start | bytes 491528 | tf_op jit(solution)/shard_map/ppermute | solution.py:195

commit v4 on v3

--- a/solution.py
+++ b/solution.py
@@ -18,7 +18,7 @@
     return lax.div(counts_ref[b] + (chunk - 1), chunk)
 
 
-def sums_kernel(cols_ref, counts_ref, blocks_ref, sums_ref, held_ref, acc_ref, sems):
+def sums_kernel(cols_hbm, counts_hbm, blocks_ref, sums_ref, held_ref, acc_ref, cols_ref, counts_ref, list_sems, sems):
     rows, slots, size, _ = blocks_ref.shape
     groups = sums_ref.shape[0]
     chunk = divisor(slots, 4)
@@ -27,16 +27,24 @@
         part = pl.ds(k * chunk, chunk)
         return pltpu.make_async_copy(blocks_ref.at[b, part], held_ref.at[b, part], sems.at[b])
 
+    counts_copy = pltpu.make_async_copy(counts_hbm, counts_ref, list_sems.at[0])
+    cols_copy = pltpu.make_async_copy(cols_hbm, cols_ref, list_sems.at[1])
+    counts_copy.start()
+    cols_copy.start()
+    for b in range(rows):
+        fetch(b, 0).start()
+    counts_copy.wait()
     for b in range(rows):
 
         def start(k, carry, b=b):
             fetch(b, k).start()
             return carry
 
-        lax.fori_loop(0, chunk_total(counts_ref, b, chunk), start, 0)
+        lax.fori_loop(1, chunk_total(counts_ref, b, chunk), start, 0)
     acc_ref[...] = jnp.zeros_like(acc_ref)
+    cols_copy.wait()
     for b in range(rows):
-        total = chunk_total(counts_ref, b, chunk)
+        total = jnp.maximum(chunk_total(counts_ref, b, chunk), 1)
 
         def finish(k, carry, b=b):
             fetch(b, k).wait()
@@ -114,9 +122,11 @@
 def second_part_kernel(which, cols_ref, counts_ref, coef_ref, own_ref, *rest):
     if which == 0:
         pieces, (out_ref, source_ref, acc_ref) = rest[:-3], rest[-3:]
-        part = pieces[0].shape[0]
+        part = out_ref.shape[0]
         for i, piece in enumerate(pieces):
-            source_ref[i * part : (i + 1) * part] = piece[...]
+            for place_yz in range(4):
+                at = (place_yz * 4 + i) * part
+                source_ref[at : at + part] = piece[place_yz * part : (place_yz + 1) * part]
     else:
         source_ref, out_ref, acc_ref = rest
     part = out_ref.shape[0]
@@ -160,6 +170,10 @@
 SMEM = pl.BlockSpec(memory_space=pltpu.SMEM)
 VMEM = pl.BlockSpec(memory_space=pltpu.VMEM)
 PARAMS = pltpu.CompilerParams(vmem_limit_bytes=VMEM_LIMIT)
+
+
+def cost(flops, bytes_accessed):
+    return pl.CostEstimate(flops=flops, bytes_accessed=bytes_accessed, transcendentals=0)
 
 
 def in_vmem(array):
@@ -182,11 +196,18 @@
             jax.ShapeDtypeStruct((groups, size), jnp.float32),
             pltpu.VMEM(blocks.shape, blocks.dtype),
         ),
-        in_specs=[SMEM, SMEM, pl.BlockSpec(memory_space=pltpu.HBM)],
+        in_specs=[pl.BlockSpec(memory_space=pltpu.HBM)] * 3,
         out_specs=(VMEM, VMEM),
-        scratch_shapes=[pltpu.VMEM((groups + 1, 8, size), jnp.float32), pltpu.SemaphoreType.DMA((rows,))],
+        scratch_shapes=[
+            pltpu.VMEM((groups + 1, 8, size), jnp.float32),
+            pltpu.SMEM(slot_cols.shape, jnp.int32),
+            pltpu.SMEM(counts.shape, jnp.int32),
+            pltpu.SemaphoreType.DMA((2,)),
+            pltpu.SemaphoreType.DMA((rows,)),
+        ],
         compiler_params=PARAMS,
-    )(slot_cols, counts, pltpu.with_memory_space_constraint(blocks, pltpu.HBM))
+        cost_estimate=cost(0, 4 * rows * size * size * slots),
+    )(*[pltpu.with_memory_space_constraint(array, pltpu.HBM) for array in (slot_cols, counts, blocks)])
 
     def flip(array, mask):
         return lax.ppermute(array, "row", [(i, i ^ mask) for i in range(n_row)])
@@ -201,6 +222,9 @@
             sums = functools.reduce(jnp.add, [part.astype(jnp.float32) for part in parts])
     else:
         sums = lax.psum(sums, "row")
+
+    def layer_cost(count):
+        return cost(2 * count * slots * size * size * width, count * slots * size * size * 2)
 
     def first_layer(sending, count, dtype, held):
         return pl.pallas_call(
@@ -218,6 +242,7 @@
             ],
             input_output_aliases={5: 1},
             compiler_params=PARAMS,
+            cost_estimate=layer_cost(count),
         )(
             slot_cols,
             counts,
@@ -238,6 +263,7 @@
             out_specs=(VMEM, VMEM) if keep_sources else VMEM,
             scratch_shapes=[pltpu.VMEM((count, size, width), jnp.float32)],
             compiler_params=PARAMS,
+            cost_estimate=layer_cost(count),
         )(slot_cols, counts, in_vmem(coefs), own, *sources)
 
     if not paired:
@@ -265,12 +291,11 @@
         compiler_params=PARAMS,
     )(own, crossed)
     away = swap(away)
-    home_y, home_z = flip(home, 2), flip(home, 4)
-    away_y, away_z = flip(away, 2), flip(away, 4)
-    home_yz, away_yz = flip(home_z, 2), flip(away_y, 4)
-    pieces = []
-    for pair in ((home, away), (home_y, away_y), (home_z, away_z), (home_yz, away_yz)):
-        pieces += [*pair, flip(pair[0], 1), flip(pair[1], 1)]
+    def spread(piece):
+        return jnp.concatenate([piece] + [flip(piece, mask) for mask in (2, 4, 6)], axis=0)
+
+    home, away = spread(home), spread(away)
+    pieces = [home, away, flip(home, 1), flip(away, 1)]
 
     part_a, source = second_call(functools.partial(second_part_kernel, 0), half, coefs, own, pieces, True)
     other_a = swap(part_a)

time: 69.1 us -> 74.5 us (1.078); the launches traced: 68.3 us -> 74.5 us
  waiting for transfers between devices: 29.5 us -> 40.4 us
  starting transfers between devices: 24.2 us -> 19 us
  Pallas kernels: 12 us -> 13.8 us
  local copies, waits for them, and re-layouts: 1.52 us -> 0.18 us
    ppermute x21 -> x15, waiting for transfers between devices: 18.7 us -> 29.9 us  [flip(): return lax.ppermute(array, 'row', [(i, i ^ mask) for i in range(n_row)])]
    ppermute x21 -> x15, starting transfers between devices: 21.1 us -> 14.9 us  [flip(): return lax.ppermute(array, 'row', [(i, i ^ mask) for i in range(n_row)])]
    unnamed x12 -> x14, local copies, waits for them, and re-layouts: 1.52 us -> 0.13 us
    ppermute x4, starting transfers between devices: 3.17 us -> 4.11 us  [swap(): return lax.ppermute(array, 'col', [(0, 1), (1, 0)])]
  transfers between devices with their start and end apart: 25 -> 19, of which waited for: 14 -> 14; matrix products, arithmetic and copies ran while one was open for 0% -> 0% of each run, Pallas kernels for 3% -> 4%
where the time goes in v4:
time: 74.5 us
  waiting for transfers between devices  40.4 us (54%)
  starting transfers between devices  19 us (26%)
  Pallas kernels  13.8 us (19%)
  other arithmetic  0.92 us (1%)
    ppermute x15, waiting for transfers between devices, flip(): return lax.ppermute(array, 'row', [(i, i ^ mask) for i in range(n_row)])  29.9 us
    ppermute x15, starting transfers between devices, flip(): return lax.ppermute(array, 'row', [(i, i ^ mask) for i in range(n_row)])  14.9 us
    ppermute x4, waiting for transfers between devices, swap(): return lax.ppermute(array, 'col', [(0, 1), (1, 0)])  10.6 us
    pallas_call x2, Pallas kernels, first_layer(): pl.pallas_call(functools.partial(first_kernel, sending), name='first_laye...  5.83 us
    ppermute x4, starting transfers between devices, swap(): return lax.ppermute(array, 'col', [(0, 1), (1, 0)])  4.11 us
    pallas_call x2, Pallas kernels, second_call(): pl.pallas_call(kernel, name='second_layer', out_shape=(out, jax.ShapeDtyp...  4.1 us
    pallas_call x1, Pallas kernels, body(): pl.pallas_call(sums_kernel, name='column_sums', out_shape=(jax.ShapeDtype...  3.86 us
  transfers between devices with their start and end apart: 19, of which 14 were waited for; matrix products, arithmetic and copies ran while one was open for 0% of the time, Pallas kernels for 4%

profile of v4, /device:TPU:0, one launch (start us, length us, event | category | flops | bytes accessed | tf_op | source)
XLA Modules:
  0.0 74.5 jit_solution(1916978191009552503)
XLA Ops:
  0.0 0.0 copy-start.1
  0.0 0.0 copy-start.3
  0.0 0.0 copy-start.2
  0.0 0.0 copy-start
  0.0 3.9 %column_sums.1 = (f32[80,128]{1,0:T(8,128)S(1)}, bf16[10,36,128,128]{3,2,1,0:T(8,128)(2,1)S(1)}) custom-call(s32[10,36]{1,0:T(8,128)} %cols_ref.7, s32[10]{0:T(128)} %bitcast.10, bf16[10,36,128,128]{3,2,1,0:T(8,128)(2,1)} %blocks_ref.1), custom_call_target="tpu_custom_call" | custom-call | bytes 23592960 | tf_op jit(solution)/shard_map/column_sums/pallas_call | solution.py:192
  3.9 3.1 %collective-permute-start.1 = (bf16[80,128]{1,0:T(8,128)(2,1)S(1)}, bf16[80,128]{1,0:T(8,128)(2,1)S(1)}, u32[]{:S(2)}, u32[]{:S(2)}) collective-permute-start(bf16[80,128]{1,0:T(8,128)(2,1)S(1)} %convert_element_type.54), channel_id=1, source_target_pairs={{0,4},{2,6},{4,0},{6,2},{8,12},{10,14},{12,8},{14,10},{16,20},{18,... | collective-permute-start | bytes 61448 | tf_op jit(solution)/shard_map/ppermute | solution.py:213
  7.0 0.0 collective-permute-start
  7.0 0.2 collective-permute-start.2
  7.2 1.6 %collective-permute-done.1 = bf16[80,128]{1,0:T(8,128)(2,1)S(1)} collective-permute-done((bf16[80,128]{1,0:T(8,128)(2,1)S(1)}, bf16[80,128]{1,0:T(8,128)(2,1)S(1)}, u32[]{:S(2)}, u32[]{:S(2)}) %collective-permute-start.1) | collective-permute-done | bytes 20512 | tf_op jit(solution)/shard_map/ppermute | solution.py:213
  8.8 0.0 collective-permute-done
  8.8 1.4 %collective-permute-done.2 = bf16[80,128]{1,0:T(8,128)(2,1)S(1)} collective-permute-done((bf16[80,128]{1,0:T(8,128)(2,1)S(1)}, bf16[80,128]{1,0:T(8,128)(2,1)S(1)}, u32[]{:S(2)}, u32[]{:S(2)}) %collective-permute-start.2) | collective-permute-done | bytes 20512 | tf_op jit(solution)/shard_map/ppermute | solution.py:213
  10.2 3.9 %collective-permute-start.5 = (bf16[80,128]{1,0:T(8,128)(2,1)S(1)}, bf16[80,128]{1,0:T(8,128)(2,1)S(1)}, u32[]{:S(2)}, u32[]{:S(2)}) collective-permute-start(bf16[80,128]{1,0:T(8,128)(2,1)S(1)} %add_convert_fusion.3), channel_id=1, source_target_pairs={{0,24},{2,26},{4,28},{6,30},{8,16},{10,18},{12,20},{14,22},{16,8},... | collective-permute-start | bytes 61448 | tf_op jit(solution)/shard_map/ppermute | solution.py:213
  14.2 0.0 collective-permute-start.4
  14.2 0.6 collective-permute-start.3
  14.8 1.2 %collective-permute-done.5 = bf16[80,128]{1,0:T(8,128)(2,1)S(1)} collective-permute-done((bf16[80,128]{1,0:T(8,128)(2,1)S(1)}, bf16[80,128]{1,0:T(8,128)(2,1)S(1)}, u32[]{:S(2)}, u32[]{:S(2)}) %collective-permute-start.5) | collective-permute-done | bytes 20512 | tf_op jit(solution)/shard_map/ppermute | solution.py:213
  16.0 2.9 %collective-permute-done.4 = bf16[80,128]{1,0:T(8,128)(2,1)S(1)} collective-permute-done((bf16[80,128]{1,0:T(8,128)(2,1)S(1)}, bf16[80,128]{1,0:T(8,128)(2,1)S(1)}, u32[]{:S(2)}, u32[]{:S(2)}) %collective-permute-start.4) | collective-permute-done | bytes 20512 | tf_op jit(solution)/shard_map/ppermute | solution.py:213
  18.9 0.0 collective-permute-done.3
  18.9 0.0 copy-done.1
  18.9 0.0 copy-done.3
  18.9 0.0 copy-done.2
  18.9 0.0 copy-done
  18.9 2.9 %first_layer.2 = (bf16[5,128,128]{2,1,0:T(8,128)(2,1)S(1)}, bf16[10,36,128,128]{3,2,1,0:T(8,128)(2,1)S(1)}) custom-call(s32[10,36]{1,0:T(8,128)S(1)} %copy-done.1, s32[10]{0:T(128)S(1)} %bitcast.11, f32[1,80,128]{2,1,0:T(8,128)S(1)} %add_bitcast_fusion.sums_ref, f32[80,128]{1,0:T(8,128)S(1)} %bitcast.8, ...), custom_call_target="tpu_custom_call", output_to_operand_aliasing={{1}: (5, {})} | custom-call | flops 754974720 | bytes 5898240 | tf_op jit(solution)/shard_map/first_layer/pallas_call | solution.py:230
  21.9 1.6 %collective-permute-start.6 = (bf16[5,128,128]{2,1,0:T(8,128)(2,1)S(1)}, bf16[5,128,128]{2,1,0:T(8,128)(2,1)S(1)}, u32[]{:S(2)}, u32[]{:S(2)}) collective-permute-start(bf16[5,128,128]{2,1,0:T(8,128)(2,1)S(1)} %get-tuple-element.20), channel_id=1, source_target_pairs={{0,1},{1,0},{2,3},{3,2},{4,5},{5,4},{6,7},{7,6},{8,9},{9,8},{10,11... | collective-permute-start | bytes 491528 | tf_op jit(solution)/shard_map/ppermute | solution.py:216
  23.5 2.9 %first_layer.3 = (f32[5,128,128]{2,1,0:T(8,128)S(1)}, bf16[10,36,128,128]{3,2,1,0:T(8,128)(2,1)S(1)}) custom-call(s32[10,36]{1,0:T(8,128)S(1)} %copy-done.1, s32[10]{0:T(128)S(1)} %bitcast.12, f32[1,80,128]{2,1,0:T(8,128)S(1)} %add_bitcast_fusion.sums_ref, f32[80,128]{1,0:T(8,128)S(1)} %bitcast.9, ...), custom_call_target="tpu_custom_call", output_to_operand_aliasing={{1}: (5, {})} | custom-call | flops 754974720 | bytes 5898240 | tf_op jit(solution)/shard_map/first_layer/pallas_call | solution.py:230
  26.4 1.4 %collective-permute-done.6 = bf16[5,128,128]{2,1,0:T(8,128)(2,1)S(1)} collective-permute-done((bf16[5,128,128]{2,1,0:T(8,128)(2,1)S(1)}, bf16[5,128,128]{2,1,0:T(8,128)(2,1)S(1)}, u32[]{:S(2)}, u32[]{:S(2)}) %collective-permute-start.6) | collective-permute-done | bytes 163872 | tf_op jit(solution)/shard_map/ppermute | solution.py:216
  27.8 1.5 %collective-permute-start.7 = (bf16[5,128,128]{2,1,0:T(8,128)(2,1)S(1)}, bf16[5,128,128]{2,1,0:T(8,128)(2,1)S(1)}, u32[]{:S(2)}, u32[]{:S(2)}) collective-permute-start(bf16[5,128,128]{2,1,0:T(8,128)(2,1)S(1)} %add_convert_fusion.2.own_ref), channel_id=1, source_target_pairs={{0,16},{2,18},{4,20},{6,22},{8,24},{10,26},{12,28},{14,30},{16,0},... | collective-permute-start | bytes 491528 | tf_op jit(solution)/shard_map/ppermute | solution.py:213
  29.4 7.9 %collective-permute-done.7.crossed_ref = bf16[5,128,128]{2,1,0:T(8,128)(2,1)S(1)} collective-permute-done((bf16[5,128,128]{2,1,0:T(8,128)(2,1)S(1)}, bf16[5,128,128]{2,1,0:T(8,128)(2,1)S(1)}, u32[]{:S(2)}, u32[]{:S(2)}) %collective-permute-start.7) | collective-permute-done | bytes 163872 | tf_op jit(solution)/shard_map/ppermute | solution.py:213
  37.3 0.4 collective-permute-start.11
  37.7 0.0 collective-permute-start.8
  37.7 0.0 collective-permute-start.10
  37.7 3.5 %collective-permute-start.9 = (bf16[5,128,128]{2,1,0:T(8,128)(2,1)S(1)}, bf16[5,128,128]{2,1,0:T(8,128)(2,1)S(1)}, u32[]{:S(2)}, u32[]{:S(2)}) collective-permute-start(bf16[5,128,128]{2,1,0:T(8,128)(2,1)S(1)} %get-tuple-element.21), channel_id=1, source_target_pairs={{0,8},{2,10},{4,12},{6,14},{8,0},{10,2},{12,4},{14,6},{16,24},{18,... | collective-permute-start | bytes 491528 | tf_op jit(solution)/shard_map/ppermute | solution.py:213
  41.2 1.5 %collective-permute-done.11 = bf16[5,128,128]{2,1,0:T(8,128)(2,1)S(1)} collective-permute-done((bf16[5,128,128]{2,1,0:T(8,128)(2,1)S(1)}, bf16[5,128,128]{2,1,0:T(8,128)(2,1)S(1)}, u32[]{:S(2)}, u32[]{:S(2)}) %collective-permute-start.11) | collective-permute-done | bytes 163872 | tf_op jit(solution)/shard_map/ppermute | solution.py:216
  42.7 0.0 collective-permute-start.12
  42.7 4.7 %collective-permute-done.8 = bf16[5,128,128]{2,1,0:T(8,128)(2,1)S(1)} collective-permute-done((bf16[5,128,128]{2,1,0:T(8,128)(2,1)S(1)}, bf16[5,128,128]{2,1,0:T(8,128)(2,1)S(1)}, u32[]{:S(2)}, u32[]{:S(2)}) %collective-permute-start.8) | collective-permute-done | bytes 163872 | tf_op jit(solution)/shard_map/ppermute | solution.py:213
  47.4 0.1 collective-permute-done.9
  47.6 0.0 collective-permute-done.10
  47.6 0.1 collective-permute-start.15
  47.7 0.3 collective-permute-start.14
  48.1 1.5 %collective-permute-start.13 = (bf16[5,128,128]{2,1,0:T(8,128)(2,1)S(1)}, bf16[5,128,128]{2,1,0:T(8,128)(2,1)S(1)}, u32[]{:S(2)}, u32[]{:S(2)}) collective-permute-start(bf16[5,128,128]{2,1,0:T(8,128)(2,1)S(1)} %collective-permute-done.11), channel_id=1, source_target_pairs={{0,8},{2,10},{4,12},{6,14},{8,0},{10,2},{12,4},{14,6},{16,24},{18,... | collective-permute-start | bytes 491528 | tf_op jit(solution)/shard_map/ppermute | solution.py:213
  49.5 0.3 collective-permute-done.12
  49.9 7.7 %collective-permute-done.13 = bf16[5,128,128]{2,1,0:T(8,128)(2,1)S(1)} collective-permute-done((bf16[5,128,128]{2,1,0:T(8,128)(2,1)S(1)}, bf16[5,128,128]{2,1,0:T(8,128)(2,1)S(1)}, u32[]{:S(2)}, u32[]{:S(2)}) %collective-permute-start.13) | collective-permute-done | bytes 163872 | tf_op jit(solution)/shard_map/ppermute | solution.py:213
  57.6 0.0 collective-permute-done.14
  57.6 0.1 collective-permute-start.16
  57.7 0.0 collective-permute-done.15.rest_2_
  57.7 2.1 %collective-permute-done.16.rest_3_ = bf16[20,128,128]{2,1,0:T(8,128)(2,1)S(1)} collective-permute-done((bf16[20,128,128]{2,1,0:T(8,128)(2,1)S(1)}, bf16[20,128,128]{2,1,0:T(8,128)(2,1)S(1)}, u32[]{:S(2)}, u32[]{:S(2)}) %collective-permute-start.16) | collective-permute-done | bytes 655392 | tf_op jit(solution)/shard_map/ppermute | solution.py:213
  59.8 2.1 %second_layer.2 = (bf16[5,128,128]{2,1,0:T(8,128)(2,1)S(1)}, bf16[80,128,128]{2,1,0:T(8,128)(2,1)S(1)}) custom-call(s32[10,36]{1,0:T(8,128)S(1)} %copy-done.1, s32[10]{0:T(128)S(1)} %bitcast.13, bf16[10,36,128,128]{3,2,1,0:T(8,128)(2,1)S(1)} %get-tuple-element.18.coef_ref, bf16[5,128,128]{2,1,0:T(8,128)(2,1)S(1)} %add_convert_fusion.2.own_ref, ...), custom_call_target="tpu_custom_call" | custom-call | flops 754974720 | bytes 5898240 | tf_op jit(solution)/shard_map/second_layer/pallas_call | solution.py:258
  61.9 2.0 %second_layer.3 = bf16[5,128,128]{2,1,0:T(8,128)(2,1)S(1)} custom-call(s32[10,36]{1,0:T(8,128)S(1)} %copy-done.1, s32[10]{0:T(128)S(1)} %bitcast.14, bf16[10,36,128,128]{3,2,1,0:T(8,128)(2,1)S(1)} %get-tuple-element.18.coef_ref, bf16[5,128,128]{2,1,0:T(8,128)(2,1)S(1)} %add_convert_fusion.2.own_ref, bf16[80,128,128]{2,1,0:T(8,128)(2,1)S(1)} %get-tuple-element.24.rest_0_), custom_call_target="tpu_custom_call" | custom-call | flops 754974720 | bytes 5898240 | tf_op jit(solution)/shard_map/second_layer/pallas_call | solution.py:258
  63.9 1.7 %collective-permute-start.18 = (bf16[5,128,128]{2,1,0:T(8,128)(2,1)S(1)}, bf16[5,128,128]{2,1,0:T(8,128)(2,1)S(1)}, u32[]{:S(2)}, u32[]{:S(2)}) collective-permute-start(bf16[5,128,128]{2,1,0:T(8,128)(2,1)S(1)} %second_layer.3), channel_id=1, source_target_pairs={{0,1},{1,0},{2,3},{3,2},{4,5},{5,4},{6,7},{7,6},{8,9},{9,8},{10,11... | collective-permute-start | bytes 491528 | tf_op jit(solution)/shard_map/ppermute | solution.py:216
  65.6 0.4 collective-permute-start.17
  66.0 5.0 %collective-permute-done.18 = bf16[5,128,128]{2,1,0:T(8,128)(2,1)S(1)} collective-permute-done((bf16[5,128,128]{2,1,0:T(8,128)(2,1)S(1)}, bf16[5,128,128]{2,1,0:T(8,128)(2,1)S(1)}, u32[]{:S(2)}, u32[]{:S(2)}) %collective-permute-start.18) | collective-permute-done | bytes 163872 | tf_op jit(solution)/shard_map/ppermute | solution.py:216
  71.1 2.6 %collective-permute-done.17 = bf16[5,128,128]{2,1,0:T(8,128)(2,1)S(1)} collective-permute-done((bf16[5,128,128]{2,1,0:T(8,128)(2,1)S(1)}, bf16[5,128,128]{2,1,0:T(8,128)(2,1)S(1)}, u32[]{:S(2)}, u32[]{:S(2)}) %collective-permute-start.17) | collective-permute-done | bytes 163872 | tf_op jit(solution)/shard_map/ppermute | solution.py:216
  73.8 0.8 %pad_maximum_fusion = bf16[10,128,128]{2,1,0:T(8,128)(2,1)} fusion(bf16[5,128,128]{2,1,0:T(8,128)(2,1)S(1)} %add_convert_fusion, bf16[5,128,128]{2,1,0:T(8,128)(2,1)S(1)} %add_convert_fusion.1), kind=kLoop, calls=%fused_computation | loop fusion | flops 163840 | bytes 655360 | tf_op jit(solution)/shard_map/concatenate | solution.py:308
  (15 shorter events, 0.3 us)
Async XLA Ops:
  0.0 18.9 %copy-start.1 = (s32[10,36]{1,0:T(8,128)S(1)}, s32[10,36]{1,0:T(8,128)}, u32[]{:S(2)}) copy-start(s32[10,36]{1,0:T(8,128)} %cols_ref.7) | copy-start | bytes 4324
  0.0 18.9 %copy-start.3 = (s32[10,1]{0,1:T(1,128)S(1)}, s32[10,1]{0,1:T(1,128)}, u32[]{:S(2)}) copy-start(s32[10,1]{0,1:T(1,128)} %param.7) | copy-start | bytes 124
  0.0 18.9 %copy-start.2 = (f32[10240]{0:T(1024)S(1)}, f32[10240]{0:T(1024)}, u32[]{:S(2)}) copy-start(f32[10240]{0:T(1024)} %param.9) | copy-start | bytes 122884
  0.0 18.9 %copy-start = (bf16[10240,128]{1,0:T(8,128)(2,1)S(1)}, bf16[10240,128]{1,0:T(8,128)(2,1)}, u32[]{:S(2)}) copy-start(bf16[10240,128]{1,0:T(8,128)(2,1)} %param.8) | copy-start | bytes 7864324
  3.9 4.9 %collective-permute-start.1 = (bf16[80,128]{1,0:T(8,128)(2,1)S(1)}, bf16[80,128]{1,0:T(8,128)(2,1)S(1)}, u32[]{:S(2)}, u32[]{:S(2)}) collective-permute-start(bf16[80,128]{1,0:T(8,128)(2,1)S(1)} %convert_element_type.54), channel_id=1, source_target_pairs={{0,4},{2,6},{4,0},{6,2},{8,12},{10,14},{12,8},{14,10},{16,20},{18,... | collective-permute-start | bytes 61448 | tf_op jit(solution)/shard_map/ppermute | solution.py:213
  7.0 1.8 %collective-permute-start = (bf16[80,128]{1,0:T(8,128)(2,1)S(1)}, bf16[80,128]{1,0:T(8,128)(2,1)S(1)}, u32[]{:S(2)}, u32[]{:S(2)}) collective-permute-start(bf16[80,128]{1,0:T(8,128)(2,1)S(1)} %convert_element_type.54), channel_id=1, source_target_pairs={{0,2},{2,0},{4,6},{6,4},{8,10},{10,8},{12,14},{14,12},{16,18},{18,... | collective-permute-start | bytes 61448 | tf_op jit(solution)/shard_map/ppermute | solution.py:213
  7.0 3.2 %collective-permute-start.2 = (bf16[80,128]{1,0:T(8,128)(2,1)S(1)}, bf16[80,128]{1,0:T(8,128)(2,1)S(1)}, u32[]{:S(2)}, u32[]{:S(2)}) collective-permute-start(bf16[80,128]{1,0:T(8,128)(2,1)S(1)} %convert_element_type.54), channel_id=1, source_target_pairs={{0,6},{2,4},{4,2},{6,0},{8,14},{10,12},{12,10},{14,8},{16,22},{18,... | collective-permute-start | bytes 61448 | tf_op jit(solution)/shard_map/ppermute | solution.py:213
  10.2 5.7 %collective-permute-start.5 = (bf16[80,128]{1,0:T(8,128)(2,1)S(1)}, bf16[80,128]{1,0:T(8,128)(2,1)S(1)}, u32[]{:S(2)}, u32[]{:S(2)}) collective-permute-start(bf16[80,128]{1,0:T(8,128)(2,1)S(1)} %add_convert_fusion.3), channel_id=1, source_target_pairs={{0,24},{2,26},{4,28},{6,30},{8,16},{10,18},{12,20},{14,22},{16,8},... | collective-permute-start | bytes 61448 | tf_op jit(solution)/shard_map/ppermute | solution.py:213
  14.2 4.7 %collective-permute-start.4 = (bf16[80,128]{1,0:T(8,128)(2,1)S(1)}, bf16[80,128]{1,0:T(8,128)(2,1)S(1)}, u32[]{:S(2)}, u32[]{:S(2)}) collective-permute-start(bf16[80,128]{1,0:T(8,128)(2,1)S(1)} %add_convert_fusion.3), channel_id=1, source_target_pairs={{0,16},{2,18},{4,20},{6,22},{8,24},{10,26},{12,28},{14,30},{16,0},... | collective-permute-start | bytes 61448 | tf_op jit(solution)/shard_map/ppermute | solution.py:213
  14.2 4.7 %collective-permute-start.3 = (bf16[80,128]{1,0:T(8,128)(2,1)S(1)}, bf16[80,128]{1,0:T(8,128)(2,1)S(1)}, u32[]{:S(2)}, u32[]{:S(2)}) collective-permute-start(bf16[80,128]{1,0:T(8,128)(2,1)S(1)} %add_convert_fusion.3), channel_id=1, source_target_pairs={{0,8},{2,10},{4,12},{6,14},{8,0},{10,2},{12,4},{14,6},{16,24},{18,... | collective-permute-start | bytes 61448 | tf_op jit(solution)/shard_map/ppermute | solution.py:213
  21.9 5.9 %collective-permute-start.6 = (bf16[5,128,128]{2,1,0:T(8,128)(2,1)S(1)}, bf16[5,128,128]{2,1,0:T(8,128)(2,1)S(1)}, u32[]{:S(2)}, u32[]{:S(2)}) collective-permute-start(bf16[5,128,128]{2,1,0:T(8,128)(2,1)S(1)} %get-tuple-element.20), channel_id=1, source_target_pairs={{0,1},{1,0},{2,3},{3,2},{4,5},{5,4},{6,7},{7,6},{8,9},{9,8},{10,11... | collective-permute-start | bytes 491528 | tf_op jit(solution)/shard_map/ppermute | solution.py:216
  27.8 9.5 %collective-permute-start.7 = (bf16[5,128,128]{2,1,0:T(8,128)(2,1)S(1)}, bf16[5,128,128]{2,1,0:T(8,128)(2,1)S(1)}, u32[]{:S(2)}, u32[]{:S(2)}) collective-permute-start(bf16[5,128,128]{2,1,0:T(8,128)(2,1)S(1)} %add_convert_fusion.2.own_ref), channel_id=1, source_target_pairs={{0,16},{2,18},{4,20},{6,22},{8,24},{10,26},{12,28},{14,30},{16,0},... | collective-permute-start | bytes 491528 | tf_op jit(solution)/shard_map/ppermute | solution.py:213
  37.3 5.4 %collective-permute-start.11 = (bf16[5,128,128]{2,1,0:T(8,128)(2,1)S(1)}, bf16[5,128,128]{2,1,0:T(8,128)(2,1)S(1)}, u32[]{:S(2)}, u32[]{:S(2)}) collective-permute-start(bf16[5,128,128]{2,1,0:T(8,128)(2,1)S(1)} %get-tuple-element.22), channel_id=1, source_target_pairs={{0,1},{1,0},{2,3},{3,2},{4,5},{5,4},{6,7},{7,6},{8,9},{9,8},{10,11... | collective-permute-start | bytes 491528 | tf_op jit(solution)/shard_map/ppermute | solution.py:216
  37.7 9.7 %collective-permute-start.8 = (bf16[5,128,128]{2,1,0:T(8,128)(2,1)S(1)}, bf16[5,128,128]{2,1,0:T(8,128)(2,1)S(1)}, u32[]{:S(2)}, u32[]{:S(2)}) collective-permute-start(bf16[5,128,128]{2,1,0:T(8,128)(2,1)S(1)} %get-tuple-element.21), channel_id=1, source_target_pairs={{0,4},{2,6},{4,0},{6,2},{8,12},{10,14},{12,8},{14,10},{16,20},{18,... | collective-permute-start | bytes 491528 | tf_op jit(solution)/shard_map/ppermute | solution.py:213
  37.7 9.9 %collective-permute-start.10 = (bf16[5,128,128]{2,1,0:T(8,128)(2,1)S(1)}, bf16[5,128,128]{2,1,0:T(8,128)(2,1)S(1)}, u32[]{:S(2)}, u32[]{:S(2)}) collective-permute-start(bf16[5,128,128]{2,1,0:T(8,128)(2,1)S(1)} %get-tuple-element.21), channel_id=1, source_target_pairs={{0,12},{2,14},{4,8},{6,10},{8,4},{10,6},{12,0},{14,2},{16,28},{18,... | collective-permute-start | bytes 491528 | tf_op jit(solution)/shard_map/ppermute | solution.py:213
  37.7 9.8 %collective-permute-start.9 = (bf16[5,128,128]{2,1,0:T(8,128)(2,1)S(1)}, bf16[5,128,128]{2,1,0:T(8,128)(2,1)S(1)}, u32[]{:S(2)}, u32[]{:S(2)}) collective-permute-start(bf16[5,128,128]{2,1,0:T(8,128)(2,1)S(1)} %get-tuple-element.21), channel_id=1, source_target_pairs={{0,8},{2,10},{4,12},{6,14},{8,0},{10,2},{12,4},{14,6},{16,24},{18,... | collective-permute-start | bytes 491528 | tf_op jit(solution)/shard_map/ppermute | solution.py:213
  42.7 7.1 %collective-permute-start.12 = (bf16[5,128,128]{2,1,0:T(8,128)(2,1)S(1)}, bf16[5,128,128]{2,1,0:T(8,128)(2,1)S(1)}, u32[]{:S(2)}, u32[]{:S(2)}) collective-permute-start(bf16[5,128,128]{2,1,0:T(8,128)(2,1)S(1)} %collective-permute-done.11), channel_id=1, source_target_pairs={{0,4},{2,6},{4,0},{6,2},{8,12},{10,14},{12,8},{14,10},{16,20},{18,... | collective-permute-start | bytes 491528 | tf_op jit(solution)/shard_map/ppermute | solution.py:213
  47.6 10.1 %collective-permute-start.15 = (bf16[20,128,128]{2,1,0:T(8,128)(2,1)S(1)}, bf16[20,128,128]{2,1,0:T(8,128)(2,1)S(1)}, u32[]{:S(2)}, u32[]{:S(2)}) collective-permute-start(bf16[20,128,128]{2,1,0:T(8,128)(2,1)S(1)} %constant_dynamic-update-slice_fusion.rest_0_), channel_id=1, source_target_pairs={{0,2},{2,0},{4,6},{6,4},{8,10},{10,8},{12,14},{14,12},{16,18},{18,... | collective-permute-start | bytes 1966088 | tf_op jit(solution)/shard_map/ppermute | solution.py:213
  47.7 9.9 %collective-permute-start.14 = (bf16[5,128,128]{2,1,0:T(8,128)(2,1)S(1)}, bf16[5,128,128]{2,1,0:T(8,128)(2,1)S(1)}, u32[]{:S(2)}, u32[]{:S(2)}) collective-permute-start(bf16[5,128,128]{2,1,0:T(8,128)(2,1)S(1)} %collective-permute-done.11), channel_id=1, source_target_pairs={{0,12},{2,14},{4,8},{6,10},{8,4},{10,6},{12,0},{14,2},{16,28},{18,... | collective-permute-start | bytes 491528 | tf_op jit(solution)/shard_map/ppermute | solution.py:213
  48.1 9.5 %collective-permute-start.13 = (bf16[5,128,128]{2,1,0:T(8,128)(2,1)S(1)}, bf16[5,128,128]{2,1,0:T(8,128)(2,1)S(1)}, u32[]{:S(2)}, u32[]{:S(2)}) collective-permute-start(bf16[5,128,128]{2,1,0:T(8,128)(2,1)S(1)} %collective-permute-done.11), channel_id=1, source_target_pairs={{0,8},{2,10},{4,12},{6,14},{8,0},{10,2},{12,4},{14,6},{16,24},{18,... | collective-permute-start | bytes 491528 | tf_op jit(solution)/shard_map/ppermute | solution.py:213
  57.6 2.2 %collective-permute-start.16 = (bf16[20,128,128]{2,1,0:T(8,128)(2,1)S(1)}, bf16[20,128,128]{2,1,0:T(8,128)(2,1)S(1)}, u32[]{:S(2)}, u32[]{:S(2)}) collective-permute-start(bf16[20,128,128]{2,1,0:T(8,128)(2,1)S(1)} %constant_dynamic-update-slice_fusion.4.rest_1_), channel_id=1, source_target_pairs={{0,2},{2,0},{4,6},{6,4},{8,10},{10,8},{12,14},{14,12},{16,18},{18,... | collective-permute-start | bytes 1966088 | tf_op jit(solution)/shard_map/ppermute | solution.py:213
  63.9 7.1 %collective-permute-start.18 = (bf16[5,128,128]{2,1,0:T(8,128)(2,1)S(1)}, bf16[5,128,128]{2,1,0:T(8,128)(2,1)S(1)}, u32[]{:S(2)}, u32[]{:S(2)}) collective-permute-start(bf16[5,128,128]{2,1,0:T(8,128)(2,1)S(1)} %second_layer.3), channel_id=1, source_target_pairs={{0,1},{1,0},{2,3},{3,2},{4,5},{5,4},{6,7},{7,6},{8,9},{9,8},{10,11... | collective-permute-start | bytes 491528 | tf_op jit(solution)/shard_map/ppermute | solution.py:216
  65.6 8.1 %collective-permute-start.17 = (bf16[5,128,128]{2,1,0:T(8,128)(2,1)S(1)}, bf16[5,128,128]{2,1,0:T(8,128)(2,1)S(1)}, u32[]{:S(2)}, u32[]{:S(2)}) collective-permute-start(bf16[5,128,128]{2,1,0:T(8,128)(2,1)S(1)} %get-tuple-element.23), channel_id=1, source_target_pairs={{0,1},{1,0},{2,3},{3,2},{4,5},{5,4},{6,7},{7,6},{8,9},{9,8},{10,11... | collective-permute-start | bytes 491528 | tf_op jit(solution)/shard_map/ppermute | solution.py:216

commit v5 on v4

--- a/solution.py
+++ b/solution.py
@@ -64,7 +64,7 @@
     sums_ref[...] = jnp.sum(acc_ref[:groups], axis=1)
 
 
-def multiply_rows(rows, counts_ref, chunk, slots, start, gather, acc_ref):
+def multiply_rows(rows, counts_ref, chunk, start, gather, acc_ref):
     def product(row, first):
         left, right = zip(*[gather(row, first + u) for u in range(chunk)])
         return jnp.dot(jnp.concatenate(left, axis=1), jnp.concatenate(right, axis=0), preferred_element_type=jnp.float32)
@@ -80,14 +80,9 @@
         lax.fori_loop(1, chunk_total(counts_ref, row, chunk), add, 0)
 
 
-def first_kernel(sending, cols_ref, counts_ref, sums_ref, added_ref, demand_ref, blocks_ref, out_ref, coef_ref, inverse_ref, acc_ref):
+def first_kernel(first_row, cols_ref, counts_ref, sums_ref, added_ref, demand_ref, blocks_ref, out_ref, sent_ref, coef_ref, inverse_ref):
     slots = blocks_ref.shape[1]
-    count = out_ref.shape[0]
-    inverse_ref[...] = (1.0 / (jnp.sum(sums_ref[...].astype(jnp.float32), axis=0) + added_ref[...]))[:, None, :]
-    base = 0
-    if sending is not None:
-        side = lax.axis_index("col")
-        base = (1 - side if sending else side) * count
+    inverse_ref[...] = (1.0 / (sums_ref[...] + added_ref[...]))[:, None, :]
 
     def gather(row, slot):
         col = cols_ref[row, slot]
@@ -97,9 +92,9 @@
         coef_ref[row, slot] = coef
         return coef, demand_ref[col]
 
-    rows = [base + b for b in range(count)]
-    multiply_rows(rows, counts_ref, divisor(slots, 12), slots, lambda b: 0.0, gather, acc_ref)
-    out_ref[...] = acc_ref[...].astype(out_ref.dtype)
+    rows = [first_row + b for b in range(out_ref.shape[0])]
+    multiply_rows(rows, counts_ref, divisor(slots, 12), lambda b: 0.0, gather, out_ref)
+    sent_ref[...] = out_ref[...].astype(sent_ref.dtype)
 
 
 def second_rows(first_row, place, cols_ref, counts_ref, coef_ref, source_ref, start, out_ref, acc_ref):
@@ -109,7 +104,7 @@
         return coef_ref[row, slot], source_ref[place(cols_ref[row, slot])]
 
     rows = [first_row + b for b in range(out_ref.shape[0])]
-    multiply_rows(rows, counts_ref, divisor(slots, 12), slots, start, gather, acc_ref)
+    multiply_rows(rows, counts_ref, divisor(slots, 12), start, gather, acc_ref)
     out_ref[...] = acc_ref[...].astype(out_ref.dtype)
 
 
@@ -119,19 +114,22 @@
     return scale
 
 
+def is_owner():
+    return lax.div(lax.axis_index("row"), 8) == lax.axis_index("col")
+
+
 def second_part_kernel(which, cols_ref, counts_ref, coef_ref, own_ref, *rest):
+    part = own_ref.shape[0]
     if which == 0:
         pieces, (out_ref, source_ref, acc_ref) = rest[:-3], rest[-3:]
-        part = out_ref.shape[0]
         for i, piece in enumerate(pieces):
             for place_yz in range(4):
                 at = (place_yz * 4 + i) * part
                 source_ref[at : at + part] = piece[place_yz * part : (place_yz + 1) * part]
     else:
         source_ref, out_ref, acc_ref = rest
-    part = out_ref.shape[0]
-    side = lax.axis_index("col")
-    near = lax.rem(lax.axis_index("row"), 8) * 2 + side
+    near = lax.rem(lax.axis_index("row"), 8) * 2
+    owner = is_owner()
     scale = exact_scale(source_ref.shape[0], part)
 
     def place(col):
@@ -139,7 +137,7 @@
         return col + part * ((piece ^ near) - piece)
 
     def start(b):
-        return jnp.where(side == which, own_ref[b].astype(jnp.float32), 0.0)
+        return jnp.where(owner, own_ref[b].astype(jnp.float32), 0.0)
 
     second_rows(which * part, place, cols_ref, counts_ref, coef_ref, source_ref, start, out_ref, acc_ref)
 
@@ -153,18 +151,30 @@
     second_rows(0, lambda col: col, cols_ref, counts_ref, coef_ref, source_ref, start, out_ref, acc_ref)
 
 
-def sort_kernel(own_ref, crossed_ref, home_ref, away_ref):
-    at_home = lax.div(lax.axis_index("row"), 8) == lax.axis_index("col")
-
-    @pl.when(at_home)
+def reduce_kernel(kept_ref, arrived_ref, *rest):
+    own_ref = rest[-1]
+    own_ref[...] = (kept_ref[...] + arrived_ref[...].astype(jnp.float32)).astype(own_ref.dtype)
+
+
+def choose_kernel(own_ref, crossed_ref, *rest):
+    home_ref = rest[-1]
+    owner = is_owner()
+
+    @pl.when(owner)
     def _():
         home_ref[...] = own_ref[...]
-        away_ref[...] = crossed_ref[...]
-
-    @pl.when(jnp.logical_not(at_home))
+
+    @pl.when(jnp.logical_not(owner))
     def _():
         home_ref[...] = crossed_ref[...]
-        away_ref[...] = own_ref[...]
+
+
+def result_kernel(first_row, mine_ref, other_ref, *rest):
+    out_ref, sum_ref, sem = rest[-3:]
+    sum_ref[...] = (mine_ref[...].astype(jnp.float32) + other_ref[...].astype(jnp.float32)).astype(sum_ref.dtype)
+    copy = pltpu.make_async_copy(sum_ref, out_ref.at[pl.ds(first_row, sum_ref.shape[0])], sem)
+    copy.start()
+    copy.wait()
 
 
 SMEM = pl.BlockSpec(memory_space=pltpu.SMEM)
@@ -226,27 +236,25 @@
     def layer_cost(count):
         return cost(2 * count * slots * size * size * width, count * slots * size * size * 2)
 
-    def first_layer(sending, count, dtype, held):
+    def first_layer(first_row, count, held):
         return pl.pallas_call(
-            functools.partial(first_kernel, sending),
+            functools.partial(first_kernel, first_row),
             name="first_layer",
             out_shape=(
-                jax.ShapeDtypeStruct((count, size, width), dtype),
+                jax.ShapeDtypeStruct((count, size, width), jnp.float32),
+                jax.ShapeDtypeStruct((count, size, width), jnp.bfloat16),
                 pltpu.VMEM(blocks.shape, blocks.dtype),
             ),
             in_specs=[SMEM, SMEM, VMEM, VMEM, VMEM, VMEM],
-            out_specs=(VMEM, VMEM),
-            scratch_shapes=[
-                pltpu.VMEM((groups, 1, size), jnp.float32),
-                pltpu.VMEM((count, size, width), jnp.float32),
-            ],
-            input_output_aliases={5: 1},
+            out_specs=(VMEM, VMEM, VMEM),
+            scratch_shapes=[pltpu.VMEM((groups, 1, size), jnp.float32)],
+            input_output_aliases={5: 2},
             compiler_params=PARAMS,
             cost_estimate=layer_cost(count),
         )(
             slot_cols,
             counts,
-            sums[None],
+            sums,
             value_added.reshape(groups, size),
             demand.reshape(groups, size, width),
             in_vmem(held),
@@ -268,44 +276,67 @@
 
     if not paired:
         group = lax.axis_index("col")
-        partial, coefs = first_layer(None, rows, jnp.float32, held)
+        partial, _, coefs = first_layer(0, rows, held)
         layer_one = lax.psum(partial, "col").astype(jnp.bfloat16)
         gathered = lax.all_gather(layer_one, "row", axis=0, tiled=True)
         source = lax.dynamic_slice_in_dim(gathered, group * groups, groups, 0)
         partial = second_call(second_kernel, rows, coefs, layer_one, [source], False)
         return lax.psum(partial, "col").astype(jnp.bfloat16).reshape(rows * size, width)
 
-    sent, coefs = first_layer(True, half, jnp.bfloat16, held)
-    arrived = swap(sent)
-    kept, coefs = first_layer(False, half, jnp.float32, coefs)
-    own = (kept + arrived.astype(jnp.float32)).astype(jnp.bfloat16)
-
-    crossed = flip(own, group_devices)
-    piece = jax.ShapeDtypeStruct(own.shape, own.dtype)
-    home, away = pl.pallas_call(
-        sort_kernel,
-        name="home_and_away",
-        out_shape=(piece, piece),
-        in_specs=[VMEM, VMEM],
-        out_specs=(VMEM, VMEM),
-        compiler_params=PARAMS,
-    )(own, crossed)
-    away = swap(away)
-    def spread(piece):
-        return jnp.concatenate([piece] + [flip(piece, mask) for mask in (2, 4, 6)], axis=0)
-
-    home, away = spread(home), spread(away)
-    pieces = [home, away, flip(home, 1), flip(away, 1)]
-
-    part_a, source = second_call(functools.partial(second_part_kernel, 0), half, coefs, own, pieces, True)
+    owners = [(c * group_devices + i, c) for c in range(2) for i in range(group_devices)]
+
+    def send(array, target):
+        pairs = [(source[0] * 2 + source[1], sink[0] * 2 + sink[1]) for source, sink in map(target, owners)]
+        return lax.ppermute(array, ("row", "col"), pairs)
+
+    def to_owner(array):
+        return send(array, lambda owner: ((owner[0], 1 - owner[1]), owner))
+
+    def across(array):
+        return send(array, lambda owner: (owner, (owner[0] ^ group_devices, owner[1])))
+
+    piece = jax.ShapeDtypeStruct((half, size, width), jnp.bfloat16)
+
+    def small_call(kernel, name, inputs, earlier):
+        return pl.pallas_call(
+            kernel,
+            name=name,
+            out_shape=piece,
+            in_specs=[VMEM] * len(inputs) + [pl.BlockSpec(memory_space=pl.ANY)] * len(earlier),
+            out_specs=VMEM,
+            compiler_params=PARAMS,
+        )(*inputs, *earlier)
+
+    kept_a, sent_a, coefs = first_layer(0, half, held)
+    kept_b, sent_b, coefs = first_layer(half, half, coefs)
+    own_a = small_call(reduce_kernel, "own_rows", [kept_a, to_owner(sent_a)], [sent_b])
+    own_b = small_call(reduce_kernel, "own_rows", [kept_b, to_owner(sent_b)], [own_a])
+    home_a = small_call(choose_kernel, "own_or_crossed", [own_a, across(own_a)], [])
+    a_y, a_z = flip(home_a, 2), flip(home_a, 4)
+    home_b = small_call(choose_kernel, "own_or_crossed", [own_b, across(own_b)], [a_y, a_z])
+    near_a = jnp.concatenate([home_a, a_y, a_z, flip(a_z, 2)], axis=0)
+    near_b = jnp.concatenate([home_b] + [flip(home_b, mask) for mask in (2, 4, 6)], axis=0)
+    pieces = [near_a, near_b, flip(near_a, 1), flip(near_b, 1)]
+
+    part_a, source = second_call(functools.partial(second_part_kernel, 0), half, coefs, own_a, pieces, True)
     other_a = swap(part_a)
-    part_b = second_call(functools.partial(second_part_kernel, 1), half, coefs, own, [source], False)
+    part_b = second_call(functools.partial(second_part_kernel, 1), half, coefs, own_b, [source], False)
     other_b = swap(part_b)
-    parts = [
-        (mine.astype(jnp.float32) + other.astype(jnp.float32)).astype(jnp.bfloat16)
-        for mine, other in ((part_a, other_a), (part_b, other_b))
-    ]
-    return jnp.concatenate(parts, axis=0).reshape(rows * size, width)
+
+    def result(first_row, inputs):
+        return pl.pallas_call(
+            functools.partial(result_kernel, first_row),
+            name="result",
+            out_shape=jax.ShapeDtypeStruct((rows, size, width), jnp.bfloat16),
+            in_specs=[VMEM, VMEM] + [pl.BlockSpec(memory_space=pltpu.HBM)] * (len(inputs) - 2),
+            out_specs=pl.BlockSpec(memory_space=pltpu.HBM),
+            scratch_shapes=[pltpu.VMEM(piece.shape, piece.dtype), pltpu.SemaphoreType.DMA],
+            input_output_aliases={2: 0} if len(inputs) > 2 else {},
+            compiler_params=PARAMS,
+        )(*inputs)
+
+    out = result(0, [part_a, other_a])
+    return result(half, [part_b, other_b, out]).reshape(rows * size, width)
 
 
 def solution(mesh):

time: 74.5 us -> 77.5 us (1.040); the launches traced: 74.5 us -> 76.2 us
  starting transfers between devices: 19 us -> 30.8 us
  waiting for transfers between devices: 40.4 us -> 29.9 us
  Pallas kernels: 13.8 us -> 15.1 us
    ppermute x0 -> x4, starting transfers between devices: none -> 8.54 us  [send(): return lax.ppermute(array, ('row', 'col'), pairs)]
    ppermute x15 -> x14, waiting for transfers between devices: 29.9 us -> 21.6 us  [flip(): return lax.ppermute(array, 'row', [(i, i ^ mask) for i in range(n_row)])]
    ppermute x4 -> x2, waiting for transfers between devices: 10.6 us -> 4.69 us  [swap(): return lax.ppermute(array, 'col', [(0, 1), (1, 0)])]
    ppermute x15 -> x14, starting transfers between devices: 14.9 us -> 19.3 us  [flip(): return lax.ppermute(array, 'row', [(i, i ^ mask) for i in range(n_row)])]
    ppermute x0 -> x4, waiting for transfers between devices: none -> 3.58 us  [send(): return lax.ppermute(array, ('row', 'col'), pairs)]
    pallas_call x3 -> x8, Pallas kernels: 5.85 us -> 7.1 us  [the longest x2 5.56 us: first_layer(): pl.pallas_call(functools.partial(first_kernel, first_row), name='first_la...]
    ppermute x4 -> x2, starting transfers between devices: 4.11 us -> 2.95 us  [swap(): return lax.ppermute(array, 'col', [(0, 1), (1, 0)])]
  transfers between devices with their start and end apart: 19 -> 20, of which waited for: 14 -> 17; matrix products, arithmetic and copies ran while one was open for 0% -> 0% of each run, Pallas kernels for 4% -> 7%
where the time goes in v5:
time: 77.5 us; the launch traced here: 76.2 us
  starting transfers between devices  30.8 us (40%)
  waiting for transfers between devices  29.9 us (39%)
  Pallas kernels  15.1 us (19%)
    ppermute x14, waiting for transfers between devices, flip(): return lax.ppermute(array, 'row', [(i, i ^ mask) for i in range(n_row)])  21.6 us
    ppermute x14, starting transfers between devices, flip(): return lax.ppermute(array, 'row', [(i, i ^ mask) for i in range(n_row)])  19.3 us
    ppermute x4, starting transfers between devices, send(): return lax.ppermute(array, ('row', 'col'), pairs)  8.54 us
    pallas_call x2, Pallas kernels, first_layer(): pl.pallas_call(functools.partial(first_kernel, first_row), name='first_la...  5.56 us
    ppermute x2, waiting for transfers between devices, swap(): return lax.ppermute(array, 'col', [(0, 1), (1, 0)])  4.69 us
    pallas_call x2, Pallas kernels, second_call(): pl.pallas_call(kernel, name='second_layer', out_shape=(out, jax.ShapeDtyp...  4.08 us
    pallas_call x1, Pallas kernels, body(): pl.pallas_call(sums_kernel, name='column_sums', out_shape=(jax.ShapeDtype...  3.92 us
    ppermute x4, waiting for transfers between devices, send(): return lax.ppermute(array, ('row', 'col'), pairs)  3.58 us
  transfers between devices with their start and end apart: 20, of which 17 were waited for; matrix products, arithmetic and copies ran while one was open for 0% of the time, Pallas kernels for 7%

profile of v5, /device:TPU:0, one launch (start us, length us, event | category | flops | bytes accessed | tf_op | source)
XLA Modules:
  0.0 76.2 jit_solution(3339046719643546722)
XLA Ops:
  0.0 0.0 copy-start.1
  0.0 0.0 copy-start.3
  0.0 0.0 copy-start.2
  0.0 0.0 copy-start
  0.0 3.9 %column_sums.1 = (f32[80,128]{1,0:T(8,128)S(1)}, bf16[10,36,128,128]{3,2,1,0:T(8,128)(2,1)S(1)}) custom-call(s32[10,36]{1,0:T(8,128)} %cols_ref.7, s32[10]{0:T(128)} %bitcast.8, bf16[10,36,128,128]{3,2,1,0:T(8,128)(2,1)} %blocks_ref.1), custom_call_target="tpu_custom_call" | custom-call | bytes 23592960 | tf_op jit(solution)/shard_map/column_sums/pallas_call | solution.py:202
  4.0 3.0 %collective-permute-start.1 = (bf16[80,128]{1,0:T(8,128)(2,1)S(1)}, bf16[80,128]{1,0:T(8,128)(2,1)S(1)}, u32[]{:S(2)}, u32[]{:S(2)}) collective-permute-start(bf16[80,128]{1,0:T(8,128)(2,1)S(1)} %convert_element_type.30), channel_id=1, source_target_pairs={{0,4},{2,6},{4,0},{6,2},{8,12},{10,14},{12,8},{14,10},{16,20},{18,... | collective-permute-start | bytes 61448 | tf_op jit(solution)/shard_map/ppermute | solution.py:223
  7.0 0.0 collective-permute-start
  7.0 0.2 collective-permute-start.2
  7.2 1.6 %collective-permute-done.1 = bf16[80,128]{1,0:T(8,128)(2,1)S(1)} collective-permute-done((bf16[80,128]{1,0:T(8,128)(2,1)S(1)}, bf16[80,128]{1,0:T(8,128)(2,1)S(1)}, u32[]{:S(2)}, u32[]{:S(2)}) %collective-permute-start.1) | collective-permute-done | bytes 20512 | tf_op jit(solution)/shard_map/ppermute | solution.py:223
  8.7 0.0 collective-permute-done
  8.7 1.4 %collective-permute-done.2 = bf16[80,128]{1,0:T(8,128)(2,1)S(1)} collective-permute-done((bf16[80,128]{1,0:T(8,128)(2,1)S(1)}, bf16[80,128]{1,0:T(8,128)(2,1)S(1)}, u32[]{:S(2)}, u32[]{:S(2)}) %collective-permute-start.2) | collective-permute-done | bytes 20512 | tf_op jit(solution)/shard_map/ppermute | solution.py:223
  10.2 3.8 %collective-permute-start.5 = (bf16[80,128]{1,0:T(8,128)(2,1)S(1)}, bf16[80,128]{1,0:T(8,128)(2,1)S(1)}, u32[]{:S(2)}, u32[]{:S(2)}) collective-permute-start(bf16[80,128]{1,0:T(8,128)(2,1)S(1)} %add_convert_fusion), channel_id=1, source_target_pairs={{0,24},{2,26},{4,28},{6,30},{8,16},{10,18},{12,20},{14,22},{16,8},... | collective-permute-start | bytes 61448 | tf_op jit(solution)/shard_map/ppermute | solution.py:223
  14.0 0.0 collective-permute-start.4
  14.0 0.7 collective-permute-start.3
  14.6 1.2 %collective-permute-done.5 = bf16[80,128]{1,0:T(8,128)(2,1)S(1)} collective-permute-done((bf16[80,128]{1,0:T(8,128)(2,1)S(1)}, bf16[80,128]{1,0:T(8,128)(2,1)S(1)}, u32[]{:S(2)}, u32[]{:S(2)}) %collective-permute-start.5) | collective-permute-done | bytes 20512 | tf_op jit(solution)/shard_map/ppermute | solution.py:223
  15.8 2.8 %collective-permute-done.4 = bf16[80,128]{1,0:T(8,128)(2,1)S(1)} collective-permute-done((bf16[80,128]{1,0:T(8,128)(2,1)S(1)}, bf16[80,128]{1,0:T(8,128)(2,1)S(1)}, u32[]{:S(2)}, u32[]{:S(2)}) %collective-permute-start.4) | collective-permute-done | bytes 20512 | tf_op jit(solution)/shard_map/ppermute | solution.py:223
  18.7 0.0 collective-permute-done.3
  18.7 0.0 copy-done.1
  18.7 0.0 copy-done.3
  18.7 0.0 copy-done.2
  18.7 0.0 copy-done
  18.7 2.8 %first_layer.2 = (f32[5,128,128]{2,1,0:T(8,128)S(1)}, bf16[5,128,128]{2,1,0:T(8,128)(2,1)S(1)}, bf16[10,36,128,128]{3,2,1,0:T(8,128)(2,1)S(1)}) custom-call(s32[10,36]{1,0:T(8,128)S(1)} %copy-done.1, s32[10]{0:T(128)S(1)} %bitcast.9, f32[80,128]{1,0:T(8,128)S(1)} %convert_add_fusion.sums_ref, ...), custom_call_target="tpu_custom_call", output_to_operand_aliasing={{2}: (5, {})} | custom-call | flops 754974720 | bytes 5898240 | tf_op jit(solution)/shard_map/first_layer/pallas_call | solution.py:240
  21.5 1.3 %collective-permute-start.7 = (bf16[5,128,128]{2,1,0:T(8,128)(2,1)S(1)}, bf16[5,128,128]{2,1,0:T(8,128)(2,1)S(1)}, u32[]{:S(2)}, u32[]{:S(2)}) collective-permute-start(bf16[5,128,128]{2,1,0:T(8,128)(2,1)S(1)} %get-tuple-element.22), channel_id=1, source_target_pairs={{1,0},{3,2},{5,4},{7,6},{9,8},{11,10},{13,12},{15,14},{16,17},{18,... | collective-permute-start | bytes 491528 | tf_op jit(solution)/shard_map/ppermute | solution.py:290
  22.8 2.8 %first_layer.3 = (f32[5,128,128]{2,1,0:T(8,128)S(1)}, bf16[5,128,128]{2,1,0:T(8,128)(2,1)S(1)}, bf16[10,36,128,128]{3,2,1,0:T(8,128)(2,1)S(1)}) custom-call(s32[10,36]{1,0:T(8,128)S(1)} %copy-done.1, s32[10]{0:T(128)S(1)} %bitcast.10, f32[80,128]{1,0:T(8,128)S(1)} %convert_add_fusion.sums_ref, ...), custom_call_target="tpu_custom_call", output_to_operand_aliasing={{2}: (5, {})} | custom-call | flops 754974720 | bytes 5898240 | tf_op jit(solution)/shard_map/first_layer/pallas_call | solution.py:240
  25.6 1.3 %collective-permute-start.6 = (bf16[5,128,128]{2,1,0:T(8,128)(2,1)S(1)}, bf16[5,128,128]{2,1,0:T(8,128)(2,1)S(1)}, u32[]{:S(2)}, u32[]{:S(2)}) collective-permute-start(bf16[5,128,128]{2,1,0:T(8,128)(2,1)S(1)} %get-tuple-element.20.rest_0_), channel_id=1, source_target_pairs={{1,0},{3,2},{5,4},{7,6},{9,8},{11,10},{13,12},{15,14},{16,17},{18,... | collective-permute-start | bytes 491528 | tf_op jit(solution)/shard_map/ppermute | solution.py:290
  26.9 1.9 %collective-permute-done.7.arrived_ref = bf16[5,128,128]{2,1,0:T(8,128)(2,1)S(1)} collective-permute-done((bf16[5,128,128]{2,1,0:T(8,128)(2,1)S(1)}, bf16[5,128,128]{2,1,0:T(8,128)(2,1)S(1)}, u32[]{:S(2)}, u32[]{:S(2)}) %collective-permute-start.7) | collective-permute-done | bytes 163872 | tf_op jit(solution)/shard_map/ppermute | solution.py:290
  28.8 3.5 %collective-permute-start.8 = (bf16[5,128,128]{2,1,0:T(8,128)(2,1)S(1)}, bf16[5,128,128]{2,1,0:T(8,128)(2,1)S(1)}, u32[]{:S(2)}, u32[]{:S(2)}) collective-permute-start(bf16[5,128,128]{2,1,0:T(8,128)(2,1)S(1)} %own_rows.2.rest_0_.own_ref), channel_id=1, source_target_pairs={{0,16},{2,18},{4,20},{6,22},{8,24},{10,26},{12,28},{14,30},{17,1},... | collective-permute-start | bytes 491528 | tf_op jit(solution)/shard_map/ppermute | solution.py:290
  32.3 0.5 collective-permute-done.6.arrived_ref
  32.9 2.5 %collective-permute-start.12 = (bf16[5,128,128]{2,1,0:T(8,128)(2,1)S(1)}, bf16[5,128,128]{2,1,0:T(8,128)(2,1)S(1)}, u32[]{:S(2)}, u32[]{:S(2)}) collective-permute-start(bf16[5,128,128]{2,1,0:T(8,128)(2,1)S(1)} %own_rows.3.own_ref), channel_id=1, source_target_pairs={{0,16},{2,18},{4,20},{6,22},{8,24},{10,26},{12,28},{14,30},{17,1},... | collective-permute-start | bytes 491528 | tf_op jit(solution)/shard_map/ppermute | solution.py:290
  35.3 1.2 %collective-permute-done.8.crossed_ref = bf16[5,128,128]{2,1,0:T(8,128)(2,1)S(1)} collective-permute-done((bf16[5,128,128]{2,1,0:T(8,128)(2,1)S(1)}, bf16[5,128,128]{2,1,0:T(8,128)(2,1)S(1)}, u32[]{:S(2)}, u32[]{:S(2)}) %collective-permute-start.8) | collective-permute-done | bytes 163872 | tf_op jit(solution)/shard_map/ppermute | solution.py:290
  36.6 7.3 %collective-permute-start.10 = (bf16[5,128,128]{2,1,0:T(8,128)(2,1)S(1)}, bf16[5,128,128]{2,1,0:T(8,128)(2,1)S(1)}, u32[]{:S(2)}, u32[]{:S(2)}) collective-permute-start(bf16[5,128,128]{2,1,0:T(8,128)(2,1)S(1)} %own_or_crossed.2), channel_id=1, source_target_pairs={{0,8},{2,10},{4,12},{6,14},{8,0},{10,2},{12,4},{14,6},{16,24},{18,... | collective-permute-start | bytes 491528 | tf_op jit(solution)/shard_map/ppermute | solution.py:223
  43.8 0.1 collective-permute-start.9
  44.0 0.0 collective-permute-done.12.crossed_ref
  44.0 3.2 %collective-permute-done.10.rest_1_ = bf16[5,128,128]{2,1,0:T(8,128)(2,1)S(1)} collective-permute-done((bf16[5,128,128]{2,1,0:T(8,128)(2,1)S(1)}, bf16[5,128,128]{2,1,0:T(8,128)(2,1)S(1)}, u32[]{:S(2)}, u32[]{:S(2)}) %collective-permute-start.10) | collective-permute-done | bytes 163872 | tf_op jit(solution)/shard_map/ppermute | solution.py:223
  47.1 2.0 %collective-permute-done.9.rest_0_ = bf16[5,128,128]{2,1,0:T(8,128)(2,1)S(1)} collective-permute-done((bf16[5,128,128]{2,1,0:T(8,128)(2,1)S(1)}, bf16[5,128,128]{2,1,0:T(8,128)(2,1)S(1)}, u32[]{:S(2)}, u32[]{:S(2)}) %collective-permute-start.9) | collective-permute-done | bytes 163872 | tf_op jit(solution)/shard_map/ppermute | solution.py:223
  49.2 0.4 collective-permute-start.15
  49.6 1.7 %collective-permute-start.14 = (bf16[5,128,128]{2,1,0:T(8,128)(2,1)S(1)}, bf16[5,128,128]{2,1,0:T(8,128)(2,1)S(1)}, u32[]{:S(2)}, u32[]{:S(2)}) collective-permute-start(bf16[5,128,128]{2,1,0:T(8,128)(2,1)S(1)} %own_or_crossed.3), channel_id=1, source_target_pairs={{0,8},{2,10},{4,12},{6,14},{8,0},{10,2},{12,4},{14,6},{16,24},{18,... | collective-permute-start | bytes 491528 | tf_op jit(solution)/shard_map/ppermute | solution.py:223
  51.3 1.5 %collective-permute-start.13 = (bf16[5,128,128]{2,1,0:T(8,128)(2,1)S(1)}, bf16[5,128,128]{2,1,0:T(8,128)(2,1)S(1)}, u32[]{:S(2)}, u32[]{:S(2)}) collective-permute-start(bf16[5,128,128]{2,1,0:T(8,128)(2,1)S(1)} %own_or_crossed.3), channel_id=1, source_target_pairs={{0,4},{2,6},{4,0},{6,2},{8,12},{10,14},{12,8},{14,10},{16,20},{18,... | collective-permute-start | bytes 491528 | tf_op jit(solution)/shard_map/ppermute | solution.py:223
  52.7 0.6 collective-permute-start.11
  53.3 2.3 %collective-permute-done.15 = bf16[5,128,128]{2,1,0:T(8,128)(2,1)S(1)} collective-permute-done((bf16[5,128,128]{2,1,0:T(8,128)(2,1)S(1)}, bf16[5,128,128]{2,1,0:T(8,128)(2,1)S(1)}, u32[]{:S(2)}, u32[]{:S(2)}) %collective-permute-start.15) | collective-permute-done | bytes 163872 | tf_op jit(solution)/shard_map/ppermute | solution.py:223
  55.6 2.0 %collective-permute-done.14 = bf16[5,128,128]{2,1,0:T(8,128)(2,1)S(1)} collective-permute-done((bf16[5,128,128]{2,1,0:T(8,128)(2,1)S(1)}, bf16[5,128,128]{2,1,0:T(8,128)(2,1)S(1)}, u32[]{:S(2)}, u32[]{:S(2)}) %collective-permute-start.14) | collective-permute-done | bytes 163872 | tf_op jit(solution)/shard_map/ppermute | solution.py:223
  57.6 1.5 %collective-permute-done.13 = bf16[5,128,128]{2,1,0:T(8,128)(2,1)S(1)} collective-permute-done((bf16[5,128,128]{2,1,0:T(8,128)(2,1)S(1)}, bf16[5,128,128]{2,1,0:T(8,128)(2,1)S(1)}, u32[]{:S(2)}, u32[]{:S(2)}) %collective-permute-start.13) | collective-permute-done | bytes 163872 | tf_op jit(solution)/shard_map/ppermute | solution.py:223
  59.1 0.1 pad_maximum_fusion.1.rest_1_
  59.1 0.1 collective-permute-start.17
  59.2 1.6 %collective-permute-done.11 = bf16[5,128,128]{2,1,0:T(8,128)(2,1)S(1)} collective-permute-done((bf16[5,128,128]{2,1,0:T(8,128)(2,1)S(1)}, bf16[5,128,128]{2,1,0:T(8,128)(2,1)S(1)}, u32[]{:S(2)}, u32[]{:S(2)}) %collective-permute-start.11) | collective-permute-done | bytes 163872 | tf_op jit(solution)/shard_map/ppermute | solution.py:223
  60.8 0.1 pad_maximum_fusion.rest_0_
  60.9 0.1 collective-permute-start.16
  61.0 0.3 collective-permute-done.17.rest_3_
  61.3 1.8 %collective-permute-done.16.rest_2_ = bf16[20,128,128]{2,1,0:T(8,128)(2,1)S(1)} collective-permute-done((bf16[20,128,128]{2,1,0:T(8,128)(2,1)S(1)}, bf16[20,128,128]{2,1,0:T(8,128)(2,1)S(1)}, u32[]{:S(2)}, u32[]{:S(2)}) %collective-permute-start.16) | collective-permute-done | bytes 655392 | tf_op jit(solution)/shard_map/ppermute | solution.py:223
  63.1 2.1 %second_layer.2 = (bf16[5,128,128]{2,1,0:T(8,128)(2,1)S(1)}, bf16[80,128,128]{2,1,0:T(8,128)(2,1)S(1)}) custom-call(s32[10,36]{1,0:T(8,128)S(1)} %copy-done.1, s32[10]{0:T(128)S(1)} %bitcast.11, bf16[10,36,128,128]{3,2,1,0:T(8,128)(2,1)S(1)} %get-tuple-element.18.coef_ref, bf16[5,128,128]{2,1,0:T(8,128)(2,1)S(1)} %own_rows.2.rest_0_.own_ref, ...), custom_call_target="tpu_custom_call" | custom-call | flops 754974720 | bytes 5898240 | tf_op jit(solution)/shard_map/second_layer/pallas_call | solution.py:266
  65.2 2.9 %collective-permute-start.19 = (bf16[5,128,128]{2,1,0:T(8,128)(2,1)S(1)}, bf16[5,128,128]{2,1,0:T(8,128)(2,1)S(1)}, u32[]{:S(2)}, u32[]{:S(2)}) collective-permute-start(bf16[5,128,128]{2,1,0:T(8,128)(2,1)S(1)} %get-tuple-element.24.mine_ref), channel_id=1, source_target_pairs={{0,1},{1,0},{2,3},{3,2},{4,5},{5,4},{6,7},{7,6},{8,9},{9,8},{10,11... | collective-permute-start | bytes 491528 | tf_op jit(solution)/shard_map/ppermute | solution.py:226
  68.1 2.0 %second_layer.3.mine_ref = bf16[5,128,128]{2,1,0:T(8,128)(2,1)S(1)} custom-call(s32[10,36]{1,0:T(8,128)S(1)} %copy-done.1, s32[10]{0:T(128)S(1)} %bitcast.12, bf16[10,36,128,128]{3,2,1,0:T(8,128)(2,1)S(1)} %get-tuple-element.18.coef_ref, bf16[5,128,128]{2,1,0:T(8,128)(2,1)S(1)} %own_rows.3.own_ref, bf16[80,128,128]{2,1,0:T(8,128)(2,1)S(1)} %get-tuple-element.23.rest_0_), custom_call_target="tpu_custom_call" | custom-call | flops 754974720 | bytes 5898240 | tf_op jit(solution)/shard_map/second_layer/pallas_call | solution.py:266
  70.0 0.1 collective-permute-start.18
  70.1 2.6 %collective-permute-done.19.other_ref = bf16[5,128,128]{2,1,0:T(8,128)(2,1)S(1)} collective-permute-done((bf16[5,128,128]{2,1,0:T(8,128)(2,1)S(1)}, bf16[5,128,128]{2,1,0:T(8,128)(2,1)S(1)}, u32[]{:S(2)}, u32[]{:S(2)}) %collective-permute-start.19) | collective-permute-done | bytes 163872 | tf_op jit(solution)/shard_map/ppermute | solution.py:226
  72.7 0.7 result.2.rest_0_
  73.4 2.1 %collective-permute-done.18.other_ref = bf16[5,128,128]{2,1,0:T(8,128)(2,1)S(1)} collective-permute-done((bf16[5,128,128]{2,1,0:T(8,128)(2,1)S(1)}, bf16[5,128,128]{2,1,0:T(8,128)(2,1)S(1)}, u32[]{:S(2)}, u32[]{:S(2)}) %collective-permute-start.18) | collective-permute-done | bytes 163872 | tf_op jit(solution)/shard_map/ppermute | solution.py:226
  75.5 0.7 result.3
  (7 shorter events, 0.1 us)
Async XLA Ops:
  0.0 18.7 %copy-start.1 = (s32[10,36]{1,0:T(8,128)S(1)}, s32[10,36]{1,0:T(8,128)}, u32[]{:S(2)}) copy-start(s32[10,36]{1,0:T(8,128)} %cols_ref.7) | copy-start | bytes 4324
  0.0 18.7 %copy-start.3 = (s32[10,1]{0,1:T(1,128)S(1)}, s32[10,1]{0,1:T(1,128)}, u32[]{:S(2)}) copy-start(s32[10,1]{0,1:T(1,128)} %param.7) | copy-start | bytes 124
  0.0 18.7 %copy-start.2 = (f32[10240]{0:T(1024)S(1)}, f32[10240]{0:T(1024)}, u32[]{:S(2)}) copy-start(f32[10240]{0:T(1024)} %param.9) | copy-start | bytes 122884
  0.0 18.7 %copy-start = (bf16[10240,128]{1,0:T(8,128)(2,1)S(1)}, bf16[10240,128]{1,0:T(8,128)(2,1)}, u32[]{:S(2)}) copy-start(bf16[10240,128]{1,0:T(8,128)(2,1)} %param.8) | copy-start | bytes 7864324
  4.0 4.8 %collective-permute-start.1 = (bf16[80,128]{1,0:T(8,128)(2,1)S(1)}, bf16[80,128]{1,0:T(8,128)(2,1)S(1)}, u32[]{:S(2)}, u32[]{:S(2)}) collective-permute-start(bf16[80,128]{1,0:T(8,128)(2,1)S(1)} %convert_element_type.30), channel_id=1, source_target_pairs={{0,4},{2,6},{4,0},{6,2},{8,12},{10,14},{12,8},{14,10},{16,20},{18,... | collective-permute-start | bytes 61448 | tf_op jit(solution)/shard_map/ppermute | solution.py:223
  7.0 1.8 %collective-permute-start = (bf16[80,128]{1,0:T(8,128)(2,1)S(1)}, bf16[80,128]{1,0:T(8,128)(2,1)S(1)}, u32[]{:S(2)}, u32[]{:S(2)}) collective-permute-start(bf16[80,128]{1,0:T(8,128)(2,1)S(1)} %convert_element_type.30), channel_id=1, source_target_pairs={{0,2},{2,0},{4,6},{6,4},{8,10},{10,8},{12,14},{14,12},{16,18},{18,... | collective-permute-start | bytes 61448 | tf_op jit(solution)/shard_map/ppermute | solution.py:223
  7.0 3.2 %collective-permute-start.2 = (bf16[80,128]{1,0:T(8,128)(2,1)S(1)}, bf16[80,128]{1,0:T(8,128)(2,1)S(1)}, u32[]{:S(2)}, u32[]{:S(2)}) collective-permute-start(bf16[80,128]{1,0:T(8,128)(2,1)S(1)} %convert_element_type.30), channel_id=1, source_target_pairs={{0,6},{2,4},{4,2},{6,0},{8,14},{10,12},{12,10},{14,8},{16,22},{18,... | collective-permute-start | bytes 61448 | tf_op jit(solution)/shard_map/ppermute | solution.py:223
  10.2 5.6 %collective-permute-start.5 = (bf16[80,128]{1,0:T(8,128)(2,1)S(1)}, bf16[80,128]{1,0:T(8,128)(2,1)S(1)}, u32[]{:S(2)}, u32[]{:S(2)}) collective-permute-start(bf16[80,128]{1,0:T(8,128)(2,1)S(1)} %add_convert_fusion), channel_id=1, source_target_pairs={{0,24},{2,26},{4,28},{6,30},{8,16},{10,18},{12,20},{14,22},{16,8},... | collective-permute-start | bytes 61448 | tf_op jit(solution)/shard_map/ppermute | solution.py:223
  14.0 4.7 %collective-permute-start.4 = (bf16[80,128]{1,0:T(8,128)(2,1)S(1)}, bf16[80,128]{1,0:T(8,128)(2,1)S(1)}, u32[]{:S(2)}, u32[]{:S(2)}) collective-permute-start(bf16[80,128]{1,0:T(8,128)(2,1)S(1)} %add_convert_fusion), channel_id=1, source_target_pairs={{0,16},{2,18},{4,20},{6,22},{8,24},{10,26},{12,28},{14,30},{16,0},... | collective-permute-start | bytes 61448 | tf_op jit(solution)/shard_map/ppermute | solution.py:223
  14.0 4.7 %collective-permute-start.3 = (bf16[80,128]{1,0:T(8,128)(2,1)S(1)}, bf16[80,128]{1,0:T(8,128)(2,1)S(1)}, u32[]{:S(2)}, u32[]{:S(2)}) collective-permute-start(bf16[80,128]{1,0:T(8,128)(2,1)S(1)} %add_convert_fusion), channel_id=1, source_target_pairs={{0,8},{2,10},{4,12},{6,14},{8,0},{10,2},{12,4},{14,6},{16,24},{18,... | collective-permute-start | bytes 61448 | tf_op jit(solution)/shard_map/ppermute | solution.py:223
  21.5 7.3 %collective-permute-start.7 = (bf16[5,128,128]{2,1,0:T(8,128)(2,1)S(1)}, bf16[5,128,128]{2,1,0:T(8,128)(2,1)S(1)}, u32[]{:S(2)}, u32[]{:S(2)}) collective-permute-start(bf16[5,128,128]{2,1,0:T(8,128)(2,1)S(1)} %get-tuple-element.22), channel_id=1, source_target_pairs={{1,0},{3,2},{5,4},{7,6},{9,8},{11,10},{13,12},{15,14},{16,17},{18,... | collective-permute-start | bytes 491528 | tf_op jit(solution)/shard_map/ppermute | solution.py:290
  25.6 7.2 %collective-permute-start.6 = (bf16[5,128,128]{2,1,0:T(8,128)(2,1)S(1)}, bf16[5,128,128]{2,1,0:T(8,128)(2,1)S(1)}, u32[]{:S(2)}, u32[]{:S(2)}) collective-permute-start(bf16[5,128,128]{2,1,0:T(8,128)(2,1)S(1)} %get-tuple-element.20.rest_0_), channel_id=1, source_target_pairs={{1,0},{3,2},{5,4},{7,6},{9,8},{11,10},{13,12},{15,14},{16,17},{18,... | collective-permute-start | bytes 491528 | tf_op jit(solution)/shard_map/ppermute | solution.py:290
  28.8 7.7 %collective-permute-start.8 = (bf16[5,128,128]{2,1,0:T(8,128)(2,1)S(1)}, bf16[5,128,128]{2,1,0:T(8,128)(2,1)S(1)}, u32[]{:S(2)}, u32[]{:S(2)}) collective-permute-start(bf16[5,128,128]{2,1,0:T(8,128)(2,1)S(1)} %own_rows.2.rest_0_.own_ref), channel_id=1, source_target_pairs={{0,16},{2,18},{4,20},{6,22},{8,24},{10,26},{12,28},{14,30},{17,1},... | collective-permute-start | bytes 491528 | tf_op jit(solution)/shard_map/ppermute | solution.py:290
  32.9 11.1 %collective-permute-start.12 = (bf16[5,128,128]{2,1,0:T(8,128)(2,1)S(1)}, bf16[5,128,128]{2,1,0:T(8,128)(2,1)S(1)}, u32[]{:S(2)}, u32[]{:S(2)}) collective-permute-start(bf16[5,128,128]{2,1,0:T(8,128)(2,1)S(1)} %own_rows.3.own_ref), channel_id=1, source_target_pairs={{0,16},{2,18},{4,20},{6,22},{8,24},{10,26},{12,28},{14,30},{17,1},... | collective-permute-start | bytes 491528 | tf_op jit(solution)/shard_map/ppermute | solution.py:290
  36.6 10.6 %collective-permute-start.10 = (bf16[5,128,128]{2,1,0:T(8,128)(2,1)S(1)}, bf16[5,128,128]{2,1,0:T(8,128)(2,1)S(1)}, u32[]{:S(2)}, u32[]{:S(2)}) collective-permute-start(bf16[5,128,128]{2,1,0:T(8,128)(2,1)S(1)} %own_or_crossed.2), channel_id=1, source_target_pairs={{0,8},{2,10},{4,12},{6,14},{8,0},{10,2},{12,4},{14,6},{16,24},{18,... | collective-permute-start | bytes 491528 | tf_op jit(solution)/shard_map/ppermute | solution.py:223
  43.8 5.3 %collective-permute-start.9 = (bf16[5,128,128]{2,1,0:T(8,128)(2,1)S(1)}, bf16[5,128,128]{2,1,0:T(8,128)(2,1)S(1)}, u32[]{:S(2)}, u32[]{:S(2)}) collective-permute-start(bf16[5,128,128]{2,1,0:T(8,128)(2,1)S(1)} %own_or_crossed.2), channel_id=1, source_target_pairs={{0,4},{2,6},{4,0},{6,2},{8,12},{10,14},{12,8},{14,10},{16,20},{18,... | collective-permute-start | bytes 491528 | tf_op jit(solution)/shard_map/ppermute | solution.py:223
  49.2 6.4 %collective-permute-start.15 = (bf16[5,128,128]{2,1,0:T(8,128)(2,1)S(1)}, bf16[5,128,128]{2,1,0:T(8,128)(2,1)S(1)}, u32[]{:S(2)}, u32[]{:S(2)}) collective-permute-start(bf16[5,128,128]{2,1,0:T(8,128)(2,1)S(1)} %own_or_crossed.3), channel_id=1, source_target_pairs={{0,12},{2,14},{4,8},{6,10},{8,4},{10,6},{12,0},{14,2},{16,28},{18,... | collective-permute-start | bytes 491528 | tf_op jit(solution)/shard_map/ppermute | solution.py:223
  49.6 8.0 %collective-permute-start.14 = (bf16[5,128,128]{2,1,0:T(8,128)(2,1)S(1)}, bf16[5,128,128]{2,1,0:T(8,128)(2,1)S(1)}, u32[]{:S(2)}, u32[]{:S(2)}) collective-permute-start(bf16[5,128,128]{2,1,0:T(8,128)(2,1)S(1)} %own_or_crossed.3), channel_id=1, source_target_pairs={{0,8},{2,10},{4,12},{6,14},{8,0},{10,2},{12,4},{14,6},{16,24},{18,... | collective-permute-start | bytes 491528 | tf_op jit(solution)/shard_map/ppermute | solution.py:223
  51.3 7.8 %collective-permute-start.13 = (bf16[5,128,128]{2,1,0:T(8,128)(2,1)S(1)}, bf16[5,128,128]{2,1,0:T(8,128)(2,1)S(1)}, u32[]{:S(2)}, u32[]{:S(2)}) collective-permute-start(bf16[5,128,128]{2,1,0:T(8,128)(2,1)S(1)} %own_or_crossed.3), channel_id=1, source_target_pairs={{0,4},{2,6},{4,0},{6,2},{8,12},{10,14},{12,8},{14,10},{16,20},{18,... | collective-permute-start | bytes 491528 | tf_op jit(solution)/shard_map/ppermute | solution.py:223
  52.7 8.1 %collective-permute-start.11 = (bf16[5,128,128]{2,1,0:T(8,128)(2,1)S(1)}, bf16[5,128,128]{2,1,0:T(8,128)(2,1)S(1)}, u32[]{:S(2)}, u32[]{:S(2)}) collective-permute-start(bf16[5,128,128]{2,1,0:T(8,128)(2,1)S(1)} %collective-permute-done.10.rest_1_), channel_id=1, source_target_pairs={{0,4},{2,6},{4,0},{6,2},{8,12},{10,14},{12,8},{14,10},{16,20},{18,... | collective-permute-start | bytes 491528 | tf_op jit(solution)/shard_map/ppermute | solution.py:223
  59.1 2.2 %collective-permute-start.17 = (bf16[20,128,128]{2,1,0:T(8,128)(2,1)S(1)}, bf16[20,128,128]{2,1,0:T(8,128)(2,1)S(1)}, u32[]{:S(2)}, u32[]{:S(2)}) collective-permute-start(bf16[20,128,128]{2,1,0:T(8,128)(2,1)S(1)} %pad_maximum_fusion.1.rest_1_), channel_id=1, source_target_pairs={{0,2},{2,0},{4,6},{6,4},{8,10},{10,8},{12,14},{14,12},{16,18},{18,... | collective-permute-start | bytes 1966088 | tf_op jit(solution)/shard_map/ppermute | solution.py:223
  60.9 2.2 %collective-permute-start.16 = (bf16[20,128,128]{2,1,0:T(8,128)(2,1)S(1)}, bf16[20,128,128]{2,1,0:T(8,128)(2,1)S(1)}, u32[]{:S(2)}, u32[]{:S(2)}) collective-permute-start(bf16[20,128,128]{2,1,0:T(8,128)(2,1)S(1)} %pad_maximum_fusion.rest_0_), channel_id=1, source_target_pairs={{0,2},{2,0},{4,6},{6,4},{8,10},{10,8},{12,14},{14,12},{16,18},{18,... | collective-permute-start | bytes 1966088 | tf_op jit(solution)/shard_map/ppermute | solution.py:223
  65.2 7.5 %collective-permute-start.19 = (bf16[5,128,128]{2,1,0:T(8,128)(2,1)S(1)}, bf16[5,128,128]{2,1,0:T(8,128)(2,1)S(1)}, u32[]{:S(2)}, u32[]{:S(2)}) collective-permute-start(bf16[5,128,128]{2,1,0:T(8,128)(2,1)S(1)} %get-tuple-element.24.mine_ref), channel_id=1, source_target_pairs={{0,1},{1,0},{2,3},{3,2},{4,5},{5,4},{6,7},{7,6},{8,9},{9,8},{10,11... | collective-permute-start | bytes 491528 | tf_op jit(solution)/shard_map/ppermute | solution.py:226
  70.0 5.5 %collective-permute-start.18 = (bf16[5,128,128]{2,1,0:T(8,128)(2,1)S(1)}, bf16[5,128,128]{2,1,0:T(8,128)(2,1)S(1)}, u32[]{:S(2)}, u32[]{:S(2)}) collective-permute-start(bf16[5,128,128]{2,1,0:T(8,128)(2,1)S(1)} %second_layer.3.mine_ref), channel_id=1, source_target_pairs={{0,1},{1,0},{2,3},{3,2},{4,5},{5,4},{6,7},{7,6},{8,9},{9,8},{10,11... | collective-permute-start | bytes 491528 | tf_op jit(solution)/shard_map/ppermute | solution.py:226

commit v6 on v4

--- a/solution.py
+++ b/solution.py
@@ -64,7 +64,7 @@
     sums_ref[...] = jnp.sum(acc_ref[:groups], axis=1)
 
 
-def multiply_rows(rows, counts_ref, chunk, slots, start, gather, acc_ref):
+def multiply_rows(rows, counts_ref, chunk, start, gather, acc_ref):
     def product(row, first):
         left, right = zip(*[gather(row, first + u) for u in range(chunk)])
         return jnp.dot(jnp.concatenate(left, axis=1), jnp.concatenate(right, axis=0), preferred_element_type=jnp.float32)
@@ -83,11 +83,11 @@
 def first_kernel(sending, cols_ref, counts_ref, sums_ref, added_ref, demand_ref, blocks_ref, out_ref, coef_ref, inverse_ref, acc_ref):
     slots = blocks_ref.shape[1]
     count = out_ref.shape[0]
-    inverse_ref[...] = (1.0 / (jnp.sum(sums_ref[...].astype(jnp.float32), axis=0) + added_ref[...]))[:, None, :]
     base = 0
     if sending is not None:
         side = lax.axis_index("col")
         base = (1 - side if sending else side) * count
+    inverse_ref[...] = (1.0 / (sums_ref[...] + added_ref[...]))[:, None, :]
 
     def gather(row, slot):
         col = cols_ref[row, slot]
@@ -98,7 +98,7 @@
         return coef, demand_ref[col]
 
     rows = [base + b for b in range(count)]
-    multiply_rows(rows, counts_ref, divisor(slots, 12), slots, lambda b: 0.0, gather, acc_ref)
+    multiply_rows(rows, counts_ref, divisor(slots, 12), lambda b: 0.0, gather, acc_ref)
     out_ref[...] = acc_ref[...].astype(out_ref.dtype)
 
 
@@ -109,7 +109,7 @@
         return coef_ref[row, slot], source_ref[place(cols_ref[row, slot])]
 
     rows = [first_row + b for b in range(out_ref.shape[0])]
-    multiply_rows(rows, counts_ref, divisor(slots, 12), slots, start, gather, acc_ref)
+    multiply_rows(rows, counts_ref, divisor(slots, 12), start, gather, acc_ref)
     out_ref[...] = acc_ref[...].astype(out_ref.dtype)
 
 
@@ -119,17 +119,21 @@
     return scale
 
 
+NEAR = ((0, 0, 0), (0, 1, 0), (0, 0, 1), (1, 0, 1))
+FAR = ((1, 0, 0), (1, 1, 0), (0, 1, 1), (1, 1, 1))
+
+
 def second_part_kernel(which, cols_ref, counts_ref, coef_ref, own_ref, *rest):
+    part = own_ref.shape[0]
     if which == 0:
-        pieces, (out_ref, source_ref, acc_ref) = rest[:-3], rest[-3:]
-        part = out_ref.shape[0]
-        for i, piece in enumerate(pieces):
-            for place_yz in range(4):
-                at = (place_yz * 4 + i) * part
-                source_ref[at : at + part] = piece[place_yz * part : (place_yz + 1) * part]
+        near_ref, far_ref, near_core_ref, far_core_ref, out_ref, source_ref, acc_ref = rest
+        for core, arrays in enumerate(((near_ref, far_ref), (near_core_ref, far_core_ref))):
+            for array, places in zip(arrays, (NEAR, FAR)):
+                for i, (z, y, away) in enumerate(places):
+                    at = ((z * 4 + y * 2 + core) * 2 + away) * part
+                    source_ref[at : at + part] = array[i * part : (i + 1) * part]
     else:
         source_ref, out_ref, acc_ref = rest
-    part = out_ref.shape[0]
     side = lax.axis_index("col")
     near = lax.rem(lax.axis_index("row"), 8) * 2 + side
     scale = exact_scale(source_ref.shape[0], part)
@@ -153,18 +157,26 @@
     second_rows(0, lambda col: col, cols_ref, counts_ref, coef_ref, source_ref, start, out_ref, acc_ref)
 
 
-def sort_kernel(own_ref, crossed_ref, home_ref, away_ref):
-    at_home = lax.div(lax.axis_index("row"), 8) == lax.axis_index("col")
-
-    @pl.when(at_home)
+def choose_kernel(own_ref, first_ref, second_ref, home_ref, away_ref):
+    owner = lax.div(lax.axis_index("row"), 8) == lax.axis_index("col")
+
+    @pl.when(owner)
     def _():
         home_ref[...] = own_ref[...]
-        away_ref[...] = crossed_ref[...]
-
-    @pl.when(jnp.logical_not(at_home))
+        away_ref[...] = first_ref[...]
+
+    @pl.when(jnp.logical_not(owner))
     def _():
-        home_ref[...] = crossed_ref[...]
-        away_ref[...] = own_ref[...]
+        home_ref[...] = first_ref[...]
+        away_ref[...] = second_ref[...]
+
+
+def result_kernel(first_row, mine_ref, other_ref, *rest):
+    out_ref, sum_ref, sem = rest[-3:]
+    sum_ref[...] = (mine_ref[...].astype(jnp.float32) + other_ref[...].astype(jnp.float32)).astype(sum_ref.dtype)
+    copy = pltpu.make_async_copy(sum_ref, out_ref.at[pl.ds(first_row, sum_ref.shape[0])], sem)
+    copy.start()
+    copy.wait()
 
 
 SMEM = pl.BlockSpec(memory_space=pltpu.SMEM)
@@ -246,7 +258,7 @@
         )(
             slot_cols,
             counts,
-            sums[None],
+            sums,
             value_added.reshape(groups, size),
             demand.reshape(groups, size, width),
             in_vmem(held),
@@ -280,32 +292,51 @@
     kept, coefs = first_layer(False, half, jnp.float32, coefs)
     own = (kept + arrived.astype(jnp.float32)).astype(jnp.bfloat16)
 
-    crossed = flip(own, group_devices)
+    first_pairs, second_pairs = [], []
+    for i in range(n_row):
+        for c in range(2):
+            me, crossed = i * 2 + c, (i ^ group_devices) * 2
+            if i // group_devices == c:
+                first_pairs.append((me, crossed + c))
+                second_pairs.append((me, me))
+            else:
+                first_pairs.append((me, i * 2 + 1 - c))
+                second_pairs.append((me, crossed + 1 - c))
+    first, second = [lax.ppermute(own, ("row", "col"), pairs) for pairs in (first_pairs, second_pairs)]
     piece = jax.ShapeDtypeStruct(own.shape, own.dtype)
     home, away = pl.pallas_call(
-        sort_kernel,
+        choose_kernel,
         name="home_and_away",
         out_shape=(piece, piece),
-        in_specs=[VMEM, VMEM],
+        in_specs=[VMEM] * 3,
         out_specs=(VMEM, VMEM),
         compiler_params=PARAMS,
-    )(own, crossed)
-    away = swap(away)
-    def spread(piece):
-        return jnp.concatenate([piece] + [flip(piece, mask) for mask in (2, 4, 6)], axis=0)
-
-    home, away = spread(home), spread(away)
-    pieces = [home, away, flip(home, 1), flip(away, 1)]
+    )(own, first, second)
+    home = jnp.concatenate([home, flip(home, 2)], axis=0)
+    away = jnp.concatenate([away, flip(away, 4)], axis=0)
+    near = jnp.concatenate([home, away], axis=0)
+    far = jnp.concatenate([flip(home, 4), flip(away, 2)], axis=0)
+    pieces = [near, far, flip(near, 1), flip(far, 1)]
 
     part_a, source = second_call(functools.partial(second_part_kernel, 0), half, coefs, own, pieces, True)
     other_a = swap(part_a)
     part_b = second_call(functools.partial(second_part_kernel, 1), half, coefs, own, [source], False)
     other_b = swap(part_b)
-    parts = [
-        (mine.astype(jnp.float32) + other.astype(jnp.float32)).astype(jnp.bfloat16)
-        for mine, other in ((part_a, other_a), (part_b, other_b))
-    ]
-    return jnp.concatenate(parts, axis=0).reshape(rows * size, width)
+
+    def result(first_row, inputs):
+        return pl.pallas_call(
+            functools.partial(result_kernel, first_row),
+            name="result",
+            out_shape=jax.ShapeDtypeStruct((rows, size, width), jnp.bfloat16),
+            in_specs=[VMEM, VMEM] + [pl.BlockSpec(memory_space=pltpu.HBM)] * (len(inputs) - 2),
+            out_specs=pl.BlockSpec(memory_space=pltpu.HBM),
+            scratch_shapes=[pltpu.VMEM(piece.shape, piece.dtype), pltpu.SemaphoreType.DMA],
+            input_output_aliases={2: 0} if len(inputs) > 2 else {},
+            compiler_params=PARAMS,
+        )(*inputs)
+
+    out = result(0, [part_a, other_a])
+    return result(half, [part_b, other_b, out]).reshape(rows * size, width)
 
 
 def solution(mesh):

time: 74.5 us -> 69.1 us (0.928)
  waiting for transfers between devices: 40.4 us -> 25.9 us
  starting transfers between devices: 19 us -> 26.5 us
  Pallas kernels: 13.8 us -> 16.6 us
  other arithmetic: 0.92 us -> 0.13 us
    ppermute x15 -> x12, waiting for transfers between devices: 29.9 us -> 18 us  [flip(): return lax.ppermute(array, 'row', [(i, i ^ mask) for i in range(n_row)])]
    ppermute x0 -> x2, starting transfers between devices: none -> 6.07 us  [body(): lax.ppermute(own, ('row', 'col'), pairs)]
    ppermute x4 -> x3, waiting for transfers between devices: 10.6 us -> 4.97 us  [swap(): return lax.ppermute(array, 'col', [(0, 1), (1, 0)])]
    ppermute x0 -> x2, waiting for transfers between devices: none -> 2.88 us  [body(): lax.ppermute(own, ('row', 'col'), pairs)]
    pallas_call x1 -> x3, Pallas kernels: 0.02 us -> 1.45 us  [the longest x2 1.43 us: result(): pl.pallas_call(functools.partial(result_kernel, first_row), name='result'...]
    ppermute x15 -> x12, starting transfers between devices: 14.9 us -> 16.1 us  [flip(): return lax.ppermute(array, 'row', [(i, i ^ mask) for i in range(n_row)])]
    ppermute x4 -> x3, starting transfers between devices: 4.11 us -> 4.4 us  [swap(): return lax.ppermute(array, 'col', [(0, 1), (1, 0)])]
  transfers between devices with their start and end apart: 19 -> 17, of which waited for: 14 -> 11; matrix products, arithmetic and copies ran while one was open for 0% -> 0% of each run, Pallas kernels for 4% -> 9%
where the time goes in v6:
time: 69.1 us; the launch traced here: 69.5 us
  starting transfers between devices  26.5 us (38%)
  waiting for transfers between devices  25.9 us (37%)
  Pallas kernels  16.6 us (24%)
    ppermute x12, waiting for transfers between devices, flip(): return lax.ppermute(array, 'row', [(i, i ^ mask) for i in range(n_row)])  18 us
    ppermute x12, starting transfers between devices, flip(): return lax.ppermute(array, 'row', [(i, i ^ mask) for i in range(n_row)])  16.1 us
    pallas_call x2, Pallas kernels, first_layer(): pl.pallas_call(functools.partial(first_kernel, sending), name='first_laye...  6.47 us
    ppermute x2, starting transfers between devices, body(): lax.ppermute(own, ('row', 'col'), pairs)  6.07 us
    ppermute x3, waiting for transfers between devices, swap(): return lax.ppermute(array, 'col', [(0, 1), (1, 0)])  4.97 us
    pallas_call x2, Pallas kernels, second_call(): pl.pallas_call(kernel, name='second_layer', out_shape=(out, jax.ShapeDtyp...  4.63 us
    ppermute x3, starting transfers between devices, swap(): return lax.ppermute(array, 'col', [(0, 1), (1, 0)])  4.4 us
    pallas_call x1, Pallas kernels, body(): pl.pallas_call(sums_kernel, name='column_sums', out_shape=(jax.ShapeDtype...  4.06 us
  transfers between devices with their start and end apart: 17, of which 11 were waited for; matrix products, arithmetic and copies ran while one was open for 0% of the time, Pallas kernels for 9%

profile of v6, /device:TPU:0, one launch (start us, length us, event | category | flops | bytes accessed | tf_op | source)
XLA Modules:
  0.0 69.5 jit_solution(16993074983530198814)
XLA Ops:
  0.0 0.0 copy-start.1
  0.0 0.0 copy-start.3
  0.0 0.0 copy-start.2
  0.0 0.0 copy-start
  0.0 4.1 %column_sums.1 = (f32[80,128]{1,0:T(8,128)S(1)}, bf16[10,36,128,128]{3,2,1,0:T(8,128)(2,1)S(1)}) custom-call(s32[10,36]{1,0:T(8,128)} %cols_ref.7, s32[10]{0:T(128)} %bitcast.8, bf16[10,36,128,128]{3,2,1,0:T(8,128)(2,1)} %blocks_ref.1), custom_call_target="tpu_custom_call" | custom-call | bytes 23592960 | tf_op jit(solution)/shard_map/column_sums/pallas_call | solution.py:204
  4.1 2.6 %collective-permute-start.1 = (bf16[80,128]{1,0:T(8,128)(2,1)S(1)}, bf16[80,128]{1,0:T(8,128)(2,1)S(1)}, u32[]{:S(2)}, u32[]{:S(2)}) collective-permute-start(bf16[80,128]{1,0:T(8,128)(2,1)S(1)} %convert_element_type.36), channel_id=1, source_target_pairs={{0,4},{2,6},{4,0},{6,2},{8,12},{10,14},{12,8},{14,10},{16,20},{18,... | collective-permute-start | bytes 61448 | tf_op jit(solution)/shard_map/ppermute | solution.py:225
  6.6 0.3 collective-permute-start
  7.0 0.0 collective-permute-start.2
  7.0 1.5 %collective-permute-done.1 = bf16[80,128]{1,0:T(8,128)(2,1)S(1)} collective-permute-done((bf16[80,128]{1,0:T(8,128)(2,1)S(1)}, bf16[80,128]{1,0:T(8,128)(2,1)S(1)}, u32[]{:S(2)}, u32[]{:S(2)}) %collective-permute-start.1) | collective-permute-done | bytes 20512 | tf_op jit(solution)/shard_map/ppermute | solution.py:225
  8.6 0.0 collective-permute-done
  8.6 1.6 %collective-permute-done.2 = bf16[80,128]{1,0:T(8,128)(2,1)S(1)} collective-permute-done((bf16[80,128]{1,0:T(8,128)(2,1)S(1)}, bf16[80,128]{1,0:T(8,128)(2,1)S(1)}, u32[]{:S(2)}, u32[]{:S(2)}) %collective-permute-start.2) | collective-permute-done | bytes 20512 | tf_op jit(solution)/shard_map/ppermute | solution.py:225
  10.2 3.1 %collective-permute-start.5 = (bf16[80,128]{1,0:T(8,128)(2,1)S(1)}, bf16[80,128]{1,0:T(8,128)(2,1)S(1)}, u32[]{:S(2)}, u32[]{:S(2)}) collective-permute-start(bf16[80,128]{1,0:T(8,128)(2,1)S(1)} %add_convert_fusion.1), channel_id=1, source_target_pairs={{0,24},{2,26},{4,28},{6,30},{8,16},{10,18},{12,20},{14,22},{16,8},... | collective-permute-start | bytes 61448 | tf_op jit(solution)/shard_map/ppermute | solution.py:225
  13.3 0.2 collective-permute-start.4
  13.5 1.2 %collective-permute-start.3 = (bf16[80,128]{1,0:T(8,128)(2,1)S(1)}, bf16[80,128]{1,0:T(8,128)(2,1)S(1)}, u32[]{:S(2)}, u32[]{:S(2)}) collective-permute-start(bf16[80,128]{1,0:T(8,128)(2,1)S(1)} %add_convert_fusion.1), channel_id=1, source_target_pairs={{0,8},{2,10},{4,12},{6,14},{8,0},{10,2},{12,4},{14,6},{16,24},{18,... | collective-permute-start | bytes 61448 | tf_op jit(solution)/shard_map/ppermute | solution.py:225
  14.7 1.2 %collective-permute-done.5 = bf16[80,128]{1,0:T(8,128)(2,1)S(1)} collective-permute-done((bf16[80,128]{1,0:T(8,128)(2,1)S(1)}, bf16[80,128]{1,0:T(8,128)(2,1)S(1)}, u32[]{:S(2)}, u32[]{:S(2)}) %collective-permute-start.5) | collective-permute-done | bytes 20512 | tf_op jit(solution)/shard_map/ppermute | solution.py:225
  15.9 2.3 %collective-permute-done.4 = bf16[80,128]{1,0:T(8,128)(2,1)S(1)} collective-permute-done((bf16[80,128]{1,0:T(8,128)(2,1)S(1)}, bf16[80,128]{1,0:T(8,128)(2,1)S(1)}, u32[]{:S(2)}, u32[]{:S(2)}) %collective-permute-start.4) | collective-permute-done | bytes 20512 | tf_op jit(solution)/shard_map/ppermute | solution.py:225
  18.2 0.0 collective-permute-done.3
  18.2 0.0 copy-done.1
  18.2 0.0 copy-done.3
  18.2 0.0 copy-done.2
  18.2 0.0 copy-done
  18.2 2.9 %first_layer.2 = (bf16[5,128,128]{2,1,0:T(8,128)(2,1)S(1)}, bf16[10,36,128,128]{3,2,1,0:T(8,128)(2,1)S(1)}) custom-call(s32[10,36]{1,0:T(8,128)S(1)} %copy-done.1, s32[10]{0:T(128)S(1)} %bitcast.9, f32[80,128]{1,0:T(8,128)S(1)} %convert_add_fusion.sums_ref, f32[80,128]{1,0:T(8,128)S(1)} %bitcast.6, ...), custom_call_target="tpu_custom_call", output_to_operand_aliasing={{1}: (5, {})} | custom-call | flops 754974720 | bytes 5898240 | tf_op jit(solution)/shard_map/first_layer/pallas_call | solution.py:242
  21.2 2.2 %collective-permute-start.6 = (bf16[5,128,128]{2,1,0:T(8,128)(2,1)S(1)}, bf16[5,128,128]{2,1,0:T(8,128)(2,1)S(1)}, u32[]{:S(2)}, u32[]{:S(2)}) collective-permute-start(bf16[5,128,128]{2,1,0:T(8,128)(2,1)S(1)} %get-tuple-element.20), channel_id=1, source_target_pairs={{0,1},{1,0},{2,3},{3,2},{4,5},{5,4},{6,7},{7,6},{8,9},{9,8},{10,11... | collective-permute-start | bytes 491528 | tf_op jit(solution)/shard_map/ppermute | solution.py:228
  23.4 3.5 %first_layer.3 = (f32[5,128,128]{2,1,0:T(8,128)S(1)}, bf16[10,36,128,128]{3,2,1,0:T(8,128)(2,1)S(1)}) custom-call(s32[10,36]{1,0:T(8,128)S(1)} %copy-done.1, s32[10]{0:T(128)S(1)} %bitcast.10, f32[80,128]{1,0:T(8,128)S(1)} %convert_add_fusion.sums_ref, f32[80,128]{1,0:T(8,128)S(1)} %bitcast.7, ...), custom_call_target="tpu_custom_call", output_to_operand_aliasing={{1}: (5, {})} | custom-call | flops 754974720 | bytes 5898240 | tf_op jit(solution)/shard_map/first_layer/pallas_call | solution.py:242
  27.0 0.0 collective-permute-done.6
  27.0 0.7 collective-permute-start.8
  27.7 5.4 %collective-permute-start.7 = (bf16[5,128,128]{2,1,0:T(8,128)(2,1)S(1)}, bf16[5,128,128]{2,1,0:T(8,128)(2,1)S(1)}, u32[]{:S(2)}, u32[]{:S(2)}) collective-permute-start(bf16[5,128,128]{2,1,0:T(8,128)(2,1)S(1)} %add_convert_fusion.own_ref), channel_id=1, source_target_pairs={{0,16},{1,0},{2,18},{3,2},{4,20},{5,4},{6,22},{7,6},{8,24},{9,8},{... | collective-permute-start | bytes 491528 | tf_op jit(solution)/shard_map/ppermute | solution.py:305
  33.1 0.0 collective-permute-done.8.second_ref
  33.1 2.9 %collective-permute-done.7.first_ref = bf16[5,128,128]{2,1,0:T(8,128)(2,1)S(1)} collective-permute-done((bf16[5,128,128]{2,1,0:T(8,128)(2,1)S(1)}, bf16[5,128,128]{2,1,0:T(8,128)(2,1)S(1)}, u32[]{:S(2)}, u32[]{:S(2)}) %collective-permute-start.7) | collective-permute-done | bytes 163872 | tf_op jit(solution)/shard_map/ppermute | solution.py:305
  36.0 1.6 %collective-permute-start.9 = (bf16[5,128,128]{2,1,0:T(8,128)(2,1)S(1)}, bf16[5,128,128]{2,1,0:T(8,128)(2,1)S(1)}, u32[]{:S(2)}, u32[]{:S(2)}) collective-permute-start(bf16[5,128,128]{2,1,0:T(8,128)(2,1)S(1)} %get-tuple-element.21), channel_id=1, source_target_pairs={{0,4},{2,6},{4,0},{6,2},{8,12},{10,14},{12,8},{14,10},{16,20},{18,... | collective-permute-start | bytes 491528 | tf_op jit(solution)/shard_map/ppermute | solution.py:225
  37.6 2.3 %collective-permute-start.10 = (bf16[5,128,128]{2,1,0:T(8,128)(2,1)S(1)}, bf16[5,128,128]{2,1,0:T(8,128)(2,1)S(1)}, u32[]{:S(2)}, u32[]{:S(2)}) collective-permute-start(bf16[5,128,128]{2,1,0:T(8,128)(2,1)S(1)} %get-tuple-element.22), channel_id=1, source_target_pairs={{0,8},{2,10},{4,12},{6,14},{8,0},{10,2},{12,4},{14,6},{16,24},{18,... | collective-permute-start | bytes 491528 | tf_op jit(solution)/shard_map/ppermute | solution.py:225
  40.0 1.4 %collective-permute-done.9 = bf16[5,128,128]{2,1,0:T(8,128)(2,1)S(1)} collective-permute-done((bf16[5,128,128]{2,1,0:T(8,128)(2,1)S(1)}, bf16[5,128,128]{2,1,0:T(8,128)(2,1)S(1)}, u32[]{:S(2)}, u32[]{:S(2)}) %collective-permute-start.9) | collective-permute-done | bytes 163872 | tf_op jit(solution)/shard_map/ppermute | solution.py:225
  41.4 4.2 %collective-permute-start.11 = (bf16[10,128,128]{2,1,0:T(8,128)(2,1)S(1)}, bf16[10,128,128]{2,1,0:T(8,128)(2,1)S(1)}, u32[]{:S(2)}, u32[]{:S(2)}) collective-permute-start(bf16[10,128,128]{2,1,0:T(8,128)(2,1)S(1)} %pad_maximum_fusion), channel_id=1, source_target_pairs={{0,8},{2,10},{4,12},{6,14},{8,0},{10,2},{12,4},{14,6},{16,24},{18,... | collective-permute-start | bytes 983048 | tf_op jit(solution)/shard_map/ppermute | solution.py:225
  45.6 0.0 collective-permute-done.10
  45.7 0.4 collective-permute-start.12
  46.1 0.1 collective-permute-start.13
  46.2 6.4 %collective-permute-done.11 = bf16[10,128,128]{2,1,0:T(8,128)(2,1)S(1)} collective-permute-done((bf16[10,128,128]{2,1,0:T(8,128)(2,1)S(1)}, bf16[10,128,128]{2,1,0:T(8,128)(2,1)S(1)}, u32[]{:S(2)}, u32[]{:S(2)}) %collective-permute-start.11) | collective-permute-done | bytes 327712 | tf_op jit(solution)/shard_map/ppermute | solution.py:225
  52.6 1.5 %collective-permute-done.12 = bf16[10,128,128]{2,1,0:T(8,128)(2,1)S(1)} collective-permute-done((bf16[10,128,128]{2,1,0:T(8,128)(2,1)S(1)}, bf16[10,128,128]{2,1,0:T(8,128)(2,1)S(1)}, u32[]{:S(2)}, u32[]{:S(2)}) %collective-permute-start.12) | collective-permute-done | bytes 327712 | tf_op jit(solution)/shard_map/ppermute | solution.py:225
  54.2 0.1 collective-permute-start.14
  54.2 0.0 collective-permute-done.13.rest_2_
  54.3 2.1 %collective-permute-done.14.rest_3_ = bf16[20,128,128]{2,1,0:T(8,128)(2,1)S(1)} collective-permute-done((bf16[20,128,128]{2,1,0:T(8,128)(2,1)S(1)}, bf16[20,128,128]{2,1,0:T(8,128)(2,1)S(1)}, u32[]{:S(2)}, u32[]{:S(2)}) %collective-permute-start.14) | collective-permute-done | bytes 655392 | tf_op jit(solution)/shard_map/ppermute | solution.py:225
  56.3 2.7 %second_layer.2 = (bf16[5,128,128]{2,1,0:T(8,128)(2,1)S(1)}, bf16[80,128,128]{2,1,0:T(8,128)(2,1)S(1)}) custom-call(s32[10,36]{1,0:T(8,128)S(1)} %copy-done.1, s32[10]{0:T(128)S(1)} %bitcast.11, bf16[10,36,128,128]{3,2,1,0:T(8,128)(2,1)S(1)} %get-tuple-element.18.coef_ref, bf16[5,128,128]{2,1,0:T(8,128)(2,1)S(1)} %add_convert_fusion.own_ref, ...), custom_call_target="tpu_custom_call" | custom-call | flops 754974720 | bytes 5898240 | tf_op jit(solution)/shard_map/second_layer/pallas_call | solution.py:270
  59.0 1.3 %collective-permute-start.16 = (bf16[5,128,128]{2,1,0:T(8,128)(2,1)S(1)}, bf16[5,128,128]{2,1,0:T(8,128)(2,1)S(1)}, u32[]{:S(2)}, u32[]{:S(2)}) collective-permute-start(bf16[5,128,128]{2,1,0:T(8,128)(2,1)S(1)} %get-tuple-element.24.mine_ref), channel_id=1, source_target_pairs={{0,1},{1,0},{2,3},{3,2},{4,5},{5,4},{6,7},{7,6},{8,9},{9,8},{10,11... | collective-permute-start | bytes 491528 | tf_op jit(solution)/shard_map/ppermute | solution.py:228
  60.3 2.0 %second_layer.3.mine_ref = bf16[5,128,128]{2,1,0:T(8,128)(2,1)S(1)} custom-call(s32[10,36]{1,0:T(8,128)S(1)} %copy-done.1, s32[10]{0:T(128)S(1)} %bitcast.12, bf16[10,36,128,128]{3,2,1,0:T(8,128)(2,1)S(1)} %get-tuple-element.18.coef_ref, bf16[5,128,128]{2,1,0:T(8,128)(2,1)S(1)} %add_convert_fusion.own_ref, bf16[80,128,128]{2,1,0:T(8,128)(2,1)S(1)} %get-tuple-element.23.rest_0_), custom_call_target="tpu_custom_call" | custom-call | flops 754974720 | bytes 5898240 | tf_op jit(solution)/shard_map/second_layer/pallas_call | solution.py:270
  62.3 0.8 %collective-permute-start.15 = (bf16[5,128,128]{2,1,0:T(8,128)(2,1)S(1)}, bf16[5,128,128]{2,1,0:T(8,128)(2,1)S(1)}, u32[]{:S(2)}, u32[]{:S(2)}) collective-permute-start(bf16[5,128,128]{2,1,0:T(8,128)(2,1)S(1)} %second_layer.3.mine_ref), channel_id=1, source_target_pairs={{0,1},{1,0},{2,3},{3,2},{4,5},{5,4},{6,7},{7,6},{8,9},{9,8},{10,11... | collective-permute-start | bytes 491528 | tf_op jit(solution)/shard_map/ppermute | solution.py:228
  63.1 2.6 %collective-permute-done.16.other_ref = bf16[5,128,128]{2,1,0:T(8,128)(2,1)S(1)} collective-permute-done((bf16[5,128,128]{2,1,0:T(8,128)(2,1)S(1)}, bf16[5,128,128]{2,1,0:T(8,128)(2,1)S(1)}, u32[]{:S(2)}, u32[]{:S(2)}) %collective-permute-start.16) | collective-permute-done | bytes 163872 | tf_op jit(solution)/shard_map/ppermute | solution.py:228
  65.7 0.7 %result.2.rest_0_ = bf16[10,128,128]{2,1,0:T(8,128)(2,1)} custom-call(bf16[5,128,128]{2,1,0:T(8,128)(2,1)S(1)} %get-tuple-element.24.mine_ref, bf16[5,128,128]{2,1,0:T(8,128)(2,1)S(1)} %collective-permute-done.16.other_ref), custom_call_target="tpu_custom_call" | custom-call | tf_op jit(solution)/shard_map/result/pallas_call | solution.py:327
  66.5 2.4 %collective-permute-done.15.other_ref = bf16[5,128,128]{2,1,0:T(8,128)(2,1)S(1)} collective-permute-done((bf16[5,128,128]{2,1,0:T(8,128)(2,1)S(1)}, bf16[5,128,128]{2,1,0:T(8,128)(2,1)S(1)}, u32[]{:S(2)}, u32[]{:S(2)}) %collective-permute-start.15) | collective-permute-done | bytes 163872 | tf_op jit(solution)/shard_map/ppermute | solution.py:228
  68.8 0.7 %result.3 = bf16[10,128,128]{2,1,0:T(8,128)(2,1)} custom-call(bf16[5,128,128]{2,1,0:T(8,128)(2,1)S(1)} %second_layer.3.mine_ref, bf16[5,128,128]{2,1,0:T(8,128)(2,1)S(1)} %collective-permute-done.15.other_ref, bf16[10,128,128]{2,1,0:T(8,128)(2,1)} %result.2.rest_0_), custom_call_target="tpu_custom_call", output_to_operand_aliasing={{}: (2, {})} | custom-call | tf_op jit(solution)/shard_map/result/pallas_call | solution.py:327
  (13 shorter events, 0.3 us)
Async XLA Ops:
  0.0 18.2 %copy-start.1 = (s32[10,36]{1,0:T(8,128)S(1)}, s32[10,36]{1,0:T(8,128)}, u32[]{:S(2)}) copy-start(s32[10,36]{1,0:T(8,128)} %cols_ref.7) | copy-start | bytes 4324
  0.0 18.2 %copy-start.3 = (s32[10,1]{0,1:T(1,128)S(1)}, s32[10,1]{0,1:T(1,128)}, u32[]{:S(2)}) copy-start(s32[10,1]{0,1:T(1,128)} %param.7) | copy-start | bytes 124
  0.0 18.2 %copy-start.2 = (f32[10240]{0:T(1024)S(1)}, f32[10240]{0:T(1024)}, u32[]{:S(2)}) copy-start(f32[10240]{0:T(1024)} %param.9) | copy-start | bytes 122884
  0.0 18.2 %copy-start = (bf16[10240,128]{1,0:T(8,128)(2,1)S(1)}, bf16[10240,128]{1,0:T(8,128)(2,1)}, u32[]{:S(2)}) copy-start(bf16[10240,128]{1,0:T(8,128)(2,1)} %param.8) | copy-start | bytes 7864324
  4.1 4.5 %collective-permute-start.1 = (bf16[80,128]{1,0:T(8,128)(2,1)S(1)}, bf16[80,128]{1,0:T(8,128)(2,1)S(1)}, u32[]{:S(2)}, u32[]{:S(2)}) collective-permute-start(bf16[80,128]{1,0:T(8,128)(2,1)S(1)} %convert_element_type.36), channel_id=1, source_target_pairs={{0,4},{2,6},{4,0},{6,2},{8,12},{10,14},{12,8},{14,10},{16,20},{18,... | collective-permute-start | bytes 61448 | tf_op jit(solution)/shard_map/ppermute | solution.py:225
  6.6 1.9 %collective-permute-start = (bf16[80,128]{1,0:T(8,128)(2,1)S(1)}, bf16[80,128]{1,0:T(8,128)(2,1)S(1)}, u32[]{:S(2)}, u32[]{:S(2)}) collective-permute-start(bf16[80,128]{1,0:T(8,128)(2,1)S(1)} %convert_element_type.36), channel_id=1, source_target_pairs={{0,2},{2,0},{4,6},{6,4},{8,10},{10,8},{12,14},{14,12},{16,18},{18,... | collective-permute-start | bytes 61448 | tf_op jit(solution)/shard_map/ppermute | solution.py:225
  7.0 3.2 %collective-permute-start.2 = (bf16[80,128]{1,0:T(8,128)(2,1)S(1)}, bf16[80,128]{1,0:T(8,128)(2,1)S(1)}, u32[]{:S(2)}, u32[]{:S(2)}) collective-permute-start(bf16[80,128]{1,0:T(8,128)(2,1)S(1)} %convert_element_type.36), channel_id=1, source_target_pairs={{0,6},{2,4},{4,2},{6,0},{8,14},{10,12},{12,10},{14,8},{16,22},{18,... | collective-permute-start | bytes 61448 | tf_op jit(solution)/shard_map/ppermute | solution.py:225
  10.2 5.6 %collective-permute-start.5 = (bf16[80,128]{1,0:T(8,128)(2,1)S(1)}, bf16[80,128]{1,0:T(8,128)(2,1)S(1)}, u32[]{:S(2)}, u32[]{:S(2)}) collective-permute-start(bf16[80,128]{1,0:T(8,128)(2,1)S(1)} %add_convert_fusion.1), channel_id=1, source_target_pairs={{0,24},{2,26},{4,28},{6,30},{8,16},{10,18},{12,20},{14,22},{16,8},... | collective-permute-start | bytes 61448 | tf_op jit(solution)/shard_map/ppermute | solution.py:225
  13.3 4.9 %collective-permute-start.4 = (bf16[80,128]{1,0:T(8,128)(2,1)S(1)}, bf16[80,128]{1,0:T(8,128)(2,1)S(1)}, u32[]{:S(2)}, u32[]{:S(2)}) collective-permute-start(bf16[80,128]{1,0:T(8,128)(2,1)S(1)} %add_convert_fusion.1), channel_id=1, source_target_pairs={{0,16},{2,18},{4,20},{6,22},{8,24},{10,26},{12,28},{14,30},{16,0},... | collective-permute-start | bytes 61448 | tf_op jit(solution)/shard_map/ppermute | solution.py:225
  13.5 4.7 %collective-permute-start.3 = (bf16[80,128]{1,0:T(8,128)(2,1)S(1)}, bf16[80,128]{1,0:T(8,128)(2,1)S(1)}, u32[]{:S(2)}, u32[]{:S(2)}) collective-permute-start(bf16[80,128]{1,0:T(8,128)(2,1)S(1)} %add_convert_fusion.1), channel_id=1, source_target_pairs={{0,8},{2,10},{4,12},{6,14},{8,0},{10,2},{12,4},{14,6},{16,24},{18,... | collective-permute-start | bytes 61448 | tf_op jit(solution)/shard_map/ppermute | solution.py:225
  21.2 5.8 %collective-permute-start.6 = (bf16[5,128,128]{2,1,0:T(8,128)(2,1)S(1)}, bf16[5,128,128]{2,1,0:T(8,128)(2,1)S(1)}, u32[]{:S(2)}, u32[]{:S(2)}) collective-permute-start(bf16[5,128,128]{2,1,0:T(8,128)(2,1)S(1)} %get-tuple-element.20), channel_id=1, source_target_pairs={{0,1},{1,0},{2,3},{3,2},{4,5},{5,4},{6,7},{7,6},{8,9},{9,8},{10,11... | collective-permute-start | bytes 491528 | tf_op jit(solution)/shard_map/ppermute | solution.py:228
  27.0 6.1 %collective-permute-start.8 = (bf16[5,128,128]{2,1,0:T(8,128)(2,1)S(1)}, bf16[5,128,128]{2,1,0:T(8,128)(2,1)S(1)}, u32[]{:S(2)}, u32[]{:S(2)}) collective-permute-start(bf16[5,128,128]{2,1,0:T(8,128)(2,1)S(1)} %add_convert_fusion.own_ref), channel_id=1, source_target_pairs={{0,0},{1,16},{2,2},{3,18},{4,4},{5,20},{6,6},{7,22},{8,8},{9,24},{... | collective-permute-start | bytes 491528 | tf_op jit(solution)/shard_map/ppermute | solution.py:305
  27.7 8.3 %collective-permute-start.7 = (bf16[5,128,128]{2,1,0:T(8,128)(2,1)S(1)}, bf16[5,128,128]{2,1,0:T(8,128)(2,1)S(1)}, u32[]{:S(2)}, u32[]{:S(2)}) collective-permute-start(bf16[5,128,128]{2,1,0:T(8,128)(2,1)S(1)} %add_convert_fusion.own_ref), channel_id=1, source_target_pairs={{0,16},{1,0},{2,18},{3,2},{4,20},{5,4},{6,22},{7,6},{8,24},{9,8},{... | collective-permute-start | bytes 491528 | tf_op jit(solution)/shard_map/ppermute | solution.py:305
  36.0 5.4 %collective-permute-start.9 = (bf16[5,128,128]{2,1,0:T(8,128)(2,1)S(1)}, bf16[5,128,128]{2,1,0:T(8,128)(2,1)S(1)}, u32[]{:S(2)}, u32[]{:S(2)}) collective-permute-start(bf16[5,128,128]{2,1,0:T(8,128)(2,1)S(1)} %get-tuple-element.21), channel_id=1, source_target_pairs={{0,4},{2,6},{4,0},{6,2},{8,12},{10,14},{12,8},{14,10},{16,20},{18,... | collective-permute-start | bytes 491528 | tf_op jit(solution)/shard_map/ppermute | solution.py:225
  37.6 8.0 %collective-permute-start.10 = (bf16[5,128,128]{2,1,0:T(8,128)(2,1)S(1)}, bf16[5,128,128]{2,1,0:T(8,128)(2,1)S(1)}, u32[]{:S(2)}, u32[]{:S(2)}) collective-permute-start(bf16[5,128,128]{2,1,0:T(8,128)(2,1)S(1)} %get-tuple-element.22), channel_id=1, source_target_pairs={{0,8},{2,10},{4,12},{6,14},{8,0},{10,2},{12,4},{14,6},{16,24},{18,... | collective-permute-start | bytes 491528 | tf_op jit(solution)/shard_map/ppermute | solution.py:225
  41.4 11.1 %collective-permute-start.11 = (bf16[10,128,128]{2,1,0:T(8,128)(2,1)S(1)}, bf16[10,128,128]{2,1,0:T(8,128)(2,1)S(1)}, u32[]{:S(2)}, u32[]{:S(2)}) collective-permute-start(bf16[10,128,128]{2,1,0:T(8,128)(2,1)S(1)} %pad_maximum_fusion), channel_id=1, source_target_pairs={{0,8},{2,10},{4,12},{6,14},{8,0},{10,2},{12,4},{14,6},{16,24},{18,... | collective-permute-start | bytes 983048 | tf_op jit(solution)/shard_map/ppermute | solution.py:225
  45.7 8.4 %collective-permute-start.12 = (bf16[10,128,128]{2,1,0:T(8,128)(2,1)S(1)}, bf16[10,128,128]{2,1,0:T(8,128)(2,1)S(1)}, u32[]{:S(2)}, u32[]{:S(2)}) collective-permute-start(bf16[10,128,128]{2,1,0:T(8,128)(2,1)S(1)} %pad_maximum_fusion.1), channel_id=1, source_target_pairs={{0,4},{2,6},{4,0},{6,2},{8,12},{10,14},{12,8},{14,10},{16,20},{18,... | collective-permute-start | bytes 983048 | tf_op jit(solution)/shard_map/ppermute | solution.py:225
  46.1 8.1 %collective-permute-start.13 = (bf16[20,128,128]{2,1,0:T(8,128)(2,1)S(1)}, bf16[20,128,128]{2,1,0:T(8,128)(2,1)S(1)}, u32[]{:S(2)}, u32[]{:S(2)}) collective-permute-start(bf16[20,128,128]{2,1,0:T(8,128)(2,1)S(1)} %constant_dynamic-update-slice_fusion.rest_0_), channel_id=1, source_target_pairs={{0,2},{2,0},{4,6},{6,4},{8,10},{10,8},{12,14},{14,12},{16,18},{18,... | collective-permute-start | bytes 1966088 | tf_op jit(solution)/shard_map/ppermute | solution.py:225
  54.2 2.2 %collective-permute-start.14 = (bf16[20,128,128]{2,1,0:T(8,128)(2,1)S(1)}, bf16[20,128,128]{2,1,0:T(8,128)(2,1)S(1)}, u32[]{:S(2)}, u32[]{:S(2)}) collective-permute-start(bf16[20,128,128]{2,1,0:T(8,128)(2,1)S(1)} %constant_dynamic-update-slice_fusion.4.rest_1_), channel_id=1, source_target_pairs={{0,2},{2,0},{4,6},{6,4},{8,10},{10,8},{12,14},{14,12},{16,18},{18,... | collective-permute-start | bytes 1966088 | tf_op jit(solution)/shard_map/ppermute | solution.py:225
  59.0 6.7 %collective-permute-start.16 = (bf16[5,128,128]{2,1,0:T(8,128)(2,1)S(1)}, bf16[5,128,128]{2,1,0:T(8,128)(2,1)S(1)}, u32[]{:S(2)}, u32[]{:S(2)}) collective-permute-start(bf16[5,128,128]{2,1,0:T(8,128)(2,1)S(1)} %get-tuple-element.24.mine_ref), channel_id=1, source_target_pairs={{0,1},{1,0},{2,3},{3,2},{4,5},{5,4},{6,7},{7,6},{8,9},{9,8},{10,11... | collective-permute-start | bytes 491528 | tf_op jit(solution)/shard_map/ppermute | solution.py:228
  62.3 6.5 %collective-permute-start.15 = (bf16[5,128,128]{2,1,0:T(8,128)(2,1)S(1)}, bf16[5,128,128]{2,1,0:T(8,128)(2,1)S(1)}, u32[]{:S(2)}, u32[]{:S(2)}) collective-permute-start(bf16[5,128,128]{2,1,0:T(8,128)(2,1)S(1)} %second_layer.3.mine_ref), channel_id=1, source_target_pairs={{0,1},{1,0},{2,3},{3,2},{4,5},{5,4},{6,7},{7,6},{8,9},{9,8},{10,11... | collective-permute-start | bytes 491528 | tf_op jit(solution)/shard_map/ppermute | solution.py:228

commit v7 on v6

--- a/solution.py
+++ b/solution.py
@@ -20,7 +20,7 @@
 
 def sums_kernel(cols_hbm, counts_hbm, blocks_ref, sums_ref, held_ref, acc_ref, cols_ref, counts_ref, list_sems, sems):
     rows, slots, size, _ = blocks_ref.shape
-    groups = sums_ref.shape[0]
+    groups = acc_ref.shape[0] - 1
     chunk = divisor(slots, 4)
 
     def fetch(b, k):
@@ -61,7 +61,14 @@
             return carry
 
         lax.fori_loop(0, total, add, 0)
-    sums_ref[...] = jnp.sum(acc_ref[:groups], axis=1)
+    sums = jnp.sum(acc_ref[:groups], axis=1)
+    if len(sums_ref.shape) == 2:
+        sums_ref[...] = sums
+    else:
+        share = groups // sums_ref.shape[0]
+        sums_ref[...] = jnp.zeros_like(sums_ref)
+        for i in range(sums_ref.shape[0]):
+            sums_ref[i, :share] = sums[i * share : (i + 1) * share]
 
 
 def multiply_rows(rows, counts_ref, chunk, start, gather, acc_ref):
@@ -87,13 +94,18 @@
     if sending is not None:
         side = lax.axis_index("col")
         base = (1 - side if sending else side) * count
-    inverse_ref[...] = (1.0 / (sums_ref[...] + added_ref[...]))[:, None, :]
+    if len(sums_ref.shape) == 2:
+        sums = sums_ref[...]
+    else:
+        share = added_ref.shape[0] // sums_ref.shape[0]
+        sums = jnp.concatenate([sums_ref[i, :share] for i in range(sums_ref.shape[0])], axis=0)
+    inverse_ref[...] = (1.0 / (sums + added_ref[...]))[:, None, :]
 
     def gather(row, slot):
         col = cols_ref[row, slot]
         live = slot < counts_ref[row]
         block = blocks_ref[row, jnp.where(live, slot, 0)].astype(jnp.float32)
-        coef = jnp.where(live, block * inverse_ref[col], 0.0).astype(jnp.bfloat16)
+        coef = (block * jnp.where(live, inverse_ref[col], 0.0)).astype(jnp.bfloat16)
         coef_ref[row, slot] = coef
         return coef, demand_ref[col]
 
@@ -119,19 +131,17 @@
     return scale
 
 
-NEAR = ((0, 0, 0), (0, 1, 0), (0, 0, 1), (1, 0, 1))
-FAR = ((1, 0, 0), (1, 1, 0), (0, 1, 1), (1, 1, 1))
+PLACES = ((0, 0), (0, 1), (1, 0), (1, 1))
 
 
 def second_part_kernel(which, cols_ref, counts_ref, coef_ref, own_ref, *rest):
     part = own_ref.shape[0]
     if which == 0:
-        near_ref, far_ref, near_core_ref, far_core_ref, out_ref, source_ref, acc_ref = rest
-        for core, arrays in enumerate(((near_ref, far_ref), (near_core_ref, far_core_ref))):
-            for array, places in zip(arrays, (NEAR, FAR)):
-                for i, (z, y, away) in enumerate(places):
-                    at = ((z * 4 + y * 2 + core) * 2 + away) * part
-                    source_ref[at : at + part] = array[i * part : (i + 1) * part]
+        pieces, (out_ref, source_ref, acc_ref) = rest[:-3], rest[-3:]
+        for array, (core, away) in zip(pieces, ((0, 0), (0, 1), (1, 0), (1, 1))):
+            for i, (z, y) in enumerate(PLACES):
+                at = ((z * 4 + y * 2 + core) * 2 + away) * part
+                source_ref[at : at + part] = array[i * part : (i + 1) * part]
     else:
         source_ref, out_ref, acc_ref = rest
     side = lax.axis_index("col")
@@ -157,18 +167,25 @@
     second_rows(0, lambda col: col, cols_ref, counts_ref, coef_ref, source_ref, start, out_ref, acc_ref)
 
 
-def choose_kernel(own_ref, first_ref, second_ref, home_ref, away_ref):
+def choose_kernel(own_ref, crossed_ref, home_ref, away_ref):
     owner = lax.div(lax.axis_index("row"), 8) == lax.axis_index("col")
 
     @pl.when(owner)
     def _():
         home_ref[...] = own_ref[...]
-        away_ref[...] = first_ref[...]
+        away_ref[...] = crossed_ref[...]
 
     @pl.when(jnp.logical_not(owner))
     def _():
-        home_ref[...] = first_ref[...]
-        away_ref[...] = second_ref[...]
+        home_ref[...] = crossed_ref[...]
+        away_ref[...] = own_ref[...]
+
+
+def join_kernel(*refs):
+    out_ref, pieces = refs[-1], refs[:4]
+    part = pieces[0].shape[0]
+    for i, piece in enumerate(pieces):
+        out_ref[i * part : (i + 1) * part] = piece[...]
 
 
 def result_kernel(first_row, mine_ref, other_ref, *rest):
@@ -197,7 +214,7 @@
     width = demand.shape[1]
     groups = demand.shape[0] // size
     group_devices = n_row // n_col
-    paired = n_col == 2 and n_row == 16 and rows % 2 == 0
+    paired = n_col == 2 and n_row == 16 and rows % 2 == 0 and groups % n_row == 0 and groups // n_row <= 8
     half = rows // 2
     counts = counts.reshape(rows)
 
@@ -205,7 +222,7 @@
         sums_kernel,
         name="column_sums",
         out_shape=(
-            jax.ShapeDtypeStruct((groups, size), jnp.float32),
+            jax.ShapeDtypeStruct((n_row, 8, size) if paired else (groups, size), jnp.float32),
             pltpu.VMEM(blocks.shape, blocks.dtype),
         ),
         in_specs=[pl.BlockSpec(memory_space=pltpu.HBM)] * 3,
@@ -228,10 +245,9 @@
         return lax.ppermute(array, "col", [(0, 1), (1, 0)])
 
     if paired:
-        for masks in ((1, 2, 3), (4, 8, 12)):
-            sums = sums.astype(jnp.bfloat16)
-            parts = [sums] + [flip(sums, m) for m in masks]
-            sums = functools.reduce(jnp.add, [part.astype(jnp.float32) for part in parts])
+        shares = lax.all_to_all(sums, "row", 0, 0)
+        share = jnp.broadcast_to(jnp.sum(shares, axis=0), sums.shape)
+        sums = lax.all_to_all(share, "row", 0, 0)
     else:
         sums = lax.psum(sums, "row")
 
@@ -292,31 +308,32 @@
     kept, coefs = first_layer(False, half, jnp.float32, coefs)
     own = (kept + arrived.astype(jnp.float32)).astype(jnp.bfloat16)
 
-    first_pairs, second_pairs = [], []
-    for i in range(n_row):
-        for c in range(2):
-            me, crossed = i * 2 + c, (i ^ group_devices) * 2
-            if i // group_devices == c:
-                first_pairs.append((me, crossed + c))
-                second_pairs.append((me, me))
-            else:
-                first_pairs.append((me, i * 2 + 1 - c))
-                second_pairs.append((me, crossed + 1 - c))
-    first, second = [lax.ppermute(own, ("row", "col"), pairs) for pairs in (first_pairs, second_pairs)]
     piece = jax.ShapeDtypeStruct(own.shape, own.dtype)
     home, away = pl.pallas_call(
         choose_kernel,
         name="home_and_away",
         out_shape=(piece, piece),
-        in_specs=[VMEM] * 3,
+        in_specs=[VMEM] * 2,
         out_specs=(VMEM, VMEM),
         compiler_params=PARAMS,
-    )(own, first, second)
-    home = jnp.concatenate([home, flip(home, 2)], axis=0)
-    away = jnp.concatenate([away, flip(away, 4)], axis=0)
-    near = jnp.concatenate([home, away], axis=0)
-    far = jnp.concatenate([flip(home, 4), flip(away, 2)], axis=0)
-    pieces = [near, far, flip(near, 1), flip(far, 1)]
+    )(own, flip(own, group_devices))
+
+    def join(pieces, earlier):
+        return pl.pallas_call(
+            join_kernel,
+            name="own_joined",
+            out_shape=jax.ShapeDtypeStruct((4 * half, size, width), own.dtype),
+            in_specs=[VMEM] * 4 + [pl.BlockSpec(memory_space=pl.ANY)] * len(earlier),
+            out_specs=VMEM,
+            compiler_params=PARAMS,
+        )(*pieces, *earlier)
+
+    away = swap(away)
+    home_z, home_y = flip(home, 4), flip(home, 2)
+    away_y, away_z, away_yz = flip(away, 2), flip(away, 4), flip(away, 6)
+    home = join([home, home_y, home_z, flip(home_z, 2)], [away_y])
+    away = join([away, away_y, away_z, away_yz], [])
+    pieces = [home, away, flip(home, 1), flip(away, 1)]
 
     part_a, source = second_call(functools.partial(second_part_kernel, 0), half, coefs, own, pieces, True)
     other_a = swap(part_a)

time: 69.1 us -> 95.1 us (1.38)
  blocking collectives: 0 us -> 23.5 us
  starting transfers between devices: 26.5 us -> 9.03 us
  local copies, waits for them, and re-layouts: 0.16 us -> 17.4 us
  waiting for transfers between devices: 25.9 us -> 28.1 us
    all_to_all x0 -> x2, blocking collectives: none -> 23.5 us  [the longest x1 14 us: body(): shares = lax.all_to_all(sums, 'row', 0, 0)]
    unnamed x12 -> x16, local copies, waits for them, and re-layouts: 0.09 us -> 17.4 us
    ppermute x12 -> x9, starting transfers between devices: 16.1 us -> 5.68 us  [flip(): return lax.ppermute(array, 'row', [(i, i ^ mask) for i in range(n_row)])]
    ppermute x2 -> x0, starting transfers between devices: 6.07 us -> none  [body(): lax.ppermute(own, ('row', 'col'), pairs)]
    ppermute x3 -> x4, waiting for transfers between devices: 4.97 us -> 9.58 us  [swap(): return lax.ppermute(array, 'col', [(0, 1), (1, 0)])]
    ppermute x2 -> x0, waiting for transfers between devices: 2.88 us -> none  [body(): lax.ppermute(own, ('row', 'col'), pairs)]
    ppermute x3 -> x4, starting transfers between devices: 4.4 us -> 3.35 us  [swap(): return lax.ppermute(array, 'col', [(0, 1), (1, 0)])]
    ppermute x12 -> x9, waiting for transfers between devices: 18 us -> 18.5 us  [flip(): return lax.ppermute(array, 'row', [(i, i ^ mask) for i in range(n_row)])]
  transfers between devices with their start and end apart: 17 -> 13, of which waited for: 11 -> 9; matrix products, arithmetic and copies ran while one was open for 0% -> 0% of each run, Pallas kernels for 9% -> 6%
where the time goes in v7:
time: 95.1 us; the launch traced here: 94.6 us
  waiting for transfers between devices  28.1 us (30%)
  blocking collectives  23.5 us (25%)
  local copies, waits for them, and re-layouts  17.4 us (18%)
  Pallas kernels  16.3 us (17%)
  starting transfers between devices  9.03 us (9%)
    ppermute x9, waiting for transfers between devices, flip(): return lax.ppermute(array, 'row', [(i, i ^ mask) for i in range(n_row)])  18.5 us
    unnamed x16, local copies, waits for them, and re-layouts  17.4 us
    all_to_all x1, blocking collectives, body(): shares = lax.all_to_all(sums, 'row', 0, 0)  14 us
    ppermute x4, waiting for transfers between devices, swap(): return lax.ppermute(array, 'col', [(0, 1), (1, 0)])  9.58 us
    all_to_all x1, blocking collectives, body(): sums = lax.all_to_all(share, 'row', 0, 0)  9.48 us
    pallas_call x2, Pallas kernels, first_layer(): pl.pallas_call(functools.partial(first_kernel, sending), name='first_laye...  6.11 us
    ppermute x9, starting transfers between devices, flip(): return lax.ppermute(array, 'row', [(i, i ^ mask) for i in range(n_row)])  5.68 us
    pallas_call x2, Pallas kernels, second_call(): pl.pallas_call(kernel, name='second_layer', out_shape=(out, jax.ShapeDtyp...  4.63 us
  transfers between devices with their start and end apart: 13, of which 9 were waited for; matrix products, arithmetic and copies ran while one was open for 0% of the time, Pallas kernels for 6%

profile of v7, /device:TPU:0, one launch (start us, length us, event | category | flops | bytes accessed | tf_op | source)
XLA Modules:
  0.0 94.6 jit_solution(6589962840509042836)
XLA Ops:
  0.0 0.0 copy-start.5
  0.0 0.0 copy-start.7
  0.0 0.0 copy-start.6
  0.0 0.0 copy-start.4
  0.0 4.1 %column_sums.1 = (f32[16,8,128]{2,1,0:T(8,128)S(1)}, bf16[10,36,128,128]{3,2,1,0:T(8,128)(2,1)S(1)}) custom-call(s32[10,36]{1,0:T(8,128)} %cols_ref.7, s32[10]{0:T(128)} %bitcast.8, bf16[10,36,128,128]{3,2,1,0:T(8,128)(2,1)} %blocks_ref.1), custom_call_target="tpu_custom_call" | custom-call | bytes 23592960 | tf_op jit(solution)/shard_map/column_sums/pallas_call | solution.py:221
  4.1 0.0 copy-start
  4.1 4.4 %copy-done = bf16[10,36,128,128]{3,2,1,0:T(8,128)(2,1)} copy-done((bf16[10,36,128,128]{3,2,1,0:T(8,128)(2,1)}, bf16[10,36,128,128]{3,2,1,0:T(8,128)(2,1)S(1)}, u32[]{:S(2)}) %copy-start) | copy-done | bytes 11796504
  8.4 14.0 %all_to_all.10 = f32[16,8,128]{2,1,0:T(8,128)S(1)} all-to-all(f32[16,8,128]{2,1,0:T(8,128)S(1)} %get-tuple-element.15), channel_id=1, replica_groups=mesh['row'=16,'col'=2] {'row'}, dimensions={0} | all-to-all | bytes 131072 | tf_op jit(solution)/shard_map/all_to_all | solution.py:248
  22.5 9.5 %all_to_all.11.sums_ref = f32[16,8,128]{2,1,0:T(8,128)S(1)} all-to-all(f32[16,8,128]{2,1,0:T(8,128)S(1)} %broadcast_in_dim.3), channel_id=1, replica_groups=mesh['row'=16,'col'=2] {'row'}, dimensions={0} | all-to-all | bytes 131072 | tf_op jit(solution)/shard_map/all_to_all | solution.py:250
  32.0 0.0 copy-done.5
  32.0 0.0 copy-done.7
  32.0 0.0 copy-done.6
  32.0 0.0 copy-done.4
  32.0 0.0 copy-start.1
  32.0 4.3 %copy-done.1 = bf16[10,36,128,128]{3,2,1,0:T(8,128)(2,1)S(1)} copy-done((bf16[10,36,128,128]{3,2,1,0:T(8,128)(2,1)S(1)}, bf16[10,36,128,128]{3,2,1,0:T(8,128)(2,1)}, u32[]{:S(2)}) %copy-start.1) | copy-done | bytes 11796504
  36.3 3.3 %first_layer.2 = (bf16[5,128,128]{2,1,0:T(8,128)(2,1)S(1)}, bf16[10,36,128,128]{3,2,1,0:T(8,128)(2,1)S(1)}) custom-call(s32[10,36]{1,0:T(8,128)S(1)} %copy-done.5, s32[10]{0:T(128)S(1)} %bitcast.9, f32[16,8,128]{2,1,0:T(8,128)S(1)} %all_to_all.11.sums_ref, f32[80,128]{1,0:T(8,128)S(1)} %bitcast.6, ...), custom_call_target="tpu_custom_call", output_to_operand_aliasing={{1}: (5, {})} | custom-call | flops 754974720 | bytes 5898240 | tf_op jit(solution)/shard_map/first_layer/pallas_call | solution.py:258
  39.7 1.1 %collective-permute-start = (bf16[5,128,128]{2,1,0:T(8,128)(2,1)S(1)}, bf16[5,128,128]{2,1,0:T(8,128)(2,1)S(1)}, u32[]{:S(2)}, u32[]{:S(2)}) collective-permute-start(bf16[5,128,128]{2,1,0:T(8,128)(2,1)S(1)} %get-tuple-element.20), channel_id=1, source_target_pairs={{0,1},{1,0},{2,3},{3,2},{4,5},{5,4},{6,7},{7,6},{8,9},{9,8},{10,11... | collective-permute-start | bytes 491528 | tf_op jit(solution)/shard_map/ppermute | solution.py:245
  40.8 2.8 %first_layer.3 = (f32[5,128,128]{2,1,0:T(8,128)S(1)}, bf16[10,36,128,128]{3,2,1,0:T(8,128)(2,1)S(1)}) custom-call(s32[10,36]{1,0:T(8,128)S(1)} %copy-done.5, s32[10]{0:T(128)S(1)} %bitcast.10, f32[16,8,128]{2,1,0:T(8,128)S(1)} %all_to_all.11.sums_ref, f32[80,128]{1,0:T(8,128)S(1)} %bitcast.7, ...), custom_call_target="tpu_custom_call", output_to_operand_aliasing={{1}: (5, {})} | custom-call | flops 754974720 | bytes 5898240 | tf_op jit(solution)/shard_map/first_layer/pallas_call | solution.py:258
  43.6 0.0 copy-start.2
  43.6 4.4 %copy-done.2 = bf16[10,36,128,128]{3,2,1,0:T(8,128)(2,1)} copy-done((bf16[10,36,128,128]{3,2,1,0:T(8,128)(2,1)}, bf16[10,36,128,128]{3,2,1,0:T(8,128)(2,1)S(1)}, u32[]{:S(2)}) %copy-start.2) | copy-done | bytes 11796504
  48.0 0.0 collective-permute-done
  48.0 1.4 %collective-permute-start.1 = (bf16[5,128,128]{2,1,0:T(8,128)(2,1)S(1)}, bf16[5,128,128]{2,1,0:T(8,128)(2,1)S(1)}, u32[]{:S(2)}, u32[]{:S(2)}) collective-permute-start(bf16[5,128,128]{2,1,0:T(8,128)(2,1)S(1)} %add_convert_fusion.own_ref), channel_id=1, source_target_pairs={{0,16},{2,18},{4,20},{6,22},{8,24},{10,26},{12,28},{14,30},{16,0},... | collective-permute-start | bytes 491528 | tf_op jit(solution)/shard_map/ppermute | solution.py:242
  49.4 8.4 %collective-permute-done.1.crossed_ref = bf16[5,128,128]{2,1,0:T(8,128)(2,1)S(1)} collective-permute-done((bf16[5,128,128]{2,1,0:T(8,128)(2,1)S(1)}, bf16[5,128,128]{2,1,0:T(8,128)(2,1)S(1)}, u32[]{:S(2)}, u32[]{:S(2)}) %collective-permute-start.1) | collective-permute-done | bytes 163872 | tf_op jit(solution)/shard_map/ppermute | solution.py:242
  57.9 0.1 collective-permute-start.5
  58.0 0.1 collective-permute-start.3
  58.0 0.1 collective-permute-start.2
  58.1 5.2 %collective-permute-done.5.refs_0_ = bf16[5,128,128]{2,1,0:T(8,128)(2,1)S(1)} collective-permute-done((bf16[5,128,128]{2,1,0:T(8,128)(2,1)S(1)}, bf16[5,128,128]{2,1,0:T(8,128)(2,1)S(1)}, u32[]{:S(2)}, u32[]{:S(2)}) %collective-permute-start.5) | collective-permute-done | bytes 163872 | tf_op jit(solution)/shard_map/ppermute | solution.py:245
  63.3 0.0 collective-permute-start.6
  63.3 0.1 collective-permute-done.3.refs_2_
  63.4 2.0 %collective-permute-start.4 = (bf16[5,128,128]{2,1,0:T(8,128)(2,1)S(1)}, bf16[5,128,128]{2,1,0:T(8,128)(2,1)S(1)}, u32[]{:S(2)}, u32[]{:S(2)}) collective-permute-start(bf16[5,128,128]{2,1,0:T(8,128)(2,1)S(1)} %collective-permute-done.3.refs_2_), channel_id=1, source_target_pairs={{0,4},{2,6},{4,0},{6,2},{8,12},{10,14},{12,8},{14,10},{16,20},{18,... | collective-permute-start | bytes 491528 | tf_op jit(solution)/shard_map/ppermute | solution.py:242
  65.3 0.4 collective-permute-start.8
  65.7 1.2 %collective-permute-start.7 = (bf16[5,128,128]{2,1,0:T(8,128)(2,1)S(1)}, bf16[5,128,128]{2,1,0:T(8,128)(2,1)S(1)}, u32[]{:S(2)}, u32[]{:S(2)}) collective-permute-start(bf16[5,128,128]{2,1,0:T(8,128)(2,1)S(1)} %collective-permute-done.5.refs_0_), channel_id=1, source_target_pairs={{0,8},{2,10},{4,12},{6,14},{8,0},{10,2},{12,4},{14,6},{16,24},{18,... | collective-permute-start | bytes 491528 | tf_op jit(solution)/shard_map/ppermute | solution.py:242
  66.8 0.0 collective-permute-done.2.refs_1_
  66.8 5.9 %collective-permute-done.6.refs_4_.refs_1_ = bf16[5,128,128]{2,1,0:T(8,128)(2,1)S(1)} collective-permute-done((bf16[5,128,128]{2,1,0:T(8,128)(2,1)S(1)}, bf16[5,128,128]{2,1,0:T(8,128)(2,1)S(1)}, u32[]{:S(2)}, u32[]{:S(2)}) %collective-permute-start.6) | collective-permute-done | bytes 163872 | tf_op jit(solution)/shard_map/ppermute | solution.py:242
  72.7 1.8 %collective-permute-done.4.refs_3_ = bf16[5,128,128]{2,1,0:T(8,128)(2,1)S(1)} collective-permute-done((bf16[5,128,128]{2,1,0:T(8,128)(2,1)S(1)}, bf16[5,128,128]{2,1,0:T(8,128)(2,1)S(1)}, u32[]{:S(2)}, u32[]{:S(2)}) %collective-permute-start.4) | collective-permute-done | bytes 163872 | tf_op jit(solution)/shard_map/ppermute | solution.py:242
  74.5 0.1 collective-permute-start.9
  74.6 0.0 collective-permute-done.8.refs_3_
  74.6 0.0 collective-permute-done.7.refs_2_
  74.7 0.5 collective-permute-start.10
  75.2 1.5 %collective-permute-done.9.rest_2_ = bf16[20,128,128]{2,1,0:T(8,128)(2,1)S(1)} collective-permute-done((bf16[20,128,128]{2,1,0:T(8,128)(2,1)S(1)}, bf16[20,128,128]{2,1,0:T(8,128)(2,1)S(1)}, u32[]{:S(2)}, u32[]{:S(2)}) %collective-permute-start.9) | collective-permute-done | bytes 655392 | tf_op jit(solution)/shard_map/ppermute | solution.py:242
  76.7 0.9 collective-permute-done.10.rest_3_
  77.6 0.0 copy-start.3
  77.6 4.3 %copy-done.3 = bf16[10,36,128,128]{3,2,1,0:T(8,128)(2,1)S(1)} copy-done((bf16[10,36,128,128]{3,2,1,0:T(8,128)(2,1)S(1)}, bf16[10,36,128,128]{3,2,1,0:T(8,128)(2,1)}, u32[]{:S(2)}) %copy-start.3) | copy-done | bytes 11796504
  82.0 2.1 %second_layer.2 = (bf16[5,128,128]{2,1,0:T(8,128)(2,1)S(1)}, bf16[80,128,128]{2,1,0:T(8,128)(2,1)S(1)}) custom-call(s32[10,36]{1,0:T(8,128)S(1)} %copy-done.5, s32[10]{0:T(128)S(1)} %bitcast.11, bf16[10,36,128,128]{3,2,1,0:T(8,128)(2,1)S(1)} %copy-done.3, bf16[5,128,128]{2,1,0:T(8,128)(2,1)S(1)} %add_convert_fusion.own_ref, ...), custom_call_target="tpu_custom_call" | custom-call | flops 754974720 | bytes 5898240 | tf_op jit(solution)/shard_map/second_layer/pallas_call | solution.py:286
  84.1 1.4 %collective-permute-start.12 = (bf16[5,128,128]{2,1,0:T(8,128)(2,1)S(1)}, bf16[5,128,128]{2,1,0:T(8,128)(2,1)S(1)}, u32[]{:S(2)}, u32[]{:S(2)}) collective-permute-start(bf16[5,128,128]{2,1,0:T(8,128)(2,1)S(1)} %get-tuple-element.24.mine_ref), channel_id=1, source_target_pairs={{0,1},{1,0},{2,3},{3,2},{4,5},{5,4},{6,7},{7,6},{8,9},{9,8},{10,11... | collective-permute-start | bytes 491528 | tf_op jit(solution)/shard_map/ppermute | solution.py:245
  85.5 2.5 %second_layer.3.mine_ref = bf16[5,128,128]{2,1,0:T(8,128)(2,1)S(1)} custom-call(s32[10,36]{1,0:T(8,128)S(1)} %copy-done.5, s32[10]{0:T(128)S(1)} %bitcast.12, bf16[10,36,128,128]{3,2,1,0:T(8,128)(2,1)S(1)} %copy-done.3, bf16[5,128,128]{2,1,0:T(8,128)(2,1)S(1)} %add_convert_fusion.own_ref, bf16[80,128,128]{2,1,0:T(8,128)(2,1)S(1)} %get-tuple-element.23.rest_0_), custom_call_target="tpu_custom_call" | custom-call | flops 754974720 | bytes 5898240 | tf_op jit(solution)/shard_map/second_layer/pallas_call | solution.py:286
  88.0 0.7 collective-permute-start.11
  88.8 2.4 %collective-permute-done.12.other_ref = bf16[5,128,128]{2,1,0:T(8,128)(2,1)S(1)} collective-permute-done((bf16[5,128,128]{2,1,0:T(8,128)(2,1)S(1)}, bf16[5,128,128]{2,1,0:T(8,128)(2,1)S(1)}, u32[]{:S(2)}, u32[]{:S(2)}) %collective-permute-start.12) | collective-permute-done | bytes 163872 | tf_op jit(solution)/shard_map/ppermute | solution.py:245
  91.2 0.7 result.2.rest_0_
  91.9 2.0 %collective-permute-done.11.other_ref = bf16[5,128,128]{2,1,0:T(8,128)(2,1)S(1)} collective-permute-done((bf16[5,128,128]{2,1,0:T(8,128)(2,1)S(1)}, bf16[5,128,128]{2,1,0:T(8,128)(2,1)S(1)}, u32[]{:S(2)}, u32[]{:S(2)}) %collective-permute-start.11) | collective-permute-done | bytes 163872 | tf_op jit(solution)/shard_map/ppermute | solution.py:245
  93.9 0.7 result.3
  (6 shorter events, 0.2 us)
Async XLA Ops:
  0.0 32.0 %copy-start.5 = (s32[10,36]{1,0:T(8,128)S(1)}, s32[10,36]{1,0:T(8,128)}, u32[]{:S(2)}) copy-start(s32[10,36]{1,0:T(8,128)} %cols_ref.7) | copy-start | bytes 4324
  0.0 32.0 %copy-start.7 = (s32[10,1]{0,1:T(1,128)S(1)}, s32[10,1]{0,1:T(1,128)}, u32[]{:S(2)}) copy-start(s32[10,1]{0,1:T(1,128)} %param.7) | copy-start | bytes 124
  0.0 32.0 %copy-start.6 = (f32[10240]{0:T(1024)S(1)}, f32[10240]{0:T(1024)}, u32[]{:S(2)}) copy-start(f32[10240]{0:T(1024)} %param.9) | copy-start | bytes 122884
  0.0 32.0 %copy-start.4 = (bf16[10240,128]{1,0:T(8,128)(2,1)S(1)}, bf16[10240,128]{1,0:T(8,128)(2,1)}, u32[]{:S(2)}) copy-start(bf16[10240,128]{1,0:T(8,128)(2,1)} %param.8) | copy-start | bytes 7864324
  4.1 4.4 %copy-start = (bf16[10,36,128,128]{3,2,1,0:T(8,128)(2,1)}, bf16[10,36,128,128]{3,2,1,0:T(8,128)(2,1)S(1)}, u32[]{:S(2)}) copy-start(bf16[10,36,128,128]{3,2,1,0:T(8,128)(2,1)S(1)} %get-tuple-element.16.blocks_ref) | copy-start | bytes 35389444
  32.0 4.4 %copy-start.1 = (bf16[10,36,128,128]{3,2,1,0:T(8,128)(2,1)S(1)}, bf16[10,36,128,128]{3,2,1,0:T(8,128)(2,1)}, u32[]{:S(2)}) copy-start(bf16[10,36,128,128]{3,2,1,0:T(8,128)(2,1)} %copy-done) | copy-start | bytes 35389444
  39.7 8.3 %collective-permute-start = (bf16[5,128,128]{2,1,0:T(8,128)(2,1)S(1)}, bf16[5,128,128]{2,1,0:T(8,128)(2,1)S(1)}, u32[]{:S(2)}, u32[]{:S(2)}) collective-permute-start(bf16[5,128,128]{2,1,0:T(8,128)(2,1)S(1)} %get-tuple-element.20), channel_id=1, source_target_pairs={{0,1},{1,0},{2,3},{3,2},{4,5},{5,4},{6,7},{7,6},{8,9},{9,8},{10,11... | collective-permute-start | bytes 491528 | tf_op jit(solution)/shard_map/ppermute | solution.py:245
  43.6 4.4 %copy-start.2 = (bf16[10,36,128,128]{3,2,1,0:T(8,128)(2,1)}, bf16[10,36,128,128]{3,2,1,0:T(8,128)(2,1)S(1)}, u32[]{:S(2)}) copy-start(bf16[10,36,128,128]{3,2,1,0:T(8,128)(2,1)S(1)} %get-tuple-element.18.coef_ref) | copy-start | bytes 35389444
  48.0 9.9 %collective-permute-start.1 = (bf16[5,128,128]{2,1,0:T(8,128)(2,1)S(1)}, bf16[5,128,128]{2,1,0:T(8,128)(2,1)S(1)}, u32[]{:S(2)}, u32[]{:S(2)}) collective-permute-start(bf16[5,128,128]{2,1,0:T(8,128)(2,1)S(1)} %add_convert_fusion.own_ref), channel_id=1, source_target_pairs={{0,16},{2,18},{4,20},{6,22},{8,24},{10,26},{12,28},{14,30},{16,0},... | collective-permute-start | bytes 491528 | tf_op jit(solution)/shard_map/ppermute | solution.py:242
  57.9 5.4 %collective-permute-start.5 = (bf16[5,128,128]{2,1,0:T(8,128)(2,1)S(1)}, bf16[5,128,128]{2,1,0:T(8,128)(2,1)S(1)}, u32[]{:S(2)}, u32[]{:S(2)}) collective-permute-start(bf16[5,128,128]{2,1,0:T(8,128)(2,1)S(1)} %get-tuple-element.22), channel_id=1, source_target_pairs={{0,1},{1,0},{2,3},{3,2},{4,5},{5,4},{6,7},{7,6},{8,9},{9,8},{10,11... | collective-permute-start | bytes 491528 | tf_op jit(solution)/shard_map/ppermute | solution.py:245
  58.0 5.4 %collective-permute-start.3 = (bf16[5,128,128]{2,1,0:T(8,128)(2,1)S(1)}, bf16[5,128,128]{2,1,0:T(8,128)(2,1)S(1)}, u32[]{:S(2)}, u32[]{:S(2)}) collective-permute-start(bf16[5,128,128]{2,1,0:T(8,128)(2,1)S(1)} %get-tuple-element.21.refs_0_), channel_id=1, source_target_pairs={{0,8},{2,10},{4,12},{6,14},{8,0},{10,2},{12,4},{14,6},{16,24},{18,... | collective-permute-start | bytes 491528 | tf_op jit(solution)/shard_map/ppermute | solution.py:242
  58.0 8.8 %collective-permute-start.2 = (bf16[5,128,128]{2,1,0:T(8,128)(2,1)S(1)}, bf16[5,128,128]{2,1,0:T(8,128)(2,1)S(1)}, u32[]{:S(2)}, u32[]{:S(2)}) collective-permute-start(bf16[5,128,128]{2,1,0:T(8,128)(2,1)S(1)} %get-tuple-element.21.refs_0_), channel_id=1, source_target_pairs={{0,4},{2,6},{4,0},{6,2},{8,12},{10,14},{12,8},{14,10},{16,20},{18,... | collective-permute-start | bytes 491528 | tf_op jit(solution)/shard_map/ppermute | solution.py:242
  63.3 9.4 %collective-permute-start.6 = (bf16[5,128,128]{2,1,0:T(8,128)(2,1)S(1)}, bf16[5,128,128]{2,1,0:T(8,128)(2,1)S(1)}, u32[]{:S(2)}, u32[]{:S(2)}) collective-permute-start(bf16[5,128,128]{2,1,0:T(8,128)(2,1)S(1)} %collective-permute-done.5.refs_0_), channel_id=1, source_target_pairs={{0,4},{2,6},{4,0},{6,2},{8,12},{10,14},{12,8},{14,10},{16,20},{18,... | collective-permute-start | bytes 491528 | tf_op jit(solution)/shard_map/ppermute | solution.py:242
  63.4 11.1 %collective-permute-start.4 = (bf16[5,128,128]{2,1,0:T(8,128)(2,1)S(1)}, bf16[5,128,128]{2,1,0:T(8,128)(2,1)S(1)}, u32[]{:S(2)}, u32[]{:S(2)}) collective-permute-start(bf16[5,128,128]{2,1,0:T(8,128)(2,1)S(1)} %collective-permute-done.3.refs_2_), channel_id=1, source_target_pairs={{0,4},{2,6},{4,0},{6,2},{8,12},{10,14},{12,8},{14,10},{16,20},{18,... | collective-permute-start | bytes 491528 | tf_op jit(solution)/shard_map/ppermute | solution.py:242
  65.3 9.3 %collective-permute-start.8 = (bf16[5,128,128]{2,1,0:T(8,128)(2,1)S(1)}, bf16[5,128,128]{2,1,0:T(8,128)(2,1)S(1)}, u32[]{:S(2)}, u32[]{:S(2)}) collective-permute-start(bf16[5,128,128]{2,1,0:T(8,128)(2,1)S(1)} %collective-permute-done.5.refs_0_), channel_id=1, source_target_pairs={{0,12},{2,14},{4,8},{6,10},{8,4},{10,6},{12,0},{14,2},{16,28},{18,... | collective-permute-start | bytes 491528 | tf_op jit(solution)/shard_map/ppermute | solution.py:242
  65.7 8.9 %collective-permute-start.7 = (bf16[5,128,128]{2,1,0:T(8,128)(2,1)S(1)}, bf16[5,128,128]{2,1,0:T(8,128)(2,1)S(1)}, u32[]{:S(2)}, u32[]{:S(2)}) collective-permute-start(bf16[5,128,128]{2,1,0:T(8,128)(2,1)S(1)} %collective-permute-done.5.refs_0_), channel_id=1, source_target_pairs={{0,8},{2,10},{4,12},{6,14},{8,0},{10,2},{12,4},{14,6},{16,24},{18,... | collective-permute-start | bytes 491528 | tf_op jit(solution)/shard_map/ppermute | solution.py:242
  74.5 2.2 %collective-permute-start.9 = (bf16[20,128,128]{2,1,0:T(8,128)(2,1)S(1)}, bf16[20,128,128]{2,1,0:T(8,128)(2,1)S(1)}, u32[]{:S(2)}, u32[]{:S(2)}) collective-permute-start(bf16[20,128,128]{2,1,0:T(8,128)(2,1)S(1)} %own_joined.2.rest_0_), channel_id=1, source_target_pairs={{0,2},{2,0},{4,6},{6,4},{8,10},{10,8},{12,14},{14,12},{16,18},{18,... | collective-permute-start | bytes 1966088 | tf_op jit(solution)/shard_map/ppermute | solution.py:242
  74.7 2.9 %collective-permute-start.10 = (bf16[20,128,128]{2,1,0:T(8,128)(2,1)S(1)}, bf16[20,128,128]{2,1,0:T(8,128)(2,1)S(1)}, u32[]{:S(2)}, u32[]{:S(2)}) collective-permute-start(bf16[20,128,128]{2,1,0:T(8,128)(2,1)S(1)} %own_joined.3.rest_1_), channel_id=1, source_target_pairs={{0,2},{2,0},{4,6},{6,4},{8,10},{10,8},{12,14},{14,12},{16,18},{18,... | collective-permute-start | bytes 1966088 | tf_op jit(solution)/shard_map/ppermute | solution.py:242
  77.6 4.4 %copy-start.3 = (bf16[10,36,128,128]{3,2,1,0:T(8,128)(2,1)S(1)}, bf16[10,36,128,128]{3,2,1,0:T(8,128)(2,1)}, u32[]{:S(2)}) copy-start(bf16[10,36,128,128]{3,2,1,0:T(8,128)(2,1)} %copy-done.2) | copy-start | bytes 35389444
  84.1 7.1 %collective-permute-start.12 = (bf16[5,128,128]{2,1,0:T(8,128)(2,1)S(1)}, bf16[5,128,128]{2,1,0:T(8,128)(2,1)S(1)}, u32[]{:S(2)}, u32[]{:S(2)}) collective-permute-start(bf16[5,128,128]{2,1,0:T(8,128)(2,1)S(1)} %get-tuple-element.24.mine_ref), channel_id=1, source_target_pairs={{0,1},{1,0},{2,3},{3,2},{4,5},{5,4},{6,7},{7,6},{8,9},{9,8},{10,11... | collective-permute-start | bytes 491528 | tf_op jit(solution)/shard_map/ppermute | solution.py:245
  88.0 5.9 %collective-permute-start.11 = (bf16[5,128,128]{2,1,0:T(8,128)(2,1)S(1)}, bf16[5,128,128]{2,1,0:T(8,128)(2,1)S(1)}, u32[]{:S(2)}, u32[]{:S(2)}) collective-permute-start(bf16[5,128,128]{2,1,0:T(8,128)(2,1)S(1)} %second_layer.3.mine_ref), channel_id=1, source_target_pairs={{0,1},{1,0},{2,3},{3,2},{4,5},{5,4},{6,7},{7,6},{8,9},{9,8},{10,11... | collective-permute-start | bytes 491528 | tf_op jit(solution)/shard_map/ppermute | solution.py:245

commit v8 on v7

--- a/solution.py
+++ b/solution.py
@@ -61,14 +61,7 @@
             return carry
 
         lax.fori_loop(0, total, add, 0)
-    sums = jnp.sum(acc_ref[:groups], axis=1)
-    if len(sums_ref.shape) == 2:
-        sums_ref[...] = sums
-    else:
-        share = groups // sums_ref.shape[0]
-        sums_ref[...] = jnp.zeros_like(sums_ref)
-        for i in range(sums_ref.shape[0]):
-            sums_ref[i, :share] = sums[i * share : (i + 1) * share]
+    sums_ref[...] = jnp.sum(acc_ref[:groups], axis=1)
 
 
 def multiply_rows(rows, counts_ref, chunk, start, gather, acc_ref):
@@ -94,12 +87,7 @@
     if sending is not None:
         side = lax.axis_index("col")
         base = (1 - side if sending else side) * count
-    if len(sums_ref.shape) == 2:
-        sums = sums_ref[...]
-    else:
-        share = added_ref.shape[0] // sums_ref.shape[0]
-        sums = jnp.concatenate([sums_ref[i, :share] for i in range(sums_ref.shape[0])], axis=0)
-    inverse_ref[...] = (1.0 / (sums + added_ref[...]))[:, None, :]
+    inverse_ref[...] = (1.0 / (sums_ref[...] + added_ref[...]))[:, None, :]
 
     def gather(row, slot):
         col = cols_ref[row, slot]
@@ -131,15 +119,17 @@
     return scale
 
 
-PLACES = ((0, 0), (0, 1), (1, 0), (1, 1))
+FIRST = ((0, 0, 0), (0, 1, 0), (1, 0, 0), (0, 0, 1), (0, 1, 1), (1, 0, 1))
+LAST = ((1, 1, 0), (1, 1, 1))
 
 
 def second_part_kernel(which, cols_ref, counts_ref, coef_ref, own_ref, *rest):
     part = own_ref.shape[0]
     if which == 0:
         pieces, (out_ref, source_ref, acc_ref) = rest[:-3], rest[-3:]
-        for array, (core, away) in zip(pieces, ((0, 0), (0, 1), (1, 0), (1, 1))):
-            for i, (z, y) in enumerate(PLACES):
+        for number, array in enumerate(pieces):
+            core = number // 2
+            for i, (z, y, away) in enumerate((FIRST, LAST)[number % 2]):
                 at = ((z * 4 + y * 2 + core) * 2 + away) * part
                 source_ref[at : at + part] = array[i * part : (i + 1) * part]
     else:
@@ -181,11 +171,13 @@
         away_ref[...] = own_ref[...]
 
 
-def join_kernel(*refs):
-    out_ref, pieces = refs[-1], refs[:4]
+def join_kernel(copies, *refs):
+    pieces, joined_ref, copy_refs = refs[: -1 - len(copies)], refs[-1 - len(copies)], refs[len(refs) - len(copies) :]
     part = pieces[0].shape[0]
     for i, piece in enumerate(pieces):
-        out_ref[i * part : (i + 1) * part] = piece[...]
+        joined_ref[i * part : (i + 1) * part] = piece[...]
+    for i, copy_ref in zip(copies, copy_refs):
+        copy_ref[...] = pieces[i][...]
 
 
 def result_kernel(first_row, mine_ref, other_ref, *rest):
@@ -214,7 +206,7 @@
     width = demand.shape[1]
     groups = demand.shape[0] // size
     group_devices = n_row // n_col
-    paired = n_col == 2 and n_row == 16 and rows % 2 == 0 and groups % n_row == 0 and groups // n_row <= 8
+    paired = n_col == 2 and n_row == 16 and rows % 2 == 0
     half = rows // 2
     counts = counts.reshape(rows)
 
@@ -222,7 +214,7 @@
         sums_kernel,
         name="column_sums",
         out_shape=(
-            jax.ShapeDtypeStruct((n_row, 8, size) if paired else (groups, size), jnp.float32),
+            jax.ShapeDtypeStruct((groups, size), jnp.float32),
             pltpu.VMEM(blocks.shape, blocks.dtype),
         ),
         in_specs=[pl.BlockSpec(memory_space=pltpu.HBM)] * 3,
@@ -245,9 +237,8 @@
         return lax.ppermute(array, "col", [(0, 1), (1, 0)])
 
     if paired:
-        shares = lax.all_to_all(sums, "row", 0, 0)
-        share = jnp.broadcast_to(jnp.sum(shares, axis=0), sums.shape)
-        sums = lax.all_to_all(share, "row", 0, 0)
+        for mask in (1, 2, 4, 8):
+            sums = sums + flip(sums.astype(jnp.bfloat16), mask).astype(jnp.float32)
     else:
         sums = lax.psum(sums, "row")
 
@@ -318,22 +309,22 @@
         compiler_params=PARAMS,
     )(own, flip(own, group_devices))
 
-    def join(pieces, earlier):
+    def join(pieces, copies):
         return pl.pallas_call(
-            join_kernel,
+            functools.partial(join_kernel, copies),
             name="own_joined",
-            out_shape=jax.ShapeDtypeStruct((4 * half, size, width), own.dtype),
-            in_specs=[VMEM] * 4 + [pl.BlockSpec(memory_space=pl.ANY)] * len(earlier),
-            out_specs=VMEM,
+            out_shape=[jax.ShapeDtypeStruct((len(pieces) * half, size, width), own.dtype)] + [piece] * len(copies),
+            in_specs=[VMEM] * len(pieces),
+            out_specs=[VMEM] * (1 + len(copies)),
             compiler_params=PARAMS,
-        )(*pieces, *earlier)
+        )(*pieces)
 
     away = swap(away)
-    home_z, home_y = flip(home, 4), flip(home, 2)
-    away_y, away_z, away_yz = flip(away, 2), flip(away, 4), flip(away, 6)
-    home = join([home, home_y, home_z, flip(home_z, 2)], [away_y])
-    away = join([away, away_y, away_z, away_yz], [])
-    pieces = [home, away, flip(home, 1), flip(away, 1)]
+    home_y, home_z = flip(home, 2), flip(home, 4)
+    away_y, away_z = flip(away, 2), flip(away, 4)
+    first, home_z, away_y = join([home, home_y, home_z, away, away_y, away_z], (2, 4))
+    (last,) = join([flip(home_z, 2), flip(away_y, 4)], ())
+    pieces = [first, last, flip(first, 1), flip(last, 1)]
 
     part_a, source = second_call(functools.partial(second_part_kernel, 0), half, coefs, own, pieces, True)
     other_a = swap(part_a)

time: 95.1 us -> 69.5 us (0.73)
  blocking collectives: 23.5 us -> 0 us
  starting transfers between devices: 9.03 us -> 26.8 us
  local copies, waits for them, and re-layouts: 17.4 us -> 0.01 us
  Pallas kernels: 16.3 us -> 12 us
  waiting for transfers between devices: 28.1 us -> 29.9 us
    all_to_all x2 -> x0, blocking collectives: 23.5 us -> none  [the longest x1 14 us: body(): shares = lax.all_to_all(sums, 'row', 0, 0)]
    unnamed x16 -> x8, local copies, waits for them, and re-layouts: 17.4 us -> 0.01 us
    ppermute x9 -> x13, starting transfers between devices: 5.68 us -> 20.8 us  [flip(): return lax.ppermute(array, 'row', [(i, i ^ mask) for i in range(n_row)])]
    ppermute x9 -> x13, waiting for transfers between devices: 18.5 us -> 21.2 us  [flip(): return lax.ppermute(array, 'row', [(i, i ^ mask) for i in range(n_row)])]
    ppermute x4, starting transfers between devices: 3.35 us -> 5.99 us  [swap(): return lax.ppermute(array, 'col', [(0, 1), (1, 0)])]
    pallas_call x2, Pallas kernels: 6.11 us -> 4.41 us  [first_layer(): pl.pallas_call(functools.partial(first_kernel, sending), name='first_laye...]
    pallas_call x2, Pallas kernels: 4.63 us -> 3 us  [second_call(): pl.pallas_call(kernel, name='second_layer', out_shape=(out, jax.ShapeDtyp...]
    pallas_call x1, Pallas kernels: 4.07 us -> 3.02 us  [body(): pl.pallas_call(sums_kernel, name='column_sums', out_shape=(jax.ShapeDtype...]
  transfers between devices with their start and end apart: 13 -> 17, of which waited for: 9 -> 15; matrix products, arithmetic and copies ran while one was open for 0% -> 0% of each run, Pallas kernels for 6% -> 6%
where the time goes in v8:
time: 69.5 us; the launch traced here: 69 us
  waiting for transfers between devices  29.9 us (43%)
  starting transfers between devices  26.8 us (39%)
  Pallas kernels  12 us (17%)
    ppermute x13, waiting for transfers between devices, flip(): return lax.ppermute(array, 'row', [(i, i ^ mask) for i in range(n_row)])  21.2 us
    ppermute x13, starting transfers between devices, flip(): return lax.ppermute(array, 'row', [(i, i ^ mask) for i in range(n_row)])  20.8 us
    ppermute x4, waiting for transfers between devices, swap(): return lax.ppermute(array, 'col', [(0, 1), (1, 0)])  8.68 us
    ppermute x4, starting transfers between devices, swap(): return lax.ppermute(array, 'col', [(0, 1), (1, 0)])  5.99 us
    pallas_call x2, Pallas kernels, first_layer(): pl.pallas_call(functools.partial(first_kernel, sending), name='first_laye...  4.41 us
    pallas_call x1, Pallas kernels, body(): pl.pallas_call(sums_kernel, name='column_sums', out_shape=(jax.ShapeDtype...  3.02 us
    pallas_call x2, Pallas kernels, second_call(): pl.pallas_call(kernel, name='second_layer', out_shape=(out, jax.ShapeDtyp...  3 us
    pallas_call x2, Pallas kernels, result(): pl.pallas_call(functools.partial(result_kernel, first_row), name='result'...  1.43 us
  transfers between devices with their start and end apart: 17, of which 15 were waited for; matrix products, arithmetic and copies ran while one was open for 0% of the time, Pallas kernels for 6%

profile of v8, /device:TPU:0, one launch (start us, length us, event | category | flops | bytes accessed | tf_op | source)
XLA Modules:
  0.0 69.0 jit_solution(11648265074633000840)
XLA Ops:
  0.0 0.0 copy-start.1
  0.0 0.0 copy-start.3
  0.0 0.0 copy-start.2
  0.0 0.0 copy-start
  0.0 3.0 %column_sums.1 = (f32[80,128]{1,0:T(8,128)S(1)}, bf16[10,36,128,128]{3,2,1,0:T(8,128)(2,1)S(1)}) custom-call(s32[10,36]{1,0:T(8,128)} %cols_ref.7, s32[10]{0:T(128)} %bitcast.8, bf16[10,36,128,128]{3,2,1,0:T(8,128)(2,1)} %blocks_ref.1), custom_call_target="tpu_custom_call" | custom-call | bytes 23592960 | tf_op jit(solution)/shard_map/column_sums/pallas_call | solution.py:213
  3.1 1.4 %collective-permute-start = (bf16[80,128]{1,0:T(8,128)(2,1)S(1)}, bf16[80,128]{1,0:T(8,128)(2,1)S(1)}, u32[]{:S(2)}, u32[]{:S(2)}) collective-permute-start(bf16[80,128]{1,0:T(8,128)(2,1)S(1)} %convert_element_type.30), channel_id=1, source_target_pairs={{0,2},{2,0},{4,6},{6,4},{8,10},{10,8},{12,14},{14,12},{16,18},{18,... | collective-permute-start | bytes 61448 | tf_op jit(solution)/shard_map/ppermute | solution.py:234
  4.5 0.8 %collective-permute-done = bf16[80,128]{1,0:T(8,128)(2,1)S(1)} collective-permute-done((bf16[80,128]{1,0:T(8,128)(2,1)S(1)}, bf16[80,128]{1,0:T(8,128)(2,1)S(1)}, u32[]{:S(2)}, u32[]{:S(2)}) %collective-permute-start) | collective-permute-done | bytes 20512 | tf_op jit(solution)/shard_map/ppermute | solution.py:234
  5.4 2.4 %collective-permute-start.1 = (bf16[80,128]{1,0:T(8,128)(2,1)S(1)}, bf16[80,128]{1,0:T(8,128)(2,1)S(1)}, u32[]{:S(2)}, u32[]{:S(2)}) collective-permute-start(bf16[80,128]{1,0:T(8,128)(2,1)S(1)} %fusion), channel_id=1, source_target_pairs={{0,4},{2,6},{4,0},{6,2},{8,12},{10,14},{12,8},{14,10},{16,20},{18,... | collective-permute-start | bytes 61448 | tf_op jit(solution)/shard_map/ppermute | solution.py:234
  7.8 1.8 %collective-permute-done.1 = bf16[80,128]{1,0:T(8,128)(2,1)S(1)} collective-permute-done((bf16[80,128]{1,0:T(8,128)(2,1)S(1)}, bf16[80,128]{1,0:T(8,128)(2,1)S(1)}, u32[]{:S(2)}, u32[]{:S(2)}) %collective-permute-start.1) | collective-permute-done | bytes 20512 | tf_op jit(solution)/shard_map/ppermute | solution.py:234
  9.6 2.0 %collective-permute-start.2 = (bf16[80,128]{1,0:T(8,128)(2,1)S(1)}, bf16[80,128]{1,0:T(8,128)(2,1)S(1)}, u32[]{:S(2)}, u32[]{:S(2)}) collective-permute-start(bf16[80,128]{1,0:T(8,128)(2,1)S(1)} %fusion.2), channel_id=1, source_target_pairs={{0,8},{2,10},{4,12},{6,14},{8,0},{10,2},{12,4},{14,6},{16,24},{18,... | collective-permute-start | bytes 61448 | tf_op jit(solution)/shard_map/ppermute | solution.py:234
  11.6 1.9 %collective-permute-done.2 = bf16[80,128]{1,0:T(8,128)(2,1)S(1)} collective-permute-done((bf16[80,128]{1,0:T(8,128)(2,1)S(1)}, bf16[80,128]{1,0:T(8,128)(2,1)S(1)}, u32[]{:S(2)}, u32[]{:S(2)}) %collective-permute-start.2) | collective-permute-done | bytes 20512 | tf_op jit(solution)/shard_map/ppermute | solution.py:234
  13.4 3.3 %collective-permute-start.3 = (bf16[80,128]{1,0:T(8,128)(2,1)S(1)}, bf16[80,128]{1,0:T(8,128)(2,1)S(1)}, u32[]{:S(2)}, u32[]{:S(2)}) collective-permute-start(bf16[80,128]{1,0:T(8,128)(2,1)S(1)} %fusion.1), channel_id=1, source_target_pairs={{0,16},{2,18},{4,20},{6,22},{8,24},{10,26},{12,28},{14,30},{16,0},... | collective-permute-start | bytes 61448 | tf_op jit(solution)/shard_map/ppermute | solution.py:234
  16.7 1.8 %collective-permute-done.3 = bf16[80,128]{1,0:T(8,128)(2,1)S(1)} collective-permute-done((bf16[80,128]{1,0:T(8,128)(2,1)S(1)}, bf16[80,128]{1,0:T(8,128)(2,1)S(1)}, u32[]{:S(2)}, u32[]{:S(2)}) %collective-permute-start.3) | collective-permute-done | bytes 20512 | tf_op jit(solution)/shard_map/ppermute | solution.py:234
  18.5 0.0 copy-done.1
  18.5 0.0 copy-done.3
  18.6 0.0 copy-done.2
  18.6 0.0 copy-done
  18.6 2.2 %first_layer.2 = (bf16[5,128,128]{2,1,0:T(8,128)(2,1)S(1)}, bf16[10,36,128,128]{3,2,1,0:T(8,128)(2,1)S(1)}) custom-call(s32[10,36]{1,0:T(8,128)S(1)} %copy-done.1, s32[10]{0:T(128)S(1)} %bitcast.9, f32[80,128]{1,0:T(8,128)S(1)} %convert_add_fusion.sums_ref, f32[80,128]{1,0:T(8,128)S(1)} %bitcast.6, ...), custom_call_target="tpu_custom_call", output_to_operand_aliasing={{1}: (5, {})} | custom-call | flops 754974720 | bytes 5898240 | tf_op jit(solution)/shard_map/first_layer/pallas_call | solution.py:249
  20.8 1.8 %collective-permute-start.4 = (bf16[5,128,128]{2,1,0:T(8,128)(2,1)S(1)}, bf16[5,128,128]{2,1,0:T(8,128)(2,1)S(1)}, u32[]{:S(2)}, u32[]{:S(2)}) collective-permute-start(bf16[5,128,128]{2,1,0:T(8,128)(2,1)S(1)} %get-tuple-element.23), channel_id=1, source_target_pairs={{0,1},{1,0},{2,3},{3,2},{4,5},{5,4},{6,7},{7,6},{8,9},{9,8},{10,11... | collective-permute-start | bytes 491528 | tf_op jit(solution)/shard_map/ppermute | solution.py:237
  22.6 2.2 %first_layer.3 = (f32[5,128,128]{2,1,0:T(8,128)S(1)}, bf16[10,36,128,128]{3,2,1,0:T(8,128)(2,1)S(1)}) custom-call(s32[10,36]{1,0:T(8,128)S(1)} %copy-done.1, s32[10]{0:T(128)S(1)} %bitcast.10, f32[80,128]{1,0:T(8,128)S(1)} %convert_add_fusion.sums_ref, f32[80,128]{1,0:T(8,128)S(1)} %bitcast.7, ...), custom_call_target="tpu_custom_call", output_to_operand_aliasing={{1}: (5, {})} | custom-call | flops 754974720 | bytes 5898240 | tf_op jit(solution)/shard_map/first_layer/pallas_call | solution.py:249
  24.8 1.4 %collective-permute-done.4 = bf16[5,128,128]{2,1,0:T(8,128)(2,1)S(1)} collective-permute-done((bf16[5,128,128]{2,1,0:T(8,128)(2,1)S(1)}, bf16[5,128,128]{2,1,0:T(8,128)(2,1)S(1)}, u32[]{:S(2)}, u32[]{:S(2)}) %collective-permute-start.4) | collective-permute-done | bytes 163872 | tf_op jit(solution)/shard_map/ppermute | solution.py:237
  26.2 3.2 %collective-permute-start.5 = (bf16[5,128,128]{2,1,0:T(8,128)(2,1)S(1)}, bf16[5,128,128]{2,1,0:T(8,128)(2,1)S(1)}, u32[]{:S(2)}, u32[]{:S(2)}) collective-permute-start(bf16[5,128,128]{2,1,0:T(8,128)(2,1)S(1)} %add_convert_fusion.own_ref), channel_id=1, source_target_pairs={{0,16},{2,18},{4,20},{6,22},{8,24},{10,26},{12,28},{14,30},{16,0},... | collective-permute-start | bytes 491528 | tf_op jit(solution)/shard_map/ppermute | solution.py:234
  29.5 5.2 %collective-permute-done.5.crossed_ref = bf16[5,128,128]{2,1,0:T(8,128)(2,1)S(1)} collective-permute-done((bf16[5,128,128]{2,1,0:T(8,128)(2,1)S(1)}, bf16[5,128,128]{2,1,0:T(8,128)(2,1)S(1)}, u32[]{:S(2)}, u32[]{:S(2)}) %collective-permute-start.5) | collective-permute-done | bytes 163872 | tf_op jit(solution)/shard_map/ppermute | solution.py:234
  34.6 2.1 %collective-permute-start.8 = (bf16[5,128,128]{2,1,0:T(8,128)(2,1)S(1)}, bf16[5,128,128]{2,1,0:T(8,128)(2,1)S(1)}, u32[]{:S(2)}, u32[]{:S(2)}) collective-permute-start(bf16[5,128,128]{2,1,0:T(8,128)(2,1)S(1)} %get-tuple-element.25), channel_id=1, source_target_pairs={{0,1},{1,0},{2,3},{3,2},{4,5},{5,4},{6,7},{7,6},{8,9},{9,8},{10,11... | collective-permute-start | bytes 491528 | tf_op jit(solution)/shard_map/ppermute | solution.py:237
  36.7 0.9 %collective-permute-start.7 = (bf16[5,128,128]{2,1,0:T(8,128)(2,1)S(1)}, bf16[5,128,128]{2,1,0:T(8,128)(2,1)S(1)}, u32[]{:S(2)}, u32[]{:S(2)}) collective-permute-start(bf16[5,128,128]{2,1,0:T(8,128)(2,1)S(1)} %get-tuple-element.24.refs_0_), channel_id=1, source_target_pairs={{0,8},{2,10},{4,12},{6,14},{8,0},{10,2},{12,4},{14,6},{16,24},{18,... | collective-permute-start | bytes 491528 | tf_op jit(solution)/shard_map/ppermute | solution.py:234
  37.7 1.2 %collective-permute-start.6 = (bf16[5,128,128]{2,1,0:T(8,128)(2,1)S(1)}, bf16[5,128,128]{2,1,0:T(8,128)(2,1)S(1)}, u32[]{:S(2)}, u32[]{:S(2)}) collective-permute-start(bf16[5,128,128]{2,1,0:T(8,128)(2,1)S(1)} %get-tuple-element.24.refs_0_), channel_id=1, source_target_pairs={{0,4},{2,6},{4,0},{6,2},{8,12},{10,14},{12,8},{14,10},{16,20},{18,... | collective-permute-start | bytes 491528 | tf_op jit(solution)/shard_map/ppermute | solution.py:234
  38.9 1.2 %collective-permute-done.8.refs_3_ = bf16[5,128,128]{2,1,0:T(8,128)(2,1)S(1)} collective-permute-done((bf16[5,128,128]{2,1,0:T(8,128)(2,1)S(1)}, bf16[5,128,128]{2,1,0:T(8,128)(2,1)S(1)}, u32[]{:S(2)}, u32[]{:S(2)}) %collective-permute-start.8) | collective-permute-done | bytes 163872 | tf_op jit(solution)/shard_map/ppermute | solution.py:237
  40.0 0.9 %collective-permute-start.10 = (bf16[5,128,128]{2,1,0:T(8,128)(2,1)S(1)}, bf16[5,128,128]{2,1,0:T(8,128)(2,1)S(1)}, u32[]{:S(2)}, u32[]{:S(2)}) collective-permute-start(bf16[5,128,128]{2,1,0:T(8,128)(2,1)S(1)} %collective-permute-done.8.refs_3_), channel_id=1, source_target_pairs={{0,8},{2,10},{4,12},{6,14},{8,0},{10,2},{12,4},{14,6},{16,24},{18,... | collective-permute-start | bytes 491528 | tf_op jit(solution)/shard_map/ppermute | solution.py:234
  41.0 1.7 %collective-permute-start.9 = (bf16[5,128,128]{2,1,0:T(8,128)(2,1)S(1)}, bf16[5,128,128]{2,1,0:T(8,128)(2,1)S(1)}, u32[]{:S(2)}, u32[]{:S(2)}) collective-permute-start(bf16[5,128,128]{2,1,0:T(8,128)(2,1)S(1)} %collective-permute-done.8.refs_3_), channel_id=1, source_target_pairs={{0,4},{2,6},{4,0},{6,2},{8,12},{10,14},{12,8},{14,10},{16,20},{18,... | collective-permute-start | bytes 491528 | tf_op jit(solution)/shard_map/ppermute | solution.py:234
  42.7 0.0 collective-permute-done.7.refs_2_
  42.7 0.3 collective-permute-done.6.refs_1_
  43.0 2.4 %collective-permute-done.10.refs_5_ = bf16[5,128,128]{2,1,0:T(8,128)(2,1)S(1)} collective-permute-done((bf16[5,128,128]{2,1,0:T(8,128)(2,1)S(1)}, bf16[5,128,128]{2,1,0:T(8,128)(2,1)S(1)}, u32[]{:S(2)}, u32[]{:S(2)}) %collective-permute-start.10) | collective-permute-done | bytes 163872 | tf_op jit(solution)/shard_map/ppermute | solution.py:234
  45.4 0.9 %collective-permute-done.9.refs_4_ = bf16[5,128,128]{2,1,0:T(8,128)(2,1)S(1)} collective-permute-done((bf16[5,128,128]{2,1,0:T(8,128)(2,1)S(1)}, bf16[5,128,128]{2,1,0:T(8,128)(2,1)S(1)}, u32[]{:S(2)}, u32[]{:S(2)}) %collective-permute-start.9) | collective-permute-done | bytes 163872 | tf_op jit(solution)/shard_map/ppermute | solution.py:234
  46.3 0.1 own_joined.2
  46.4 0.1 collective-permute-start.13
  46.5 1.8 %collective-permute-start.11 = (bf16[5,128,128]{2,1,0:T(8,128)(2,1)S(1)}, bf16[5,128,128]{2,1,0:T(8,128)(2,1)S(1)}, u32[]{:S(2)}, u32[]{:S(2)}) collective-permute-start(bf16[5,128,128]{2,1,0:T(8,128)(2,1)S(1)} %get-tuple-element.27), channel_id=1, source_target_pairs={{0,4},{2,6},{4,0},{6,2},{8,12},{10,14},{12,8},{14,10},{16,20},{18,... | collective-permute-start | bytes 491528 | tf_op jit(solution)/shard_map/ppermute | solution.py:234
  48.3 1.7 %collective-permute-start.12 = (bf16[5,128,128]{2,1,0:T(8,128)(2,1)S(1)}, bf16[5,128,128]{2,1,0:T(8,128)(2,1)S(1)}, u32[]{:S(2)}, u32[]{:S(2)}) collective-permute-start(bf16[5,128,128]{2,1,0:T(8,128)(2,1)S(1)} %get-tuple-element.28), channel_id=1, source_target_pairs={{0,8},{2,10},{4,12},{6,14},{8,0},{10,2},{12,4},{14,6},{16,24},{18,... | collective-permute-start | bytes 491528 | tf_op jit(solution)/shard_map/ppermute | solution.py:234
  49.9 3.2 %collective-permute-done.11.refs_0_ = bf16[5,128,128]{2,1,0:T(8,128)(2,1)S(1)} collective-permute-done((bf16[5,128,128]{2,1,0:T(8,128)(2,1)S(1)}, bf16[5,128,128]{2,1,0:T(8,128)(2,1)S(1)}, u32[]{:S(2)}, u32[]{:S(2)}) %collective-permute-start.11) | collective-permute-done | bytes 163872 | tf_op jit(solution)/shard_map/ppermute | solution.py:234
  53.1 1.4 %collective-permute-done.12.refs_1_ = bf16[5,128,128]{2,1,0:T(8,128)(2,1)S(1)} collective-permute-done((bf16[5,128,128]{2,1,0:T(8,128)(2,1)S(1)}, bf16[5,128,128]{2,1,0:T(8,128)(2,1)S(1)}, u32[]{:S(2)}, u32[]{:S(2)}) %collective-permute-start.12) | collective-permute-done | bytes 163872 | tf_op jit(solution)/shard_map/ppermute | solution.py:234
  54.6 0.1 collective-permute-start.14
  54.6 1.6 %collective-permute-done.14.rest_3_ = bf16[10,128,128]{2,1,0:T(8,128)(2,1)S(1)} collective-permute-done((bf16[10,128,128]{2,1,0:T(8,128)(2,1)S(1)}, bf16[10,128,128]{2,1,0:T(8,128)(2,1)S(1)}, u32[]{:S(2)}, u32[]{:S(2)}) %collective-permute-start.14) | collective-permute-done | bytes 327712 | tf_op jit(solution)/shard_map/ppermute | solution.py:234
  56.3 0.0 collective-permute-done.13.rest_2_
  56.3 1.6 %second_layer.2 = (bf16[5,128,128]{2,1,0:T(8,128)(2,1)S(1)}, bf16[80,128,128]{2,1,0:T(8,128)(2,1)S(1)}) custom-call(s32[10,36]{1,0:T(8,128)S(1)} %copy-done.1, s32[10]{0:T(128)S(1)} %bitcast.11, bf16[10,36,128,128]{3,2,1,0:T(8,128)(2,1)S(1)} %get-tuple-element.21.coef_ref, bf16[5,128,128]{2,1,0:T(8,128)(2,1)S(1)} %add_convert_fusion.own_ref, ...), custom_call_target="tpu_custom_call" | custom-call | flops 754974720 | bytes 5898240 | tf_op jit(solution)/shard_map/second_layer/pallas_call | solution.py:277
  57.9 1.8 %collective-permute-start.16 = (bf16[5,128,128]{2,1,0:T(8,128)(2,1)S(1)}, bf16[5,128,128]{2,1,0:T(8,128)(2,1)S(1)}, u32[]{:S(2)}, u32[]{:S(2)}) collective-permute-start(bf16[5,128,128]{2,1,0:T(8,128)(2,1)S(1)} %get-tuple-element.30.mine_ref), channel_id=1, source_target_pairs={{0,1},{1,0},{2,3},{3,2},{4,5},{5,4},{6,7},{7,6},{8,9},{9,8},{10,11... | collective-permute-start | bytes 491528 | tf_op jit(solution)/shard_map/ppermute | solution.py:237
  59.7 1.4 %second_layer.3.mine_ref = bf16[5,128,128]{2,1,0:T(8,128)(2,1)S(1)} custom-call(s32[10,36]{1,0:T(8,128)S(1)} %copy-done.1, s32[10]{0:T(128)S(1)} %bitcast.12, bf16[10,36,128,128]{3,2,1,0:T(8,128)(2,1)S(1)} %get-tuple-element.21.coef_ref, bf16[5,128,128]{2,1,0:T(8,128)(2,1)S(1)} %add_convert_fusion.own_ref, bf16[80,128,128]{2,1,0:T(8,128)(2,1)S(1)} %get-tuple-element.29.rest_0_), custom_call_target="tpu_custom_call" | custom-call | flops 754974720 | bytes 5898240 | tf_op jit(solution)/shard_map/second_layer/pallas_call | solution.py:277
  61.1 0.3 collective-permute-start.15
  61.4 3.3 %collective-permute-done.16.other_ref = bf16[5,128,128]{2,1,0:T(8,128)(2,1)S(1)} collective-permute-done((bf16[5,128,128]{2,1,0:T(8,128)(2,1)S(1)}, bf16[5,128,128]{2,1,0:T(8,128)(2,1)S(1)}, u32[]{:S(2)}, u32[]{:S(2)}) %collective-permute-start.16) | collective-permute-done | bytes 163872 | tf_op jit(solution)/shard_map/ppermute | solution.py:237
  64.7 0.7 %result.2.rest_0_ = bf16[10,128,128]{2,1,0:T(8,128)(2,1)} custom-call(bf16[5,128,128]{2,1,0:T(8,128)(2,1)S(1)} %get-tuple-element.30.mine_ref, bf16[5,128,128]{2,1,0:T(8,128)(2,1)S(1)} %collective-permute-done.16.other_ref), custom_call_target="tpu_custom_call" | custom-call | tf_op jit(solution)/shard_map/result/pallas_call | solution.py:335
  65.5 2.8 %collective-permute-done.15.other_ref = bf16[5,128,128]{2,1,0:T(8,128)(2,1)S(1)} collective-permute-done((bf16[5,128,128]{2,1,0:T(8,128)(2,1)S(1)}, bf16[5,128,128]{2,1,0:T(8,128)(2,1)S(1)}, u32[]{:S(2)}, u32[]{:S(2)}) %collective-permute-start.15) | collective-permute-done | bytes 163872 | tf_op jit(solution)/shard_map/ppermute | solution.py:237
  68.3 0.7 %result.3 = bf16[10,128,128]{2,1,0:T(8,128)(2,1)} custom-call(bf16[5,128,128]{2,1,0:T(8,128)(2,1)S(1)} %second_layer.3.mine_ref, bf16[5,128,128]{2,1,0:T(8,128)(2,1)S(1)} %collective-permute-done.15.other_ref, bf16[10,128,128]{2,1,0:T(8,128)(2,1)} %result.2.rest_0_), custom_call_target="tpu_custom_call", output_to_operand_aliasing={{}: (2, {})} | custom-call | tf_op jit(solution)/shard_map/result/pallas_call | solution.py:335
  (8 shorter events, 0.1 us)
Async XLA Ops:
  0.0 18.5 %copy-start.1 = (s32[10,36]{1,0:T(8,128)S(1)}, s32[10,36]{1,0:T(8,128)}, u32[]{:S(2)}) copy-start(s32[10,36]{1,0:T(8,128)} %cols_ref.7) | copy-start | bytes 4324
  0.0 18.5 %copy-start.3 = (s32[10,1]{0,1:T(1,128)S(1)}, s32[10,1]{0,1:T(1,128)}, u32[]{:S(2)}) copy-start(s32[10,1]{0,1:T(1,128)} %param.7) | copy-start | bytes 124
  0.0 18.5 %copy-start.2 = (f32[10240]{0:T(1024)S(1)}, f32[10240]{0:T(1024)}, u32[]{:S(2)}) copy-start(f32[10240]{0:T(1024)} %param.9) | copy-start | bytes 122884
  0.0 18.6 %copy-start = (bf16[10240,128]{1,0:T(8,128)(2,1)S(1)}, bf16[10240,128]{1,0:T(8,128)(2,1)}, u32[]{:S(2)}) copy-start(bf16[10240,128]{1,0:T(8,128)(2,1)} %param.8) | copy-start | bytes 7864324
  3.1 2.3 %collective-permute-start = (bf16[80,128]{1,0:T(8,128)(2,1)S(1)}, bf16[80,128]{1,0:T(8,128)(2,1)S(1)}, u32[]{:S(2)}, u32[]{:S(2)}) collective-permute-start(bf16[80,128]{1,0:T(8,128)(2,1)S(1)} %convert_element_type.30), channel_id=1, source_target_pairs={{0,2},{2,0},{4,6},{6,4},{8,10},{10,8},{12,14},{14,12},{16,18},{18,... | collective-permute-start | bytes 61448 | tf_op jit(solution)/shard_map/ppermute | solution.py:234
  5.4 4.2 %collective-permute-start.1 = (bf16[80,128]{1,0:T(8,128)(2,1)S(1)}, bf16[80,128]{1,0:T(8,128)(2,1)S(1)}, u32[]{:S(2)}, u32[]{:S(2)}) collective-permute-start(bf16[80,128]{1,0:T(8,128)(2,1)S(1)} %fusion), channel_id=1, source_target_pairs={{0,4},{2,6},{4,0},{6,2},{8,12},{10,14},{12,8},{14,10},{16,20},{18,... | collective-permute-start | bytes 61448 | tf_op jit(solution)/shard_map/ppermute | solution.py:234
  9.6 3.8 %collective-permute-start.2 = (bf16[80,128]{1,0:T(8,128)(2,1)S(1)}, bf16[80,128]{1,0:T(8,128)(2,1)S(1)}, u32[]{:S(2)}, u32[]{:S(2)}) collective-permute-start(bf16[80,128]{1,0:T(8,128)(2,1)S(1)} %fusion.2), channel_id=1, source_target_pairs={{0,8},{2,10},{4,12},{6,14},{8,0},{10,2},{12,4},{14,6},{16,24},{18,... | collective-permute-start | bytes 61448 | tf_op jit(solution)/shard_map/ppermute | solution.py:234
  13.4 5.1 %collective-permute-start.3 = (bf16[80,128]{1,0:T(8,128)(2,1)S(1)}, bf16[80,128]{1,0:T(8,128)(2,1)S(1)}, u32[]{:S(2)}, u32[]{:S(2)}) collective-permute-start(bf16[80,128]{1,0:T(8,128)(2,1)S(1)} %fusion.1), channel_id=1, source_target_pairs={{0,16},{2,18},{4,20},{6,22},{8,24},{10,26},{12,28},{14,30},{16,0},... | collective-permute-start | bytes 61448 | tf_op jit(solution)/shard_map/ppermute | solution.py:234
  20.8 5.4 %collective-permute-start.4 = (bf16[5,128,128]{2,1,0:T(8,128)(2,1)S(1)}, bf16[5,128,128]{2,1,0:T(8,128)(2,1)S(1)}, u32[]{:S(2)}, u32[]{:S(2)}) collective-permute-start(bf16[5,128,128]{2,1,0:T(8,128)(2,1)S(1)} %get-tuple-element.23), channel_id=1, source_target_pairs={{0,1},{1,0},{2,3},{3,2},{4,5},{5,4},{6,7},{7,6},{8,9},{9,8},{10,11... | collective-permute-start | bytes 491528 | tf_op jit(solution)/shard_map/ppermute | solution.py:237
  26.2 8.4 %collective-permute-start.5 = (bf16[5,128,128]{2,1,0:T(8,128)(2,1)S(1)}, bf16[5,128,128]{2,1,0:T(8,128)(2,1)S(1)}, u32[]{:S(2)}, u32[]{:S(2)}) collective-permute-start(bf16[5,128,128]{2,1,0:T(8,128)(2,1)S(1)} %add_convert_fusion.own_ref), channel_id=1, source_target_pairs={{0,16},{2,18},{4,20},{6,22},{8,24},{10,26},{12,28},{14,30},{16,0},... | collective-permute-start | bytes 491528 | tf_op jit(solution)/shard_map/ppermute | solution.py:234
  34.6 5.4 %collective-permute-start.8 = (bf16[5,128,128]{2,1,0:T(8,128)(2,1)S(1)}, bf16[5,128,128]{2,1,0:T(8,128)(2,1)S(1)}, u32[]{:S(2)}, u32[]{:S(2)}) collective-permute-start(bf16[5,128,128]{2,1,0:T(8,128)(2,1)S(1)} %get-tuple-element.25), channel_id=1, source_target_pairs={{0,1},{1,0},{2,3},{3,2},{4,5},{5,4},{6,7},{7,6},{8,9},{9,8},{10,11... | collective-permute-start | bytes 491528 | tf_op jit(solution)/shard_map/ppermute | solution.py:237
  36.7 6.0 %collective-permute-start.7 = (bf16[5,128,128]{2,1,0:T(8,128)(2,1)S(1)}, bf16[5,128,128]{2,1,0:T(8,128)(2,1)S(1)}, u32[]{:S(2)}, u32[]{:S(2)}) collective-permute-start(bf16[5,128,128]{2,1,0:T(8,128)(2,1)S(1)} %get-tuple-element.24.refs_0_), channel_id=1, source_target_pairs={{0,8},{2,10},{4,12},{6,14},{8,0},{10,2},{12,4},{14,6},{16,24},{18,... | collective-permute-start | bytes 491528 | tf_op jit(solution)/shard_map/ppermute | solution.py:234
  37.7 5.3 %collective-permute-start.6 = (bf16[5,128,128]{2,1,0:T(8,128)(2,1)S(1)}, bf16[5,128,128]{2,1,0:T(8,128)(2,1)S(1)}, u32[]{:S(2)}, u32[]{:S(2)}) collective-permute-start(bf16[5,128,128]{2,1,0:T(8,128)(2,1)S(1)} %get-tuple-element.24.refs_0_), channel_id=1, source_target_pairs={{0,4},{2,6},{4,0},{6,2},{8,12},{10,14},{12,8},{14,10},{16,20},{18,... | collective-permute-start | bytes 491528 | tf_op jit(solution)/shard_map/ppermute | solution.py:234
  40.0 5.3 %collective-permute-start.10 = (bf16[5,128,128]{2,1,0:T(8,128)(2,1)S(1)}, bf16[5,128,128]{2,1,0:T(8,128)(2,1)S(1)}, u32[]{:S(2)}, u32[]{:S(2)}) collective-permute-start(bf16[5,128,128]{2,1,0:T(8,128)(2,1)S(1)} %collective-permute-done.8.refs_3_), channel_id=1, source_target_pairs={{0,8},{2,10},{4,12},{6,14},{8,0},{10,2},{12,4},{14,6},{16,24},{18,... | collective-permute-start | bytes 491528 | tf_op jit(solution)/shard_map/ppermute | solution.py:234
  41.0 5.3 %collective-permute-start.9 = (bf16[5,128,128]{2,1,0:T(8,128)(2,1)S(1)}, bf16[5,128,128]{2,1,0:T(8,128)(2,1)S(1)}, u32[]{:S(2)}, u32[]{:S(2)}) collective-permute-start(bf16[5,128,128]{2,1,0:T(8,128)(2,1)S(1)} %collective-permute-done.8.refs_3_), channel_id=1, source_target_pairs={{0,4},{2,6},{4,0},{6,2},{8,12},{10,14},{12,8},{14,10},{16,20},{18,... | collective-permute-start | bytes 491528 | tf_op jit(solution)/shard_map/ppermute | solution.py:234
  46.4 9.9 %collective-permute-start.13 = (bf16[30,128,128]{2,1,0:T(8,128)(2,1)S(1)}, bf16[30,128,128]{2,1,0:T(8,128)(2,1)S(1)}, u32[]{:S(2)}, u32[]{:S(2)}) collective-permute-start(bf16[30,128,128]{2,1,0:T(8,128)(2,1)S(1)} %get-tuple-element.26.rest_0_), channel_id=1, source_target_pairs={{0,2},{2,0},{4,6},{6,4},{8,10},{10,8},{12,14},{14,12},{16,18},{18,... | collective-permute-start | bytes 2949128 | tf_op jit(solution)/shard_map/ppermute | solution.py:234
  46.5 6.6 %collective-permute-start.11 = (bf16[5,128,128]{2,1,0:T(8,128)(2,1)S(1)}, bf16[5,128,128]{2,1,0:T(8,128)(2,1)S(1)}, u32[]{:S(2)}, u32[]{:S(2)}) collective-permute-start(bf16[5,128,128]{2,1,0:T(8,128)(2,1)S(1)} %get-tuple-element.27), channel_id=1, source_target_pairs={{0,4},{2,6},{4,0},{6,2},{8,12},{10,14},{12,8},{14,10},{16,20},{18,... | collective-permute-start | bytes 491528 | tf_op jit(solution)/shard_map/ppermute | solution.py:234
  48.3 6.3 %collective-permute-start.12 = (bf16[5,128,128]{2,1,0:T(8,128)(2,1)S(1)}, bf16[5,128,128]{2,1,0:T(8,128)(2,1)S(1)}, u32[]{:S(2)}, u32[]{:S(2)}) collective-permute-start(bf16[5,128,128]{2,1,0:T(8,128)(2,1)S(1)} %get-tuple-element.28), channel_id=1, source_target_pairs={{0,8},{2,10},{4,12},{6,14},{8,0},{10,2},{12,4},{14,6},{16,24},{18,... | collective-permute-start | bytes 491528 | tf_op jit(solution)/shard_map/ppermute | solution.py:234
  54.6 1.7 %collective-permute-start.14 = (bf16[10,128,128]{2,1,0:T(8,128)(2,1)S(1)}, bf16[10,128,128]{2,1,0:T(8,128)(2,1)S(1)}, u32[]{:S(2)}, u32[]{:S(2)}) collective-permute-start(bf16[10,128,128]{2,1,0:T(8,128)(2,1)S(1)} %own_joined.3.rest_1_), channel_id=1, source_target_pairs={{0,2},{2,0},{4,6},{6,4},{8,10},{10,8},{12,14},{14,12},{16,18},{18,... | collective-permute-start | bytes 983048 | tf_op jit(solution)/shard_map/ppermute | solution.py:234
  57.9 6.9 %collective-permute-start.16 = (bf16[5,128,128]{2,1,0:T(8,128)(2,1)S(1)}, bf16[5,128,128]{2,1,0:T(8,128)(2,1)S(1)}, u32[]{:S(2)}, u32[]{:S(2)}) collective-permute-start(bf16[5,128,128]{2,1,0:T(8,128)(2,1)S(1)} %get-tuple-element.30.mine_ref), channel_id=1, source_target_pairs={{0,1},{1,0},{2,3},{3,2},{4,5},{5,4},{6,7},{7,6},{8,9},{9,8},{10,11... | collective-permute-start | bytes 491528 | tf_op jit(solution)/shard_map/ppermute | solution.py:237
  61.1 7.1 %collective-permute-start.15 = (bf16[5,128,128]{2,1,0:T(8,128)(2,1)S(1)}, bf16[5,128,128]{2,1,0:T(8,128)(2,1)S(1)}, u32[]{:S(2)}, u32[]{:S(2)}) collective-permute-start(bf16[5,128,128]{2,1,0:T(8,128)(2,1)S(1)} %second_layer.3.mine_ref), channel_id=1, source_target_pairs={{0,1},{1,0},{2,3},{3,2},{4,5},{5,4},{6,7},{7,6},{8,9},{9,8},{10,11... | collective-permute-start | bytes 491528 | tf_op jit(solution)/shard_map/ppermute | solution.py:237

commit v9 on v8

--- a/solution.py
+++ b/solution.py
@@ -119,17 +119,15 @@
     return scale
 
 
-FIRST = ((0, 0, 0), (0, 1, 0), (1, 0, 0), (0, 0, 1), (0, 1, 1), (1, 0, 1))
-LAST = ((1, 1, 0), (1, 1, 1))
+PLACES = ((0, 0), (0, 1), (1, 0), (1, 1))
 
 
 def second_part_kernel(which, cols_ref, counts_ref, coef_ref, own_ref, *rest):
     part = own_ref.shape[0]
     if which == 0:
         pieces, (out_ref, source_ref, acc_ref) = rest[:-3], rest[-3:]
-        for number, array in enumerate(pieces):
-            core = number // 2
-            for i, (z, y, away) in enumerate((FIRST, LAST)[number % 2]):
+        for array, (core, away) in zip(pieces, ((0, 0), (0, 1), (1, 0), (1, 1))):
+            for i, (z, y) in enumerate(PLACES):
                 at = ((z * 4 + y * 2 + core) * 2 + away) * part
                 source_ref[at : at + part] = array[i * part : (i + 1) * part]
     else:
@@ -171,13 +169,11 @@
         away_ref[...] = own_ref[...]
 
 
-def join_kernel(copies, *refs):
-    pieces, joined_ref, copy_refs = refs[: -1 - len(copies)], refs[-1 - len(copies)], refs[len(refs) - len(copies) :]
+def join_kernel(*refs):
+    pieces, joined_ref = refs[:-1], refs[-1]
     part = pieces[0].shape[0]
     for i, piece in enumerate(pieces):
         joined_ref[i * part : (i + 1) * part] = piece[...]
-    for i, copy_ref in zip(copies, copy_refs):
-        copy_ref[...] = pieces[i][...]
 
 
 def result_kernel(first_row, mine_ref, other_ref, *rest):
@@ -237,8 +233,10 @@
         return lax.ppermute(array, "col", [(0, 1), (1, 0)])
 
     if paired:
-        for mask in (1, 2, 4, 8):
-            sums = sums + flip(sums.astype(jnp.bfloat16), mask).astype(jnp.float32)
+        sums = sums + flip(sums.astype(jnp.bfloat16), 1).astype(jnp.float32)
+        shared = sums.astype(jnp.bfloat16)
+        for part in [flip(shared, mask) for mask in (12, 14, 8, 10, 4, 6, 2)]:
+            sums = sums + part.astype(jnp.float32)
     else:
         sums = lax.psum(sums, "row")
 
@@ -309,22 +307,23 @@
         compiler_params=PARAMS,
     )(own, flip(own, group_devices))
 
-    def join(pieces, copies):
+    def join(pieces):
         return pl.pallas_call(
-            functools.partial(join_kernel, copies),
+            join_kernel,
             name="own_joined",
-            out_shape=[jax.ShapeDtypeStruct((len(pieces) * half, size, width), own.dtype)] + [piece] * len(copies),
+            out_shape=jax.ShapeDtypeStruct((len(pieces) * half, size, width), own.dtype),
             in_specs=[VMEM] * len(pieces),
-            out_specs=[VMEM] * (1 + len(copies)),
+            out_specs=VMEM,
             compiler_params=PARAMS,
         )(*pieces)
 
-    away = swap(away)
-    home_y, home_z = flip(home, 2), flip(home, 4)
-    away_y, away_z = flip(away, 2), flip(away, 4)
-    first, home_z, away_y = join([home, home_y, home_z, away, away_y, away_z], (2, 4))
-    (last,) = join([flip(home_z, 2), flip(away_y, 4)], ())
-    pieces = [first, last, flip(first, 1), flip(last, 1)]
+    def move(array, mask):
+        pairs = [(i * 2 + c, (i ^ mask) * 2 + 1 - c) for i in range(n_row) for c in range(2)]
+        return lax.ppermute(array, ("row", "col"), pairs)
+
+    away = join([move(away, mask) for mask in (0, 2, 4, 6)])
+    home = join([home] + [flip(home, mask) for mask in (2, 4, 6)])
+    pieces = [home, away, flip(home, 1), flip(away, 1)]
 
     part_a, source = second_call(functools.partial(second_part_kernel, 0), half, coefs, own, pieces, True)
     other_a = swap(part_a)

time: 69.5 us -> 69.5 us (level); the launches traced: 69 us -> 69.9 us
  starting transfers between devices: 26.8 us -> 23.9 us
  Pallas kernels: 12 us -> 14.9 us
  waiting for transfers between devices: 29.9 us -> 30.9 us
    ppermute x0 -> x4, waiting for transfers between devices: none -> 8.79 us  [move(): return lax.ppermute(array, ('row', 'col'), pairs)]
    ppermute x13 -> x14, starting transfers between devices: 20.8 us -> 14.3 us  [flip(): return lax.ppermute(array, 'row', [(i, i ^ mask) for i in range(n_row)])]
    ppermute x0 -> x4, starting transfers between devices: none -> 5.92 us  [move(): return lax.ppermute(array, ('row', 'col'), pairs)]
    ppermute x13 -> x14, waiting for transfers between devices: 21.2 us -> 16 us  [flip(): return lax.ppermute(array, 'row', [(i, i ^ mask) for i in range(n_row)])]
    ppermute x4 -> x3, waiting for transfers between devices: 8.68 us -> 6.09 us  [swap(): return lax.ppermute(array, 'col', [(0, 1), (1, 0)])]
    ppermute x4 -> x3, starting transfers between devices: 5.99 us -> 3.65 us  [swap(): return lax.ppermute(array, 'col', [(0, 1), (1, 0)])]
    pallas_call x2, Pallas kernels: 4.41 us -> 5.56 us  [first_layer(): pl.pallas_call(functools.partial(first_kernel, sending), name='first_laye...]
    pallas_call x2, Pallas kernels: 3 us -> 4.08 us  [second_call(): pl.pallas_call(kernel, name='second_layer', out_shape=(out, jax.ShapeDtyp...]
  transfers between devices with their start and end apart: 17 -> 21, of which waited for: 15 -> 15; matrix products, arithmetic and copies ran while one was open for 0% -> 0% of each run, Pallas kernels for 6% -> 8%
where the time goes in v9:
time: 69.5 us; the launch traced here: 69.9 us
  waiting for transfers between devices  30.9 us (44%)
  starting transfers between devices  23.9 us (34%)
  Pallas kernels  14.9 us (21%)
    ppermute x14, waiting for transfers between devices, flip(): return lax.ppermute(array, 'row', [(i, i ^ mask) for i in range(n_row)])  16 us
    ppermute x14, starting transfers between devices, flip(): return lax.ppermute(array, 'row', [(i, i ^ mask) for i in range(n_row)])  14.3 us
    ppermute x4, waiting for transfers between devices, move(): return lax.ppermute(array, ('row', 'col'), pairs)  8.79 us
    ppermute x3, waiting for transfers between devices, swap(): return lax.ppermute(array, 'col', [(0, 1), (1, 0)])  6.09 us
    ppermute x4, starting transfers between devices, move(): return lax.ppermute(array, ('row', 'col'), pairs)  5.92 us
    pallas_call x2, Pallas kernels, first_layer(): pl.pallas_call(functools.partial(first_kernel, sending), name='first_laye...  5.56 us
    pallas_call x2, Pallas kernels, second_call(): pl.pallas_call(kernel, name='second_layer', out_shape=(out, jax.ShapeDtyp...  4.08 us
    pallas_call x1, Pallas kernels, body(): pl.pallas_call(sums_kernel, name='column_sums', out_shape=(jax.ShapeDtype...  3.73 us
  transfers between devices with their start and end apart: 21, of which 15 were waited for; matrix products, arithmetic and copies ran while one was open for 0% of the time, Pallas kernels for 8%

profile of v9, /device:TPU:0, one launch (start us, length us, event | category | flops | bytes accessed | tf_op | source)
XLA Modules:
  0.0 69.9 jit_solution(9527613648571428263)
XLA Ops:
  0.0 0.0 copy-start.1
  0.0 0.0 copy-start.3
  0.0 0.0 copy-start.2
  0.0 0.0 copy-start
  0.0 3.7 %column_sums.1 = (f32[80,128]{1,0:T(8,128)S(1)}, bf16[10,36,128,128]{3,2,1,0:T(8,128)(2,1)S(1)}) custom-call(s32[10,36]{1,0:T(8,128)} %cols_ref.7, s32[10]{0:T(128)} %bitcast.8, bf16[10,36,128,128]{3,2,1,0:T(8,128)(2,1)} %blocks_ref.1), custom_call_target="tpu_custom_call" | custom-call | bytes 23592960 | tf_op jit(solution)/shard_map/column_sums/pallas_call | solution.py:209
  3.8 0.6 collective-permute-start
  4.4 0.8 %collective-permute-done = bf16[80,128]{1,0:T(8,128)(2,1)S(1)} collective-permute-done((bf16[80,128]{1,0:T(8,128)(2,1)S(1)}, bf16[80,128]{1,0:T(8,128)(2,1)S(1)}, u32[]{:S(2)}, u32[]{:S(2)}) %collective-permute-start) | collective-permute-done | bytes 20512 | tf_op jit(solution)/shard_map/ppermute | solution.py:230
  5.2 2.8 %collective-permute-start.7 = (bf16[80,128]{1,0:T(8,128)(2,1)S(1)}, bf16[80,128]{1,0:T(8,128)(2,1)S(1)}, u32[]{:S(2)}, u32[]{:S(2)}) collective-permute-start(bf16[80,128]{1,0:T(8,128)(2,1)S(1)} %fusion), channel_id=1, source_target_pairs={{0,4},{2,6},{4,0},{6,2},{8,12},{10,14},{12,8},{14,10},{16,20},{18,... | collective-permute-start | bytes 61448 | tf_op jit(solution)/shard_map/ppermute | solution.py:230
  8.0 1.8 %collective-permute-start.6 = (bf16[80,128]{1,0:T(8,128)(2,1)S(1)}, bf16[80,128]{1,0:T(8,128)(2,1)S(1)}, u32[]{:S(2)}, u32[]{:S(2)}) collective-permute-start(bf16[80,128]{1,0:T(8,128)(2,1)S(1)} %fusion), channel_id=1, source_target_pairs={{0,12},{2,14},{4,8},{6,10},{8,4},{10,6},{12,0},{14,2},{16,28},{18,... | collective-permute-start | bytes 61448 | tf_op jit(solution)/shard_map/ppermute | solution.py:230
  9.8 0.0 collective-permute-start.5
  9.8 3.8 %collective-permute-start.4 = (bf16[80,128]{1,0:T(8,128)(2,1)S(1)}, bf16[80,128]{1,0:T(8,128)(2,1)S(1)}, u32[]{:S(2)}, u32[]{:S(2)}) collective-permute-start(bf16[80,128]{1,0:T(8,128)(2,1)S(1)} %fusion), channel_id=1, source_target_pairs={{0,20},{2,22},{4,16},{6,18},{8,28},{10,30},{12,24},{14,26},{16,4},... | collective-permute-start | bytes 61448 | tf_op jit(solution)/shard_map/ppermute | solution.py:230
  13.5 0.3 collective-permute-start.3
  13.8 0.0 collective-permute-done.7
  13.8 3.9 %collective-permute-start.2 = (bf16[80,128]{1,0:T(8,128)(2,1)S(1)}, bf16[80,128]{1,0:T(8,128)(2,1)S(1)}, u32[]{:S(2)}, u32[]{:S(2)}) collective-permute-start(bf16[80,128]{1,0:T(8,128)(2,1)S(1)} %fusion), channel_id=1, source_target_pairs={{0,28},{2,30},{4,24},{6,26},{8,20},{10,22},{12,16},{14,18},{16,12}... | collective-permute-start | bytes 61448 | tf_op jit(solution)/shard_map/ppermute | solution.py:230
  17.8 0.0 collective-permute-done.6
  17.8 0.0 collective-permute-start.1
  17.8 0.0 collective-permute-done.5
  17.8 0.0 collective-permute-done.4
  17.8 0.4 collective-permute-done.3
  18.2 2.1 %collective-permute-done.2 = bf16[80,128]{1,0:T(8,128)(2,1)S(1)} collective-permute-done((bf16[80,128]{1,0:T(8,128)(2,1)S(1)}, bf16[80,128]{1,0:T(8,128)(2,1)S(1)}, u32[]{:S(2)}, u32[]{:S(2)}) %collective-permute-start.2) | collective-permute-done | bytes 20512 | tf_op jit(solution)/shard_map/ppermute | solution.py:230
  20.3 3.0 %collective-permute-done.1 = bf16[80,128]{1,0:T(8,128)(2,1)S(1)} collective-permute-done((bf16[80,128]{1,0:T(8,128)(2,1)S(1)}, bf16[80,128]{1,0:T(8,128)(2,1)S(1)}, u32[]{:S(2)}, u32[]{:S(2)}) %collective-permute-start.1) | collective-permute-done | bytes 20512 | tf_op jit(solution)/shard_map/ppermute | solution.py:230
  23.4 0.0 copy-done.1
  23.4 0.0 copy-done.3
  23.4 0.0 copy-done.2
  23.4 0.0 copy-done
  23.4 2.8 %first_layer.2 = (bf16[5,128,128]{2,1,0:T(8,128)(2,1)S(1)}, bf16[10,36,128,128]{3,2,1,0:T(8,128)(2,1)S(1)}) custom-call(s32[10,36]{1,0:T(8,128)S(1)} %copy-done.1, s32[10]{0:T(128)S(1)} %bitcast.9, f32[80,128]{1,0:T(8,128)S(1)} %convert_add_fusion.sums_ref, f32[80,128]{1,0:T(8,128)S(1)} %bitcast.6, ...), custom_call_target="tpu_custom_call", output_to_operand_aliasing={{1}: (5, {})} | custom-call | flops 754974720 | bytes 5898240 | tf_op jit(solution)/shard_map/first_layer/pallas_call | solution.py:247
  26.3 1.5 %collective-permute-start.8 = (bf16[5,128,128]{2,1,0:T(8,128)(2,1)S(1)}, bf16[5,128,128]{2,1,0:T(8,128)(2,1)S(1)}, u32[]{:S(2)}, u32[]{:S(2)}) collective-permute-start(bf16[5,128,128]{2,1,0:T(8,128)(2,1)S(1)} %get-tuple-element.20), channel_id=1, source_target_pairs={{0,1},{1,0},{2,3},{3,2},{4,5},{5,4},{6,7},{7,6},{8,9},{9,8},{10,11... | collective-permute-start | bytes 491528 | tf_op jit(solution)/shard_map/ppermute | solution.py:233
  27.8 2.8 %first_layer.3 = (f32[5,128,128]{2,1,0:T(8,128)S(1)}, bf16[10,36,128,128]{3,2,1,0:T(8,128)(2,1)S(1)}) custom-call(s32[10,36]{1,0:T(8,128)S(1)} %copy-done.1, s32[10]{0:T(128)S(1)} %bitcast.10, f32[80,128]{1,0:T(8,128)S(1)} %convert_add_fusion.sums_ref, f32[80,128]{1,0:T(8,128)S(1)} %bitcast.7, ...), custom_call_target="tpu_custom_call", output_to_operand_aliasing={{1}: (5, {})} | custom-call | flops 754974720 | bytes 5898240 | tf_op jit(solution)/shard_map/first_layer/pallas_call | solution.py:247
  30.5 1.1 %collective-permute-done.8 = bf16[5,128,128]{2,1,0:T(8,128)(2,1)S(1)} collective-permute-done((bf16[5,128,128]{2,1,0:T(8,128)(2,1)S(1)}, bf16[5,128,128]{2,1,0:T(8,128)(2,1)S(1)}, u32[]{:S(2)}, u32[]{:S(2)}) %collective-permute-start.8) | collective-permute-done | bytes 163872 | tf_op jit(solution)/shard_map/ppermute | solution.py:233
  31.7 0.1 collective-permute-start.9
  31.8 6.7 %collective-permute-done.9.crossed_ref = bf16[5,128,128]{2,1,0:T(8,128)(2,1)S(1)} collective-permute-done((bf16[5,128,128]{2,1,0:T(8,128)(2,1)S(1)}, bf16[5,128,128]{2,1,0:T(8,128)(2,1)S(1)}, u32[]{:S(2)}, u32[]{:S(2)}) %collective-permute-start.9) | collective-permute-done | bytes 163872 | tf_op jit(solution)/shard_map/ppermute | solution.py:230
  38.5 0.3 collective-permute-start.16
  38.8 2.3 %collective-permute-start.15 = (bf16[5,128,128]{2,1,0:T(8,128)(2,1)S(1)}, bf16[5,128,128]{2,1,0:T(8,128)(2,1)S(1)}, u32[]{:S(2)}, u32[]{:S(2)}) collective-permute-start(bf16[5,128,128]{2,1,0:T(8,128)(2,1)S(1)} %get-tuple-element.22), channel_id=1, source_target_pairs={{0,9},{1,8},{2,11},{3,10},{4,13},{5,12},{6,15},{7,14},{8,1},{9,0},... | collective-permute-start | bytes 491528 | tf_op jit(solution)/shard_map/ppermute | solution.py:322
  41.2 2.3 %collective-permute-start.14 = (bf16[5,128,128]{2,1,0:T(8,128)(2,1)S(1)}, bf16[5,128,128]{2,1,0:T(8,128)(2,1)S(1)}, u32[]{:S(2)}, u32[]{:S(2)}) collective-permute-start(bf16[5,128,128]{2,1,0:T(8,128)(2,1)S(1)} %get-tuple-element.22), channel_id=1, source_target_pairs={{0,5},{1,4},{2,7},{3,6},{4,1},{5,0},{6,3},{7,2},{8,13},{9,12},{10,... | collective-permute-start | bytes 491528 | tf_op jit(solution)/shard_map/ppermute | solution.py:322
  43.4 1.0 %collective-permute-start.13 = (bf16[5,128,128]{2,1,0:T(8,128)(2,1)S(1)}, bf16[5,128,128]{2,1,0:T(8,128)(2,1)S(1)}, u32[]{:S(2)}, u32[]{:S(2)}) collective-permute-start(bf16[5,128,128]{2,1,0:T(8,128)(2,1)S(1)} %get-tuple-element.22), channel_id=1, source_target_pairs={{0,1},{1,0},{2,3},{3,2},{4,5},{5,4},{6,7},{7,6},{8,9},{9,8},{10,11... | collective-permute-start | bytes 491528 | tf_op jit(solution)/shard_map/ppermute | solution.py:322
  44.4 0.0 collective-permute-start.12
  44.4 3.2 %collective-permute-done.16.refs_3_ = bf16[5,128,128]{2,1,0:T(8,128)(2,1)S(1)} collective-permute-done((bf16[5,128,128]{2,1,0:T(8,128)(2,1)S(1)}, bf16[5,128,128]{2,1,0:T(8,128)(2,1)S(1)}, u32[]{:S(2)}, u32[]{:S(2)}) %collective-permute-start.16) | collective-permute-done | bytes 163872 | tf_op jit(solution)/shard_map/ppermute | solution.py:322
  47.6 0.0 collective-permute-start.11
  47.6 1.8 %collective-permute-done.15.refs_2_ = bf16[5,128,128]{2,1,0:T(8,128)(2,1)S(1)} collective-permute-done((bf16[5,128,128]{2,1,0:T(8,128)(2,1)S(1)}, bf16[5,128,128]{2,1,0:T(8,128)(2,1)S(1)}, u32[]{:S(2)}, u32[]{:S(2)}) %collective-permute-start.15) | collective-permute-done | bytes 163872 | tf_op jit(solution)/shard_map/ppermute | solution.py:322
  49.4 0.9 %collective-permute-start.10 = (bf16[5,128,128]{2,1,0:T(8,128)(2,1)S(1)}, bf16[5,128,128]{2,1,0:T(8,128)(2,1)S(1)}, u32[]{:S(2)}, u32[]{:S(2)}) collective-permute-start(bf16[5,128,128]{2,1,0:T(8,128)(2,1)S(1)} %get-tuple-element.21.refs_0_), channel_id=1, source_target_pairs={{0,4},{2,6},{4,0},{6,2},{8,12},{10,14},{12,8},{14,10},{16,20},{18,... | collective-permute-start | bytes 491528 | tf_op jit(solution)/shard_map/ppermute | solution.py:230
  50.3 1.7 %collective-permute-done.14.refs_1_ = bf16[5,128,128]{2,1,0:T(8,128)(2,1)S(1)} collective-permute-done((bf16[5,128,128]{2,1,0:T(8,128)(2,1)S(1)}, bf16[5,128,128]{2,1,0:T(8,128)(2,1)S(1)}, u32[]{:S(2)}, u32[]{:S(2)}) %collective-permute-start.14) | collective-permute-done | bytes 163872 | tf_op jit(solution)/shard_map/ppermute | solution.py:322
  52.0 2.2 %collective-permute-done.13.refs_0_ = bf16[5,128,128]{2,1,0:T(8,128)(2,1)S(1)} collective-permute-done((bf16[5,128,128]{2,1,0:T(8,128)(2,1)S(1)}, bf16[5,128,128]{2,1,0:T(8,128)(2,1)S(1)}, u32[]{:S(2)}, u32[]{:S(2)}) %collective-permute-start.13) | collective-permute-done | bytes 163872 | tf_op jit(solution)/shard_map/ppermute | solution.py:322
  54.2 0.1 collective-permute-start.18
  54.2 0.0 collective-permute-done.12.refs_3_
  54.2 0.0 collective-permute-done.11.refs_2_
  54.3 0.5 collective-permute-done.10.refs_1_
  54.8 0.1 collective-permute-start.17
  54.9 1.5 %collective-permute-done.18.rest_3_ = bf16[20,128,128]{2,1,0:T(8,128)(2,1)S(1)} collective-permute-done((bf16[20,128,128]{2,1,0:T(8,128)(2,1)S(1)}, bf16[20,128,128]{2,1,0:T(8,128)(2,1)S(1)}, u32[]{:S(2)}, u32[]{:S(2)}) %collective-permute-start.18) | collective-permute-done | bytes 655392 | tf_op jit(solution)/shard_map/ppermute | solution.py:230
  56.3 0.9 %collective-permute-done.17.rest_2_ = bf16[20,128,128]{2,1,0:T(8,128)(2,1)S(1)} collective-permute-done((bf16[20,128,128]{2,1,0:T(8,128)(2,1)S(1)}, bf16[20,128,128]{2,1,0:T(8,128)(2,1)S(1)}, u32[]{:S(2)}, u32[]{:S(2)}) %collective-permute-start.17) | collective-permute-done | bytes 655392 | tf_op jit(solution)/shard_map/ppermute | solution.py:230
  57.3 2.1 %second_layer.2 = (bf16[5,128,128]{2,1,0:T(8,128)(2,1)S(1)}, bf16[80,128,128]{2,1,0:T(8,128)(2,1)S(1)}) custom-call(s32[10,36]{1,0:T(8,128)S(1)} %copy-done.1, s32[10]{0:T(128)S(1)} %bitcast.11, bf16[10,36,128,128]{3,2,1,0:T(8,128)(2,1)S(1)} %get-tuple-element.18.coef_ref, bf16[5,128,128]{2,1,0:T(8,128)(2,1)S(1)} %add_convert_fusion.own_ref, ...), custom_call_target="tpu_custom_call" | custom-call | flops 754974720 | bytes 5898240 | tf_op jit(solution)/shard_map/second_layer/pallas_call | solution.py:275
  59.4 1.1 %collective-permute-start.20 = (bf16[5,128,128]{2,1,0:T(8,128)(2,1)S(1)}, bf16[5,128,128]{2,1,0:T(8,128)(2,1)S(1)}, u32[]{:S(2)}, u32[]{:S(2)}) collective-permute-start(bf16[5,128,128]{2,1,0:T(8,128)(2,1)S(1)} %get-tuple-element.24.mine_ref), channel_id=1, source_target_pairs={{0,1},{1,0},{2,3},{3,2},{4,5},{5,4},{6,7},{7,6},{8,9},{9,8},{10,11... | collective-permute-start | bytes 491528 | tf_op jit(solution)/shard_map/ppermute | solution.py:233
  60.5 2.0 %second_layer.3.mine_ref = bf16[5,128,128]{2,1,0:T(8,128)(2,1)S(1)} custom-call(s32[10,36]{1,0:T(8,128)S(1)} %copy-done.1, s32[10]{0:T(128)S(1)} %bitcast.12, bf16[10,36,128,128]{3,2,1,0:T(8,128)(2,1)S(1)} %get-tuple-element.18.coef_ref, bf16[5,128,128]{2,1,0:T(8,128)(2,1)S(1)} %add_convert_fusion.own_ref, bf16[80,128,128]{2,1,0:T(8,128)(2,1)S(1)} %get-tuple-element.23.rest_0_), custom_call_target="tpu_custom_call" | custom-call | flops 754974720 | bytes 5898240 | tf_op jit(solution)/shard_map/second_layer/pallas_call | solution.py:275
  62.5 1.0 %collective-permute-start.19 = (bf16[5,128,128]{2,1,0:T(8,128)(2,1)S(1)}, bf16[5,128,128]{2,1,0:T(8,128)(2,1)S(1)}, u32[]{:S(2)}, u32[]{:S(2)}) collective-permute-start(bf16[5,128,128]{2,1,0:T(8,128)(2,1)S(1)} %second_layer.3.mine_ref), channel_id=1, source_target_pairs={{0,1},{1,0},{2,3},{3,2},{4,5},{5,4},{6,7},{7,6},{8,9},{9,8},{10,11... | collective-permute-start | bytes 491528 | tf_op jit(solution)/shard_map/ppermute | solution.py:233
  63.5 2.8 %collective-permute-done.20.other_ref = bf16[5,128,128]{2,1,0:T(8,128)(2,1)S(1)} collective-permute-done((bf16[5,128,128]{2,1,0:T(8,128)(2,1)S(1)}, bf16[5,128,128]{2,1,0:T(8,128)(2,1)S(1)}, u32[]{:S(2)}, u32[]{:S(2)}) %collective-permute-start.20) | collective-permute-done | bytes 163872 | tf_op jit(solution)/shard_map/ppermute | solution.py:233
  66.3 0.7 %result.2.rest_0_ = bf16[10,128,128]{2,1,0:T(8,128)(2,1)} custom-call(bf16[5,128,128]{2,1,0:T(8,128)(2,1)S(1)} %get-tuple-element.24.mine_ref, bf16[5,128,128]{2,1,0:T(8,128)(2,1)S(1)} %collective-permute-done.20.other_ref), custom_call_target="tpu_custom_call" | custom-call | tf_op jit(solution)/shard_map/result/pallas_call | solution.py:334
  67.0 2.2 %collective-permute-done.19.other_ref = bf16[5,128,128]{2,1,0:T(8,128)(2,1)S(1)} collective-permute-done((bf16[5,128,128]{2,1,0:T(8,128)(2,1)S(1)}, bf16[5,128,128]{2,1,0:T(8,128)(2,1)S(1)}, u32[]{:S(2)}, u32[]{:S(2)}) %collective-permute-start.19) | collective-permute-done | bytes 163872 | tf_op jit(solution)/shard_map/ppermute | solution.py:233
  69.2 0.7 %result.3 = bf16[10,128,128]{2,1,0:T(8,128)(2,1)} custom-call(bf16[5,128,128]{2,1,0:T(8,128)(2,1)S(1)} %second_layer.3.mine_ref, bf16[5,128,128]{2,1,0:T(8,128)(2,1)S(1)} %collective-permute-done.19.other_ref, bf16[10,128,128]{2,1,0:T(8,128)(2,1)} %result.2.rest_0_), custom_call_target="tpu_custom_call", output_to_operand_aliasing={{}: (2, {})} | custom-call | tf_op jit(solution)/shard_map/result/pallas_call | solution.py:334
  (7 shorter events, 0.2 us)
Async XLA Ops:
  0.0 23.4 %copy-start.1 = (s32[10,36]{1,0:T(8,128)S(1)}, s32[10,36]{1,0:T(8,128)}, u32[]{:S(2)}) copy-start(s32[10,36]{1,0:T(8,128)} %cols_ref.7) | copy-start | bytes 4324
  0.0 23.4 %copy-start.3 = (s32[10,1]{0,1:T(1,128)S(1)}, s32[10,1]{0,1:T(1,128)}, u32[]{:S(2)}) copy-start(s32[10,1]{0,1:T(1,128)} %param.7) | copy-start | bytes 124
  0.0 23.4 %copy-start.2 = (f32[10240]{0:T(1024)S(1)}, f32[10240]{0:T(1024)}, u32[]{:S(2)}) copy-start(f32[10240]{0:T(1024)} %param.9) | copy-start | bytes 122884
  0.0 23.4 %copy-start = (bf16[10240,128]{1,0:T(8,128)(2,1)S(1)}, bf16[10240,128]{1,0:T(8,128)(2,1)}, u32[]{:S(2)}) copy-start(bf16[10240,128]{1,0:T(8,128)(2,1)} %param.8) | copy-start | bytes 7864324
  3.8 1.5 %collective-permute-start = (bf16[80,128]{1,0:T(8,128)(2,1)S(1)}, bf16[80,128]{1,0:T(8,128)(2,1)S(1)}, u32[]{:S(2)}, u32[]{:S(2)}) collective-permute-start(bf16[80,128]{1,0:T(8,128)(2,1)S(1)} %convert_element_type.36), channel_id=1, source_target_pairs={{0,2},{2,0},{4,6},{6,4},{8,10},{10,8},{12,14},{14,12},{16,18},{18,... | collective-permute-start | bytes 61448 | tf_op jit(solution)/shard_map/ppermute | solution.py:230
  5.2 8.6 %collective-permute-start.7 = (bf16[80,128]{1,0:T(8,128)(2,1)S(1)}, bf16[80,128]{1,0:T(8,128)(2,1)S(1)}, u32[]{:S(2)}, u32[]{:S(2)}) collective-permute-start(bf16[80,128]{1,0:T(8,128)(2,1)S(1)} %fusion), channel_id=1, source_target_pairs={{0,4},{2,6},{4,0},{6,2},{8,12},{10,14},{12,8},{14,10},{16,20},{18,... | collective-permute-start | bytes 61448 | tf_op jit(solution)/shard_map/ppermute | solution.py:230
  8.0 9.8 %collective-permute-start.6 = (bf16[80,128]{1,0:T(8,128)(2,1)S(1)}, bf16[80,128]{1,0:T(8,128)(2,1)S(1)}, u32[]{:S(2)}, u32[]{:S(2)}) collective-permute-start(bf16[80,128]{1,0:T(8,128)(2,1)S(1)} %fusion), channel_id=1, source_target_pairs={{0,12},{2,14},{4,8},{6,10},{8,4},{10,6},{12,0},{14,2},{16,28},{18,... | collective-permute-start | bytes 61448 | tf_op jit(solution)/shard_map/ppermute | solution.py:230
  9.8 8.0 %collective-permute-start.5 = (bf16[80,128]{1,0:T(8,128)(2,1)S(1)}, bf16[80,128]{1,0:T(8,128)(2,1)S(1)}, u32[]{:S(2)}, u32[]{:S(2)}) collective-permute-start(bf16[80,128]{1,0:T(8,128)(2,1)S(1)} %fusion), channel_id=1, source_target_pairs={{0,8},{2,10},{4,12},{6,14},{8,0},{10,2},{12,4},{14,6},{16,24},{18,... | collective-permute-start | bytes 61448 | tf_op jit(solution)/shard_map/ppermute | solution.py:230
  9.8 8.0 %collective-permute-start.4 = (bf16[80,128]{1,0:T(8,128)(2,1)S(1)}, bf16[80,128]{1,0:T(8,128)(2,1)S(1)}, u32[]{:S(2)}, u32[]{:S(2)}) collective-permute-start(bf16[80,128]{1,0:T(8,128)(2,1)S(1)} %fusion), channel_id=1, source_target_pairs={{0,20},{2,22},{4,16},{6,18},{8,28},{10,30},{12,24},{14,26},{16,4},... | collective-permute-start | bytes 61448 | tf_op jit(solution)/shard_map/ppermute | solution.py:230
  13.5 4.7 %collective-permute-start.3 = (bf16[80,128]{1,0:T(8,128)(2,1)S(1)}, bf16[80,128]{1,0:T(8,128)(2,1)S(1)}, u32[]{:S(2)}, u32[]{:S(2)}) collective-permute-start(bf16[80,128]{1,0:T(8,128)(2,1)S(1)} %fusion), channel_id=1, source_target_pairs={{0,16},{2,18},{4,20},{6,22},{8,24},{10,26},{12,28},{14,30},{16,0},... | collective-permute-start | bytes 61448 | tf_op jit(solution)/shard_map/ppermute | solution.py:230
  13.8 6.5 %collective-permute-start.2 = (bf16[80,128]{1,0:T(8,128)(2,1)S(1)}, bf16[80,128]{1,0:T(8,128)(2,1)S(1)}, u32[]{:S(2)}, u32[]{:S(2)}) collective-permute-start(bf16[80,128]{1,0:T(8,128)(2,1)S(1)} %fusion), channel_id=1, source_target_pairs={{0,28},{2,30},{4,24},{6,26},{8,20},{10,22},{12,16},{14,18},{16,12}... | collective-permute-start | bytes 61448 | tf_op jit(solution)/shard_map/ppermute | solution.py:230
  17.8 5.6 %collective-permute-start.1 = (bf16[80,128]{1,0:T(8,128)(2,1)S(1)}, bf16[80,128]{1,0:T(8,128)(2,1)S(1)}, u32[]{:S(2)}, u32[]{:S(2)}) collective-permute-start(bf16[80,128]{1,0:T(8,128)(2,1)S(1)} %fusion), channel_id=1, source_target_pairs={{0,24},{2,26},{4,28},{6,30},{8,16},{10,18},{12,20},{14,22},{16,8},... | collective-permute-start | bytes 61448 | tf_op jit(solution)/shard_map/ppermute | solution.py:230
  26.3 5.4 %collective-permute-start.8 = (bf16[5,128,128]{2,1,0:T(8,128)(2,1)S(1)}, bf16[5,128,128]{2,1,0:T(8,128)(2,1)S(1)}, u32[]{:S(2)}, u32[]{:S(2)}) collective-permute-start(bf16[5,128,128]{2,1,0:T(8,128)(2,1)S(1)} %get-tuple-element.20), channel_id=1, source_target_pairs={{0,1},{1,0},{2,3},{3,2},{4,5},{5,4},{6,7},{7,6},{8,9},{9,8},{10,11... | collective-permute-start | bytes 491528 | tf_op jit(solution)/shard_map/ppermute | solution.py:233
  31.7 6.8 %collective-permute-start.9 = (bf16[5,128,128]{2,1,0:T(8,128)(2,1)S(1)}, bf16[5,128,128]{2,1,0:T(8,128)(2,1)S(1)}, u32[]{:S(2)}, u32[]{:S(2)}) collective-permute-start(bf16[5,128,128]{2,1,0:T(8,128)(2,1)S(1)} %add_convert_fusion.own_ref), channel_id=1, source_target_pairs={{0,16},{2,18},{4,20},{6,22},{8,24},{10,26},{12,28},{14,30},{16,0},... | collective-permute-start | bytes 491528 | tf_op jit(solution)/shard_map/ppermute | solution.py:230
  38.5 9.1 %collective-permute-start.16 = (bf16[5,128,128]{2,1,0:T(8,128)(2,1)S(1)}, bf16[5,128,128]{2,1,0:T(8,128)(2,1)S(1)}, u32[]{:S(2)}, u32[]{:S(2)}) collective-permute-start(bf16[5,128,128]{2,1,0:T(8,128)(2,1)S(1)} %get-tuple-element.22), channel_id=1, source_target_pairs={{0,13},{1,12},{2,15},{3,14},{4,9},{5,8},{6,11},{7,10},{8,5},{9,4},... | collective-permute-start | bytes 491528 | tf_op jit(solution)/shard_map/ppermute | solution.py:322
  38.8 10.6 %collective-permute-start.15 = (bf16[5,128,128]{2,1,0:T(8,128)(2,1)S(1)}, bf16[5,128,128]{2,1,0:T(8,128)(2,1)S(1)}, u32[]{:S(2)}, u32[]{:S(2)}) collective-permute-start(bf16[5,128,128]{2,1,0:T(8,128)(2,1)S(1)} %get-tuple-element.22), channel_id=1, source_target_pairs={{0,9},{1,8},{2,11},{3,10},{4,13},{5,12},{6,15},{7,14},{8,1},{9,0},... | collective-permute-start | bytes 491528 | tf_op jit(solution)/shard_map/ppermute | solution.py:322
  41.2 10.8 %collective-permute-start.14 = (bf16[5,128,128]{2,1,0:T(8,128)(2,1)S(1)}, bf16[5,128,128]{2,1,0:T(8,128)(2,1)S(1)}, u32[]{:S(2)}, u32[]{:S(2)}) collective-permute-start(bf16[5,128,128]{2,1,0:T(8,128)(2,1)S(1)} %get-tuple-element.22), channel_id=1, source_target_pairs={{0,5},{1,4},{2,7},{3,6},{4,1},{5,0},{6,3},{7,2},{8,13},{9,12},{10,... | collective-permute-start | bytes 491528 | tf_op jit(solution)/shard_map/ppermute | solution.py:322
  43.4 10.7 %collective-permute-start.13 = (bf16[5,128,128]{2,1,0:T(8,128)(2,1)S(1)}, bf16[5,128,128]{2,1,0:T(8,128)(2,1)S(1)}, u32[]{:S(2)}, u32[]{:S(2)}) collective-permute-start(bf16[5,128,128]{2,1,0:T(8,128)(2,1)S(1)} %get-tuple-element.22), channel_id=1, source_target_pairs={{0,1},{1,0},{2,3},{3,2},{4,5},{5,4},{6,7},{7,6},{8,9},{9,8},{10,11... | collective-permute-start | bytes 491528 | tf_op jit(solution)/shard_map/ppermute | solution.py:322
  44.4 9.8 %collective-permute-start.12 = (bf16[5,128,128]{2,1,0:T(8,128)(2,1)S(1)}, bf16[5,128,128]{2,1,0:T(8,128)(2,1)S(1)}, u32[]{:S(2)}, u32[]{:S(2)}) collective-permute-start(bf16[5,128,128]{2,1,0:T(8,128)(2,1)S(1)} %get-tuple-element.21.refs_0_), channel_id=1, source_target_pairs={{0,12},{2,14},{4,8},{6,10},{8,4},{10,6},{12,0},{14,2},{16,28},{18,... | collective-permute-start | bytes 491528 | tf_op jit(solution)/shard_map/ppermute | solution.py:230
  47.6 6.7 %collective-permute-start.11 = (bf16[5,128,128]{2,1,0:T(8,128)(2,1)S(1)}, bf16[5,128,128]{2,1,0:T(8,128)(2,1)S(1)}, u32[]{:S(2)}, u32[]{:S(2)}) collective-permute-start(bf16[5,128,128]{2,1,0:T(8,128)(2,1)S(1)} %get-tuple-element.21.refs_0_), channel_id=1, source_target_pairs={{0,8},{2,10},{4,12},{6,14},{8,0},{10,2},{12,4},{14,6},{16,24},{18,... | collective-permute-start | bytes 491528 | tf_op jit(solution)/shard_map/ppermute | solution.py:230
  49.4 5.3 %collective-permute-start.10 = (bf16[5,128,128]{2,1,0:T(8,128)(2,1)S(1)}, bf16[5,128,128]{2,1,0:T(8,128)(2,1)S(1)}, u32[]{:S(2)}, u32[]{:S(2)}) collective-permute-start(bf16[5,128,128]{2,1,0:T(8,128)(2,1)S(1)} %get-tuple-element.21.refs_0_), channel_id=1, source_target_pairs={{0,4},{2,6},{4,0},{6,2},{8,12},{10,14},{12,8},{14,10},{16,20},{18,... | collective-permute-start | bytes 491528 | tf_op jit(solution)/shard_map/ppermute | solution.py:230
  54.2 2.2 %collective-permute-start.18 = (bf16[20,128,128]{2,1,0:T(8,128)(2,1)S(1)}, bf16[20,128,128]{2,1,0:T(8,128)(2,1)S(1)}, u32[]{:S(2)}, u32[]{:S(2)}) collective-permute-start(bf16[20,128,128]{2,1,0:T(8,128)(2,1)S(1)} %own_joined.3.rest_1_), channel_id=1, source_target_pairs={{0,2},{2,0},{4,6},{6,4},{8,10},{10,8},{12,14},{14,12},{16,18},{18,... | collective-permute-start | bytes 1966088 | tf_op jit(solution)/shard_map/ppermute | solution.py:230
  54.8 2.5 %collective-permute-start.17 = (bf16[20,128,128]{2,1,0:T(8,128)(2,1)S(1)}, bf16[20,128,128]{2,1,0:T(8,128)(2,1)S(1)}, u32[]{:S(2)}, u32[]{:S(2)}) collective-permute-start(bf16[20,128,128]{2,1,0:T(8,128)(2,1)S(1)} %own_joined.2.rest_0_), channel_id=1, source_target_pairs={{0,2},{2,0},{4,6},{6,4},{8,10},{10,8},{12,14},{14,12},{16,18},{18,... | collective-permute-start | bytes 1966088 | tf_op jit(solution)/shard_map/ppermute | solution.py:230
  59.4 6.9 %collective-permute-start.20 = (bf16[5,128,128]{2,1,0:T(8,128)(2,1)S(1)}, bf16[5,128,128]{2,1,0:T(8,128)(2,1)S(1)}, u32[]{:S(2)}, u32[]{:S(2)}) collective-permute-start(bf16[5,128,128]{2,1,0:T(8,128)(2,1)S(1)} %get-tuple-element.24.mine_ref), channel_id=1, source_target_pairs={{0,1},{1,0},{2,3},{3,2},{4,5},{5,4},{6,7},{7,6},{8,9},{9,8},{10,11... | collective-permute-start | bytes 491528 | tf_op jit(solution)/shard_map/ppermute | solution.py:233
  62.5 6.7 %collective-permute-start.19 = (bf16[5,128,128]{2,1,0:T(8,128)(2,1)S(1)}, bf16[5,128,128]{2,1,0:T(8,128)(2,1)S(1)}, u32[]{:S(2)}, u32[]{:S(2)}) collective-permute-start(bf16[5,128,128]{2,1,0:T(8,128)(2,1)S(1)} %second_layer.3.mine_ref), channel_id=1, source_target_pairs={{0,1},{1,0},{2,3},{3,2},{4,5},{5,4},{6,7},{7,6},{8,9},{9,8},{10,11... | collective-permute-start | bytes 491528 | tf_op jit(solution)/shard_map/ppermute | solution.py:233

commit v10 on v9

--- a/solution.py
+++ b/solution.py
@@ -21,11 +21,11 @@
 def sums_kernel(cols_hbm, counts_hbm, blocks_ref, sums_ref, held_ref, acc_ref, cols_ref, counts_ref, list_sems, sems):
     rows, slots, size, _ = blocks_ref.shape
     groups = acc_ref.shape[0] - 1
-    chunk = divisor(slots, 4)
+    chunk = divisor(slots, 12)
 
     def fetch(b, k):
         part = pl.ds(k * chunk, chunk)
-        return pltpu.make_async_copy(blocks_ref.at[b, part], held_ref.at[b, part], sems.at[b])
+        return pltpu.make_async_copy(blocks_ref.at[b, part], held_ref.at[b, part], sems.at[b, k])
 
     counts_copy = pltpu.make_async_copy(counts_hbm, counts_ref, list_sems.at[0])
     cols_copy = pltpu.make_async_copy(cols_hbm, cols_ref, list_sems.at[1])
@@ -33,34 +33,32 @@
     cols_copy.start()
     for b in range(rows):
         fetch(b, 0).start()
+    acc_ref[...] = jnp.zeros_like(acc_ref)
     counts_copy.wait()
-    for b in range(rows):
-
-        def start(k, carry, b=b):
-            fetch(b, k).start()
-            return carry
-
-        lax.fori_loop(1, chunk_total(counts_ref, b, chunk), start, 0)
-    acc_ref[...] = jnp.zeros_like(acc_ref)
     cols_copy.wait()
     for b in range(rows):
-        total = jnp.maximum(chunk_total(counts_ref, b, chunk), 1)
-
-        def finish(k, carry, b=b):
-            fetch(b, k).wait()
-            return carry
-
-        lax.fori_loop(0, total, finish, 0)
-
-        def add(k, carry, b=b):
-            for u in range(chunk):
-                slot = k * chunk + u
-                col = jnp.where(slot < counts_ref[b], cols_ref[b, slot], groups)
-                block = held_ref[b, slot].astype(jnp.float32)
-                acc_ref[col] += jnp.sum(block.reshape(size // 8, 8, size), axis=0)
-            return carry
-
-        lax.fori_loop(0, total, add, 0)
+        for k in range(1, slots // chunk):
+
+            @pl.when(counts_ref[b] > k * chunk)
+            def _(b=b, k=k):
+                fetch(b, k).start()
+
+    def add(b, k):
+        fetch(b, k).wait()
+        for slot in range(k * chunk, (k + 1) * chunk):
+            col = jnp.where(slot < counts_ref[b], cols_ref[b, slot], groups)
+            block = held_ref[b, slot].astype(jnp.float32)
+            acc_ref[col] += jnp.sum(block.reshape(size // 8, 8, size), axis=0)
+
+    for b in range(rows):
+        add(b, 0)
+    for b in range(rows):
+        for k in range(1, slots // chunk):
+
+            @pl.when(counts_ref[b] > k * chunk)
+            def _(b=b, k=k):
+                add(b, k)
+
     sums_ref[...] = jnp.sum(acc_ref[:groups], axis=1)
 
 
@@ -81,7 +79,7 @@
 
 
 def first_kernel(sending, cols_ref, counts_ref, sums_ref, added_ref, demand_ref, blocks_ref, out_ref, coef_ref, inverse_ref, acc_ref):
-    slots = blocks_ref.shape[1]
+    slots, size = blocks_ref.shape[1:3]
     count = out_ref.shape[0]
     base = 0
     if sending is not None:
@@ -91,9 +89,9 @@
 
     def gather(row, slot):
         col = cols_ref[row, slot]
-        live = slot < counts_ref[row]
-        block = blocks_ref[row, jnp.where(live, slot, 0)].astype(jnp.float32)
-        coef = (block * jnp.where(live, inverse_ref[col], 0.0)).astype(jnp.bfloat16)
+        scale = jnp.where(slot < counts_ref[row], inverse_ref[col], 0.0)
+        scale = jnp.broadcast_to(scale, (16, size)).astype(jnp.bfloat16)
+        coef = (blocks_ref[row, slot].reshape(size // 16, 16, size) * scale).reshape(size, size)
         coef_ref[row, slot] = coef
         return coef, demand_ref[col]
 
@@ -119,15 +117,20 @@
     return scale
 
 
-PLACES = ((0, 0), (0, 1), (1, 0), (1, 1))
+GATHERED = (
+    ((0, 0, 0), (0, 1, 0), (1, 0, 0), (1, 1, 0)),
+    ((0, 0, 1), (0, 1, 1), (1, 0, 1)),
+    ((1, 1, 1),),
+)
 
 
 def second_part_kernel(which, cols_ref, counts_ref, coef_ref, own_ref, *rest):
     part = own_ref.shape[0]
     if which == 0:
         pieces, (out_ref, source_ref, acc_ref) = rest[:-3], rest[-3:]
-        for array, (core, away) in zip(pieces, ((0, 0), (0, 1), (1, 0), (1, 1))):
-            for i, (z, y) in enumerate(PLACES):
+        for number, array in enumerate(pieces):
+            core = number // len(GATHERED)
+            for i, (z, y, away) in enumerate(GATHERED[number % len(GATHERED)]):
                 at = ((z * 4 + y * 2 + core) * 2 + away) * part
                 source_ref[at : at + part] = array[i * part : (i + 1) * part]
     else:
@@ -220,7 +223,7 @@
             pltpu.SMEM(slot_cols.shape, jnp.int32),
             pltpu.SMEM(counts.shape, jnp.int32),
             pltpu.SemaphoreType.DMA((2,)),
-            pltpu.SemaphoreType.DMA((rows,)),
+            pltpu.SemaphoreType.DMA((rows, slots // divisor(slots, 12))),
         ],
         compiler_params=PARAMS,
         cost_estimate=cost(0, 4 * rows * size * size * slots),
@@ -233,10 +236,10 @@
         return lax.ppermute(array, "col", [(0, 1), (1, 0)])
 
     if paired:
-        sums = sums + flip(sums.astype(jnp.bfloat16), 1).astype(jnp.float32)
-        shared = sums.astype(jnp.bfloat16)
-        for part in [flip(shared, mask) for mask in (12, 14, 8, 10, 4, 6, 2)]:
-            sums = sums + part.astype(jnp.float32)
+        for masks in ((1, 2, 3), (4, 8, 12)):
+            sums = sums.astype(jnp.bfloat16)
+            parts = [sums] + [flip(sums, m) for m in masks]
+            sums = functools.reduce(jnp.add, [part.astype(jnp.float32) for part in parts])
     else:
         sums = lax.psum(sums, "row")
 
@@ -317,13 +320,11 @@
             compiler_params=PARAMS,
         )(*pieces)
 
-    def move(array, mask):
-        pairs = [(i * 2 + c, (i ^ mask) * 2 + 1 - c) for i in range(n_row) for c in range(2)]
-        return lax.ppermute(array, ("row", "col"), pairs)
-
-    away = join([move(away, mask) for mask in (0, 2, 4, 6)])
-    home = join([home] + [flip(home, mask) for mask in (2, 4, 6)])
-    pieces = [home, away, flip(home, 1), flip(away, 1)]
+    away = swap(away)
+    home_y, home_z = flip(home, 2), flip(home, 4)
+    away_y, away_z = flip(away, 2), flip(away, 4)
+    gathered = [join([home, home_y, home_z, flip(home_z, 2)]), join([away, away_y, away_z]), flip(away_y, 4)]
+    pieces = gathered + [flip(part, 1) for part in gathered]
 
     part_a, source = second_call(functools.partial(second_part_kernel, 0), half, coefs, own, pieces, True)
     other_a = swap(part_a)

time: 69.5 us -> 70.6 us (1.016)
  waiting for transfers between devices: 30.9 us -> 40.9 us
  starting transfers between devices: 23.9 us -> 18.9 us
  Pallas kernels: 14.9 us -> 11.2 us
    ppermute x14 -> x16, waiting for transfers between devices: 16 us -> 32.2 us  [flip(): return lax.ppermute(array, 'row', [(i, i ^ mask) for i in range(n_row)])]
    ppermute x4 -> x0, waiting for transfers between devices: 8.79 us -> none  [move(): return lax.ppermute(array, ('row', 'col'), pairs)]
    ppermute x4 -> x0, starting transfers between devices: 5.92 us -> none  [move(): return lax.ppermute(array, ('row', 'col'), pairs)]
    ppermute x3 -> x4, waiting for transfers between devices: 6.09 us -> 8.69 us  [swap(): return lax.ppermute(array, 'col', [(0, 1), (1, 0)])]
    ppermute x3 -> x4, starting transfers between devices: 3.65 us -> 5.42 us  [swap(): return lax.ppermute(array, 'col', [(0, 1), (1, 0)])]
    pallas_call x2, Pallas kernels: 5.56 us -> 3.86 us  [first_layer(): pl.pallas_call(functools.partial(first_kernel, sending), name='first_laye...]
    pallas_call x2, Pallas kernels: 4.08 us -> 3 us  [second_call(): pl.pallas_call(kernel, name='second_layer', out_shape=(out, jax.ShapeDtyp...]
    pallas_call x1, Pallas kernels: 3.73 us -> 2.78 us  [body(): pl.pallas_call(sums_kernel, name='column_sums', out_shape=(jax.ShapeDtype...]
  transfers between devices with their start and end apart: 21 -> 20, of which waited for: 15 -> 14; matrix products, arithmetic and copies ran while one was open for 0% -> 0% of each run, Pallas kernels for 8% -> 6%
where the time goes in v10:
time: 70.6 us; the launch traced here: 71.2 us
  waiting for transfers between devices  40.9 us (58%)
  starting transfers between devices  18.9 us (27%)
  Pallas kernels  11.2 us (16%)
    ppermute x16, waiting for transfers between devices, flip(): return lax.ppermute(array, 'row', [(i, i ^ mask) for i in range(n_row)])  32.2 us
    ppermute x16, starting transfers between devices, flip(): return lax.ppermute(array, 'row', [(i, i ^ mask) for i in range(n_row)])  13.5 us
    ppermute x4, waiting for transfers between devices, swap(): return lax.ppermute(array, 'col', [(0, 1), (1, 0)])  8.69 us
    ppermute x4, starting transfers between devices, swap(): return lax.ppermute(array, 'col', [(0, 1), (1, 0)])  5.42 us
    pallas_call x2, Pallas kernels, first_layer(): pl.pallas_call(functools.partial(first_kernel, sending), name='first_laye...  3.86 us
    pallas_call x2, Pallas kernels, second_call(): pl.pallas_call(kernel, name='second_layer', out_shape=(out, jax.ShapeDtyp...  3 us
    pallas_call x1, Pallas kernels, body(): pl.pallas_call(sums_kernel, name='column_sums', out_shape=(jax.ShapeDtype...  2.78 us
    pallas_call x2, Pallas kernels, result(): pl.pallas_call(functools.partial(result_kernel, first_row), name='result'...  1.43 us
  transfers between devices with their start and end apart: 20, of which 14 were waited for; matrix products, arithmetic and copies ran while one was open for 0% of the time, Pallas kernels for 6%

profile of v10, /device:TPU:0, one launch (start us, length us, event | category | flops | bytes accessed | tf_op | source)
XLA Modules:
  0.0 71.2 jit_solution(5927415648693130582)
XLA Ops:
  0.0 0.0 copy-start.1
  0.0 0.0 copy-start.3
  0.0 0.0 copy-start.2
  0.0 0.0 copy-start
  0.0 2.8 %column_sums.1 = (f32[80,128]{1,0:T(8,128)S(1)}, bf16[10,36,128,128]{3,2,1,0:T(8,128)(2,1)S(1)}) custom-call(s32[10,36]{1,0:T(8,128)} %cols_ref.7, s32[10]{0:T(128)} %bitcast.8, bf16[10,36,128,128]{3,2,1,0:T(8,128)(2,1)} %blocks_ref.1), custom_call_target="tpu_custom_call" | custom-call | bytes 23592960 | tf_op jit(solution)/shard_map/column_sums/pallas_call | solution.py:212
  2.8 4.0 %collective-permute-start.1 = (bf16[80,128]{1,0:T(8,128)(2,1)S(1)}, bf16[80,128]{1,0:T(8,128)(2,1)S(1)}, u32[]{:S(2)}, u32[]{:S(2)}) collective-permute-start(bf16[80,128]{1,0:T(8,128)(2,1)S(1)} %convert_element_type.36), channel_id=1, source_target_pairs={{0,4},{2,6},{4,0},{6,2},{8,12},{10,14},{12,8},{14,10},{16,20},{18,... | collective-permute-start | bytes 61448 | tf_op jit(solution)/shard_map/ppermute | solution.py:233
  6.8 0.0 collective-permute-start
  6.8 0.2 collective-permute-start.2
  7.1 1.6 %collective-permute-done.1 = bf16[80,128]{1,0:T(8,128)(2,1)S(1)} collective-permute-done((bf16[80,128]{1,0:T(8,128)(2,1)S(1)}, bf16[80,128]{1,0:T(8,128)(2,1)S(1)}, u32[]{:S(2)}, u32[]{:S(2)}) %collective-permute-start.1) | collective-permute-done | bytes 20512 | tf_op jit(solution)/shard_map/ppermute | solution.py:233
  8.6 0.0 collective-permute-done
  8.6 1.4 %collective-permute-done.2 = bf16[80,128]{1,0:T(8,128)(2,1)S(1)} collective-permute-done((bf16[80,128]{1,0:T(8,128)(2,1)S(1)}, bf16[80,128]{1,0:T(8,128)(2,1)S(1)}, u32[]{:S(2)}, u32[]{:S(2)}) %collective-permute-start.2) | collective-permute-done | bytes 20512 | tf_op jit(solution)/shard_map/ppermute | solution.py:233
  10.1 4.1 %collective-permute-start.5 = (bf16[80,128]{1,0:T(8,128)(2,1)S(1)}, bf16[80,128]{1,0:T(8,128)(2,1)S(1)}, u32[]{:S(2)}, u32[]{:S(2)}) collective-permute-start(bf16[80,128]{1,0:T(8,128)(2,1)S(1)} %add_convert_fusion.1), channel_id=1, source_target_pairs={{0,24},{2,26},{4,28},{6,30},{8,16},{10,18},{12,20},{14,22},{16,8},... | collective-permute-start | bytes 61448 | tf_op jit(solution)/shard_map/ppermute | solution.py:233
  14.2 0.0 collective-permute-start.4
  14.2 0.6 collective-permute-start.3
  14.9 1.2 %collective-permute-done.5 = bf16[80,128]{1,0:T(8,128)(2,1)S(1)} collective-permute-done((bf16[80,128]{1,0:T(8,128)(2,1)S(1)}, bf16[80,128]{1,0:T(8,128)(2,1)S(1)}, u32[]{:S(2)}, u32[]{:S(2)}) %collective-permute-start.5) | collective-permute-done | bytes 20512 | tf_op jit(solution)/shard_map/ppermute | solution.py:233
  16.0 2.9 %collective-permute-done.4 = bf16[80,128]{1,0:T(8,128)(2,1)S(1)} collective-permute-done((bf16[80,128]{1,0:T(8,128)(2,1)S(1)}, bf16[80,128]{1,0:T(8,128)(2,1)S(1)}, u32[]{:S(2)}, u32[]{:S(2)}) %collective-permute-start.4) | collective-permute-done | bytes 20512 | tf_op jit(solution)/shard_map/ppermute | solution.py:233
  18.9 0.0 collective-permute-done.3
  18.9 0.0 copy-done.1
  18.9 0.0 copy-done.3
  18.9 0.0 copy-done.2
  18.9 0.0 copy-done
  19.0 1.9 %first_layer.2 = (bf16[5,128,128]{2,1,0:T(8,128)(2,1)S(1)}, bf16[10,36,128,128]{3,2,1,0:T(8,128)(2,1)S(1)}) custom-call(s32[10,36]{1,0:T(8,128)S(1)} %copy-done.1, s32[10]{0:T(128)S(1)} %bitcast.9, f32[80,128]{1,0:T(8,128)S(1)} %convert_add_fusion.sums_ref, f32[80,128]{1,0:T(8,128)S(1)} %bitcast.6, ...), custom_call_target="tpu_custom_call", output_to_operand_aliasing={{1}: (5, {})} | custom-call | flops 754974720 | bytes 5898240 | tf_op jit(solution)/shard_map/first_layer/pallas_call | solution.py:250
  20.9 1.6 %collective-permute-start.6 = (bf16[5,128,128]{2,1,0:T(8,128)(2,1)S(1)}, bf16[5,128,128]{2,1,0:T(8,128)(2,1)S(1)}, u32[]{:S(2)}, u32[]{:S(2)}) collective-permute-start(bf16[5,128,128]{2,1,0:T(8,128)(2,1)S(1)} %get-tuple-element.20), channel_id=1, source_target_pairs={{0,1},{1,0},{2,3},{3,2},{4,5},{5,4},{6,7},{7,6},{8,9},{9,8},{10,11... | collective-permute-start | bytes 491528 | tf_op jit(solution)/shard_map/ppermute | solution.py:236
  22.5 1.9 %first_layer.3 = (f32[5,128,128]{2,1,0:T(8,128)S(1)}, bf16[10,36,128,128]{3,2,1,0:T(8,128)(2,1)S(1)}) custom-call(s32[10,36]{1,0:T(8,128)S(1)} %copy-done.1, s32[10]{0:T(128)S(1)} %bitcast.10, f32[80,128]{1,0:T(8,128)S(1)} %convert_add_fusion.sums_ref, f32[80,128]{1,0:T(8,128)S(1)} %bitcast.7, ...), custom_call_target="tpu_custom_call", output_to_operand_aliasing={{1}: (5, {})} | custom-call | flops 754974720 | bytes 5898240 | tf_op jit(solution)/shard_map/first_layer/pallas_call | solution.py:250
  24.4 3.5 %collective-permute-done.6 = bf16[5,128,128]{2,1,0:T(8,128)(2,1)S(1)} collective-permute-done((bf16[5,128,128]{2,1,0:T(8,128)(2,1)S(1)}, bf16[5,128,128]{2,1,0:T(8,128)(2,1)S(1)}, u32[]{:S(2)}, u32[]{:S(2)}) %collective-permute-start.6) | collective-permute-done | bytes 163872 | tf_op jit(solution)/shard_map/ppermute | solution.py:236
  27.9 0.6 collective-permute-start.7
  28.5 7.8 %collective-permute-done.7.crossed_ref = bf16[5,128,128]{2,1,0:T(8,128)(2,1)S(1)} collective-permute-done((bf16[5,128,128]{2,1,0:T(8,128)(2,1)S(1)}, bf16[5,128,128]{2,1,0:T(8,128)(2,1)S(1)}, u32[]{:S(2)}, u32[]{:S(2)}) %collective-permute-start.7) | collective-permute-done | bytes 163872 | tf_op jit(solution)/shard_map/ppermute | solution.py:233
  36.4 0.1 collective-permute-start.9
  36.5 1.7 %collective-permute-start.11 = (bf16[5,128,128]{2,1,0:T(8,128)(2,1)S(1)}, bf16[5,128,128]{2,1,0:T(8,128)(2,1)S(1)}, u32[]{:S(2)}, u32[]{:S(2)}) collective-permute-start(bf16[5,128,128]{2,1,0:T(8,128)(2,1)S(1)} %get-tuple-element.22), channel_id=1, source_target_pairs={{0,1},{1,0},{2,3},{3,2},{4,5},{5,4},{6,7},{7,6},{8,9},{9,8},{10,11... | collective-permute-start | bytes 491528 | tf_op jit(solution)/shard_map/ppermute | solution.py:236
  38.2 0.0 collective-permute-start.8
  38.2 4.4 %collective-permute-done.9.refs_2_ = bf16[5,128,128]{2,1,0:T(8,128)(2,1)S(1)} collective-permute-done((bf16[5,128,128]{2,1,0:T(8,128)(2,1)S(1)}, bf16[5,128,128]{2,1,0:T(8,128)(2,1)S(1)}, u32[]{:S(2)}, u32[]{:S(2)}) %collective-permute-start.9) | collective-permute-done | bytes 163872 | tf_op jit(solution)/shard_map/ppermute | solution.py:233
  42.6 0.0 collective-permute-start.10
  42.6 0.1 collective-permute-done.11.refs_0_
  42.7 1.7 %collective-permute-start.13 = (bf16[5,128,128]{2,1,0:T(8,128)(2,1)S(1)}, bf16[5,128,128]{2,1,0:T(8,128)(2,1)S(1)}, u32[]{:S(2)}, u32[]{:S(2)}) collective-permute-start(bf16[5,128,128]{2,1,0:T(8,128)(2,1)S(1)} %collective-permute-done.11.refs_0_), channel_id=1, source_target_pairs={{0,8},{2,10},{4,12},{6,14},{8,0},{10,2},{12,4},{14,6},{16,24},{18,... | collective-permute-start | bytes 491528 | tf_op jit(solution)/shard_map/ppermute | solution.py:233
  44.3 0.6 collective-permute-start.12
  44.9 0.0 collective-permute-done.8.refs_1_
  44.9 4.7 %collective-permute-done.10.refs_3_ = bf16[5,128,128]{2,1,0:T(8,128)(2,1)S(1)} collective-permute-done((bf16[5,128,128]{2,1,0:T(8,128)(2,1)S(1)}, bf16[5,128,128]{2,1,0:T(8,128)(2,1)S(1)}, u32[]{:S(2)}, u32[]{:S(2)}) %collective-permute-start.10) | collective-permute-done | bytes 163872 | tf_op jit(solution)/shard_map/ppermute | solution.py:233
  49.7 0.1 collective-permute-start.15
  49.7 0.0 collective-permute-done.13.refs_2_
  49.8 1.6 %collective-permute-done.12.refs_1_ = bf16[5,128,128]{2,1,0:T(8,128)(2,1)S(1)} collective-permute-done((bf16[5,128,128]{2,1,0:T(8,128)(2,1)S(1)}, bf16[5,128,128]{2,1,0:T(8,128)(2,1)S(1)}, u32[]{:S(2)}, u32[]{:S(2)}) %collective-permute-start.12) | collective-permute-done | bytes 163872 | tf_op jit(solution)/shard_map/ppermute | solution.py:233
  51.4 0.1 collective-permute-start.16
  51.5 1.4 %collective-permute-start.14 = (bf16[5,128,128]{2,1,0:T(8,128)(2,1)S(1)}, bf16[5,128,128]{2,1,0:T(8,128)(2,1)S(1)}, u32[]{:S(2)}, u32[]{:S(2)}) collective-permute-start(bf16[5,128,128]{2,1,0:T(8,128)(2,1)S(1)} %collective-permute-done.12.refs_1_), channel_id=1, source_target_pairs={{0,8},{2,10},{4,12},{6,14},{8,0},{10,2},{12,4},{14,6},{16,24},{18,... | collective-permute-start | bytes 491528 | tf_op jit(solution)/shard_map/ppermute | solution.py:233
  52.9 5.2 %collective-permute-done.14.rest_2_ = bf16[5,128,128]{2,1,0:T(8,128)(2,1)S(1)} collective-permute-done((bf16[5,128,128]{2,1,0:T(8,128)(2,1)S(1)}, bf16[5,128,128]{2,1,0:T(8,128)(2,1)S(1)}, u32[]{:S(2)}, u32[]{:S(2)}) %collective-permute-start.14) | collective-permute-done | bytes 163872 | tf_op jit(solution)/shard_map/ppermute | solution.py:233
  58.1 0.0 collective-permute-start.17
  58.1 1.4 %collective-permute-done.17.rest_5_ = bf16[5,128,128]{2,1,0:T(8,128)(2,1)S(1)} collective-permute-done((bf16[5,128,128]{2,1,0:T(8,128)(2,1)S(1)}, bf16[5,128,128]{2,1,0:T(8,128)(2,1)S(1)}, u32[]{:S(2)}, u32[]{:S(2)}) %collective-permute-start.17) | collective-permute-done | bytes 163872 | tf_op jit(solution)/shard_map/ppermute | solution.py:233
  59.5 0.0 collective-permute-done.16.rest_4_
  59.5 0.0 collective-permute-done.15.rest_3_
  59.5 1.6 %second_layer.2 = (bf16[5,128,128]{2,1,0:T(8,128)(2,1)S(1)}, bf16[80,128,128]{2,1,0:T(8,128)(2,1)S(1)}) custom-call(s32[10,36]{1,0:T(8,128)S(1)} %copy-done.1, s32[10]{0:T(128)S(1)} %bitcast.11, bf16[10,36,128,128]{3,2,1,0:T(8,128)(2,1)S(1)} %get-tuple-element.18.coef_ref, bf16[5,128,128]{2,1,0:T(8,128)(2,1)S(1)} %add_convert_fusion.own_ref, ...), custom_call_target="tpu_custom_call" | custom-call | flops 754974720 | bytes 5898240 | tf_op jit(solution)/shard_map/second_layer/pallas_call | solution.py:278
  61.1 1.6 %collective-permute-start.19 = (bf16[5,128,128]{2,1,0:T(8,128)(2,1)S(1)}, bf16[5,128,128]{2,1,0:T(8,128)(2,1)S(1)}, u32[]{:S(2)}, u32[]{:S(2)}) collective-permute-start(bf16[5,128,128]{2,1,0:T(8,128)(2,1)S(1)} %get-tuple-element.24.mine_ref), channel_id=1, source_target_pairs={{0,1},{1,0},{2,3},{3,2},{4,5},{5,4},{6,7},{7,6},{8,9},{9,8},{10,11... | collective-permute-start | bytes 491528 | tf_op jit(solution)/shard_map/ppermute | solution.py:236
  62.7 1.4 %second_layer.3.mine_ref = bf16[5,128,128]{2,1,0:T(8,128)(2,1)S(1)} custom-call(s32[10,36]{1,0:T(8,128)S(1)} %copy-done.1, s32[10]{0:T(128)S(1)} %bitcast.12, bf16[10,36,128,128]{3,2,1,0:T(8,128)(2,1)S(1)} %get-tuple-element.18.coef_ref, bf16[5,128,128]{2,1,0:T(8,128)(2,1)S(1)} %add_convert_fusion.own_ref, bf16[80,128,128]{2,1,0:T(8,128)(2,1)S(1)} %get-tuple-element.23.rest_0_), custom_call_target="tpu_custom_call" | custom-call | flops 754974720 | bytes 5898240 | tf_op jit(solution)/shard_map/second_layer/pallas_call | solution.py:278
  64.1 0.5 collective-permute-start.18
  64.7 3.3 %collective-permute-done.19.other_ref = bf16[5,128,128]{2,1,0:T(8,128)(2,1)S(1)} collective-permute-done((bf16[5,128,128]{2,1,0:T(8,128)(2,1)S(1)}, bf16[5,128,128]{2,1,0:T(8,128)(2,1)S(1)}, u32[]{:S(2)}, u32[]{:S(2)}) %collective-permute-start.19) | collective-permute-done | bytes 163872 | tf_op jit(solution)/shard_map/ppermute | solution.py:236
  67.9 0.7 %result.2.rest_0_ = bf16[10,128,128]{2,1,0:T(8,128)(2,1)} custom-call(bf16[5,128,128]{2,1,0:T(8,128)(2,1)S(1)} %get-tuple-element.24.mine_ref, bf16[5,128,128]{2,1,0:T(8,128)(2,1)S(1)} %collective-permute-done.19.other_ref), custom_call_target="tpu_custom_call" | custom-call | tf_op jit(solution)/shard_map/result/pallas_call | solution.py:335
  68.7 1.9 %collective-permute-done.18.other_ref = bf16[5,128,128]{2,1,0:T(8,128)(2,1)S(1)} collective-permute-done((bf16[5,128,128]{2,1,0:T(8,128)(2,1)S(1)}, bf16[5,128,128]{2,1,0:T(8,128)(2,1)S(1)}, u32[]{:S(2)}, u32[]{:S(2)}) %collective-permute-start.18) | collective-permute-done | bytes 163872 | tf_op jit(solution)/shard_map/ppermute | solution.py:236
  70.5 0.7 %result.3 = bf16[10,128,128]{2,1,0:T(8,128)(2,1)} custom-call(bf16[5,128,128]{2,1,0:T(8,128)(2,1)S(1)} %second_layer.3.mine_ref, bf16[5,128,128]{2,1,0:T(8,128)(2,1)S(1)} %collective-permute-done.18.other_ref, bf16[10,128,128]{2,1,0:T(8,128)(2,1)} %result.2.rest_0_), custom_call_target="tpu_custom_call", output_to_operand_aliasing={{}: (2, {})} | custom-call | tf_op jit(solution)/shard_map/result/pallas_call | solution.py:335
  (7 shorter events, 0.2 us)
Async XLA Ops:
  0.0 18.9 %copy-start.1 = (s32[10,36]{1,0:T(8,128)S(1)}, s32[10,36]{1,0:T(8,128)}, u32[]{:S(2)}) copy-start(s32[10,36]{1,0:T(8,128)} %cols_ref.7) | copy-start | bytes 4324
  0.0 18.9 %copy-start.3 = (s32[10,1]{0,1:T(1,128)S(1)}, s32[10,1]{0,1:T(1,128)}, u32[]{:S(2)}) copy-start(s32[10,1]{0,1:T(1,128)} %param.7) | copy-start | bytes 124
  0.0 18.9 %copy-start.2 = (f32[10240]{0:T(1024)S(1)}, f32[10240]{0:T(1024)}, u32[]{:S(2)}) copy-start(f32[10240]{0:T(1024)} %param.9) | copy-start | bytes 122884
  0.0 18.9 %copy-start = (bf16[10240,128]{1,0:T(8,128)(2,1)S(1)}, bf16[10240,128]{1,0:T(8,128)(2,1)}, u32[]{:S(2)}) copy-start(bf16[10240,128]{1,0:T(8,128)(2,1)} %param.8) | copy-start | bytes 7864324
  2.8 5.8 %collective-permute-start.1 = (bf16[80,128]{1,0:T(8,128)(2,1)S(1)}, bf16[80,128]{1,0:T(8,128)(2,1)S(1)}, u32[]{:S(2)}, u32[]{:S(2)}) collective-permute-start(bf16[80,128]{1,0:T(8,128)(2,1)S(1)} %convert_element_type.36), channel_id=1, source_target_pairs={{0,4},{2,6},{4,0},{6,2},{8,12},{10,14},{12,8},{14,10},{16,20},{18,... | collective-permute-start | bytes 61448 | tf_op jit(solution)/shard_map/ppermute | solution.py:233
  6.8 1.8 %collective-permute-start = (bf16[80,128]{1,0:T(8,128)(2,1)S(1)}, bf16[80,128]{1,0:T(8,128)(2,1)S(1)}, u32[]{:S(2)}, u32[]{:S(2)}) collective-permute-start(bf16[80,128]{1,0:T(8,128)(2,1)S(1)} %convert_element_type.36), channel_id=1, source_target_pairs={{0,2},{2,0},{4,6},{6,4},{8,10},{10,8},{12,14},{14,12},{16,18},{18,... | collective-permute-start | bytes 61448 | tf_op jit(solution)/shard_map/ppermute | solution.py:233
  6.8 3.2 %collective-permute-start.2 = (bf16[80,128]{1,0:T(8,128)(2,1)S(1)}, bf16[80,128]{1,0:T(8,128)(2,1)S(1)}, u32[]{:S(2)}, u32[]{:S(2)}) collective-permute-start(bf16[80,128]{1,0:T(8,128)(2,1)S(1)} %convert_element_type.36), channel_id=1, source_target_pairs={{0,6},{2,4},{4,2},{6,0},{8,14},{10,12},{12,10},{14,8},{16,22},{18,... | collective-permute-start | bytes 61448 | tf_op jit(solution)/shard_map/ppermute | solution.py:233
  10.1 5.9 %collective-permute-start.5 = (bf16[80,128]{1,0:T(8,128)(2,1)S(1)}, bf16[80,128]{1,0:T(8,128)(2,1)S(1)}, u32[]{:S(2)}, u32[]{:S(2)}) collective-permute-start(bf16[80,128]{1,0:T(8,128)(2,1)S(1)} %add_convert_fusion.1), channel_id=1, source_target_pairs={{0,24},{2,26},{4,28},{6,30},{8,16},{10,18},{12,20},{14,22},{16,8},... | collective-permute-start | bytes 61448 | tf_op jit(solution)/shard_map/ppermute | solution.py:233
  14.2 4.7 %collective-permute-start.4 = (bf16[80,128]{1,0:T(8,128)(2,1)S(1)}, bf16[80,128]{1,0:T(8,128)(2,1)S(1)}, u32[]{:S(2)}, u32[]{:S(2)}) collective-permute-start(bf16[80,128]{1,0:T(8,128)(2,1)S(1)} %add_convert_fusion.1), channel_id=1, source_target_pairs={{0,16},{2,18},{4,20},{6,22},{8,24},{10,26},{12,28},{14,30},{16,0},... | collective-permute-start | bytes 61448 | tf_op jit(solution)/shard_map/ppermute | solution.py:233
  14.2 4.7 %collective-permute-start.3 = (bf16[80,128]{1,0:T(8,128)(2,1)S(1)}, bf16[80,128]{1,0:T(8,128)(2,1)S(1)}, u32[]{:S(2)}, u32[]{:S(2)}) collective-permute-start(bf16[80,128]{1,0:T(8,128)(2,1)S(1)} %add_convert_fusion.1), channel_id=1, source_target_pairs={{0,8},{2,10},{4,12},{6,14},{8,0},{10,2},{12,4},{14,6},{16,24},{18,... | collective-permute-start | bytes 61448 | tf_op jit(solution)/shard_map/ppermute | solution.py:233
  20.9 7.0 %collective-permute-start.6 = (bf16[5,128,128]{2,1,0:T(8,128)(2,1)S(1)}, bf16[5,128,128]{2,1,0:T(8,128)(2,1)S(1)}, u32[]{:S(2)}, u32[]{:S(2)}) collective-permute-start(bf16[5,128,128]{2,1,0:T(8,128)(2,1)S(1)} %get-tuple-element.20), channel_id=1, source_target_pairs={{0,1},{1,0},{2,3},{3,2},{4,5},{5,4},{6,7},{7,6},{8,9},{9,8},{10,11... | collective-permute-start | bytes 491528 | tf_op jit(solution)/shard_map/ppermute | solution.py:236
  27.9 8.4 %collective-permute-start.7 = (bf16[5,128,128]{2,1,0:T(8,128)(2,1)S(1)}, bf16[5,128,128]{2,1,0:T(8,128)(2,1)S(1)}, u32[]{:S(2)}, u32[]{:S(2)}) collective-permute-start(bf16[5,128,128]{2,1,0:T(8,128)(2,1)S(1)} %add_convert_fusion.own_ref), channel_id=1, source_target_pairs={{0,16},{2,18},{4,20},{6,22},{8,24},{10,26},{12,28},{14,30},{16,0},... | collective-permute-start | bytes 491528 | tf_op jit(solution)/shard_map/ppermute | solution.py:233
  36.4 6.2 %collective-permute-start.9 = (bf16[5,128,128]{2,1,0:T(8,128)(2,1)S(1)}, bf16[5,128,128]{2,1,0:T(8,128)(2,1)S(1)}, u32[]{:S(2)}, u32[]{:S(2)}) collective-permute-start(bf16[5,128,128]{2,1,0:T(8,128)(2,1)S(1)} %get-tuple-element.21.refs_0_), channel_id=1, source_target_pairs={{0,8},{2,10},{4,12},{6,14},{8,0},{10,2},{12,4},{14,6},{16,24},{18,... | collective-permute-start | bytes 491528 | tf_op jit(solution)/shard_map/ppermute | solution.py:233
  36.5 6.2 %collective-permute-start.11 = (bf16[5,128,128]{2,1,0:T(8,128)(2,1)S(1)}, bf16[5,128,128]{2,1,0:T(8,128)(2,1)S(1)}, u32[]{:S(2)}, u32[]{:S(2)}) collective-permute-start(bf16[5,128,128]{2,1,0:T(8,128)(2,1)S(1)} %get-tuple-element.22), channel_id=1, source_target_pairs={{0,1},{1,0},{2,3},{3,2},{4,5},{5,4},{6,7},{7,6},{8,9},{9,8},{10,11... | collective-permute-start | bytes 491528 | tf_op jit(solution)/shard_map/ppermute | solution.py:236
  38.2 6.7 %collective-permute-start.8 = (bf16[5,128,128]{2,1,0:T(8,128)(2,1)S(1)}, bf16[5,128,128]{2,1,0:T(8,128)(2,1)S(1)}, u32[]{:S(2)}, u32[]{:S(2)}) collective-permute-start(bf16[5,128,128]{2,1,0:T(8,128)(2,1)S(1)} %get-tuple-element.21.refs_0_), channel_id=1, source_target_pairs={{0,4},{2,6},{4,0},{6,2},{8,12},{10,14},{12,8},{14,10},{16,20},{18,... | collective-permute-start | bytes 491528 | tf_op jit(solution)/shard_map/ppermute | solution.py:233
  42.6 7.0 %collective-permute-start.10 = (bf16[5,128,128]{2,1,0:T(8,128)(2,1)S(1)}, bf16[5,128,128]{2,1,0:T(8,128)(2,1)S(1)}, u32[]{:S(2)}, u32[]{:S(2)}) collective-permute-start(bf16[5,128,128]{2,1,0:T(8,128)(2,1)S(1)} %collective-permute-done.9.refs_2_), channel_id=1, source_target_pairs={{0,4},{2,6},{4,0},{6,2},{8,12},{10,14},{12,8},{14,10},{16,20},{18,... | collective-permute-start | bytes 491528 | tf_op jit(solution)/shard_map/ppermute | solution.py:233
  42.7 7.1 %collective-permute-start.13 = (bf16[5,128,128]{2,1,0:T(8,128)(2,1)S(1)}, bf16[5,128,128]{2,1,0:T(8,128)(2,1)S(1)}, u32[]{:S(2)}, u32[]{:S(2)}) collective-permute-start(bf16[5,128,128]{2,1,0:T(8,128)(2,1)S(1)} %collective-permute-done.11.refs_0_), channel_id=1, source_target_pairs={{0,8},{2,10},{4,12},{6,14},{8,0},{10,2},{12,4},{14,6},{16,24},{18,... | collective-permute-start | bytes 491528 | tf_op jit(solution)/shard_map/ppermute | solution.py:233
  44.3 7.0 %collective-permute-start.12 = (bf16[5,128,128]{2,1,0:T(8,128)(2,1)S(1)}, bf16[5,128,128]{2,1,0:T(8,128)(2,1)S(1)}, u32[]{:S(2)}, u32[]{:S(2)}) collective-permute-start(bf16[5,128,128]{2,1,0:T(8,128)(2,1)S(1)} %collective-permute-done.11.refs_0_), channel_id=1, source_target_pairs={{0,4},{2,6},{4,0},{6,2},{8,12},{10,14},{12,8},{14,10},{16,20},{18,... | collective-permute-start | bytes 491528 | tf_op jit(solution)/shard_map/ppermute | solution.py:233
  49.7 9.8 %collective-permute-start.15 = (bf16[20,128,128]{2,1,0:T(8,128)(2,1)S(1)}, bf16[20,128,128]{2,1,0:T(8,128)(2,1)S(1)}, u32[]{:S(2)}, u32[]{:S(2)}) collective-permute-start(bf16[20,128,128]{2,1,0:T(8,128)(2,1)S(1)} %own_joined.2.rest_0_), channel_id=1, source_target_pairs={{0,2},{2,0},{4,6},{6,4},{8,10},{10,8},{12,14},{14,12},{16,18},{18,... | collective-permute-start | bytes 1966088 | tf_op jit(solution)/shard_map/ppermute | solution.py:233
  51.4 8.1 %collective-permute-start.16 = (bf16[15,128,128]{2,1,0:T(8,128)(2,1)S(1)}, bf16[15,128,128]{2,1,0:T(8,128)(2,1)S(1)}, u32[]{:S(2)}, u32[]{:S(2)}) collective-permute-start(bf16[15,128,128]{2,1,0:T(8,128)(2,1)S(1)} %own_joined.3.rest_1_), channel_id=1, source_target_pairs={{0,2},{2,0},{4,6},{6,4},{8,10},{10,8},{12,14},{14,12},{16,18},{18,... | collective-permute-start | bytes 1474568 | tf_op jit(solution)/shard_map/ppermute | solution.py:233
  51.5 6.6 %collective-permute-start.14 = (bf16[5,128,128]{2,1,0:T(8,128)(2,1)S(1)}, bf16[5,128,128]{2,1,0:T(8,128)(2,1)S(1)}, u32[]{:S(2)}, u32[]{:S(2)}) collective-permute-start(bf16[5,128,128]{2,1,0:T(8,128)(2,1)S(1)} %collective-permute-done.12.refs_1_), channel_id=1, source_target_pairs={{0,8},{2,10},{4,12},{6,14},{8,0},{10,2},{12,4},{14,6},{16,24},{18,... | collective-permute-start | bytes 491528 | tf_op jit(solution)/shard_map/ppermute | solution.py:233
  58.1 1.4 %collective-permute-start.17 = (bf16[5,128,128]{2,1,0:T(8,128)(2,1)S(1)}, bf16[5,128,128]{2,1,0:T(8,128)(2,1)S(1)}, u32[]{:S(2)}, u32[]{:S(2)}) collective-permute-start(bf16[5,128,128]{2,1,0:T(8,128)(2,1)S(1)} %collective-permute-done.14.rest_2_), channel_id=1, source_target_pairs={{0,2},{2,0},{4,6},{6,4},{8,10},{10,8},{12,14},{14,12},{16,18},{18,... | collective-permute-start | bytes 491528 | tf_op jit(solution)/shard_map/ppermute | solution.py:233
  61.1 6.8 %collective-permute-start.19 = (bf16[5,128,128]{2,1,0:T(8,128)(2,1)S(1)}, bf16[5,128,128]{2,1,0:T(8,128)(2,1)S(1)}, u32[]{:S(2)}, u32[]{:S(2)}) collective-permute-start(bf16[5,128,128]{2,1,0:T(8,128)(2,1)S(1)} %get-tuple-element.24.mine_ref), channel_id=1, source_target_pairs={{0,1},{1,0},{2,3},{3,2},{4,5},{5,4},{6,7},{7,6},{8,9},{9,8},{10,11... | collective-permute-start | bytes 491528 | tf_op jit(solution)/shard_map/ppermute | solution.py:236
  64.1 6.4 %collective-permute-start.18 = (bf16[5,128,128]{2,1,0:T(8,128)(2,1)S(1)}, bf16[5,128,128]{2,1,0:T(8,128)(2,1)S(1)}, u32[]{:S(2)}, u32[]{:S(2)}) collective-permute-start(bf16[5,128,128]{2,1,0:T(8,128)(2,1)S(1)} %second_layer.3.mine_ref), channel_id=1, source_target_pairs={{0,1},{1,0},{2,3},{3,2},{4,5},{5,4},{6,7},{7,6},{8,9},{9,8},{10,11... | collective-permute-start | bytes 491528 | tf_op jit(solution)/shard_map/ppermute | solution.py:236

commit v11 on v10

--- a/solution.py
+++ b/solution.py
@@ -117,20 +117,15 @@
     return scale
 
 
-GATHERED = (
-    ((0, 0, 0), (0, 1, 0), (1, 0, 0), (1, 1, 0)),
-    ((0, 0, 1), (0, 1, 1), (1, 0, 1)),
-    ((1, 1, 1),),
-)
+PLACES = ((0, 0), (0, 1), (1, 0), (1, 1))
 
 
 def second_part_kernel(which, cols_ref, counts_ref, coef_ref, own_ref, *rest):
     part = own_ref.shape[0]
     if which == 0:
         pieces, (out_ref, source_ref, acc_ref) = rest[:-3], rest[-3:]
-        for number, array in enumerate(pieces):
-            core = number // len(GATHERED)
-            for i, (z, y, away) in enumerate(GATHERED[number % len(GATHERED)]):
+        for array, (core, away) in zip(pieces, ((0, 0), (0, 1), (1, 0), (1, 1))):
+            for i, (z, y) in enumerate(PLACES):
                 at = ((z * 4 + y * 2 + core) * 2 + away) * part
                 source_ref[at : at + part] = array[i * part : (i + 1) * part]
     else:
@@ -320,10 +315,7 @@
             compiler_params=PARAMS,
         )(*pieces)
 
-    away = swap(away)
-    home_y, home_z = flip(home, 2), flip(home, 4)
-    away_y, away_z = flip(away, 2), flip(away, 4)
-    gathered = [join([home, home_y, home_z, flip(home_z, 2)]), join([away, away_y, away_z]), flip(away_y, 4)]
+    gathered = [join([part] + [flip(part, mask) for mask in (2, 4, 6)]) for part in (home, swap(away))]
     pieces = gathered + [flip(part, 1) for part in gathered]
 
     part_a, source = second_call(functools.partial(second_part_kernel, 0), half, coefs, own, pieces, True)

time: 70.6 us -> 68.3 us (0.967)
  waiting for transfers between devices: 40.9 us -> 31.5 us
  Pallas kernels: 11.2 us -> 17.1 us
    ppermute x16 -> x15, waiting for transfers between devices: 32.2 us -> 23.4 us  [flip(): return lax.ppermute(array, 'row', [(i, i ^ mask) for i in range(n_row)])]
    ppermute x16 -> x15, starting transfers between devices: 13.5 us -> 16.1 us  [flip(): return lax.ppermute(array, 'row', [(i, i ^ mask) for i in range(n_row)])]
    pallas_call x2, Pallas kernels: 3 us -> 5.16 us  [second_call(): pl.pallas_call(kernel, name='second_layer', out_shape=(out, jax.ShapeDtyp...]
    pallas_call x2, Pallas kernels: 3.86 us -> 6 us  [first_layer(): pl.pallas_call(functools.partial(first_kernel, sending), name='first_laye...]
    ppermute x4, starting transfers between devices: 5.42 us -> 3.51 us  [swap(): return lax.ppermute(array, 'col', [(0, 1), (1, 0)])]
    pallas_call x1, Pallas kernels: 2.78 us -> 4.42 us  [body(): pl.pallas_call(sums_kernel, name='column_sums', out_shape=(jax.ShapeDtype...]
  transfers between devices with their start and end apart: 20 -> 19, of which waited for: 14 -> 14; matrix products, arithmetic and copies ran while one was open for 0% -> 0% of each run, Pallas kernels for 6% -> 9%
where the time goes in v11:
time: 68.3 us; the launch traced here: 68.4 us
  waiting for transfers between devices  31.5 us (46%)
  starting transfers between devices  19.6 us (29%)
  Pallas kernels  17.1 us (25%)
    ppermute x15, waiting for transfers between devices, flip(): return lax.ppermute(array, 'row', [(i, i ^ mask) for i in range(n_row)])  23.4 us
    ppermute x15, starting transfers between devices, flip(): return lax.ppermute(array, 'row', [(i, i ^ mask) for i in range(n_row)])  16.1 us
    ppermute x4, waiting for transfers between devices, swap(): return lax.ppermute(array, 'col', [(0, 1), (1, 0)])  8.09 us
    pallas_call x2, Pallas kernels, first_layer(): pl.pallas_call(functools.partial(first_kernel, sending), name='first_laye...  6 us
    pallas_call x2, Pallas kernels, second_call(): pl.pallas_call(kernel, name='second_layer', out_shape=(out, jax.ShapeDtyp...  5.16 us
    pallas_call x1, Pallas kernels, body(): pl.pallas_call(sums_kernel, name='column_sums', out_shape=(jax.ShapeDtype...  4.42 us
    ppermute x4, starting transfers between devices, swap(): return lax.ppermute(array, 'col', [(0, 1), (1, 0)])  3.51 us
    pallas_call x2, Pallas kernels, result(): pl.pallas_call(functools.partial(result_kernel, first_row), name='result'...  1.43 us
  transfers between devices with their start and end apart: 19, of which 14 were waited for; matrix products, arithmetic and copies ran while one was open for 0% of the time, Pallas kernels for 9%

profile of v11, /device:TPU:0, one launch (start us, length us, event | category | flops | bytes accessed | tf_op | source)
XLA Modules:
  0.0 68.4 jit_solution(11049183410061998602)
XLA Ops:
  0.0 0.0 copy-start.1
  0.0 0.0 copy-start.3
  0.0 0.0 copy-start.2
  0.0 0.0 copy-start
  0.0 4.4 %column_sums.1 = (f32[80,128]{1,0:T(8,128)S(1)}, bf16[10,36,128,128]{3,2,1,0:T(8,128)(2,1)S(1)}) custom-call(s32[10,36]{1,0:T(8,128)} %cols_ref.7, s32[10]{0:T(128)} %bitcast.8, bf16[10,36,128,128]{3,2,1,0:T(8,128)(2,1)} %blocks_ref.1), custom_call_target="tpu_custom_call" | custom-call | bytes 23592960 | tf_op jit(solution)/shard_map/column_sums/pallas_call | solution.py:207
  4.4 2.4 %collective-permute-start.1 = (bf16[80,128]{1,0:T(8,128)(2,1)S(1)}, bf16[80,128]{1,0:T(8,128)(2,1)S(1)}, u32[]{:S(2)}, u32[]{:S(2)}) collective-permute-start(bf16[80,128]{1,0:T(8,128)(2,1)S(1)} %convert_element_type.36), channel_id=1, source_target_pairs={{0,4},{2,6},{4,0},{6,2},{8,12},{10,14},{12,8},{14,10},{16,20},{18,... | collective-permute-start | bytes 61448 | tf_op jit(solution)/shard_map/ppermute | solution.py:228
  6.9 0.0 collective-permute-start
  6.9 0.2 collective-permute-start.2
  7.1 1.6 %collective-permute-done.1 = bf16[80,128]{1,0:T(8,128)(2,1)S(1)} collective-permute-done((bf16[80,128]{1,0:T(8,128)(2,1)S(1)}, bf16[80,128]{1,0:T(8,128)(2,1)S(1)}, u32[]{:S(2)}, u32[]{:S(2)}) %collective-permute-start.1) | collective-permute-done | bytes 20512 | tf_op jit(solution)/shard_map/ppermute | solution.py:228
  8.7 0.0 collective-permute-done
  8.7 1.4 %collective-permute-done.2 = bf16[80,128]{1,0:T(8,128)(2,1)S(1)} collective-permute-done((bf16[80,128]{1,0:T(8,128)(2,1)S(1)}, bf16[80,128]{1,0:T(8,128)(2,1)S(1)}, u32[]{:S(2)}, u32[]{:S(2)}) %collective-permute-start.2) | collective-permute-done | bytes 20512 | tf_op jit(solution)/shard_map/ppermute | solution.py:228
  10.1 3.7 %collective-permute-start.5 = (bf16[80,128]{1,0:T(8,128)(2,1)S(1)}, bf16[80,128]{1,0:T(8,128)(2,1)S(1)}, u32[]{:S(2)}, u32[]{:S(2)}) collective-permute-start(bf16[80,128]{1,0:T(8,128)(2,1)S(1)} %add_convert_fusion.1), channel_id=1, source_target_pairs={{0,24},{2,26},{4,28},{6,30},{8,16},{10,18},{12,20},{14,22},{16,8},... | collective-permute-start | bytes 61448 | tf_op jit(solution)/shard_map/ppermute | solution.py:228
  13.8 0.0 collective-permute-start.4
  13.8 0.8 %collective-permute-start.3 = (bf16[80,128]{1,0:T(8,128)(2,1)S(1)}, bf16[80,128]{1,0:T(8,128)(2,1)S(1)}, u32[]{:S(2)}, u32[]{:S(2)}) collective-permute-start(bf16[80,128]{1,0:T(8,128)(2,1)S(1)} %add_convert_fusion.1), channel_id=1, source_target_pairs={{0,8},{2,10},{4,12},{6,14},{8,0},{10,2},{12,4},{14,6},{16,24},{18,... | collective-permute-start | bytes 61448 | tf_op jit(solution)/shard_map/ppermute | solution.py:228
  14.6 1.2 %collective-permute-done.5 = bf16[80,128]{1,0:T(8,128)(2,1)S(1)} collective-permute-done((bf16[80,128]{1,0:T(8,128)(2,1)S(1)}, bf16[80,128]{1,0:T(8,128)(2,1)S(1)}, u32[]{:S(2)}, u32[]{:S(2)}) %collective-permute-start.5) | collective-permute-done | bytes 20512 | tf_op jit(solution)/shard_map/ppermute | solution.py:228
  15.8 2.7 %collective-permute-done.4 = bf16[80,128]{1,0:T(8,128)(2,1)S(1)} collective-permute-done((bf16[80,128]{1,0:T(8,128)(2,1)S(1)}, bf16[80,128]{1,0:T(8,128)(2,1)S(1)}, u32[]{:S(2)}, u32[]{:S(2)}) %collective-permute-start.4) | collective-permute-done | bytes 20512 | tf_op jit(solution)/shard_map/ppermute | solution.py:228
  18.5 0.0 collective-permute-done.3
  18.5 0.0 copy-done.1
  18.5 0.0 copy-done.3
  18.5 0.0 copy-done.2
  18.5 0.0 copy-done
  18.5 3.5 %first_layer.2 = (bf16[5,128,128]{2,1,0:T(8,128)(2,1)S(1)}, bf16[10,36,128,128]{3,2,1,0:T(8,128)(2,1)S(1)}) custom-call(s32[10,36]{1,0:T(8,128)S(1)} %copy-done.1, s32[10]{0:T(128)S(1)} %bitcast.9, f32[80,128]{1,0:T(8,128)S(1)} %convert_add_fusion.sums_ref, f32[80,128]{1,0:T(8,128)S(1)} %bitcast.6, ...), custom_call_target="tpu_custom_call", output_to_operand_aliasing={{1}: (5, {})} | custom-call | flops 754974720 | bytes 5898240 | tf_op jit(solution)/shard_map/first_layer/pallas_call | solution.py:245
  22.1 0.5 collective-permute-start.6
  22.6 2.5 %first_layer.3 = (f32[5,128,128]{2,1,0:T(8,128)S(1)}, bf16[10,36,128,128]{3,2,1,0:T(8,128)(2,1)S(1)}) custom-call(s32[10,36]{1,0:T(8,128)S(1)} %copy-done.1, s32[10]{0:T(128)S(1)} %bitcast.10, f32[80,128]{1,0:T(8,128)S(1)} %convert_add_fusion.sums_ref, f32[80,128]{1,0:T(8,128)S(1)} %bitcast.7, ...), custom_call_target="tpu_custom_call", output_to_operand_aliasing={{1}: (5, {})} | custom-call | flops 754974720 | bytes 5898240 | tf_op jit(solution)/shard_map/first_layer/pallas_call | solution.py:245
  25.0 2.4 %collective-permute-done.6 = bf16[5,128,128]{2,1,0:T(8,128)(2,1)S(1)} collective-permute-done((bf16[5,128,128]{2,1,0:T(8,128)(2,1)S(1)}, bf16[5,128,128]{2,1,0:T(8,128)(2,1)S(1)}, u32[]{:S(2)}, u32[]{:S(2)}) %collective-permute-start.6) | collective-permute-done | bytes 163872 | tf_op jit(solution)/shard_map/ppermute | solution.py:231
  27.5 1.0 %collective-permute-start.7 = (bf16[5,128,128]{2,1,0:T(8,128)(2,1)S(1)}, bf16[5,128,128]{2,1,0:T(8,128)(2,1)S(1)}, u32[]{:S(2)}, u32[]{:S(2)}) collective-permute-start(bf16[5,128,128]{2,1,0:T(8,128)(2,1)S(1)} %add_convert_fusion.own_ref), channel_id=1, source_target_pairs={{0,16},{2,18},{4,20},{6,22},{8,24},{10,26},{12,28},{14,30},{16,0},... | collective-permute-start | bytes 491528 | tf_op jit(solution)/shard_map/ppermute | solution.py:228
  28.5 6.6 %collective-permute-done.7.crossed_ref = bf16[5,128,128]{2,1,0:T(8,128)(2,1)S(1)} collective-permute-done((bf16[5,128,128]{2,1,0:T(8,128)(2,1)S(1)}, bf16[5,128,128]{2,1,0:T(8,128)(2,1)S(1)}, u32[]{:S(2)}, u32[]{:S(2)}) %collective-permute-start.7) | collective-permute-done | bytes 163872 | tf_op jit(solution)/shard_map/ppermute | solution.py:228
  35.2 0.9 %collective-permute-start.11 = (bf16[5,128,128]{2,1,0:T(8,128)(2,1)S(1)}, bf16[5,128,128]{2,1,0:T(8,128)(2,1)S(1)}, u32[]{:S(2)}, u32[]{:S(2)}) collective-permute-start(bf16[5,128,128]{2,1,0:T(8,128)(2,1)S(1)} %get-tuple-element.22), channel_id=1, source_target_pairs={{0,1},{1,0},{2,3},{3,2},{4,5},{5,4},{6,7},{7,6},{8,9},{9,8},{10,11... | collective-permute-start | bytes 491528 | tf_op jit(solution)/shard_map/ppermute | solution.py:231
  36.1 0.9 %collective-permute-start.10 = (bf16[5,128,128]{2,1,0:T(8,128)(2,1)S(1)}, bf16[5,128,128]{2,1,0:T(8,128)(2,1)S(1)}, u32[]{:S(2)}, u32[]{:S(2)}) collective-permute-start(bf16[5,128,128]{2,1,0:T(8,128)(2,1)S(1)} %get-tuple-element.21.refs_0_), channel_id=1, source_target_pairs={{0,12},{2,14},{4,8},{6,10},{8,4},{10,6},{12,0},{14,2},{16,28},{18,... | collective-permute-start | bytes 491528 | tf_op jit(solution)/shard_map/ppermute | solution.py:228
  37.0 1.8 %collective-permute-start.9 = (bf16[5,128,128]{2,1,0:T(8,128)(2,1)S(1)}, bf16[5,128,128]{2,1,0:T(8,128)(2,1)S(1)}, u32[]{:S(2)}, u32[]{:S(2)}) collective-permute-start(bf16[5,128,128]{2,1,0:T(8,128)(2,1)S(1)} %get-tuple-element.21.refs_0_), channel_id=1, source_target_pairs={{0,8},{2,10},{4,12},{6,14},{8,0},{10,2},{12,4},{14,6},{16,24},{18,... | collective-permute-start | bytes 491528 | tf_op jit(solution)/shard_map/ppermute | solution.py:228
  38.7 0.8 %collective-permute-start.8 = (bf16[5,128,128]{2,1,0:T(8,128)(2,1)S(1)}, bf16[5,128,128]{2,1,0:T(8,128)(2,1)S(1)}, u32[]{:S(2)}, u32[]{:S(2)}) collective-permute-start(bf16[5,128,128]{2,1,0:T(8,128)(2,1)S(1)} %get-tuple-element.21.refs_0_), channel_id=1, source_target_pairs={{0,4},{2,6},{4,0},{6,2},{8,12},{10,14},{12,8},{14,10},{16,20},{18,... | collective-permute-start | bytes 491528 | tf_op jit(solution)/shard_map/ppermute | solution.py:228
  39.5 1.4 %collective-permute-done.11.refs_0_ = bf16[5,128,128]{2,1,0:T(8,128)(2,1)S(1)} collective-permute-done((bf16[5,128,128]{2,1,0:T(8,128)(2,1)S(1)}, bf16[5,128,128]{2,1,0:T(8,128)(2,1)S(1)}, u32[]{:S(2)}, u32[]{:S(2)}) %collective-permute-start.11) | collective-permute-done | bytes 163872 | tf_op jit(solution)/shard_map/ppermute | solution.py:231
  41.0 0.0 collective-permute-start.14
  41.0 3.6 %collective-permute-start.13 = (bf16[5,128,128]{2,1,0:T(8,128)(2,1)S(1)}, bf16[5,128,128]{2,1,0:T(8,128)(2,1)S(1)}, u32[]{:S(2)}, u32[]{:S(2)}) collective-permute-start(bf16[5,128,128]{2,1,0:T(8,128)(2,1)S(1)} %collective-permute-done.11.refs_0_), channel_id=1, source_target_pairs={{0,8},{2,10},{4,12},{6,14},{8,0},{10,2},{12,4},{14,6},{16,24},{18,... | collective-permute-start | bytes 491528 | tf_op jit(solution)/shard_map/ppermute | solution.py:228
  44.5 0.0 collective-permute-done.10.refs_3_
  44.5 0.8 %collective-permute-start.12 = (bf16[5,128,128]{2,1,0:T(8,128)(2,1)S(1)}, bf16[5,128,128]{2,1,0:T(8,128)(2,1)S(1)}, u32[]{:S(2)}, u32[]{:S(2)}) collective-permute-start(bf16[5,128,128]{2,1,0:T(8,128)(2,1)S(1)} %collective-permute-done.11.refs_0_), channel_id=1, source_target_pairs={{0,4},{2,6},{4,0},{6,2},{8,12},{10,14},{12,8},{14,10},{16,20},{18,... | collective-permute-start | bytes 491528 | tf_op jit(solution)/shard_map/ppermute | solution.py:228
  45.3 2.0 %collective-permute-done.9.refs_2_ = bf16[5,128,128]{2,1,0:T(8,128)(2,1)S(1)} collective-permute-done((bf16[5,128,128]{2,1,0:T(8,128)(2,1)S(1)}, bf16[5,128,128]{2,1,0:T(8,128)(2,1)S(1)}, u32[]{:S(2)}, u32[]{:S(2)}) %collective-permute-start.9) | collective-permute-done | bytes 163872 | tf_op jit(solution)/shard_map/ppermute | solution.py:228
  47.4 2.1 %collective-permute-done.8.refs_1_ = bf16[5,128,128]{2,1,0:T(8,128)(2,1)S(1)} collective-permute-done((bf16[5,128,128]{2,1,0:T(8,128)(2,1)S(1)}, bf16[5,128,128]{2,1,0:T(8,128)(2,1)S(1)}, u32[]{:S(2)}, u32[]{:S(2)}) %collective-permute-start.8) | collective-permute-done | bytes 163872 | tf_op jit(solution)/shard_map/ppermute | solution.py:228
  49.5 0.1 collective-permute-start.15
  49.6 1.3 %collective-permute-done.14.refs_3_ = bf16[5,128,128]{2,1,0:T(8,128)(2,1)S(1)} collective-permute-done((bf16[5,128,128]{2,1,0:T(8,128)(2,1)S(1)}, bf16[5,128,128]{2,1,0:T(8,128)(2,1)S(1)}, u32[]{:S(2)}, u32[]{:S(2)}) %collective-permute-start.14) | collective-permute-done | bytes 163872 | tf_op jit(solution)/shard_map/ppermute | solution.py:228
  50.8 2.4 %collective-permute-done.13.refs_2_ = bf16[5,128,128]{2,1,0:T(8,128)(2,1)S(1)} collective-permute-done((bf16[5,128,128]{2,1,0:T(8,128)(2,1)S(1)}, bf16[5,128,128]{2,1,0:T(8,128)(2,1)S(1)}, u32[]{:S(2)}, u32[]{:S(2)}) %collective-permute-start.13) | collective-permute-done | bytes 163872 | tf_op jit(solution)/shard_map/ppermute | solution.py:228
  53.2 0.0 collective-permute-done.12.refs_1_
  53.2 0.1 collective-permute-start.16
  53.3 0.0 collective-permute-done.15.rest_2_
  53.3 2.1 %collective-permute-done.16.rest_3_ = bf16[20,128,128]{2,1,0:T(8,128)(2,1)S(1)} collective-permute-done((bf16[20,128,128]{2,1,0:T(8,128)(2,1)S(1)}, bf16[20,128,128]{2,1,0:T(8,128)(2,1)S(1)}, u32[]{:S(2)}, u32[]{:S(2)}) %collective-permute-start.16) | collective-permute-done | bytes 655392 | tf_op jit(solution)/shard_map/ppermute | solution.py:228
  55.4 2.1 %second_layer.2 = (bf16[5,128,128]{2,1,0:T(8,128)(2,1)S(1)}, bf16[80,128,128]{2,1,0:T(8,128)(2,1)S(1)}) custom-call(s32[10,36]{1,0:T(8,128)S(1)} %copy-done.1, s32[10]{0:T(128)S(1)} %bitcast.11, bf16[10,36,128,128]{3,2,1,0:T(8,128)(2,1)S(1)} %get-tuple-element.18.coef_ref, bf16[5,128,128]{2,1,0:T(8,128)(2,1)S(1)} %add_convert_fusion.own_ref, ...), custom_call_target="tpu_custom_call" | custom-call | flops 754974720 | bytes 5898240 | tf_op jit(solution)/shard_map/second_layer/pallas_call | solution.py:273
  57.5 1.7 %collective-permute-start.18 = (bf16[5,128,128]{2,1,0:T(8,128)(2,1)S(1)}, bf16[5,128,128]{2,1,0:T(8,128)(2,1)S(1)}, u32[]{:S(2)}, u32[]{:S(2)}) collective-permute-start(bf16[5,128,128]{2,1,0:T(8,128)(2,1)S(1)} %get-tuple-element.24.mine_ref), channel_id=1, source_target_pairs={{0,1},{1,0},{2,3},{3,2},{4,5},{5,4},{6,7},{7,6},{8,9},{9,8},{10,11... | collective-permute-start | bytes 491528 | tf_op jit(solution)/shard_map/ppermute | solution.py:231
  59.3 3.0 %second_layer.3.mine_ref = bf16[5,128,128]{2,1,0:T(8,128)(2,1)S(1)} custom-call(s32[10,36]{1,0:T(8,128)S(1)} %copy-done.1, s32[10]{0:T(128)S(1)} %bitcast.12, bf16[10,36,128,128]{3,2,1,0:T(8,128)(2,1)S(1)} %get-tuple-element.18.coef_ref, bf16[5,128,128]{2,1,0:T(8,128)(2,1)S(1)} %add_convert_fusion.own_ref, bf16[80,128,128]{2,1,0:T(8,128)(2,1)S(1)} %get-tuple-element.23.rest_0_), custom_call_target="tpu_custom_call" | custom-call | flops 754974720 | bytes 5898240 | tf_op jit(solution)/shard_map/second_layer/pallas_call | solution.py:273
  62.3 0.4 collective-permute-start.17
  62.8 1.2 %collective-permute-done.18.other_ref = bf16[5,128,128]{2,1,0:T(8,128)(2,1)S(1)} collective-permute-done((bf16[5,128,128]{2,1,0:T(8,128)(2,1)S(1)}, bf16[5,128,128]{2,1,0:T(8,128)(2,1)S(1)}, u32[]{:S(2)}, u32[]{:S(2)}) %collective-permute-start.18) | collective-permute-done | bytes 163872 | tf_op jit(solution)/shard_map/ppermute | solution.py:231
  63.9 0.7 %result.2.rest_0_ = bf16[10,128,128]{2,1,0:T(8,128)(2,1)} custom-call(bf16[5,128,128]{2,1,0:T(8,128)(2,1)S(1)} %get-tuple-element.24.mine_ref, bf16[5,128,128]{2,1,0:T(8,128)(2,1)S(1)} %collective-permute-done.18.other_ref), custom_call_target="tpu_custom_call" | custom-call | tf_op jit(solution)/shard_map/result/pallas_call | solution.py:327
  64.6 3.1 %collective-permute-done.17.other_ref = bf16[5,128,128]{2,1,0:T(8,128)(2,1)S(1)} collective-permute-done((bf16[5,128,128]{2,1,0:T(8,128)(2,1)S(1)}, bf16[5,128,128]{2,1,0:T(8,128)(2,1)S(1)}, u32[]{:S(2)}, u32[]{:S(2)}) %collective-permute-start.17) | collective-permute-done | bytes 163872 | tf_op jit(solution)/shard_map/ppermute | solution.py:231
  67.7 0.7 %result.3 = bf16[10,128,128]{2,1,0:T(8,128)(2,1)} custom-call(bf16[5,128,128]{2,1,0:T(8,128)(2,1)S(1)} %second_layer.3.mine_ref, bf16[5,128,128]{2,1,0:T(8,128)(2,1)S(1)} %collective-permute-done.17.other_ref, bf16[10,128,128]{2,1,0:T(8,128)(2,1)} %result.2.rest_0_), custom_call_target="tpu_custom_call", output_to_operand_aliasing={{}: (2, {})} | custom-call | tf_op jit(solution)/shard_map/result/pallas_call | solution.py:327
  (7 shorter events, 0.2 us)
Async XLA Ops:
  0.0 18.5 %copy-start.1 = (s32[10,36]{1,0:T(8,128)S(1)}, s32[10,36]{1,0:T(8,128)}, u32[]{:S(2)}) copy-start(s32[10,36]{1,0:T(8,128)} %cols_ref.7) | copy-start | bytes 4324
  0.0 18.5 %copy-start.3 = (s32[10,1]{0,1:T(1,128)S(1)}, s32[10,1]{0,1:T(1,128)}, u32[]{:S(2)}) copy-start(s32[10,1]{0,1:T(1,128)} %param.7) | copy-start | bytes 124
  0.0 18.5 %copy-start.2 = (f32[10240]{0:T(1024)S(1)}, f32[10240]{0:T(1024)}, u32[]{:S(2)}) copy-start(f32[10240]{0:T(1024)} %param.9) | copy-start | bytes 122884
  0.0 18.5 %copy-start = (bf16[10240,128]{1,0:T(8,128)(2,1)S(1)}, bf16[10240,128]{1,0:T(8,128)(2,1)}, u32[]{:S(2)}) copy-start(bf16[10240,128]{1,0:T(8,128)(2,1)} %param.8) | copy-start | bytes 7864324
  4.4 4.2 %collective-permute-start.1 = (bf16[80,128]{1,0:T(8,128)(2,1)S(1)}, bf16[80,128]{1,0:T(8,128)(2,1)S(1)}, u32[]{:S(2)}, u32[]{:S(2)}) collective-permute-start(bf16[80,128]{1,0:T(8,128)(2,1)S(1)} %convert_element_type.36), channel_id=1, source_target_pairs={{0,4},{2,6},{4,0},{6,2},{8,12},{10,14},{12,8},{14,10},{16,20},{18,... | collective-permute-start | bytes 61448 | tf_op jit(solution)/shard_map/ppermute | solution.py:228
  6.9 1.8 %collective-permute-start = (bf16[80,128]{1,0:T(8,128)(2,1)S(1)}, bf16[80,128]{1,0:T(8,128)(2,1)S(1)}, u32[]{:S(2)}, u32[]{:S(2)}) collective-permute-start(bf16[80,128]{1,0:T(8,128)(2,1)S(1)} %convert_element_type.36), channel_id=1, source_target_pairs={{0,2},{2,0},{4,6},{6,4},{8,10},{10,8},{12,14},{14,12},{16,18},{18,... | collective-permute-start | bytes 61448 | tf_op jit(solution)/shard_map/ppermute | solution.py:228
  6.9 3.2 %collective-permute-start.2 = (bf16[80,128]{1,0:T(8,128)(2,1)S(1)}, bf16[80,128]{1,0:T(8,128)(2,1)S(1)}, u32[]{:S(2)}, u32[]{:S(2)}) collective-permute-start(bf16[80,128]{1,0:T(8,128)(2,1)S(1)} %convert_element_type.36), channel_id=1, source_target_pairs={{0,6},{2,4},{4,2},{6,0},{8,14},{10,12},{12,10},{14,8},{16,22},{18,... | collective-permute-start | bytes 61448 | tf_op jit(solution)/shard_map/ppermute | solution.py:228
  10.1 5.7 %collective-permute-start.5 = (bf16[80,128]{1,0:T(8,128)(2,1)S(1)}, bf16[80,128]{1,0:T(8,128)(2,1)S(1)}, u32[]{:S(2)}, u32[]{:S(2)}) collective-permute-start(bf16[80,128]{1,0:T(8,128)(2,1)S(1)} %add_convert_fusion.1), channel_id=1, source_target_pairs={{0,24},{2,26},{4,28},{6,30},{8,16},{10,18},{12,20},{14,22},{16,8},... | collective-permute-start | bytes 61448 | tf_op jit(solution)/shard_map/ppermute | solution.py:228
  13.8 4.7 %collective-permute-start.4 = (bf16[80,128]{1,0:T(8,128)(2,1)S(1)}, bf16[80,128]{1,0:T(8,128)(2,1)S(1)}, u32[]{:S(2)}, u32[]{:S(2)}) collective-permute-start(bf16[80,128]{1,0:T(8,128)(2,1)S(1)} %add_convert_fusion.1), channel_id=1, source_target_pairs={{0,16},{2,18},{4,20},{6,22},{8,24},{10,26},{12,28},{14,30},{16,0},... | collective-permute-start | bytes 61448 | tf_op jit(solution)/shard_map/ppermute | solution.py:228
  13.8 4.7 %collective-permute-start.3 = (bf16[80,128]{1,0:T(8,128)(2,1)S(1)}, bf16[80,128]{1,0:T(8,128)(2,1)S(1)}, u32[]{:S(2)}, u32[]{:S(2)}) collective-permute-start(bf16[80,128]{1,0:T(8,128)(2,1)S(1)} %add_convert_fusion.1), channel_id=1, source_target_pairs={{0,8},{2,10},{4,12},{6,14},{8,0},{10,2},{12,4},{14,6},{16,24},{18,... | collective-permute-start | bytes 61448 | tf_op jit(solution)/shard_map/ppermute | solution.py:228
  22.1 5.4 %collective-permute-start.6 = (bf16[5,128,128]{2,1,0:T(8,128)(2,1)S(1)}, bf16[5,128,128]{2,1,0:T(8,128)(2,1)S(1)}, u32[]{:S(2)}, u32[]{:S(2)}) collective-permute-start(bf16[5,128,128]{2,1,0:T(8,128)(2,1)S(1)} %get-tuple-element.20), channel_id=1, source_target_pairs={{0,1},{1,0},{2,3},{3,2},{4,5},{5,4},{6,7},{7,6},{8,9},{9,8},{10,11... | collective-permute-start | bytes 491528 | tf_op jit(solution)/shard_map/ppermute | solution.py:231
  27.5 7.7 %collective-permute-start.7 = (bf16[5,128,128]{2,1,0:T(8,128)(2,1)S(1)}, bf16[5,128,128]{2,1,0:T(8,128)(2,1)S(1)}, u32[]{:S(2)}, u32[]{:S(2)}) collective-permute-start(bf16[5,128,128]{2,1,0:T(8,128)(2,1)S(1)} %add_convert_fusion.own_ref), channel_id=1, source_target_pairs={{0,16},{2,18},{4,20},{6,22},{8,24},{10,26},{12,28},{14,30},{16,0},... | collective-permute-start | bytes 491528 | tf_op jit(solution)/shard_map/ppermute | solution.py:228
  35.2 5.8 %collective-permute-start.11 = (bf16[5,128,128]{2,1,0:T(8,128)(2,1)S(1)}, bf16[5,128,128]{2,1,0:T(8,128)(2,1)S(1)}, u32[]{:S(2)}, u32[]{:S(2)}) collective-permute-start(bf16[5,128,128]{2,1,0:T(8,128)(2,1)S(1)} %get-tuple-element.22), channel_id=1, source_target_pairs={{0,1},{1,0},{2,3},{3,2},{4,5},{5,4},{6,7},{7,6},{8,9},{9,8},{10,11... | collective-permute-start | bytes 491528 | tf_op jit(solution)/shard_map/ppermute | solution.py:231
  36.1 8.5 %collective-permute-start.10 = (bf16[5,128,128]{2,1,0:T(8,128)(2,1)S(1)}, bf16[5,128,128]{2,1,0:T(8,128)(2,1)S(1)}, u32[]{:S(2)}, u32[]{:S(2)}) collective-permute-start(bf16[5,128,128]{2,1,0:T(8,128)(2,1)S(1)} %get-tuple-element.21.refs_0_), channel_id=1, source_target_pairs={{0,12},{2,14},{4,8},{6,10},{8,4},{10,6},{12,0},{14,2},{16,28},{18,... | collective-permute-start | bytes 491528 | tf_op jit(solution)/shard_map/ppermute | solution.py:228
  37.0 10.4 %collective-permute-start.9 = (bf16[5,128,128]{2,1,0:T(8,128)(2,1)S(1)}, bf16[5,128,128]{2,1,0:T(8,128)(2,1)S(1)}, u32[]{:S(2)}, u32[]{:S(2)}) collective-permute-start(bf16[5,128,128]{2,1,0:T(8,128)(2,1)S(1)} %get-tuple-element.21.refs_0_), channel_id=1, source_target_pairs={{0,8},{2,10},{4,12},{6,14},{8,0},{10,2},{12,4},{14,6},{16,24},{18,... | collective-permute-start | bytes 491528 | tf_op jit(solution)/shard_map/ppermute | solution.py:228
  38.7 10.7 %collective-permute-start.8 = (bf16[5,128,128]{2,1,0:T(8,128)(2,1)S(1)}, bf16[5,128,128]{2,1,0:T(8,128)(2,1)S(1)}, u32[]{:S(2)}, u32[]{:S(2)}) collective-permute-start(bf16[5,128,128]{2,1,0:T(8,128)(2,1)S(1)} %get-tuple-element.21.refs_0_), channel_id=1, source_target_pairs={{0,4},{2,6},{4,0},{6,2},{8,12},{10,14},{12,8},{14,10},{16,20},{18,... | collective-permute-start | bytes 491528 | tf_op jit(solution)/shard_map/ppermute | solution.py:228
  41.0 9.9 %collective-permute-start.14 = (bf16[5,128,128]{2,1,0:T(8,128)(2,1)S(1)}, bf16[5,128,128]{2,1,0:T(8,128)(2,1)S(1)}, u32[]{:S(2)}, u32[]{:S(2)}) collective-permute-start(bf16[5,128,128]{2,1,0:T(8,128)(2,1)S(1)} %collective-permute-done.11.refs_0_), channel_id=1, source_target_pairs={{0,12},{2,14},{4,8},{6,10},{8,4},{10,6},{12,0},{14,2},{16,28},{18,... | collective-permute-start | bytes 491528 | tf_op jit(solution)/shard_map/ppermute | solution.py:228
  41.0 12.2 %collective-permute-start.13 = (bf16[5,128,128]{2,1,0:T(8,128)(2,1)S(1)}, bf16[5,128,128]{2,1,0:T(8,128)(2,1)S(1)}, u32[]{:S(2)}, u32[]{:S(2)}) collective-permute-start(bf16[5,128,128]{2,1,0:T(8,128)(2,1)S(1)} %collective-permute-done.11.refs_0_), channel_id=1, source_target_pairs={{0,8},{2,10},{4,12},{6,14},{8,0},{10,2},{12,4},{14,6},{16,24},{18,... | collective-permute-start | bytes 491528 | tf_op jit(solution)/shard_map/ppermute | solution.py:228
  44.5 8.7 %collective-permute-start.12 = (bf16[5,128,128]{2,1,0:T(8,128)(2,1)S(1)}, bf16[5,128,128]{2,1,0:T(8,128)(2,1)S(1)}, u32[]{:S(2)}, u32[]{:S(2)}) collective-permute-start(bf16[5,128,128]{2,1,0:T(8,128)(2,1)S(1)} %collective-permute-done.11.refs_0_), channel_id=1, source_target_pairs={{0,4},{2,6},{4,0},{6,2},{8,12},{10,14},{12,8},{14,10},{16,20},{18,... | collective-permute-start | bytes 491528 | tf_op jit(solution)/shard_map/ppermute | solution.py:228
  49.5 3.8 %collective-permute-start.15 = (bf16[20,128,128]{2,1,0:T(8,128)(2,1)S(1)}, bf16[20,128,128]{2,1,0:T(8,128)(2,1)S(1)}, u32[]{:S(2)}, u32[]{:S(2)}) collective-permute-start(bf16[20,128,128]{2,1,0:T(8,128)(2,1)S(1)} %own_joined.2.rest_0_), channel_id=1, source_target_pairs={{0,2},{2,0},{4,6},{6,4},{8,10},{10,8},{12,14},{14,12},{16,18},{18,... | collective-permute-start | bytes 1966088 | tf_op jit(solution)/shard_map/ppermute | solution.py:228
  53.2 2.2 %collective-permute-start.16 = (bf16[20,128,128]{2,1,0:T(8,128)(2,1)S(1)}, bf16[20,128,128]{2,1,0:T(8,128)(2,1)S(1)}, u32[]{:S(2)}, u32[]{:S(2)}) collective-permute-start(bf16[20,128,128]{2,1,0:T(8,128)(2,1)S(1)} %own_joined.3.rest_1_), channel_id=1, source_target_pairs={{0,2},{2,0},{4,6},{6,4},{8,10},{10,8},{12,14},{14,12},{16,18},{18,... | collective-permute-start | bytes 1966088 | tf_op jit(solution)/shard_map/ppermute | solution.py:228
  57.5 6.4 %collective-permute-start.18 = (bf16[5,128,128]{2,1,0:T(8,128)(2,1)S(1)}, bf16[5,128,128]{2,1,0:T(8,128)(2,1)S(1)}, u32[]{:S(2)}, u32[]{:S(2)}) collective-permute-start(bf16[5,128,128]{2,1,0:T(8,128)(2,1)S(1)} %get-tuple-element.24.mine_ref), channel_id=1, source_target_pairs={{0,1},{1,0},{2,3},{3,2},{4,5},{5,4},{6,7},{7,6},{8,9},{9,8},{10,11... | collective-permute-start | bytes 491528 | tf_op jit(solution)/shard_map/ppermute | solution.py:231
  62.3 5.4 %collective-permute-start.17 = (bf16[5,128,128]{2,1,0:T(8,128)(2,1)S(1)}, bf16[5,128,128]{2,1,0:T(8,128)(2,1)S(1)}, u32[]{:S(2)}, u32[]{:S(2)}) collective-permute-start(bf16[5,128,128]{2,1,0:T(8,128)(2,1)S(1)} %second_layer.3.mine_ref), channel_id=1, source_target_pairs={{0,1},{1,0},{2,3},{3,2},{4,5},{5,4},{6,7},{7,6},{8,9},{9,8},{10,11... | collective-permute-start | bytes 491528 | tf_op jit(solution)/shard_map/ppermute | solution.py:231

commit v12 on v11

--- a/solution.py
+++ b/solution.py
@@ -12,10 +12,6 @@
 
 def divisor(slot_count, most):
     return max(size for size in range(1, most + 1) if slot_count % size == 0)
-
-
-def chunk_total(counts_ref, b, chunk):
-    return lax.div(counts_ref[b] + (chunk - 1), chunk)
 
 
 def sums_kernel(cols_hbm, counts_hbm, blocks_ref, sums_ref, held_ref, acc_ref, cols_ref, counts_ref, list_sems, sems):
@@ -62,7 +58,7 @@
     sums_ref[...] = jnp.sum(acc_ref[:groups], axis=1)
 
 
-def multiply_rows(rows, counts_ref, chunk, start, gather, acc_ref):
+def multiply_rows(rows, totals, chunk, start, gather, acc_ref):
     def product(row, first):
         left, right = zip(*[gather(row, first + u) for u in range(chunk)])
         return jnp.dot(jnp.concatenate(left, axis=1), jnp.concatenate(right, axis=0), preferred_element_type=jnp.float32)
@@ -75,10 +71,11 @@
             acc_ref[b] += product(row, k * chunk)
             return carry
 
-        lax.fori_loop(1, chunk_total(counts_ref, row, chunk), add, 0)
-
-
-def first_kernel(sending, cols_ref, counts_ref, sums_ref, added_ref, demand_ref, blocks_ref, out_ref, coef_ref, inverse_ref, acc_ref):
+        lax.fori_loop(1, lax.div(totals[b] + (chunk - 1), chunk), add, 0)
+
+
+def first_kernel(sending, cols_ref, counts_ref, sums_ref, added_ref, demand_ref, blocks_ref, *rest):
+    out_ref, coef_ref, inverse_ref, acc_ref = rest[-4:]
     slots, size = blocks_ref.shape[1:3]
     count = out_ref.shape[0]
     base = 0
@@ -96,7 +93,7 @@
         return coef, demand_ref[col]
 
     rows = [base + b for b in range(count)]
-    multiply_rows(rows, counts_ref, divisor(slots, 12), lambda b: 0.0, gather, acc_ref)
+    multiply_rows(rows, [counts_ref[row] for row in rows], divisor(slots, 12), lambda b: 0.0, gather, acc_ref)
     out_ref[...] = acc_ref[...].astype(out_ref.dtype)
 
 
@@ -107,7 +104,7 @@
         return coef_ref[row, slot], source_ref[place(cols_ref[row, slot])]
 
     rows = [first_row + b for b in range(out_ref.shape[0])]
-    multiply_rows(rows, counts_ref, divisor(slots, 12), start, gather, acc_ref)
+    multiply_rows(rows, [counts_ref[row] for row in rows], divisor(slots, 12), start, gather, acc_ref)
     out_ref[...] = acc_ref[...].astype(out_ref.dtype)
 
 
@@ -117,31 +114,67 @@
     return scale
 
 
-PLACES = ((0, 0), (0, 1), (1, 0), (1, 1))
-
-
-def second_part_kernel(which, cols_ref, counts_ref, coef_ref, own_ref, *rest):
-    part = own_ref.shape[0]
-    if which == 0:
-        pieces, (out_ref, source_ref, acc_ref) = rest[:-3], rest[-3:]
-        for array, (core, away) in zip(pieces, ((0, 0), (0, 1), (1, 0), (1, 1))):
-            for i, (z, y) in enumerate(PLACES):
-                at = ((z * 4 + y * 2 + core) * 2 + away) * part
-                source_ref[at : at + part] = array[i * part : (i + 1) * part]
-    else:
-        source_ref, out_ref, acc_ref = rest
+FIRST_CHUNK, LAST_CHUNK = 8, 4
+
+
+def plan_kernel(part, cols_ref, counts_ref, _, first_ref, last_ref, totals_ref):
+    rows, slots = cols_ref.shape
+    near = lax.rem(lax.axis_index("row"), 8) * 2 + lax.axis_index("col")
+    scale = exact_scale(16 * part, part)
+    for b in range(rows):
+
+        def add(slot, ends, b=b):
+            first, last = ends
+            col = cols_ref[b, slot]
+            piece = lax.shift_right_logical(col * scale, 16)
+            place = piece ^ near
+            group = place & 3
+            entry = slot * 256 + lax.shift_right_logical(place, 2) * part + col - part * piece
+            is_last = (group == 3).astype(jnp.int32)
+            first_ref[b, first] = entry + group * (4 * part)
+            last_ref[b, last] = entry
+            return first + 1 - is_last, last + is_last
+
+        first, last = lax.fori_loop(0, counts_ref[b], add, (0, 0))
+        totals_ref[0, b] = first
+        totals_ref[1, b] = last
+        for ref, end, chunk in ((first_ref, first, FIRST_CHUNK), (last_ref, last, LAST_CHUNK)):
+            for u in range(chunk):
+                ref[b, end + u] = 0
+
+
+def list_gather(list_ref, totals_ref, which, coef_ref, source_ref):
+    def gather(row, i):
+        entry = list_ref[row, i]
+        coef = coef_ref[row, lax.shift_right_logical(entry, 8)]
+        return jnp.where(i < totals_ref[which, row], coef, jnp.zeros_like(coef)), source_ref[entry & 255]
+
+    return gather
+
+
+def second_first_kernel(list_ref, totals_ref, coef_ref, *rest):
+    pieces, (out_ref, source_ref) = rest[:-2], rest[-2:]
+    length = pieces[0].shape[0]
+    for i, piece in enumerate(pieces):
+        source_ref[i * length : (i + 1) * length] = piece[...]
+    gather = list_gather(list_ref, totals_ref, 0, coef_ref, source_ref)
+    rows = list(range(out_ref.shape[0]))
+    totals = [totals_ref[0, row] for row in rows]
+    multiply_rows(rows, totals, FIRST_CHUNK, lambda b: 0.0, gather, out_ref)
+
+
+def second_last_kernel(which, list_ref, totals_ref, coef_ref, sum_ref, own_ref, source_ref, out_ref, acc_ref):
+    count = out_ref.shape[0]
     side = lax.axis_index("col")
-    near = lax.rem(lax.axis_index("row"), 8) * 2 + side
-    scale = exact_scale(source_ref.shape[0], part)
-
-    def place(col):
-        piece = lax.shift_right_logical(col * scale, 16)
-        return col + part * ((piece ^ near) - piece)
+    gather = list_gather(list_ref, totals_ref, 1, coef_ref, source_ref)
+    rows = [which * count + b for b in range(count)]
+    totals = [totals_ref[1, row] for row in rows]
 
     def start(b):
-        return jnp.where(side == which, own_ref[b].astype(jnp.float32), 0.0)
-
-    second_rows(which * part, place, cols_ref, counts_ref, coef_ref, source_ref, start, out_ref, acc_ref)
+        return sum_ref[rows[b]] + jnp.where(side == which, own_ref[b].astype(jnp.float32), 0.0)
+
+    multiply_rows(rows, totals, LAST_CHUNK, start, gather, acc_ref)
+    out_ref[...] = acc_ref[...].astype(out_ref.dtype)
 
 
 def second_kernel(cols_ref, counts_ref, coef_ref, own_ref, source_ref, out_ref, acc_ref):
@@ -170,7 +203,7 @@
 def join_kernel(*refs):
     pieces, joined_ref = refs[:-1], refs[-1]
     part = pieces[0].shape[0]
-    for i, piece in enumerate(pieces):
+    for i, piece in zip((0, 3, 2, 1), pieces):
         joined_ref[i * part : (i + 1) * part] = piece[...]
 
 
@@ -200,7 +233,7 @@
     width = demand.shape[1]
     groups = demand.shape[0] // size
     group_devices = n_row // n_col
-    paired = n_col == 2 and n_row == 16 and rows % 2 == 0
+    paired = n_col == 2 and n_row == 16 and rows % 2 == 0 and rows <= 12
     half = rows // 2
     counts = counts.reshape(rows)
 
@@ -231,9 +264,23 @@
         return lax.ppermute(array, "col", [(0, 1), (1, 0)])
 
     if paired:
-        for masks in ((1, 2, 3), (4, 8, 12)):
+        for masks in ((1, 2, 3), (12, 8, 4)):
             sums = sums.astype(jnp.bfloat16)
             parts = [sums] + [flip(sums, m) for m in masks]
+            if masks[0] == 12:
+                plan = pl.pallas_call(
+                    functools.partial(plan_kernel, half),
+                    name="slot_plan",
+                    out_shape=(
+                        jax.ShapeDtypeStruct((rows, slots + FIRST_CHUNK), jnp.int32),
+                        jax.ShapeDtypeStruct((rows, slots + FIRST_CHUNK), jnp.int32),
+                        jax.ShapeDtypeStruct((2, rows), jnp.int32),
+                    ),
+                    in_specs=[SMEM, SMEM, pl.BlockSpec(memory_space=pl.ANY)],
+                    out_specs=(SMEM, SMEM, SMEM),
+                    compiler_params=PARAMS,
+                    cost_estimate=cost(10**9, 10**6),
+                )(slot_cols, counts, sums)
             sums = functools.reduce(jnp.add, [part.astype(jnp.float32) for part in parts])
     else:
         sums = lax.psum(sums, "row")
@@ -241,7 +288,7 @@
     def layer_cost(count):
         return cost(2 * count * slots * size * size * width, count * slots * size * size * 2)
 
-    def first_layer(sending, count, dtype, held):
+    def first_layer(sending, count, dtype, held, earlier=()):
         return pl.pallas_call(
             functools.partial(first_kernel, sending),
             name="first_layer",
@@ -249,7 +296,7 @@
                 jax.ShapeDtypeStruct((count, size, width), dtype),
                 pltpu.VMEM(blocks.shape, blocks.dtype),
             ),
-            in_specs=[SMEM, SMEM, VMEM, VMEM, VMEM, VMEM],
+            in_specs=[SMEM, SMEM, VMEM, VMEM, VMEM, VMEM] + [pl.BlockSpec(memory_space=pl.ANY)] * len(earlier),
             out_specs=(VMEM, VMEM),
             scratch_shapes=[
                 pltpu.VMEM((groups, 1, size), jnp.float32),
@@ -265,21 +312,20 @@
             value_added.reshape(groups, size),
             demand.reshape(groups, size, width),
             in_vmem(held),
+            *earlier,
         )
 
-    def second_call(kernel, count, coefs, own, sources, keep_sources):
-        dtype = jnp.bfloat16 if paired else jnp.float32
-        out = jax.ShapeDtypeStruct((count, size, width), dtype)
+    def second_call(kernel, count, lists, inputs, scratch_shapes, dtype):
         return pl.pallas_call(
             kernel,
             name="second_layer",
-            out_shape=(out, jax.ShapeDtypeStruct((groups, size, width), jnp.bfloat16)) if keep_sources else out,
-            in_specs=[SMEM, SMEM] + [VMEM] * (2 + len(sources)),
-            out_specs=(VMEM, VMEM) if keep_sources else VMEM,
-            scratch_shapes=[pltpu.VMEM((count, size, width), jnp.float32)],
+            out_shape=jax.ShapeDtypeStruct((count, size, width), dtype),
+            in_specs=[SMEM] * 2 + [VMEM] * len(inputs),
+            out_specs=VMEM,
+            scratch_shapes=scratch_shapes,
             compiler_params=PARAMS,
             cost_estimate=layer_cost(count),
-        )(slot_cols, counts, in_vmem(coefs), own, *sources)
+        )(*lists, in_vmem(inputs[0]), *inputs[1:])
 
     if not paired:
         group = lax.axis_index("col")
@@ -287,10 +333,12 @@
         layer_one = lax.psum(partial, "col").astype(jnp.bfloat16)
         gathered = lax.all_gather(layer_one, "row", axis=0, tiled=True)
         source = lax.dynamic_slice_in_dim(gathered, group * groups, groups, 0)
-        partial = second_call(second_kernel, rows, coefs, layer_one, [source], False)
+        sums_shape = pltpu.VMEM((rows, size, width), jnp.float32)
+        lists, inputs = [slot_cols, counts], [coefs, layer_one, source]
+        partial = second_call(second_kernel, rows, lists, inputs, [sums_shape], jnp.float32)
         return lax.psum(partial, "col").astype(jnp.bfloat16).reshape(rows * size, width)
 
-    sent, coefs = first_layer(True, half, jnp.bfloat16, held)
+    sent, coefs = first_layer(True, half, jnp.bfloat16, held, plan)
     arrived = swap(sent)
     kept, coefs = first_layer(False, half, jnp.float32, coefs)
     own = (kept + arrived.astype(jnp.float32)).astype(jnp.bfloat16)
@@ -315,12 +363,25 @@
             compiler_params=PARAMS,
         )(*pieces)
 
-    gathered = [join([part] + [flip(part, mask) for mask in (2, 4, 6)]) for part in (home, swap(away))]
-    pieces = gathered + [flip(part, 1) for part in gathered]
-
-    part_a, source = second_call(functools.partial(second_part_kernel, 0), half, coefs, own, pieces, True)
+    def spread(part):
+        return join([part, flip(part, 6), flip(part, 4), flip(part, 2)])
+
+    home, away = spread(home), spread(swap(away))
+    home_core, away_core = flip(home, 1), flip(away, 1)
+    first_list, last_list, totals = plan
+    sources = pltpu.VMEM((3 * home.shape[0], size, width), jnp.bfloat16)
+    lists, inputs = [first_list, totals], [coefs, home, away, home_core]
+    total = second_call(second_first_kernel, rows, lists, inputs, [sources], jnp.float32)
+
+    def last_pass(which):
+        kernel = functools.partial(second_last_kernel, which)
+        sums_shape = pltpu.VMEM((half, size, width), jnp.float32)
+        lists, inputs = [last_list, totals], [coefs, total, own, away_core]
+        return second_call(kernel, half, lists, inputs, [sums_shape], jnp.bfloat16)
+
+    part_a = last_pass(0)
     other_a = swap(part_a)
-    part_b = second_call(functools.partial(second_part_kernel, 1), half, coefs, own, [source], False)
+    part_b = last_pass(1)
     other_b = swap(part_b)
 
     def result(first_row, inputs):

time: 68.3 us -> 69.3 us (1.015)
  waiting for transfers between devices: 31.5 us -> 34.6 us
  starting transfers between devices: 19.6 us -> 16.7 us
  Pallas kernels: 17.1 us -> 18.1 us
    ppermute x15, starting transfers between devices: 16.1 us -> 12.4 us  [flip(): return lax.ppermute(array, 'row', [(i, i ^ mask) for i in range(n_row)])]
    pallas_call x2 -> x4, Pallas kernels: 5.16 us -> 8.28 us  [the longest x3 5.32 us: second_call(): pl.pallas_call(kernel, name='second_layer', out_shape=jax.ShapeDtypeStruc...]
    ppermute x15, waiting for transfers between devices: 23.4 us -> 25.1 us  [flip(): return lax.ppermute(array, 'row', [(i, i ^ mask) for i in range(n_row)])]
    pallas_call x2, Pallas kernels: 6 us -> 4.39 us  [first_layer(): pl.pallas_call(functools.partial(first_kernel, sending), name='first_laye...]
    ppermute x4, waiting for transfers between devices: 8.09 us -> 9.48 us  [swap(): return lax.ppermute(array, 'col', [(0, 1), (1, 0)])]
    ppermute x4, starting transfers between devices: 3.51 us -> 4.34 us  [swap(): return lax.ppermute(array, 'col', [(0, 1), (1, 0)])]
  transfers between devices with their start and end apart: 19 -> 19, of which waited for: 14 -> 12; matrix products, arithmetic and copies ran while one was open for 0% -> 0% of each run, Pallas kernels for 9% -> 14%
where the time goes in v12:
time: 69.3 us; the launch traced here: 69.7 us
  waiting for transfers between devices  34.6 us (50%)
  Pallas kernels  18.1 us (26%)
  starting transfers between devices  16.7 us (24%)
    ppermute x15, waiting for transfers between devices, flip(): return lax.ppermute(array, 'row', [(i, i ^ mask) for i in range(n_row)])  25.1 us
    ppermute x15, starting transfers between devices, flip(): return lax.ppermute(array, 'row', [(i, i ^ mask) for i in range(n_row)])  12.4 us
    ppermute x4, waiting for transfers between devices, swap(): return lax.ppermute(array, 'col', [(0, 1), (1, 0)])  9.48 us
    pallas_call x3, Pallas kernels, second_call(): pl.pallas_call(kernel, name='second_layer', out_shape=jax.ShapeDtypeStruc...  5.32 us
    pallas_call x2, Pallas kernels, first_layer(): pl.pallas_call(functools.partial(first_kernel, sending), name='first_laye...  4.39 us
    ppermute x4, starting transfers between devices, swap(): return lax.ppermute(array, 'col', [(0, 1), (1, 0)])  4.34 us
    pallas_call x1, Pallas kernels, body(): pl.pallas_call(sums_kernel, name='column_sums', out_shape=(jax.ShapeDtype...  3.86 us
    pallas_call x1, Pallas kernels, body(): pl.pallas_call(functools.partial(plan_kernel, half), name='slot_plan', ou...  2.96 us
  transfers between devices with their start and end apart: 19, of which 12 were waited for; matrix products, arithmetic and copies ran while one was open for 0% of the time, Pallas kernels for 14%

profile of v12, /device:TPU:0, one launch (start us, length us, event | category | flops | bytes accessed | tf_op | source)
XLA Modules:
  0.0 69.7 jit_solution(5044827432849983526)
XLA Ops:
  0.0 0.0 copy-start.2
  0.0 0.0 copy-start.3
  0.0 0.0 copy-start.1
  0.0 0.0 copy-start
  0.0 3.9 %column_sums.1 = (f32[80,128]{1,0:T(8,128)S(1)}, bf16[10,36,128,128]{3,2,1,0:T(8,128)(2,1)S(1)}) custom-call(s32[10,36]{1,0:T(8,128)} %cols_ref.5, s32[10]{0:T(128)} %bitcast.8, bf16[10,36,128,128]{3,2,1,0:T(8,128)(2,1)} %blocks_ref.1), custom_call_target="tpu_custom_call" | custom-call | bytes 23592960 | tf_op jit(solution)/shard_map/column_sums/pallas_call | solution.py:240
  3.9 3.4 %collective-permute-start.1 = (bf16[80,128]{1,0:T(8,128)(2,1)S(1)}, bf16[80,128]{1,0:T(8,128)(2,1)S(1)}, u32[]{:S(2)}, u32[]{:S(2)}) collective-permute-start(bf16[80,128]{1,0:T(8,128)(2,1)S(1)} %convert_element_type.36), channel_id=1, source_target_pairs={{0,4},{2,6},{4,0},{6,2},{8,12},{10,14},{12,8},{14,10},{16,20},{18,... | collective-permute-start | bytes 61448 | tf_op jit(solution)/shard_map/ppermute | solution.py:261
  7.3 0.0 collective-permute-start
  7.3 0.2 collective-permute-start.2
  7.5 1.6 %collective-permute-done.1 = bf16[80,128]{1,0:T(8,128)(2,1)S(1)} collective-permute-done((bf16[80,128]{1,0:T(8,128)(2,1)S(1)}, bf16[80,128]{1,0:T(8,128)(2,1)S(1)}, u32[]{:S(2)}, u32[]{:S(2)}) %collective-permute-start.1) | collective-permute-done | bytes 20512 | tf_op jit(solution)/shard_map/ppermute | solution.py:261
  9.1 0.0 collective-permute-done
  9.1 1.4 %collective-permute-done.2 = bf16[80,128]{1,0:T(8,128)(2,1)S(1)} collective-permute-done((bf16[80,128]{1,0:T(8,128)(2,1)S(1)}, bf16[80,128]{1,0:T(8,128)(2,1)S(1)}, u32[]{:S(2)}, u32[]{:S(2)}) %collective-permute-start.2) | collective-permute-done | bytes 20512 | tf_op jit(solution)/shard_map/ppermute | solution.py:261
  10.6 0.7 collective-permute-start.5
  11.2 3.3 %collective-permute-start.4 = (bf16[80,128]{1,0:T(8,128)(2,1)S(1)}, bf16[80,128]{1,0:T(8,128)(2,1)S(1)}, u32[]{:S(2)}, u32[]{:S(2)}) collective-permute-start(bf16[80,128]{1,0:T(8,128)(2,1)S(1)} %add_convert_fusion.1._), channel_id=1, source_target_pairs={{0,16},{2,18},{4,20},{6,22},{8,24},{10,26},{12,28},{14,30},{16,0},... | collective-permute-start | bytes 61448 | tf_op jit(solution)/shard_map/ppermute | solution.py:261
  14.5 0.5 collective-permute-start.3
  15.0 0.0 copy-done.2
  15.0 0.0 copy-done.3
  15.0 3.0 %slot_plan.1 = (s32[10,44]{1,0:T(8,128)S(1)}, s32[10,44]{1,0:T(8,128)S(1)}, s32[2,10]{1,0:T(2,128)S(1)}) custom-call(s32[10,36]{1,0:T(8,128)S(1)} %copy-done.2, s32[10]{0:T(128)S(1)} %bitcast.9, bf16[80,128]{1,0:T(8,128)(2,1)S(1)} %add_convert_fusion.1._), custom_call_target="tpu_custom_call" | custom-call | flops 1000000000 | bytes 1000000 | tf_op jit(solution)/shard_map/slot_plan/pallas_call | solution.py:271
  18.0 0.0 collective-permute-done.5
  18.0 0.0 collective-permute-done.4
  18.0 2.1 %collective-permute-done.3 = bf16[80,128]{1,0:T(8,128)(2,1)S(1)} collective-permute-done((bf16[80,128]{1,0:T(8,128)(2,1)S(1)}, bf16[80,128]{1,0:T(8,128)(2,1)S(1)}, u32[]{:S(2)}, u32[]{:S(2)}) %collective-permute-start.3) | collective-permute-done | bytes 20512 | tf_op jit(solution)/shard_map/ppermute | solution.py:261
  20.1 0.0 copy-done.1
  20.1 0.0 copy-done
  20.2 1.9 %first_layer.2 = (bf16[5,128,128]{2,1,0:T(8,128)(2,1)S(1)}, bf16[10,36,128,128]{3,2,1,0:T(8,128)(2,1)S(1)}) custom-call(s32[10,36]{1,0:T(8,128)S(1)} %copy-done.2, s32[10]{0:T(128)S(1)} %bitcast.10, f32[80,128]{1,0:T(8,128)S(1)} %convert_add_fusion.sums_ref, f32[80,128]{1,0:T(8,128)S(1)} %bitcast.6, ...), custom_call_target="tpu_custom_call", output_to_operand_aliasing={{1}: (5, {})} | custom-call | flops 754974720 | bytes 5898240 | tf_op jit(solution)/shard_map/first_layer/pallas_call | solution.py:292
  22.1 2.1 %collective-permute-start.6 = (bf16[5,128,128]{2,1,0:T(8,128)(2,1)S(1)}, bf16[5,128,128]{2,1,0:T(8,128)(2,1)S(1)}, u32[]{:S(2)}, u32[]{:S(2)}) collective-permute-start(bf16[5,128,128]{2,1,0:T(8,128)(2,1)S(1)} %get-tuple-element.24), channel_id=1, source_target_pairs={{0,1},{1,0},{2,3},{3,2},{4,5},{5,4},{6,7},{7,6},{8,9},{9,8},{10,11... | collective-permute-start | bytes 491528 | tf_op jit(solution)/shard_map/ppermute | solution.py:264
  24.2 2.5 %first_layer.3 = (f32[5,128,128]{2,1,0:T(8,128)S(1)}, bf16[10,36,128,128]{3,2,1,0:T(8,128)(2,1)S(1)}) custom-call(s32[10,36]{1,0:T(8,128)S(1)} %copy-done.2, s32[10]{0:T(128)S(1)} %bitcast.11, f32[80,128]{1,0:T(8,128)S(1)} %convert_add_fusion.sums_ref, f32[80,128]{1,0:T(8,128)S(1)} %bitcast.7, ...), custom_call_target="tpu_custom_call", output_to_operand_aliasing={{1}: (5, {})} | custom-call | flops 754974720 | bytes 5898240 | tf_op jit(solution)/shard_map/first_layer/pallas_call | solution.py:292
  26.7 1.5 %collective-permute-done.6 = bf16[5,128,128]{2,1,0:T(8,128)(2,1)S(1)} collective-permute-done((bf16[5,128,128]{2,1,0:T(8,128)(2,1)S(1)}, bf16[5,128,128]{2,1,0:T(8,128)(2,1)S(1)}, u32[]{:S(2)}, u32[]{:S(2)}) %collective-permute-start.6) | collective-permute-done | bytes 163872 | tf_op jit(solution)/shard_map/ppermute | solution.py:264
  28.2 0.1 collective-permute-start.7
  28.3 9.5 %collective-permute-done.7.crossed_ref = bf16[5,128,128]{2,1,0:T(8,128)(2,1)S(1)} collective-permute-done((bf16[5,128,128]{2,1,0:T(8,128)(2,1)S(1)}, bf16[5,128,128]{2,1,0:T(8,128)(2,1)S(1)}, u32[]{:S(2)}, u32[]{:S(2)}) %collective-permute-start.7) | collective-permute-done | bytes 163872 | tf_op jit(solution)/shard_map/ppermute | solution.py:261
  37.8 0.1 collective-permute-start.11
  37.9 0.1 collective-permute-start.10
  38.0 0.3 collective-permute-start.9
  38.3 3.2 %collective-permute-start.8 = (bf16[5,128,128]{2,1,0:T(8,128)(2,1)S(1)}, bf16[5,128,128]{2,1,0:T(8,128)(2,1)S(1)}, u32[]{:S(2)}, u32[]{:S(2)}) collective-permute-start(bf16[5,128,128]{2,1,0:T(8,128)(2,1)S(1)} %get-tuple-element.25.refs_0_), channel_id=1, source_target_pairs={{0,12},{2,14},{4,8},{6,10},{8,4},{10,6},{12,0},{14,2},{16,28},{18,... | collective-permute-start | bytes 491528 | tf_op jit(solution)/shard_map/ppermute | solution.py:261
  41.5 1.8 %collective-permute-done.11.refs_0_ = bf16[5,128,128]{2,1,0:T(8,128)(2,1)S(1)} collective-permute-done((bf16[5,128,128]{2,1,0:T(8,128)(2,1)S(1)}, bf16[5,128,128]{2,1,0:T(8,128)(2,1)S(1)}, u32[]{:S(2)}, u32[]{:S(2)}) %collective-permute-start.11) | collective-permute-done | bytes 163872 | tf_op jit(solution)/shard_map/ppermute | solution.py:264
  43.2 0.0 collective-permute-start.14
  43.2 0.0 collective-permute-start.13
  43.2 2.9 %collective-permute-done.10.refs_3_ = bf16[5,128,128]{2,1,0:T(8,128)(2,1)S(1)} collective-permute-done((bf16[5,128,128]{2,1,0:T(8,128)(2,1)S(1)}, bf16[5,128,128]{2,1,0:T(8,128)(2,1)S(1)}, u32[]{:S(2)}, u32[]{:S(2)}) %collective-permute-start.10) | collective-permute-done | bytes 163872 | tf_op jit(solution)/shard_map/ppermute | solution.py:261
  46.2 0.6 collective-permute-start.12
  46.7 0.0 collective-permute-done.9.refs_2_
  46.7 3.5 %collective-permute-done.8.refs_1_ = bf16[5,128,128]{2,1,0:T(8,128)(2,1)S(1)} collective-permute-done((bf16[5,128,128]{2,1,0:T(8,128)(2,1)S(1)}, bf16[5,128,128]{2,1,0:T(8,128)(2,1)S(1)}, u32[]{:S(2)}, u32[]{:S(2)}) %collective-permute-start.8) | collective-permute-done | bytes 163872 | tf_op jit(solution)/shard_map/ppermute | solution.py:261
  50.3 0.1 collective-permute-start.15
  50.3 1.7 %collective-permute-done.14.refs_3_ = bf16[5,128,128]{2,1,0:T(8,128)(2,1)S(1)} collective-permute-done((bf16[5,128,128]{2,1,0:T(8,128)(2,1)S(1)}, bf16[5,128,128]{2,1,0:T(8,128)(2,1)S(1)}, u32[]{:S(2)}, u32[]{:S(2)}) %collective-permute-start.14) | collective-permute-done | bytes 163872 | tf_op jit(solution)/shard_map/ppermute | solution.py:261
  52.1 0.0 collective-permute-done.13.refs_2_
  52.1 2.3 %collective-permute-done.12.refs_1_ = bf16[5,128,128]{2,1,0:T(8,128)(2,1)S(1)} collective-permute-done((bf16[5,128,128]{2,1,0:T(8,128)(2,1)S(1)}, bf16[5,128,128]{2,1,0:T(8,128)(2,1)S(1)}, u32[]{:S(2)}, u32[]{:S(2)}) %collective-permute-start.12) | collective-permute-done | bytes 163872 | tf_op jit(solution)/shard_map/ppermute | solution.py:261
  54.4 0.1 collective-permute-start.16
  54.5 0.0 collective-permute-done.15.rest_2_
  54.5 2.8 %second_layer.3.sum_ref = f32[10,128,128]{2,1,0:T(8,128)S(1)} custom-call(s32[10,44]{1,0:T(8,128)S(1)} %get-tuple-element.20.rest_0_.list_ref, s32[2,10]{1,0:T(2,128)S(1)} %get-tuple-element.18.rest_2_.totals_ref, bf16[10,36,128,128]{3,2,1,0:T(8,128)(2,1)S(1)} %get-tuple-element.22.coef_ref, bf16[20,128,128]{2,1,0:T(8,128)(2,1)S(1)} %own_joined.2.rest_0_, ...), custom_call_target="tpu_custom_call" | custom-call | flops 1509949440 | bytes 11796480 | tf_op jit(solution)/shard_map/second_layer/pallas_call | solution.py:319
  57.3 0.0 collective-permute-done.16.source_ref
  57.3 1.5 %second_layer.5.mine_ref = bf16[5,128,128]{2,1,0:T(8,128)(2,1)S(1)} custom-call(s32[10,44]{1,0:T(8,128)S(1)} %get-tuple-element.17.rest_1_.list_ref, s32[2,10]{1,0:T(2,128)S(1)} %get-tuple-element.18.rest_2_.totals_ref, bf16[10,36,128,128]{3,2,1,0:T(8,128)(2,1)S(1)} %get-tuple-element.22.coef_ref, f32[10,128,128]{2,1,0:T(8,128)S(1)} %second_layer.3.sum_ref, ...), custom_call_target="tpu_custom_call" | custom-call | flops 754974720 | bytes 5898240 | tf_op jit(solution)/shard_map/second_layer/pallas_call | solution.py:319
  58.8 1.7 %collective-permute-start.18 = (bf16[5,128,128]{2,1,0:T(8,128)(2,1)S(1)}, bf16[5,128,128]{2,1,0:T(8,128)(2,1)S(1)}, u32[]{:S(2)}, u32[]{:S(2)}) collective-permute-start(bf16[5,128,128]{2,1,0:T(8,128)(2,1)S(1)} %second_layer.5.mine_ref), channel_id=1, source_target_pairs={{0,1},{1,0},{2,3},{3,2},{4,5},{5,4},{6,7},{7,6},{8,9},{9,8},{10,11... | collective-permute-start | bytes 491528 | tf_op jit(solution)/shard_map/ppermute | solution.py:264
  60.5 1.1 %second_layer.4.mine_ref = bf16[5,128,128]{2,1,0:T(8,128)(2,1)S(1)} custom-call(s32[10,44]{1,0:T(8,128)S(1)} %get-tuple-element.17.rest_1_.list_ref, s32[2,10]{1,0:T(2,128)S(1)} %get-tuple-element.18.rest_2_.totals_ref, bf16[10,36,128,128]{3,2,1,0:T(8,128)(2,1)S(1)} %get-tuple-element.22.coef_ref, f32[10,128,128]{2,1,0:T(8,128)S(1)} %second_layer.3.sum_ref, ...), custom_call_target="tpu_custom_call" | custom-call | flops 754974720 | bytes 5898240 | tf_op jit(solution)/shard_map/second_layer/pallas_call | solution.py:319
  61.6 0.4 collective-permute-start.17
  62.0 3.4 %collective-permute-done.18.other_ref = bf16[5,128,128]{2,1,0:T(8,128)(2,1)S(1)} collective-permute-done((bf16[5,128,128]{2,1,0:T(8,128)(2,1)S(1)}, bf16[5,128,128]{2,1,0:T(8,128)(2,1)S(1)}, u32[]{:S(2)}, u32[]{:S(2)}) %collective-permute-start.18) | collective-permute-done | bytes 163872 | tf_op jit(solution)/shard_map/ppermute | solution.py:264
  65.5 0.7 %result.2.rest_0_ = bf16[10,128,128]{2,1,0:T(8,128)(2,1)} custom-call(bf16[5,128,128]{2,1,0:T(8,128)(2,1)S(1)} %second_layer.5.mine_ref, bf16[5,128,128]{2,1,0:T(8,128)(2,1)S(1)} %collective-permute-done.18.other_ref), custom_call_target="tpu_custom_call" | custom-call | tf_op jit(solution)/shard_map/result/pallas_call | solution.py:388
  66.2 2.8 %collective-permute-done.17.other_ref = bf16[5,128,128]{2,1,0:T(8,128)(2,1)S(1)} collective-permute-done((bf16[5,128,128]{2,1,0:T(8,128)(2,1)S(1)}, bf16[5,128,128]{2,1,0:T(8,128)(2,1)S(1)}, u32[]{:S(2)}, u32[]{:S(2)}) %collective-permute-start.17) | collective-permute-done | bytes 163872 | tf_op jit(solution)/shard_map/ppermute | solution.py:264
  69.0 0.7 %result.3 = bf16[10,128,128]{2,1,0:T(8,128)(2,1)} custom-call(bf16[5,128,128]{2,1,0:T(8,128)(2,1)S(1)} %second_layer.4.mine_ref, bf16[5,128,128]{2,1,0:T(8,128)(2,1)S(1)} %collective-permute-done.17.other_ref, bf16[10,128,128]{2,1,0:T(8,128)(2,1)} %result.2.rest_0_), custom_call_target="tpu_custom_call", output_to_operand_aliasing={{}: (2, {})} | custom-call | tf_op jit(solution)/shard_map/result/pallas_call | solution.py:388
  (7 shorter events, 0.2 us)
Async XLA Ops:
  0.0 15.0 %copy-start.2 = (s32[10,36]{1,0:T(8,128)S(1)}, s32[10,36]{1,0:T(8,128)}, u32[]{:S(2)}) copy-start(s32[10,36]{1,0:T(8,128)} %cols_ref.5) | copy-start | bytes 4324
  0.0 15.0 %copy-start.3 = (s32[10,1]{0,1:T(1,128)S(1)}, s32[10,1]{0,1:T(1,128)}, u32[]{:S(2)}) copy-start(s32[10,1]{0,1:T(1,128)} %param.7) | copy-start | bytes 124
  0.0 20.1 %copy-start.1 = (f32[10240]{0:T(1024)S(1)}, f32[10240]{0:T(1024)}, u32[]{:S(2)}) copy-start(f32[10240]{0:T(1024)} %param.9) | copy-start | bytes 122884
  0.0 20.1 %copy-start = (bf16[10240,128]{1,0:T(8,128)(2,1)S(1)}, bf16[10240,128]{1,0:T(8,128)(2,1)}, u32[]{:S(2)}) copy-start(bf16[10240,128]{1,0:T(8,128)(2,1)} %param.8) | copy-start | bytes 7864324
  3.9 5.2 %collective-permute-start.1 = (bf16[80,128]{1,0:T(8,128)(2,1)S(1)}, bf16[80,128]{1,0:T(8,128)(2,1)S(1)}, u32[]{:S(2)}, u32[]{:S(2)}) collective-permute-start(bf16[80,128]{1,0:T(8,128)(2,1)S(1)} %convert_element_type.36), channel_id=1, source_target_pairs={{0,4},{2,6},{4,0},{6,2},{8,12},{10,14},{12,8},{14,10},{16,20},{18,... | collective-permute-start | bytes 61448 | tf_op jit(solution)/shard_map/ppermute | solution.py:261
  7.3 1.8 %collective-permute-start = (bf16[80,128]{1,0:T(8,128)(2,1)S(1)}, bf16[80,128]{1,0:T(8,128)(2,1)S(1)}, u32[]{:S(2)}, u32[]{:S(2)}) collective-permute-start(bf16[80,128]{1,0:T(8,128)(2,1)S(1)} %convert_element_type.36), channel_id=1, source_target_pairs={{0,2},{2,0},{4,6},{6,4},{8,10},{10,8},{12,14},{14,12},{16,18},{18,... | collective-permute-start | bytes 61448 | tf_op jit(solution)/shard_map/ppermute | solution.py:261
  7.3 3.2 %collective-permute-start.2 = (bf16[80,128]{1,0:T(8,128)(2,1)S(1)}, bf16[80,128]{1,0:T(8,128)(2,1)S(1)}, u32[]{:S(2)}, u32[]{:S(2)}) collective-permute-start(bf16[80,128]{1,0:T(8,128)(2,1)S(1)} %convert_element_type.36), channel_id=1, source_target_pairs={{0,6},{2,4},{4,2},{6,0},{8,14},{10,12},{12,10},{14,8},{16,22},{18,... | collective-permute-start | bytes 61448 | tf_op jit(solution)/shard_map/ppermute | solution.py:261
  10.6 7.4 %collective-permute-start.5 = (bf16[80,128]{1,0:T(8,128)(2,1)S(1)}, bf16[80,128]{1,0:T(8,128)(2,1)S(1)}, u32[]{:S(2)}, u32[]{:S(2)}) collective-permute-start(bf16[80,128]{1,0:T(8,128)(2,1)S(1)} %add_convert_fusion.1._), channel_id=1, source_target_pairs={{0,8},{2,10},{4,12},{6,14},{8,0},{10,2},{12,4},{14,6},{16,24},{18,... | collective-permute-start | bytes 61448 | tf_op jit(solution)/shard_map/ppermute | solution.py:261
  11.2 6.7 %collective-permute-start.4 = (bf16[80,128]{1,0:T(8,128)(2,1)S(1)}, bf16[80,128]{1,0:T(8,128)(2,1)S(1)}, u32[]{:S(2)}, u32[]{:S(2)}) collective-permute-start(bf16[80,128]{1,0:T(8,128)(2,1)S(1)} %add_convert_fusion.1._), channel_id=1, source_target_pairs={{0,16},{2,18},{4,20},{6,22},{8,24},{10,26},{12,28},{14,30},{16,0},... | collective-permute-start | bytes 61448 | tf_op jit(solution)/shard_map/ppermute | solution.py:261
  14.5 5.6 %collective-permute-start.3 = (bf16[80,128]{1,0:T(8,128)(2,1)S(1)}, bf16[80,128]{1,0:T(8,128)(2,1)S(1)}, u32[]{:S(2)}, u32[]{:S(2)}) collective-permute-start(bf16[80,128]{1,0:T(8,128)(2,1)S(1)} %add_convert_fusion.1._), channel_id=1, source_target_pairs={{0,24},{2,26},{4,28},{6,30},{8,16},{10,18},{12,20},{14,22},{16,8},... | collective-permute-start | bytes 61448 | tf_op jit(solution)/shard_map/ppermute | solution.py:261
  22.1 6.1 %collective-permute-start.6 = (bf16[5,128,128]{2,1,0:T(8,128)(2,1)S(1)}, bf16[5,128,128]{2,1,0:T(8,128)(2,1)S(1)}, u32[]{:S(2)}, u32[]{:S(2)}) collective-permute-start(bf16[5,128,128]{2,1,0:T(8,128)(2,1)S(1)} %get-tuple-element.24), channel_id=1, source_target_pairs={{0,1},{1,0},{2,3},{3,2},{4,5},{5,4},{6,7},{7,6},{8,9},{9,8},{10,11... | collective-permute-start | bytes 491528 | tf_op jit(solution)/shard_map/ppermute | solution.py:264
  28.2 9.6 %collective-permute-start.7 = (bf16[5,128,128]{2,1,0:T(8,128)(2,1)S(1)}, bf16[5,128,128]{2,1,0:T(8,128)(2,1)S(1)}, u32[]{:S(2)}, u32[]{:S(2)}) collective-permute-start(bf16[5,128,128]{2,1,0:T(8,128)(2,1)S(1)} %add_convert_fusion.own_ref), channel_id=1, source_target_pairs={{0,16},{2,18},{4,20},{6,22},{8,24},{10,26},{12,28},{14,30},{16,0},... | collective-permute-start | bytes 491528 | tf_op jit(solution)/shard_map/ppermute | solution.py:261
  37.8 5.4 %collective-permute-start.11 = (bf16[5,128,128]{2,1,0:T(8,128)(2,1)S(1)}, bf16[5,128,128]{2,1,0:T(8,128)(2,1)S(1)}, u32[]{:S(2)}, u32[]{:S(2)}) collective-permute-start(bf16[5,128,128]{2,1,0:T(8,128)(2,1)S(1)} %get-tuple-element.26), channel_id=1, source_target_pairs={{0,1},{1,0},{2,3},{3,2},{4,5},{5,4},{6,7},{7,6},{8,9},{9,8},{10,11... | collective-permute-start | bytes 491528 | tf_op jit(solution)/shard_map/ppermute | solution.py:264
  37.9 8.2 %collective-permute-start.10 = (bf16[5,128,128]{2,1,0:T(8,128)(2,1)S(1)}, bf16[5,128,128]{2,1,0:T(8,128)(2,1)S(1)}, u32[]{:S(2)}, u32[]{:S(2)}) collective-permute-start(bf16[5,128,128]{2,1,0:T(8,128)(2,1)S(1)} %get-tuple-element.25.refs_0_), channel_id=1, source_target_pairs={{0,4},{2,6},{4,0},{6,2},{8,12},{10,14},{12,8},{14,10},{16,20},{18,... | collective-permute-start | bytes 491528 | tf_op jit(solution)/shard_map/ppermute | solution.py:261
  38.0 8.7 %collective-permute-start.9 = (bf16[5,128,128]{2,1,0:T(8,128)(2,1)S(1)}, bf16[5,128,128]{2,1,0:T(8,128)(2,1)S(1)}, u32[]{:S(2)}, u32[]{:S(2)}) collective-permute-start(bf16[5,128,128]{2,1,0:T(8,128)(2,1)S(1)} %get-tuple-element.25.refs_0_), channel_id=1, source_target_pairs={{0,8},{2,10},{4,12},{6,14},{8,0},{10,2},{12,4},{14,6},{16,24},{18,... | collective-permute-start | bytes 491528 | tf_op jit(solution)/shard_map/ppermute | solution.py:261
  38.3 11.9 %collective-permute-start.8 = (bf16[5,128,128]{2,1,0:T(8,128)(2,1)S(1)}, bf16[5,128,128]{2,1,0:T(8,128)(2,1)S(1)}, u32[]{:S(2)}, u32[]{:S(2)}) collective-permute-start(bf16[5,128,128]{2,1,0:T(8,128)(2,1)S(1)} %get-tuple-element.25.refs_0_), channel_id=1, source_target_pairs={{0,12},{2,14},{4,8},{6,10},{8,4},{10,6},{12,0},{14,2},{16,28},{18,... | collective-permute-start | bytes 491528 | tf_op jit(solution)/shard_map/ppermute | solution.py:261
  43.2 8.9 %collective-permute-start.14 = (bf16[5,128,128]{2,1,0:T(8,128)(2,1)S(1)}, bf16[5,128,128]{2,1,0:T(8,128)(2,1)S(1)}, u32[]{:S(2)}, u32[]{:S(2)}) collective-permute-start(bf16[5,128,128]{2,1,0:T(8,128)(2,1)S(1)} %collective-permute-done.11.refs_0_), channel_id=1, source_target_pairs={{0,4},{2,6},{4,0},{6,2},{8,12},{10,14},{12,8},{14,10},{16,20},{18,... | collective-permute-start | bytes 491528 | tf_op jit(solution)/shard_map/ppermute | solution.py:261
  43.2 8.9 %collective-permute-start.13 = (bf16[5,128,128]{2,1,0:T(8,128)(2,1)S(1)}, bf16[5,128,128]{2,1,0:T(8,128)(2,1)S(1)}, u32[]{:S(2)}, u32[]{:S(2)}) collective-permute-start(bf16[5,128,128]{2,1,0:T(8,128)(2,1)S(1)} %collective-permute-done.11.refs_0_), channel_id=1, source_target_pairs={{0,8},{2,10},{4,12},{6,14},{8,0},{10,2},{12,4},{14,6},{16,24},{18,... | collective-permute-start | bytes 491528 | tf_op jit(solution)/shard_map/ppermute | solution.py:261
  46.2 8.2 %collective-permute-start.12 = (bf16[5,128,128]{2,1,0:T(8,128)(2,1)S(1)}, bf16[5,128,128]{2,1,0:T(8,128)(2,1)S(1)}, u32[]{:S(2)}, u32[]{:S(2)}) collective-permute-start(bf16[5,128,128]{2,1,0:T(8,128)(2,1)S(1)} %collective-permute-done.11.refs_0_), channel_id=1, source_target_pairs={{0,12},{2,14},{4,8},{6,10},{8,4},{10,6},{12,0},{14,2},{16,28},{18,... | collective-permute-start | bytes 491528 | tf_op jit(solution)/shard_map/ppermute | solution.py:261
  50.3 4.3 %collective-permute-start.15 = (bf16[20,128,128]{2,1,0:T(8,128)(2,1)S(1)}, bf16[20,128,128]{2,1,0:T(8,128)(2,1)S(1)}, u32[]{:S(2)}, u32[]{:S(2)}) collective-permute-start(bf16[20,128,128]{2,1,0:T(8,128)(2,1)S(1)} %own_joined.2.rest_0_), channel_id=1, source_target_pairs={{0,2},{2,0},{4,6},{6,4},{8,10},{10,8},{12,14},{14,12},{16,18},{18,... | collective-permute-start | bytes 1966088 | tf_op jit(solution)/shard_map/ppermute | solution.py:261
  54.4 2.9 %collective-permute-start.16 = (bf16[20,128,128]{2,1,0:T(8,128)(2,1)S(1)}, bf16[20,128,128]{2,1,0:T(8,128)(2,1)S(1)}, u32[]{:S(2)}, u32[]{:S(2)}) collective-permute-start(bf16[20,128,128]{2,1,0:T(8,128)(2,1)S(1)} %own_joined.3.rest_1_), channel_id=1, source_target_pairs={{0,2},{2,0},{4,6},{6,4},{8,10},{10,8},{12,14},{14,12},{16,18},{18,... | collective-permute-start | bytes 1966088 | tf_op jit(solution)/shard_map/ppermute | solution.py:261
  58.8 6.7 %collective-permute-start.18 = (bf16[5,128,128]{2,1,0:T(8,128)(2,1)S(1)}, bf16[5,128,128]{2,1,0:T(8,128)(2,1)S(1)}, u32[]{:S(2)}, u32[]{:S(2)}) collective-permute-start(bf16[5,128,128]{2,1,0:T(8,128)(2,1)S(1)} %second_layer.5.mine_ref), channel_id=1, source_target_pairs={{0,1},{1,0},{2,3},{3,2},{4,5},{5,4},{6,7},{7,6},{8,9},{9,8},{10,11... | collective-permute-start | bytes 491528 | tf_op jit(solution)/shard_map/ppermute | solution.py:264
  61.6 7.4 %collective-permute-start.17 = (bf16[5,128,128]{2,1,0:T(8,128)(2,1)S(1)}, bf16[5,128,128]{2,1,0:T(8,128)(2,1)S(1)}, u32[]{:S(2)}, u32[]{:S(2)}) collective-permute-start(bf16[5,128,128]{2,1,0:T(8,128)(2,1)S(1)} %second_layer.4.mine_ref), channel_id=1, source_target_pairs={{0,1},{1,0},{2,3},{3,2},{4,5},{5,4},{6,7},{7,6},{8,9},{9,8},{10,11... | collective-permute-start | bytes 491528 | tf_op jit(solution)/shard_map/ppermute | solution.py:264

commit v13 on v10

--- a/solution.py
+++ b/solution.py
@@ -10,72 +10,70 @@
 VMEM_LIMIT = 12 * 1024 * 1024
 
 
-def divisor(slot_count, most):
-    return max(size for size in range(1, most + 1) if slot_count % size == 0)
-
-
-def chunk_total(counts_ref, b, chunk):
-    return lax.div(counts_ref[b] + (chunk - 1), chunk)
+def slot_ranges(slots):
+    first = min(12, slots)
+    return [range(first)] + ([range(first, slots)] if slots > first else [])
 
 
 def sums_kernel(cols_hbm, counts_hbm, blocks_ref, sums_ref, held_ref, acc_ref, cols_ref, counts_ref, list_sems, sems):
     rows, slots, size, _ = blocks_ref.shape
     groups = acc_ref.shape[0] - 1
-    chunk = divisor(slots, 12)
-
-    def fetch(b, k):
-        part = pl.ds(k * chunk, chunk)
-        return pltpu.make_async_copy(blocks_ref.at[b, part], held_ref.at[b, part], sems.at[b, k])
+    first, *others = slot_ranges(slots)
+
+    def fetch(b, part):
+        span = pl.ds(part.start, len(part))
+        return pltpu.make_async_copy(blocks_ref.at[b, span], held_ref.at[b, span], sems.at[b, min(part.start, 1)])
 
     counts_copy = pltpu.make_async_copy(counts_hbm, counts_ref, list_sems.at[0])
     cols_copy = pltpu.make_async_copy(cols_hbm, cols_ref, list_sems.at[1])
     counts_copy.start()
     cols_copy.start()
     for b in range(rows):
-        fetch(b, 0).start()
+        fetch(b, first).start()
     acc_ref[...] = jnp.zeros_like(acc_ref)
     counts_copy.wait()
     cols_copy.wait()
     for b in range(rows):
-        for k in range(1, slots // chunk):
-
-            @pl.when(counts_ref[b] > k * chunk)
-            def _(b=b, k=k):
-                fetch(b, k).start()
-
-    def add(b, k):
-        fetch(b, k).wait()
-        for slot in range(k * chunk, (k + 1) * chunk):
+        for part in others:
+
+            @pl.when(counts_ref[b] > part.start)
+            def _(b=b, part=part):
+                fetch(b, part).start()
+
+    def add(b, part):
+        fetch(b, part).wait()
+        for slot in part:
             col = jnp.where(slot < counts_ref[b], cols_ref[b, slot], groups)
             block = held_ref[b, slot].astype(jnp.float32)
             acc_ref[col] += jnp.sum(block.reshape(size // 8, 8, size), axis=0)
 
     for b in range(rows):
-        add(b, 0)
+        add(b, first)
     for b in range(rows):
-        for k in range(1, slots // chunk):
-
-            @pl.when(counts_ref[b] > k * chunk)
-            def _(b=b, k=k):
-                add(b, k)
+        for part in others:
+
+            @pl.when(counts_ref[b] > part.start)
+            def _(b=b, part=part):
+                add(b, part)
 
     sums_ref[...] = jnp.sum(acc_ref[:groups], axis=1)
 
 
-def multiply_rows(rows, counts_ref, chunk, start, gather, acc_ref):
-    def product(row, first):
-        left, right = zip(*[gather(row, first + u) for u in range(chunk)])
+def multiply_rows(rows, counts_ref, slots, start, gather, acc_ref):
+    first, *others = slot_ranges(slots)
+
+    def product(row, part):
+        left, right = zip(*[gather(row, slot) for slot in part])
         return jnp.dot(jnp.concatenate(left, axis=1), jnp.concatenate(right, axis=0), preferred_element_type=jnp.float32)
 
     for b, row in enumerate(rows):
-        acc_ref[b] = start(b) + product(row, 0)
+        acc_ref[b] = start(b) + product(row, first)
     for b, row in enumerate(rows):
-
-        def add(k, carry, b=b, row=row):
-            acc_ref[b] += product(row, k * chunk)
-            return carry
-
-        lax.fori_loop(1, chunk_total(counts_ref, row, chunk), add, 0)
+        for part in others:
+
+            @pl.when(counts_ref[row] > part.start)
+            def _(b=b, row=row, part=part):
+                acc_ref[b] += product(row, part)
 
 
 def first_kernel(sending, cols_ref, counts_ref, sums_ref, added_ref, demand_ref, blocks_ref, out_ref, coef_ref, inverse_ref, acc_ref):
@@ -96,7 +94,7 @@
         return coef, demand_ref[col]
 
     rows = [base + b for b in range(count)]
-    multiply_rows(rows, counts_ref, divisor(slots, 12), lambda b: 0.0, gather, acc_ref)
+    multiply_rows(rows, counts_ref, slots, lambda b: 0.0, gather, acc_ref)
     out_ref[...] = acc_ref[...].astype(out_ref.dtype)
 
 
@@ -107,7 +105,7 @@
         return coef_ref[row, slot], source_ref[place(cols_ref[row, slot])]
 
     rows = [first_row + b for b in range(out_ref.shape[0])]
-    multiply_rows(rows, counts_ref, divisor(slots, 12), start, gather, acc_ref)
+    multiply_rows(rows, counts_ref, slots, start, gather, acc_ref)
     out_ref[...] = acc_ref[...].astype(out_ref.dtype)
 
 
@@ -118,9 +116,8 @@
 
 
 GATHERED = (
-    ((0, 0, 0), (0, 1, 0), (1, 0, 0), (1, 1, 0)),
-    ((0, 0, 1), (0, 1, 1), (1, 0, 1)),
-    ((1, 1, 1),),
+    ((0, 0, 0), (1, 0, 0), (1, 1, 0), (0, 1, 0)),
+    ((0, 0, 1), (0, 1, 1), (1, 0, 1), (1, 1, 1)),
 )
 
 
@@ -223,7 +220,7 @@
             pltpu.SMEM(slot_cols.shape, jnp.int32),
             pltpu.SMEM(counts.shape, jnp.int32),
             pltpu.SemaphoreType.DMA((2,)),
-            pltpu.SemaphoreType.DMA((rows, slots // divisor(slots, 12))),
+            pltpu.SemaphoreType.DMA((rows, 2)),
         ],
         compiler_params=PARAMS,
         cost_estimate=cost(0, 4 * rows * size * size * slots),
@@ -321,9 +318,9 @@
         )(*pieces)
 
     away = swap(away)
-    home_y, home_z = flip(home, 2), flip(home, 4)
-    away_y, away_z = flip(away, 2), flip(away, 4)
-    gathered = [join([home, home_y, home_z, flip(home_z, 2)]), join([away, away_y, away_z]), flip(away_y, 4)]
+    near_home = join([home, flip(home, 4), flip(home, 6), flip(home, 2)])
+    near_away = join([away, flip(away, 2), flip(away, 4), flip(away, 6)])
+    gathered = [near_home, near_away]
     pieces = gathered + [flip(part, 1) for part in gathered]
 
     part_a, source = second_call(functools.partial(second_part_kernel, 0), half, coefs, own, pieces, True)

time: 70.6 us -> 69.1 us (0.979)
  waiting for transfers between devices: 40.9 us -> 35 us
  Pallas kernels: 11.2 us -> 15.4 us
    ppermute x16 -> x15, waiting for transfers between devices: 32.2 us -> 27.6 us  [flip(): return lax.ppermute(array, 'row', [(i, i ^ mask) for i in range(n_row)])]
    pallas_call x2, Pallas kernels: 3.86 us -> 5.44 us  [first_layer(): pl.pallas_call(functools.partial(first_kernel, sending), name='first_laye...]
    pallas_call x1, Pallas kernels: 2.78 us -> 4.19 us  [body(): pl.pallas_call(sums_kernel, name='column_sums', out_shape=(jax.ShapeDtype...]
    ppermute x4, waiting for transfers between devices: 8.69 us -> 7.38 us  [swap(): return lax.ppermute(array, 'col', [(0, 1), (1, 0)])]
    pallas_call x2, Pallas kernels: 3 us -> 4.24 us  [second_call(): pl.pallas_call(kernel, name='second_layer', out_shape=(out, jax.ShapeDtyp...]
    ppermute x4, starting transfers between devices: 5.42 us -> 4.68 us  [swap(): return lax.ppermute(array, 'col', [(0, 1), (1, 0)])]
    ppermute x16 -> x15, starting transfers between devices: 13.5 us -> 13.8 us  [flip(): return lax.ppermute(array, 'row', [(i, i ^ mask) for i in range(n_row)])]
  transfers between devices with their start and end apart: 20 -> 19, of which waited for: 14 -> 14; matrix products, arithmetic and copies ran while one was open for 0% -> 0% of each run, Pallas kernels for 6% -> 8%
where the time goes in v13:
time: 69.1 us; the launch traced here: 69.3 us
  waiting for transfers between devices  35 us (51%)
  starting transfers between devices  18.5 us (27%)
  Pallas kernels  15.4 us (22%)
    ppermute x15, waiting for transfers between devices, flip(): return lax.ppermute(array, 'row', [(i, i ^ mask) for i in range(n_row)])  27.6 us
    ppermute x15, starting transfers between devices, flip(): return lax.ppermute(array, 'row', [(i, i ^ mask) for i in range(n_row)])  13.8 us
    ppermute x4, waiting for transfers between devices, swap(): return lax.ppermute(array, 'col', [(0, 1), (1, 0)])  7.38 us
    pallas_call x2, Pallas kernels, first_layer(): pl.pallas_call(functools.partial(first_kernel, sending), name='first_laye...  5.44 us
    ppermute x4, starting transfers between devices, swap(): return lax.ppermute(array, 'col', [(0, 1), (1, 0)])  4.68 us
    pallas_call x2, Pallas kernels, second_call(): pl.pallas_call(kernel, name='second_layer', out_shape=(out, jax.ShapeDtyp...  4.24 us
    pallas_call x1, Pallas kernels, body(): pl.pallas_call(sums_kernel, name='column_sums', out_shape=(jax.ShapeDtype...  4.19 us
    pallas_call x2, Pallas kernels, result(): pl.pallas_call(functools.partial(result_kernel, first_row), name='result'...  1.43 us
  transfers between devices with their start and end apart: 19, of which 14 were waited for; matrix products, arithmetic and copies ran while one was open for 0% of the time, Pallas kernels for 8%

profile of v13, /device:TPU:0, one launch (start us, length us, event | category | flops | bytes accessed | tf_op | source)
XLA Modules:
  0.0 69.3 jit_solution(1041334218522584862)
XLA Ops:
  0.0 0.0 copy-start.1
  0.0 0.0 copy-start.3
  0.0 0.0 copy-start.2
  0.0 0.0 copy-start
  0.0 4.2 %column_sums.1 = (f32[80,128]{1,0:T(8,128)S(1)}, bf16[10,36,128,128]{3,2,1,0:T(8,128)(2,1)S(1)}) custom-call(s32[10,36]{1,0:T(8,128)} %cols_ref.7, s32[10]{0:T(128)} %bitcast.8, bf16[10,36,128,128]{3,2,1,0:T(8,128)(2,1)} %blocks_ref.1), custom_call_target="tpu_custom_call" | custom-call | bytes 23592960 | tf_op jit(solution)/shard_map/column_sums/pallas_call | solution.py:209
  4.2 2.8 %collective-permute-start.1 = (bf16[80,128]{1,0:T(8,128)(2,1)S(1)}, bf16[80,128]{1,0:T(8,128)(2,1)S(1)}, u32[]{:S(2)}, u32[]{:S(2)}) collective-permute-start(bf16[80,128]{1,0:T(8,128)(2,1)S(1)} %convert_element_type.36), channel_id=1, source_target_pairs={{0,4},{2,6},{4,0},{6,2},{8,12},{10,14},{12,8},{14,10},{16,20},{18,... | collective-permute-start | bytes 61448 | tf_op jit(solution)/shard_map/ppermute | solution.py:230
  7.0 0.0 collective-permute-start
  7.0 0.2 collective-permute-start.2
  7.2 1.6 %collective-permute-done.1 = bf16[80,128]{1,0:T(8,128)(2,1)S(1)} collective-permute-done((bf16[80,128]{1,0:T(8,128)(2,1)S(1)}, bf16[80,128]{1,0:T(8,128)(2,1)S(1)}, u32[]{:S(2)}, u32[]{:S(2)}) %collective-permute-start.1) | collective-permute-done | bytes 20512 | tf_op jit(solution)/shard_map/ppermute | solution.py:230
  8.8 0.0 collective-permute-done
  8.8 1.4 %collective-permute-done.2 = bf16[80,128]{1,0:T(8,128)(2,1)S(1)} collective-permute-done((bf16[80,128]{1,0:T(8,128)(2,1)S(1)}, bf16[80,128]{1,0:T(8,128)(2,1)S(1)}, u32[]{:S(2)}, u32[]{:S(2)}) %collective-permute-start.2) | collective-permute-done | bytes 20512 | tf_op jit(solution)/shard_map/ppermute | solution.py:230
  10.2 3.5 %collective-permute-start.5 = (bf16[80,128]{1,0:T(8,128)(2,1)S(1)}, bf16[80,128]{1,0:T(8,128)(2,1)S(1)}, u32[]{:S(2)}, u32[]{:S(2)}) collective-permute-start(bf16[80,128]{1,0:T(8,128)(2,1)S(1)} %add_convert_fusion.1), channel_id=1, source_target_pairs={{0,24},{2,26},{4,28},{6,30},{8,16},{10,18},{12,20},{14,22},{16,8},... | collective-permute-start | bytes 61448 | tf_op jit(solution)/shard_map/ppermute | solution.py:230
  13.7 0.0 collective-permute-start.4
  13.8 1.0 %collective-permute-start.3 = (bf16[80,128]{1,0:T(8,128)(2,1)S(1)}, bf16[80,128]{1,0:T(8,128)(2,1)S(1)}, u32[]{:S(2)}, u32[]{:S(2)}) collective-permute-start(bf16[80,128]{1,0:T(8,128)(2,1)S(1)} %add_convert_fusion.1), channel_id=1, source_target_pairs={{0,8},{2,10},{4,12},{6,14},{8,0},{10,2},{12,4},{14,6},{16,24},{18,... | collective-permute-start | bytes 61448 | tf_op jit(solution)/shard_map/ppermute | solution.py:230
  14.7 1.2 %collective-permute-done.5 = bf16[80,128]{1,0:T(8,128)(2,1)S(1)} collective-permute-done((bf16[80,128]{1,0:T(8,128)(2,1)S(1)}, bf16[80,128]{1,0:T(8,128)(2,1)S(1)}, u32[]{:S(2)}, u32[]{:S(2)}) %collective-permute-start.5) | collective-permute-done | bytes 20512 | tf_op jit(solution)/shard_map/ppermute | solution.py:230
  15.9 2.5 %collective-permute-done.4 = bf16[80,128]{1,0:T(8,128)(2,1)S(1)} collective-permute-done((bf16[80,128]{1,0:T(8,128)(2,1)S(1)}, bf16[80,128]{1,0:T(8,128)(2,1)S(1)}, u32[]{:S(2)}, u32[]{:S(2)}) %collective-permute-start.4) | collective-permute-done | bytes 20512 | tf_op jit(solution)/shard_map/ppermute | solution.py:230
  18.4 0.0 collective-permute-done.3
  18.5 0.0 copy-done.1
  18.5 0.0 copy-done.3
  18.5 0.0 copy-done.2
  18.5 0.0 copy-done
  18.5 2.5 %first_layer.2 = (bf16[5,128,128]{2,1,0:T(8,128)(2,1)S(1)}, bf16[10,36,128,128]{3,2,1,0:T(8,128)(2,1)S(1)}) custom-call(s32[10,36]{1,0:T(8,128)S(1)} %copy-done.1, s32[10]{0:T(128)S(1)} %bitcast.9, f32[80,128]{1,0:T(8,128)S(1)} %convert_add_fusion.sums_ref, f32[80,128]{1,0:T(8,128)S(1)} %bitcast.6, ...), custom_call_target="tpu_custom_call", output_to_operand_aliasing={{1}: (5, {})} | custom-call | flops 754974720 | bytes 5898240 | tf_op jit(solution)/shard_map/first_layer/pallas_call | solution.py:247
  21.0 2.1 %collective-permute-start.6 = (bf16[5,128,128]{2,1,0:T(8,128)(2,1)S(1)}, bf16[5,128,128]{2,1,0:T(8,128)(2,1)S(1)}, u32[]{:S(2)}, u32[]{:S(2)}) collective-permute-start(bf16[5,128,128]{2,1,0:T(8,128)(2,1)S(1)} %get-tuple-element.20), channel_id=1, source_target_pairs={{0,1},{1,0},{2,3},{3,2},{4,5},{5,4},{6,7},{7,6},{8,9},{9,8},{10,11... | collective-permute-start | bytes 491528 | tf_op jit(solution)/shard_map/ppermute | solution.py:233
  23.0 3.0 %first_layer.3 = (f32[5,128,128]{2,1,0:T(8,128)S(1)}, bf16[10,36,128,128]{3,2,1,0:T(8,128)(2,1)S(1)}) custom-call(s32[10,36]{1,0:T(8,128)S(1)} %copy-done.1, s32[10]{0:T(128)S(1)} %bitcast.10, f32[80,128]{1,0:T(8,128)S(1)} %convert_add_fusion.sums_ref, f32[80,128]{1,0:T(8,128)S(1)} %bitcast.7, ...), custom_call_target="tpu_custom_call", output_to_operand_aliasing={{1}: (5, {})} | custom-call | flops 754974720 | bytes 5898240 | tf_op jit(solution)/shard_map/first_layer/pallas_call | solution.py:247
  26.0 0.3 collective-permute-done.6
  26.4 2.7 %collective-permute-start.7 = (bf16[5,128,128]{2,1,0:T(8,128)(2,1)S(1)}, bf16[5,128,128]{2,1,0:T(8,128)(2,1)S(1)}, u32[]{:S(2)}, u32[]{:S(2)}) collective-permute-start(bf16[5,128,128]{2,1,0:T(8,128)(2,1)S(1)} %add_convert_fusion.own_ref), channel_id=1, source_target_pairs={{0,16},{2,18},{4,20},{6,22},{8,24},{10,26},{12,28},{14,30},{16,0},... | collective-permute-start | bytes 491528 | tf_op jit(solution)/shard_map/ppermute | solution.py:230
  29.1 7.1 %collective-permute-done.7.crossed_ref = bf16[5,128,128]{2,1,0:T(8,128)(2,1)S(1)} collective-permute-done((bf16[5,128,128]{2,1,0:T(8,128)(2,1)S(1)}, bf16[5,128,128]{2,1,0:T(8,128)(2,1)S(1)}, u32[]{:S(2)}, u32[]{:S(2)}) %collective-permute-start.7) | collective-permute-done | bytes 163872 | tf_op jit(solution)/shard_map/ppermute | solution.py:230
  36.2 0.4 collective-permute-start.11
  36.7 0.0 collective-permute-start.10
  36.7 1.0 %collective-permute-start.9 = (bf16[5,128,128]{2,1,0:T(8,128)(2,1)S(1)}, bf16[5,128,128]{2,1,0:T(8,128)(2,1)S(1)}, u32[]{:S(2)}, u32[]{:S(2)}) collective-permute-start(bf16[5,128,128]{2,1,0:T(8,128)(2,1)S(1)} %get-tuple-element.21.refs_0_), channel_id=1, source_target_pairs={{0,12},{2,14},{4,8},{6,10},{8,4},{10,6},{12,0},{14,2},{16,28},{18,... | collective-permute-start | bytes 491528 | tf_op jit(solution)/shard_map/ppermute | solution.py:230
  37.7 2.5 %collective-permute-start.8 = (bf16[5,128,128]{2,1,0:T(8,128)(2,1)S(1)}, bf16[5,128,128]{2,1,0:T(8,128)(2,1)S(1)}, u32[]{:S(2)}, u32[]{:S(2)}) collective-permute-start(bf16[5,128,128]{2,1,0:T(8,128)(2,1)S(1)} %get-tuple-element.21.refs_0_), channel_id=1, source_target_pairs={{0,8},{2,10},{4,12},{6,14},{8,0},{10,2},{12,4},{14,6},{16,24},{18,... | collective-permute-start | bytes 491528 | tf_op jit(solution)/shard_map/ppermute | solution.py:230
  40.2 2.3 %collective-permute-done.11.refs_0_ = bf16[5,128,128]{2,1,0:T(8,128)(2,1)S(1)} collective-permute-done((bf16[5,128,128]{2,1,0:T(8,128)(2,1)S(1)}, bf16[5,128,128]{2,1,0:T(8,128)(2,1)S(1)}, u32[]{:S(2)}, u32[]{:S(2)}) %collective-permute-start.11) | collective-permute-done | bytes 163872 | tf_op jit(solution)/shard_map/ppermute | solution.py:233
  42.4 0.0 collective-permute-start.14
  42.4 0.0 collective-permute-start.13
  42.4 3.7 %collective-permute-done.10.refs_3_ = bf16[5,128,128]{2,1,0:T(8,128)(2,1)S(1)} collective-permute-done((bf16[5,128,128]{2,1,0:T(8,128)(2,1)S(1)}, bf16[5,128,128]{2,1,0:T(8,128)(2,1)S(1)}, u32[]{:S(2)}, u32[]{:S(2)}) %collective-permute-start.10) | collective-permute-done | bytes 163872 | tf_op jit(solution)/shard_map/ppermute | solution.py:230
  46.1 0.0 collective-permute-start.12
  46.1 0.0 collective-permute-done.9.refs_2_
  46.1 2.7 %collective-permute-done.8.refs_1_ = bf16[5,128,128]{2,1,0:T(8,128)(2,1)S(1)} collective-permute-done((bf16[5,128,128]{2,1,0:T(8,128)(2,1)S(1)}, bf16[5,128,128]{2,1,0:T(8,128)(2,1)S(1)}, u32[]{:S(2)}, u32[]{:S(2)}) %collective-permute-start.8) | collective-permute-done | bytes 163872 | tf_op jit(solution)/shard_map/ppermute | solution.py:230
  48.8 0.1 collective-permute-start.15
  48.9 2.8 %collective-permute-done.14.refs_3_ = bf16[5,128,128]{2,1,0:T(8,128)(2,1)S(1)} collective-permute-done((bf16[5,128,128]{2,1,0:T(8,128)(2,1)S(1)}, bf16[5,128,128]{2,1,0:T(8,128)(2,1)S(1)}, u32[]{:S(2)}, u32[]{:S(2)}) %collective-permute-start.14) | collective-permute-done | bytes 163872 | tf_op jit(solution)/shard_map/ppermute | solution.py:230
  51.7 2.5 %collective-permute-done.13.refs_2_ = bf16[5,128,128]{2,1,0:T(8,128)(2,1)S(1)} collective-permute-done((bf16[5,128,128]{2,1,0:T(8,128)(2,1)S(1)}, bf16[5,128,128]{2,1,0:T(8,128)(2,1)S(1)}, u32[]{:S(2)}, u32[]{:S(2)}) %collective-permute-start.13) | collective-permute-done | bytes 163872 | tf_op jit(solution)/shard_map/ppermute | solution.py:230
  54.3 0.0 collective-permute-done.12.refs_1_
  54.3 0.1 collective-permute-start.16
  54.4 0.0 collective-permute-done.15.rest_2_
  54.4 2.1 %collective-permute-done.16.rest_3_ = bf16[20,128,128]{2,1,0:T(8,128)(2,1)S(1)} collective-permute-done((bf16[20,128,128]{2,1,0:T(8,128)(2,1)S(1)}, bf16[20,128,128]{2,1,0:T(8,128)(2,1)S(1)}, u32[]{:S(2)}, u32[]{:S(2)}) %collective-permute-start.16) | collective-permute-done | bytes 655392 | tf_op jit(solution)/shard_map/ppermute | solution.py:230
  56.5 2.5 %second_layer.2 = (bf16[5,128,128]{2,1,0:T(8,128)(2,1)S(1)}, bf16[80,128,128]{2,1,0:T(8,128)(2,1)S(1)}) custom-call(s32[10,36]{1,0:T(8,128)S(1)} %copy-done.1, s32[10]{0:T(128)S(1)} %bitcast.11, bf16[10,36,128,128]{3,2,1,0:T(8,128)(2,1)S(1)} %get-tuple-element.18.coef_ref, bf16[5,128,128]{2,1,0:T(8,128)(2,1)S(1)} %add_convert_fusion.own_ref, ...), custom_call_target="tpu_custom_call" | custom-call | flops 754974720 | bytes 5898240 | tf_op jit(solution)/shard_map/second_layer/pallas_call | solution.py:275
  58.9 1.7 %collective-permute-start.18 = (bf16[5,128,128]{2,1,0:T(8,128)(2,1)S(1)}, bf16[5,128,128]{2,1,0:T(8,128)(2,1)S(1)}, u32[]{:S(2)}, u32[]{:S(2)}) collective-permute-start(bf16[5,128,128]{2,1,0:T(8,128)(2,1)S(1)} %get-tuple-element.24.mine_ref), channel_id=1, source_target_pairs={{0,1},{1,0},{2,3},{3,2},{4,5},{5,4},{6,7},{7,6},{8,9},{9,8},{10,11... | collective-permute-start | bytes 491528 | tf_op jit(solution)/shard_map/ppermute | solution.py:233
  60.7 1.8 %second_layer.3.mine_ref = bf16[5,128,128]{2,1,0:T(8,128)(2,1)S(1)} custom-call(s32[10,36]{1,0:T(8,128)S(1)} %copy-done.1, s32[10]{0:T(128)S(1)} %bitcast.12, bf16[10,36,128,128]{3,2,1,0:T(8,128)(2,1)S(1)} %get-tuple-element.18.coef_ref, bf16[5,128,128]{2,1,0:T(8,128)(2,1)S(1)} %add_convert_fusion.own_ref, bf16[80,128,128]{2,1,0:T(8,128)(2,1)S(1)} %get-tuple-element.23.rest_0_), custom_call_target="tpu_custom_call" | custom-call | flops 754974720 | bytes 5898240 | tf_op jit(solution)/shard_map/second_layer/pallas_call | solution.py:275
  62.5 0.4 collective-permute-start.17
  62.9 2.4 %collective-permute-done.18.other_ref = bf16[5,128,128]{2,1,0:T(8,128)(2,1)S(1)} collective-permute-done((bf16[5,128,128]{2,1,0:T(8,128)(2,1)S(1)}, bf16[5,128,128]{2,1,0:T(8,128)(2,1)S(1)}, u32[]{:S(2)}, u32[]{:S(2)}) %collective-permute-start.18) | collective-permute-done | bytes 163872 | tf_op jit(solution)/shard_map/ppermute | solution.py:233
  65.3 0.7 %result.2.rest_0_ = bf16[10,128,128]{2,1,0:T(8,128)(2,1)} custom-call(bf16[5,128,128]{2,1,0:T(8,128)(2,1)S(1)} %get-tuple-element.24.mine_ref, bf16[5,128,128]{2,1,0:T(8,128)(2,1)S(1)} %collective-permute-done.18.other_ref), custom_call_target="tpu_custom_call" | custom-call | tf_op jit(solution)/shard_map/result/pallas_call | solution.py:332
  66.0 2.4 %collective-permute-done.17.other_ref = bf16[5,128,128]{2,1,0:T(8,128)(2,1)S(1)} collective-permute-done((bf16[5,128,128]{2,1,0:T(8,128)(2,1)S(1)}, bf16[5,128,128]{2,1,0:T(8,128)(2,1)S(1)}, u32[]{:S(2)}, u32[]{:S(2)}) %collective-permute-start.17) | collective-permute-done | bytes 163872 | tf_op jit(solution)/shard_map/ppermute | solution.py:233
  68.4 0.7 %result.3 = bf16[10,128,128]{2,1,0:T(8,128)(2,1)} custom-call(bf16[5,128,128]{2,1,0:T(8,128)(2,1)S(1)} %second_layer.3.mine_ref, bf16[5,128,128]{2,1,0:T(8,128)(2,1)S(1)} %collective-permute-done.17.other_ref, bf16[10,128,128]{2,1,0:T(8,128)(2,1)} %result.2.rest_0_), custom_call_target="tpu_custom_call", output_to_operand_aliasing={{}: (2, {})} | custom-call | tf_op jit(solution)/shard_map/result/pallas_call | solution.py:332
  (7 shorter events, 0.2 us)
Async XLA Ops:
  0.0 18.5 %copy-start.1 = (s32[10,36]{1,0:T(8,128)S(1)}, s32[10,36]{1,0:T(8,128)}, u32[]{:S(2)}) copy-start(s32[10,36]{1,0:T(8,128)} %cols_ref.7) | copy-start | bytes 4324
  0.0 18.5 %copy-start.3 = (s32[10,1]{0,1:T(1,128)S(1)}, s32[10,1]{0,1:T(1,128)}, u32[]{:S(2)}) copy-start(s32[10,1]{0,1:T(1,128)} %param.7) | copy-start | bytes 124
  0.0 18.5 %copy-start.2 = (f32[10240]{0:T(1024)S(1)}, f32[10240]{0:T(1024)}, u32[]{:S(2)}) copy-start(f32[10240]{0:T(1024)} %param.9) | copy-start | bytes 122884
  0.0 18.5 %copy-start = (bf16[10240,128]{1,0:T(8,128)(2,1)S(1)}, bf16[10240,128]{1,0:T(8,128)(2,1)}, u32[]{:S(2)}) copy-start(bf16[10240,128]{1,0:T(8,128)(2,1)} %param.8) | copy-start | bytes 7864324
  4.2 4.6 %collective-permute-start.1 = (bf16[80,128]{1,0:T(8,128)(2,1)S(1)}, bf16[80,128]{1,0:T(8,128)(2,1)S(1)}, u32[]{:S(2)}, u32[]{:S(2)}) collective-permute-start(bf16[80,128]{1,0:T(8,128)(2,1)S(1)} %convert_element_type.36), channel_id=1, source_target_pairs={{0,4},{2,6},{4,0},{6,2},{8,12},{10,14},{12,8},{14,10},{16,20},{18,... | collective-permute-start | bytes 61448 | tf_op jit(solution)/shard_map/ppermute | solution.py:230
  7.0 1.8 %collective-permute-start = (bf16[80,128]{1,0:T(8,128)(2,1)S(1)}, bf16[80,128]{1,0:T(8,128)(2,1)S(1)}, u32[]{:S(2)}, u32[]{:S(2)}) collective-permute-start(bf16[80,128]{1,0:T(8,128)(2,1)S(1)} %convert_element_type.36), channel_id=1, source_target_pairs={{0,2},{2,0},{4,6},{6,4},{8,10},{10,8},{12,14},{14,12},{16,18},{18,... | collective-permute-start | bytes 61448 | tf_op jit(solution)/shard_map/ppermute | solution.py:230
  7.0 3.2 %collective-permute-start.2 = (bf16[80,128]{1,0:T(8,128)(2,1)S(1)}, bf16[80,128]{1,0:T(8,128)(2,1)S(1)}, u32[]{:S(2)}, u32[]{:S(2)}) collective-permute-start(bf16[80,128]{1,0:T(8,128)(2,1)S(1)} %convert_element_type.36), channel_id=1, source_target_pairs={{0,6},{2,4},{4,2},{6,0},{8,14},{10,12},{12,10},{14,8},{16,22},{18,... | collective-permute-start | bytes 61448 | tf_op jit(solution)/shard_map/ppermute | solution.py:230
  10.2 5.6 %collective-permute-start.5 = (bf16[80,128]{1,0:T(8,128)(2,1)S(1)}, bf16[80,128]{1,0:T(8,128)(2,1)S(1)}, u32[]{:S(2)}, u32[]{:S(2)}) collective-permute-start(bf16[80,128]{1,0:T(8,128)(2,1)S(1)} %add_convert_fusion.1), channel_id=1, source_target_pairs={{0,24},{2,26},{4,28},{6,30},{8,16},{10,18},{12,20},{14,22},{16,8},... | collective-permute-start | bytes 61448 | tf_op jit(solution)/shard_map/ppermute | solution.py:230
  13.7 4.7 %collective-permute-start.4 = (bf16[80,128]{1,0:T(8,128)(2,1)S(1)}, bf16[80,128]{1,0:T(8,128)(2,1)S(1)}, u32[]{:S(2)}, u32[]{:S(2)}) collective-permute-start(bf16[80,128]{1,0:T(8,128)(2,1)S(1)} %add_convert_fusion.1), channel_id=1, source_target_pairs={{0,16},{2,18},{4,20},{6,22},{8,24},{10,26},{12,28},{14,30},{16,0},... | collective-permute-start | bytes 61448 | tf_op jit(solution)/shard_map/ppermute | solution.py:230
  13.8 4.7 %collective-permute-start.3 = (bf16[80,128]{1,0:T(8,128)(2,1)S(1)}, bf16[80,128]{1,0:T(8,128)(2,1)S(1)}, u32[]{:S(2)}, u32[]{:S(2)}) collective-permute-start(bf16[80,128]{1,0:T(8,128)(2,1)S(1)} %add_convert_fusion.1), channel_id=1, source_target_pairs={{0,8},{2,10},{4,12},{6,14},{8,0},{10,2},{12,4},{14,6},{16,24},{18,... | collective-permute-start | bytes 61448 | tf_op jit(solution)/shard_map/ppermute | solution.py:230
  21.0 5.4 %collective-permute-start.6 = (bf16[5,128,128]{2,1,0:T(8,128)(2,1)S(1)}, bf16[5,128,128]{2,1,0:T(8,128)(2,1)S(1)}, u32[]{:S(2)}, u32[]{:S(2)}) collective-permute-start(bf16[5,128,128]{2,1,0:T(8,128)(2,1)S(1)} %get-tuple-element.20), channel_id=1, source_target_pairs={{0,1},{1,0},{2,3},{3,2},{4,5},{5,4},{6,7},{7,6},{8,9},{9,8},{10,11... | collective-permute-start | bytes 491528 | tf_op jit(solution)/shard_map/ppermute | solution.py:233
  26.4 9.8 %collective-permute-start.7 = (bf16[5,128,128]{2,1,0:T(8,128)(2,1)S(1)}, bf16[5,128,128]{2,1,0:T(8,128)(2,1)S(1)}, u32[]{:S(2)}, u32[]{:S(2)}) collective-permute-start(bf16[5,128,128]{2,1,0:T(8,128)(2,1)S(1)} %add_convert_fusion.own_ref), channel_id=1, source_target_pairs={{0,16},{2,18},{4,20},{6,22},{8,24},{10,26},{12,28},{14,30},{16,0},... | collective-permute-start | bytes 491528 | tf_op jit(solution)/shard_map/ppermute | solution.py:230
  36.2 6.2 %collective-permute-start.11 = (bf16[5,128,128]{2,1,0:T(8,128)(2,1)S(1)}, bf16[5,128,128]{2,1,0:T(8,128)(2,1)S(1)}, u32[]{:S(2)}, u32[]{:S(2)}) collective-permute-start(bf16[5,128,128]{2,1,0:T(8,128)(2,1)S(1)} %get-tuple-element.22), channel_id=1, source_target_pairs={{0,1},{1,0},{2,3},{3,2},{4,5},{5,4},{6,7},{7,6},{8,9},{9,8},{10,11... | collective-permute-start | bytes 491528 | tf_op jit(solution)/shard_map/ppermute | solution.py:233
  36.7 9.5 %collective-permute-start.10 = (bf16[5,128,128]{2,1,0:T(8,128)(2,1)S(1)}, bf16[5,128,128]{2,1,0:T(8,128)(2,1)S(1)}, u32[]{:S(2)}, u32[]{:S(2)}) collective-permute-start(bf16[5,128,128]{2,1,0:T(8,128)(2,1)S(1)} %get-tuple-element.21.refs_0_), channel_id=1, source_target_pairs={{0,4},{2,6},{4,0},{6,2},{8,12},{10,14},{12,8},{14,10},{16,20},{18,... | collective-permute-start | bytes 491528 | tf_op jit(solution)/shard_map/ppermute | solution.py:230
  36.7 9.5 %collective-permute-start.9 = (bf16[5,128,128]{2,1,0:T(8,128)(2,1)S(1)}, bf16[5,128,128]{2,1,0:T(8,128)(2,1)S(1)}, u32[]{:S(2)}, u32[]{:S(2)}) collective-permute-start(bf16[5,128,128]{2,1,0:T(8,128)(2,1)S(1)} %get-tuple-element.21.refs_0_), channel_id=1, source_target_pairs={{0,12},{2,14},{4,8},{6,10},{8,4},{10,6},{12,0},{14,2},{16,28},{18,... | collective-permute-start | bytes 491528 | tf_op jit(solution)/shard_map/ppermute | solution.py:230
  37.7 11.1 %collective-permute-start.8 = (bf16[5,128,128]{2,1,0:T(8,128)(2,1)S(1)}, bf16[5,128,128]{2,1,0:T(8,128)(2,1)S(1)}, u32[]{:S(2)}, u32[]{:S(2)}) collective-permute-start(bf16[5,128,128]{2,1,0:T(8,128)(2,1)S(1)} %get-tuple-element.21.refs_0_), channel_id=1, source_target_pairs={{0,8},{2,10},{4,12},{6,14},{8,0},{10,2},{12,4},{14,6},{16,24},{18,... | collective-permute-start | bytes 491528 | tf_op jit(solution)/shard_map/ppermute | solution.py:230
  42.4 9.3 %collective-permute-start.14 = (bf16[5,128,128]{2,1,0:T(8,128)(2,1)S(1)}, bf16[5,128,128]{2,1,0:T(8,128)(2,1)S(1)}, u32[]{:S(2)}, u32[]{:S(2)}) collective-permute-start(bf16[5,128,128]{2,1,0:T(8,128)(2,1)S(1)} %collective-permute-done.11.refs_0_), channel_id=1, source_target_pairs={{0,12},{2,14},{4,8},{6,10},{8,4},{10,6},{12,0},{14,2},{16,28},{18,... | collective-permute-start | bytes 491528 | tf_op jit(solution)/shard_map/ppermute | solution.py:230
  42.4 11.8 %collective-permute-start.13 = (bf16[5,128,128]{2,1,0:T(8,128)(2,1)S(1)}, bf16[5,128,128]{2,1,0:T(8,128)(2,1)S(1)}, u32[]{:S(2)}, u32[]{:S(2)}) collective-permute-start(bf16[5,128,128]{2,1,0:T(8,128)(2,1)S(1)} %collective-permute-done.11.refs_0_), channel_id=1, source_target_pairs={{0,8},{2,10},{4,12},{6,14},{8,0},{10,2},{12,4},{14,6},{16,24},{18,... | collective-permute-start | bytes 491528 | tf_op jit(solution)/shard_map/ppermute | solution.py:230
  46.1 8.1 %collective-permute-start.12 = (bf16[5,128,128]{2,1,0:T(8,128)(2,1)S(1)}, bf16[5,128,128]{2,1,0:T(8,128)(2,1)S(1)}, u32[]{:S(2)}, u32[]{:S(2)}) collective-permute-start(bf16[5,128,128]{2,1,0:T(8,128)(2,1)S(1)} %collective-permute-done.11.refs_0_), channel_id=1, source_target_pairs={{0,4},{2,6},{4,0},{6,2},{8,12},{10,14},{12,8},{14,10},{16,20},{18,... | collective-permute-start | bytes 491528 | tf_op jit(solution)/shard_map/ppermute | solution.py:230
  48.8 5.6 %collective-permute-start.15 = (bf16[20,128,128]{2,1,0:T(8,128)(2,1)S(1)}, bf16[20,128,128]{2,1,0:T(8,128)(2,1)S(1)}, u32[]{:S(2)}, u32[]{:S(2)}) collective-permute-start(bf16[20,128,128]{2,1,0:T(8,128)(2,1)S(1)} %own_joined.2.rest_0_), channel_id=1, source_target_pairs={{0,2},{2,0},{4,6},{6,4},{8,10},{10,8},{12,14},{14,12},{16,18},{18,... | collective-permute-start | bytes 1966088 | tf_op jit(solution)/shard_map/ppermute | solution.py:230
  54.3 2.2 %collective-permute-start.16 = (bf16[20,128,128]{2,1,0:T(8,128)(2,1)S(1)}, bf16[20,128,128]{2,1,0:T(8,128)(2,1)S(1)}, u32[]{:S(2)}, u32[]{:S(2)}) collective-permute-start(bf16[20,128,128]{2,1,0:T(8,128)(2,1)S(1)} %own_joined.3.rest_1_), channel_id=1, source_target_pairs={{0,2},{2,0},{4,6},{6,4},{8,10},{10,8},{12,14},{14,12},{16,18},{18,... | collective-permute-start | bytes 1966088 | tf_op jit(solution)/shard_map/ppermute | solution.py:230
  58.9 6.4 %collective-permute-start.18 = (bf16[5,128,128]{2,1,0:T(8,128)(2,1)S(1)}, bf16[5,128,128]{2,1,0:T(8,128)(2,1)S(1)}, u32[]{:S(2)}, u32[]{:S(2)}) collective-permute-start(bf16[5,128,128]{2,1,0:T(8,128)(2,1)S(1)} %get-tuple-element.24.mine_ref), channel_id=1, source_target_pairs={{0,1},{1,0},{2,3},{3,2},{4,5},{5,4},{6,7},{7,6},{8,9},{9,8},{10,11... | collective-permute-start | bytes 491528 | tf_op jit(solution)/shard_map/ppermute | solution.py:233
  62.5 5.9 %collective-permute-start.17 = (bf16[5,128,128]{2,1,0:T(8,128)(2,1)S(1)}, bf16[5,128,128]{2,1,0:T(8,128)(2,1)S(1)}, u32[]{:S(2)}, u32[]{:S(2)}) collective-permute-start(bf16[5,128,128]{2,1,0:T(8,128)(2,1)S(1)} %second_layer.3.mine_ref), channel_id=1, source_target_pairs={{0,1},{1,0},{2,3},{3,2},{4,5},{5,4},{6,7},{7,6},{8,9},{9,8},{10,11... | collective-permute-start | bytes 491528 | tf_op jit(solution)/shard_map/ppermute | solution.py:233

commit v14 on v13

--- a/solution.py
+++ b/solution.py
@@ -56,7 +56,13 @@
             def _(b=b, part=part):
                 add(b, part)
 
-    sums_ref[...] = jnp.sum(acc_ref[:groups], axis=1)
+    sums = jnp.sum(acc_ref[:groups], axis=1).astype(sums_ref.dtype)
+    sums_ref[...] = jnp.broadcast_to(sums, sums_ref.shape)
+
+
+def add_kernel(parts_ref, out_ref):
+    sums = sum(parts_ref[i].astype(jnp.float32) for i in range(parts_ref.shape[0]))
+    out_ref[...] = jnp.broadcast_to(sums.astype(out_ref.dtype), out_ref.shape)
 
 
 def multiply_rows(rows, counts_ref, slots, start, gather, acc_ref):
@@ -83,7 +89,10 @@
     if sending is not None:
         side = lax.axis_index("col")
         base = (1 - side if sending else side) * count
-    inverse_ref[...] = (1.0 / (sums_ref[...] + added_ref[...]))[:, None, :]
+    totals = added_ref[...]
+    for i in range(sums_ref.shape[0]):
+        totals = totals + sums_ref[i].astype(jnp.float32)
+    inverse_ref[...] = (1.0 / totals)[:, None, :]
 
     def gather(row, slot):
         col = cols_ref[row, slot]
@@ -116,7 +125,7 @@
 
 
 GATHERED = (
-    ((0, 0, 0), (1, 0, 0), (1, 1, 0), (0, 1, 0)),
+    ((0, 0, 0), (0, 1, 0), (1, 0, 0), (1, 1, 0)),
     ((0, 0, 1), (0, 1, 1), (1, 0, 1), (1, 1, 1)),
 )
 
@@ -210,7 +219,7 @@
         sums_kernel,
         name="column_sums",
         out_shape=(
-            jax.ShapeDtypeStruct((groups, size), jnp.float32),
+            jax.ShapeDtypeStruct((4, groups, size) if paired else (groups, size), jnp.bfloat16 if paired else jnp.float32),
             pltpu.VMEM(blocks.shape, blocks.dtype),
         ),
         in_specs=[pl.BlockSpec(memory_space=pltpu.HBM)] * 3,
@@ -233,12 +242,20 @@
         return lax.ppermute(array, "col", [(0, 1), (1, 0)])
 
     if paired:
-        for masks in ((1, 2, 3), (4, 8, 12)):
-            sums = sums.astype(jnp.bfloat16)
-            parts = [sums] + [flip(sums, m) for m in masks]
-            sums = functools.reduce(jnp.add, [part.astype(jnp.float32) for part in parts])
+        squares = [[i * 4 + j for j in range(4)] for i in range(4)]
+        lines = [[i + j * 4 for j in range(4)] for i in range(4)]
+        sums = lax.all_to_all(sums, "row", 0, 0, axis_index_groups=squares)
+        sums = pl.pallas_call(
+            add_kernel,
+            name="own_sums",
+            out_shape=jax.ShapeDtypeStruct(sums.shape, sums.dtype),
+            in_specs=[VMEM],
+            out_specs=VMEM,
+            compiler_params=PARAMS,
+        )(sums)
+        sums = lax.all_to_all(sums, "row", 0, 0, axis_index_groups=lines)
     else:
-        sums = lax.psum(sums, "row")
+        sums = lax.psum(sums, "row")[None]
 
     def layer_cost(count):
         return cost(2 * count * slots * size * size * width, count * slots * size * size * 2)
@@ -318,9 +335,7 @@
         )(*pieces)
 
     away = swap(away)
-    near_home = join([home, flip(home, 4), flip(home, 6), flip(home, 2)])
-    near_away = join([away, flip(away, 2), flip(away, 4), flip(away, 6)])
-    gathered = [near_home, near_away]
+    gathered = [join([part] + [flip(part, mask) for mask in (2, 4, 6)]) for part in (home, away)]
     pieces = gathered + [flip(part, 1) for part in gathered]
 
     part_a, source = second_call(functools.partial(second_part_kernel, 0), half, coefs, own, pieces, True)

time: 69.1 us -> 69.9 us (1.012); the launches traced: 69.3 us -> 70.9 us
  blocking collectives: 0 us -> 18.9 us
  waiting for transfers between devices: 35 us -> 23.2 us
  starting transfers between devices: 18.5 us -> 15.2 us
  Pallas kernels: 15.4 us -> 13.3 us
    all_to_all x0 -> x2, blocking collectives: none -> 18.9 us  [the longest x1 11 us: body(): sums = lax.all_to_all(sums, 'row', 0, 0, axis_index_groups=lines)]
    ppermute x15 -> x9, waiting for transfers between devices: 27.6 us -> 16.9 us  [flip(): return lax.ppermute(array, 'row', [(i, i ^ mask) for i in range(n_row)])]
    ppermute x15 -> x9, starting transfers between devices: 13.8 us -> 8.93 us  [flip(): return lax.ppermute(array, 'row', [(i, i ^ mask) for i in range(n_row)])]
    ppermute x4, starting transfers between devices: 4.68 us -> 6.23 us  [swap(): return lax.ppermute(array, 'col', [(0, 1), (1, 0)])]
    ppermute x4, waiting for transfers between devices: 7.38 us -> 6.32 us  [swap(): return lax.ppermute(array, 'col', [(0, 1), (1, 0)])]
    pallas_call x2, Pallas kernels: 5.44 us -> 4.45 us  [first_layer(): pl.pallas_call(functools.partial(first_kernel, sending), name='first_laye...]
    pallas_call x2, Pallas kernels: 4.24 us -> 3.52 us  [second_call(): pl.pallas_call(kernel, name='second_layer', out_shape=(out, jax.ShapeDtyp...]
  transfers between devices with their start and end apart: 19 -> 13, of which waited for: 14 -> 9; matrix products, arithmetic and copies ran while one was open for 0% -> 0% of each run, Pallas kernels for 8% -> 7%
where the time goes in v14:
time: 69.9 us; the launch traced here: 70.9 us
  waiting for transfers between devices  23.2 us (33%)
  blocking collectives  18.9 us (27%)
  starting transfers between devices  15.2 us (22%)
  Pallas kernels  13.3 us (19%)
    ppermute x9, waiting for transfers between devices, flip(): return lax.ppermute(array, 'row', [(i, i ^ mask) for i in range(n_row)])  16.9 us
    all_to_all x1, blocking collectives, body(): sums = lax.all_to_all(sums, 'row', 0, 0, axis_index_groups=lines)  11 us
    ppermute x9, starting transfers between devices, flip(): return lax.ppermute(array, 'row', [(i, i ^ mask) for i in range(n_row)])  8.93 us
    all_to_all x1, blocking collectives, body(): sums = lax.all_to_all(sums, 'row', 0, 0, axis_index_groups=squares)  7.9 us
    ppermute x4, waiting for transfers between devices, swap(): return lax.ppermute(array, 'col', [(0, 1), (1, 0)])  6.32 us
    ppermute x4, starting transfers between devices, swap(): return lax.ppermute(array, 'col', [(0, 1), (1, 0)])  6.23 us
    pallas_call x2, Pallas kernels, first_layer(): pl.pallas_call(functools.partial(first_kernel, sending), name='first_laye...  4.45 us
    pallas_call x1, Pallas kernels, body(): pl.pallas_call(sums_kernel, name='column_sums', out_shape=(jax.ShapeDtype...  3.79 us
  transfers between devices with their start and end apart: 13, of which 9 were waited for; matrix products, arithmetic and copies ran while one was open for 0% of the time, Pallas kernels for 7%

profile of v14, /device:TPU:0, one launch (start us, length us, event | category | flops | bytes accessed | tf_op | source)
XLA Modules:
  0.0 70.9 jit_solution(13020092196333927206)
XLA Ops:
  0.0 0.0 copy-start.1
  0.0 0.0 copy-start.3
  0.0 0.0 copy-start.2
  0.0 0.0 copy-start
  0.0 3.8 %column_sums.1 = (bf16[4,80,128]{2,1,0:T(8,128)(2,1)S(1)}, bf16[10,36,128,128]{3,2,1,0:T(8,128)(2,1)S(1)}) custom-call(s32[10,36]{1,0:T(8,128)} %cols_ref.7, s32[10]{0:T(128)} %bitcast.8, bf16[10,36,128,128]{3,2,1,0:T(8,128)(2,1)} %blocks_ref.1), custom_call_target="tpu_custom_call" | custom-call | bytes 23592960 | tf_op jit(solution)/shard_map/column_sums/pallas_call | solution.py:218
  3.8 7.9 %all_to_all.10.parts_ref = bf16[4,80,128]{2,1,0:T(8,128)(2,1)S(1)} all-to-all(bf16[4,80,128]{2,1,0:T(8,128)(2,1)S(1)} %get-tuple-element.15), channel_id=1, replica_groups={{0,2,4,6},{8,10,12,14},{16,18,20,22},{24,26,28,30},{1,3,5,7},{9,11,13,1..., dimensions={0} | all-to-all | bytes 163840 | tf_op jit(solution)/shard_map/all_to_all | solution.py:247
  11.7 11.0 %all_to_all.11.sums_ref = bf16[4,80,128]{2,1,0:T(8,128)(2,1)S(1)} all-to-all(bf16[4,80,128]{2,1,0:T(8,128)(2,1)S(1)} %own_sums.1), channel_id=1, replica_groups={{0,8,16,24},{2,10,18,26},{4,12,20,28},{6,14,22,30},{1,9,17,25},{3,11,19..., dimensions={0} | all-to-all | bytes 163840 | tf_op jit(solution)/shard_map/all_to_all | solution.py:256
  22.7 0.0 copy-done.1
  22.7 0.0 copy-done.3
  22.7 0.0 copy-done.2
  22.7 0.0 copy-done
  22.8 2.0 %first_layer.2 = (bf16[5,128,128]{2,1,0:T(8,128)(2,1)S(1)}, bf16[10,36,128,128]{3,2,1,0:T(8,128)(2,1)S(1)}) custom-call(s32[10,36]{1,0:T(8,128)S(1)} %copy-done.1, s32[10]{0:T(128)S(1)} %bitcast.9, bf16[4,80,128]{2,1,0:T(8,128)(2,1)S(1)} %all_to_all.11.sums_ref, f32[80,128]{1,0:T(8,128)S(1)} %bitcast.6, ...), custom_call_target="tpu_custom_call", output_to_operand_aliasing={{1}: (5, {})} | custom-call | flops 754974720 | bytes 5898240 | tf_op jit(solution)/shard_map/first_layer/pallas_call | solution.py:264
  24.7 2.1 %collective-permute-start = (bf16[5,128,128]{2,1,0:T(8,128)(2,1)S(1)}, bf16[5,128,128]{2,1,0:T(8,128)(2,1)S(1)}, u32[]{:S(2)}, u32[]{:S(2)}) collective-permute-start(bf16[5,128,128]{2,1,0:T(8,128)(2,1)S(1)} %get-tuple-element.20), channel_id=1, source_target_pairs={{0,1},{1,0},{2,3},{3,2},{4,5},{5,4},{6,7},{7,6},{8,9},{9,8},{10,11... | collective-permute-start | bytes 491528 | tf_op jit(solution)/shard_map/ppermute | solution.py:242
  26.8 2.5 %first_layer.3 = (f32[5,128,128]{2,1,0:T(8,128)S(1)}, bf16[10,36,128,128]{3,2,1,0:T(8,128)(2,1)S(1)}) custom-call(s32[10,36]{1,0:T(8,128)S(1)} %copy-done.1, s32[10]{0:T(128)S(1)} %bitcast.10, bf16[4,80,128]{2,1,0:T(8,128)(2,1)S(1)} %all_to_all.11.sums_ref, f32[80,128]{1,0:T(8,128)S(1)} %bitcast.7, ...), custom_call_target="tpu_custom_call", output_to_operand_aliasing={{1}: (5, {})} | custom-call | flops 754974720 | bytes 5898240 | tf_op jit(solution)/shard_map/first_layer/pallas_call | solution.py:264
  29.3 0.8 %collective-permute-done = bf16[5,128,128]{2,1,0:T(8,128)(2,1)S(1)} collective-permute-done((bf16[5,128,128]{2,1,0:T(8,128)(2,1)S(1)}, bf16[5,128,128]{2,1,0:T(8,128)(2,1)S(1)}, u32[]{:S(2)}, u32[]{:S(2)}) %collective-permute-start) | collective-permute-done | bytes 163872 | tf_op jit(solution)/shard_map/ppermute | solution.py:242
  30.2 1.4 %collective-permute-start.1 = (bf16[5,128,128]{2,1,0:T(8,128)(2,1)S(1)}, bf16[5,128,128]{2,1,0:T(8,128)(2,1)S(1)}, u32[]{:S(2)}, u32[]{:S(2)}) collective-permute-start(bf16[5,128,128]{2,1,0:T(8,128)(2,1)S(1)} %add_convert_fusion.own_ref), channel_id=1, source_target_pairs={{0,16},{2,18},{4,20},{6,22},{8,24},{10,26},{12,28},{14,30},{16,0},... | collective-permute-start | bytes 491528 | tf_op jit(solution)/shard_map/ppermute | solution.py:239
  31.5 6.7 %collective-permute-done.1.crossed_ref = bf16[5,128,128]{2,1,0:T(8,128)(2,1)S(1)} collective-permute-done((bf16[5,128,128]{2,1,0:T(8,128)(2,1)S(1)}, bf16[5,128,128]{2,1,0:T(8,128)(2,1)S(1)}, u32[]{:S(2)}, u32[]{:S(2)}) %collective-permute-start.1) | collective-permute-done | bytes 163872 | tf_op jit(solution)/shard_map/ppermute | solution.py:239
  38.2 2.0 %collective-permute-start.5 = (bf16[5,128,128]{2,1,0:T(8,128)(2,1)S(1)}, bf16[5,128,128]{2,1,0:T(8,128)(2,1)S(1)}, u32[]{:S(2)}, u32[]{:S(2)}) collective-permute-start(bf16[5,128,128]{2,1,0:T(8,128)(2,1)S(1)} %get-tuple-element.22), channel_id=1, source_target_pairs={{0,1},{1,0},{2,3},{3,2},{4,5},{5,4},{6,7},{7,6},{8,9},{9,8},{10,11... | collective-permute-start | bytes 491528 | tf_op jit(solution)/shard_map/ppermute | solution.py:242
  40.2 0.0 collective-permute-start.4
  40.2 1.7 %collective-permute-start.3 = (bf16[5,128,128]{2,1,0:T(8,128)(2,1)S(1)}, bf16[5,128,128]{2,1,0:T(8,128)(2,1)S(1)}, u32[]{:S(2)}, u32[]{:S(2)}) collective-permute-start(bf16[5,128,128]{2,1,0:T(8,128)(2,1)S(1)} %get-tuple-element.21.refs_0_), channel_id=1, source_target_pairs={{0,8},{2,10},{4,12},{6,14},{8,0},{10,2},{12,4},{14,6},{16,24},{18,... | collective-permute-start | bytes 491528 | tf_op jit(solution)/shard_map/ppermute | solution.py:239
  41.9 1.8 %collective-permute-start.2 = (bf16[5,128,128]{2,1,0:T(8,128)(2,1)S(1)}, bf16[5,128,128]{2,1,0:T(8,128)(2,1)S(1)}, u32[]{:S(2)}, u32[]{:S(2)}) collective-permute-start(bf16[5,128,128]{2,1,0:T(8,128)(2,1)S(1)} %get-tuple-element.21.refs_0_), channel_id=1, source_target_pairs={{0,4},{2,6},{4,0},{6,2},{8,12},{10,14},{12,8},{14,10},{16,20},{18,... | collective-permute-start | bytes 491528 | tf_op jit(solution)/shard_map/ppermute | solution.py:239
  43.7 0.0 collective-permute-done.5.refs_0_
  43.7 0.0 collective-permute-start.8
  43.7 3.6 %collective-permute-start.7 = (bf16[5,128,128]{2,1,0:T(8,128)(2,1)S(1)}, bf16[5,128,128]{2,1,0:T(8,128)(2,1)S(1)}, u32[]{:S(2)}, u32[]{:S(2)}) collective-permute-start(bf16[5,128,128]{2,1,0:T(8,128)(2,1)S(1)} %collective-permute-done.5.refs_0_), channel_id=1, source_target_pairs={{0,8},{2,10},{4,12},{6,14},{8,0},{10,2},{12,4},{14,6},{16,24},{18,... | collective-permute-start | bytes 491528 | tf_op jit(solution)/shard_map/ppermute | solution.py:239
  47.3 0.9 %collective-permute-done.4.refs_3_ = bf16[5,128,128]{2,1,0:T(8,128)(2,1)S(1)} collective-permute-done((bf16[5,128,128]{2,1,0:T(8,128)(2,1)S(1)}, bf16[5,128,128]{2,1,0:T(8,128)(2,1)S(1)}, u32[]{:S(2)}, u32[]{:S(2)}) %collective-permute-start.4) | collective-permute-done | bytes 163872 | tf_op jit(solution)/shard_map/ppermute | solution.py:239
  48.2 0.3 collective-permute-start.6
  48.5 2.0 %collective-permute-done.3.refs_2_ = bf16[5,128,128]{2,1,0:T(8,128)(2,1)S(1)} collective-permute-done((bf16[5,128,128]{2,1,0:T(8,128)(2,1)S(1)}, bf16[5,128,128]{2,1,0:T(8,128)(2,1)S(1)}, u32[]{:S(2)}, u32[]{:S(2)}) %collective-permute-start.3) | collective-permute-done | bytes 163872 | tf_op jit(solution)/shard_map/ppermute | solution.py:239
  50.5 2.6 %collective-permute-done.2.refs_1_ = bf16[5,128,128]{2,1,0:T(8,128)(2,1)S(1)} collective-permute-done((bf16[5,128,128]{2,1,0:T(8,128)(2,1)S(1)}, bf16[5,128,128]{2,1,0:T(8,128)(2,1)S(1)}, u32[]{:S(2)}, u32[]{:S(2)}) %collective-permute-start.2) | collective-permute-done | bytes 163872 | tf_op jit(solution)/shard_map/ppermute | solution.py:239
  53.2 0.1 collective-permute-start.9
  53.3 0.0 collective-permute-done.8.refs_3_
  53.3 2.6 %collective-permute-done.7.refs_2_ = bf16[5,128,128]{2,1,0:T(8,128)(2,1)S(1)} collective-permute-done((bf16[5,128,128]{2,1,0:T(8,128)(2,1)S(1)}, bf16[5,128,128]{2,1,0:T(8,128)(2,1)S(1)}, u32[]{:S(2)}, u32[]{:S(2)}) %collective-permute-start.7) | collective-permute-done | bytes 163872 | tf_op jit(solution)/shard_map/ppermute | solution.py:239
  55.9 0.0 collective-permute-done.6.refs_1_
  56.0 0.1 collective-permute-start.10
  56.0 0.0 collective-permute-done.9.rest_2_
  56.0 2.1 %collective-permute-done.10.rest_3_ = bf16[20,128,128]{2,1,0:T(8,128)(2,1)S(1)} collective-permute-done((bf16[20,128,128]{2,1,0:T(8,128)(2,1)S(1)}, bf16[20,128,128]{2,1,0:T(8,128)(2,1)S(1)}, u32[]{:S(2)}, u32[]{:S(2)}) %collective-permute-start.10) | collective-permute-done | bytes 655392 | tf_op jit(solution)/shard_map/ppermute | solution.py:239
  58.1 2.1 %second_layer.2 = (bf16[5,128,128]{2,1,0:T(8,128)(2,1)S(1)}, bf16[80,128,128]{2,1,0:T(8,128)(2,1)S(1)}) custom-call(s32[10,36]{1,0:T(8,128)S(1)} %copy-done.1, s32[10]{0:T(128)S(1)} %bitcast.11, bf16[10,36,128,128]{3,2,1,0:T(8,128)(2,1)S(1)} %get-tuple-element.18.coef_ref, bf16[5,128,128]{2,1,0:T(8,128)(2,1)S(1)} %add_convert_fusion.own_ref, ...), custom_call_target="tpu_custom_call" | custom-call | flops 754974720 | bytes 5898240 | tf_op jit(solution)/shard_map/second_layer/pallas_call | solution.py:292
  60.2 1.7 %collective-permute-start.12 = (bf16[5,128,128]{2,1,0:T(8,128)(2,1)S(1)}, bf16[5,128,128]{2,1,0:T(8,128)(2,1)S(1)}, u32[]{:S(2)}, u32[]{:S(2)}) collective-permute-start(bf16[5,128,128]{2,1,0:T(8,128)(2,1)S(1)} %get-tuple-element.24.mine_ref), channel_id=1, source_target_pairs={{0,1},{1,0},{2,3},{3,2},{4,5},{5,4},{6,7},{7,6},{8,9},{9,8},{10,11... | collective-permute-start | bytes 491528 | tf_op jit(solution)/shard_map/ppermute | solution.py:242
  62.0 1.4 %second_layer.3.mine_ref = bf16[5,128,128]{2,1,0:T(8,128)(2,1)S(1)} custom-call(s32[10,36]{1,0:T(8,128)S(1)} %copy-done.1, s32[10]{0:T(128)S(1)} %bitcast.12, bf16[10,36,128,128]{3,2,1,0:T(8,128)(2,1)S(1)} %get-tuple-element.18.coef_ref, bf16[5,128,128]{2,1,0:T(8,128)(2,1)S(1)} %add_convert_fusion.own_ref, bf16[80,128,128]{2,1,0:T(8,128)(2,1)S(1)} %get-tuple-element.23.rest_0_), custom_call_target="tpu_custom_call" | custom-call | flops 754974720 | bytes 5898240 | tf_op jit(solution)/shard_map/second_layer/pallas_call | solution.py:292
  63.4 0.4 collective-permute-start.11
  63.8 3.3 %collective-permute-done.12.other_ref = bf16[5,128,128]{2,1,0:T(8,128)(2,1)S(1)} collective-permute-done((bf16[5,128,128]{2,1,0:T(8,128)(2,1)S(1)}, bf16[5,128,128]{2,1,0:T(8,128)(2,1)S(1)}, u32[]{:S(2)}, u32[]{:S(2)}) %collective-permute-start.12) | collective-permute-done | bytes 163872 | tf_op jit(solution)/shard_map/ppermute | solution.py:242
  67.1 0.7 %result.2.rest_0_ = bf16[10,128,128]{2,1,0:T(8,128)(2,1)} custom-call(bf16[5,128,128]{2,1,0:T(8,128)(2,1)S(1)} %get-tuple-element.24.mine_ref, bf16[5,128,128]{2,1,0:T(8,128)(2,1)S(1)} %collective-permute-done.12.other_ref), custom_call_target="tpu_custom_call" | custom-call | tf_op jit(solution)/shard_map/result/pallas_call | solution.py:347
  67.8 2.2 %collective-permute-done.11.other_ref = bf16[5,128,128]{2,1,0:T(8,128)(2,1)S(1)} collective-permute-done((bf16[5,128,128]{2,1,0:T(8,128)(2,1)S(1)}, bf16[5,128,128]{2,1,0:T(8,128)(2,1)S(1)}, u32[]{:S(2)}, u32[]{:S(2)}) %collective-permute-start.11) | collective-permute-done | bytes 163872 | tf_op jit(solution)/shard_map/ppermute | solution.py:242
  70.0 0.7 %result.3 = bf16[10,128,128]{2,1,0:T(8,128)(2,1)} custom-call(bf16[5,128,128]{2,1,0:T(8,128)(2,1)S(1)} %second_layer.3.mine_ref, bf16[5,128,128]{2,1,0:T(8,128)(2,1)S(1)} %collective-permute-done.11.other_ref, bf16[10,128,128]{2,1,0:T(8,128)(2,1)} %result.2.rest_0_), custom_call_target="tpu_custom_call", output_to_operand_aliasing={{}: (2, {})} | custom-call | tf_op jit(solution)/shard_map/result/pallas_call | solution.py:347
  (5 shorter events, 0.2 us)
Async XLA Ops:
  0.0 22.7 %copy-start.1 = (s32[10,36]{1,0:T(8,128)S(1)}, s32[10,36]{1,0:T(8,128)}, u32[]{:S(2)}) copy-start(s32[10,36]{1,0:T(8,128)} %cols_ref.7) | copy-start | bytes 4324
  0.0 22.7 %copy-start.3 = (s32[10,1]{0,1:T(1,128)S(1)}, s32[10,1]{0,1:T(1,128)}, u32[]{:S(2)}) copy-start(s32[10,1]{0,1:T(1,128)} %param.7) | copy-start | bytes 124
  0.0 22.7 %copy-start.2 = (f32[10240]{0:T(1024)S(1)}, f32[10240]{0:T(1024)}, u32[]{:S(2)}) copy-start(f32[10240]{0:T(1024)} %param.9) | copy-start | bytes 122884
  0.0 22.7 %copy-start = (bf16[10240,128]{1,0:T(8,128)(2,1)S(1)}, bf16[10240,128]{1,0:T(8,128)(2,1)}, u32[]{:S(2)}) copy-start(bf16[10240,128]{1,0:T(8,128)(2,1)} %param.8) | copy-start | bytes 7864324
  24.7 5.4 %collective-permute-start = (bf16[5,128,128]{2,1,0:T(8,128)(2,1)S(1)}, bf16[5,128,128]{2,1,0:T(8,128)(2,1)S(1)}, u32[]{:S(2)}, u32[]{:S(2)}) collective-permute-start(bf16[5,128,128]{2,1,0:T(8,128)(2,1)S(1)} %get-tuple-element.20), channel_id=1, source_target_pairs={{0,1},{1,0},{2,3},{3,2},{4,5},{5,4},{6,7},{7,6},{8,9},{9,8},{10,11... | collective-permute-start | bytes 491528 | tf_op jit(solution)/shard_map/ppermute | solution.py:242
  30.2 8.0 %collective-permute-start.1 = (bf16[5,128,128]{2,1,0:T(8,128)(2,1)S(1)}, bf16[5,128,128]{2,1,0:T(8,128)(2,1)S(1)}, u32[]{:S(2)}, u32[]{:S(2)}) collective-permute-start(bf16[5,128,128]{2,1,0:T(8,128)(2,1)S(1)} %add_convert_fusion.own_ref), channel_id=1, source_target_pairs={{0,16},{2,18},{4,20},{6,22},{8,24},{10,26},{12,28},{14,30},{16,0},... | collective-permute-start | bytes 491528 | tf_op jit(solution)/shard_map/ppermute | solution.py:239
  38.2 5.5 %collective-permute-start.5 = (bf16[5,128,128]{2,1,0:T(8,128)(2,1)S(1)}, bf16[5,128,128]{2,1,0:T(8,128)(2,1)S(1)}, u32[]{:S(2)}, u32[]{:S(2)}) collective-permute-start(bf16[5,128,128]{2,1,0:T(8,128)(2,1)S(1)} %get-tuple-element.22), channel_id=1, source_target_pairs={{0,1},{1,0},{2,3},{3,2},{4,5},{5,4},{6,7},{7,6},{8,9},{9,8},{10,11... | collective-permute-start | bytes 491528 | tf_op jit(solution)/shard_map/ppermute | solution.py:242
  40.2 7.9 %collective-permute-start.4 = (bf16[5,128,128]{2,1,0:T(8,128)(2,1)S(1)}, bf16[5,128,128]{2,1,0:T(8,128)(2,1)S(1)}, u32[]{:S(2)}, u32[]{:S(2)}) collective-permute-start(bf16[5,128,128]{2,1,0:T(8,128)(2,1)S(1)} %get-tuple-element.21.refs_0_), channel_id=1, source_target_pairs={{0,12},{2,14},{4,8},{6,10},{8,4},{10,6},{12,0},{14,2},{16,28},{18,... | collective-permute-start | bytes 491528 | tf_op jit(solution)/shard_map/ppermute | solution.py:239
  40.2 10.3 %collective-permute-start.3 = (bf16[5,128,128]{2,1,0:T(8,128)(2,1)S(1)}, bf16[5,128,128]{2,1,0:T(8,128)(2,1)S(1)}, u32[]{:S(2)}, u32[]{:S(2)}) collective-permute-start(bf16[5,128,128]{2,1,0:T(8,128)(2,1)S(1)} %get-tuple-element.21.refs_0_), channel_id=1, source_target_pairs={{0,8},{2,10},{4,12},{6,14},{8,0},{10,2},{12,4},{14,6},{16,24},{18,... | collective-permute-start | bytes 491528 | tf_op jit(solution)/shard_map/ppermute | solution.py:239
  41.9 11.2 %collective-permute-start.2 = (bf16[5,128,128]{2,1,0:T(8,128)(2,1)S(1)}, bf16[5,128,128]{2,1,0:T(8,128)(2,1)S(1)}, u32[]{:S(2)}, u32[]{:S(2)}) collective-permute-start(bf16[5,128,128]{2,1,0:T(8,128)(2,1)S(1)} %get-tuple-element.21.refs_0_), channel_id=1, source_target_pairs={{0,4},{2,6},{4,0},{6,2},{8,12},{10,14},{12,8},{14,10},{16,20},{18,... | collective-permute-start | bytes 491528 | tf_op jit(solution)/shard_map/ppermute | solution.py:239
  43.7 9.6 %collective-permute-start.8 = (bf16[5,128,128]{2,1,0:T(8,128)(2,1)S(1)}, bf16[5,128,128]{2,1,0:T(8,128)(2,1)S(1)}, u32[]{:S(2)}, u32[]{:S(2)}) collective-permute-start(bf16[5,128,128]{2,1,0:T(8,128)(2,1)S(1)} %collective-permute-done.5.refs_0_), channel_id=1, source_target_pairs={{0,12},{2,14},{4,8},{6,10},{8,4},{10,6},{12,0},{14,2},{16,28},{18,... | collective-permute-start | bytes 491528 | tf_op jit(solution)/shard_map/ppermute | solution.py:239
  43.7 12.2 %collective-permute-start.7 = (bf16[5,128,128]{2,1,0:T(8,128)(2,1)S(1)}, bf16[5,128,128]{2,1,0:T(8,128)(2,1)S(1)}, u32[]{:S(2)}, u32[]{:S(2)}) collective-permute-start(bf16[5,128,128]{2,1,0:T(8,128)(2,1)S(1)} %collective-permute-done.5.refs_0_), channel_id=1, source_target_pairs={{0,8},{2,10},{4,12},{6,14},{8,0},{10,2},{12,4},{14,6},{16,24},{18,... | collective-permute-start | bytes 491528 | tf_op jit(solution)/shard_map/ppermute | solution.py:239
  48.2 7.7 %collective-permute-start.6 = (bf16[5,128,128]{2,1,0:T(8,128)(2,1)S(1)}, bf16[5,128,128]{2,1,0:T(8,128)(2,1)S(1)}, u32[]{:S(2)}, u32[]{:S(2)}) collective-permute-start(bf16[5,128,128]{2,1,0:T(8,128)(2,1)S(1)} %collective-permute-done.5.refs_0_), channel_id=1, source_target_pairs={{0,4},{2,6},{4,0},{6,2},{8,12},{10,14},{12,8},{14,10},{16,20},{18,... | collective-permute-start | bytes 491528 | tf_op jit(solution)/shard_map/ppermute | solution.py:239
  53.2 2.8 %collective-permute-start.9 = (bf16[20,128,128]{2,1,0:T(8,128)(2,1)S(1)}, bf16[20,128,128]{2,1,0:T(8,128)(2,1)S(1)}, u32[]{:S(2)}, u32[]{:S(2)}) collective-permute-start(bf16[20,128,128]{2,1,0:T(8,128)(2,1)S(1)} %own_joined.2.rest_0_), channel_id=1, source_target_pairs={{0,2},{2,0},{4,6},{6,4},{8,10},{10,8},{12,14},{14,12},{16,18},{18,... | collective-permute-start | bytes 1966088 | tf_op jit(solution)/shard_map/ppermute | solution.py:239
  56.0 2.2 %collective-permute-start.10 = (bf16[20,128,128]{2,1,0:T(8,128)(2,1)S(1)}, bf16[20,128,128]{2,1,0:T(8,128)(2,1)S(1)}, u32[]{:S(2)}, u32[]{:S(2)}) collective-permute-start(bf16[20,128,128]{2,1,0:T(8,128)(2,1)S(1)} %own_joined.3.rest_1_), channel_id=1, source_target_pairs={{0,2},{2,0},{4,6},{6,4},{8,10},{10,8},{12,14},{14,12},{16,18},{18,... | collective-permute-start | bytes 1966088 | tf_op jit(solution)/shard_map/ppermute | solution.py:239
  60.2 6.9 %collective-permute-start.12 = (bf16[5,128,128]{2,1,0:T(8,128)(2,1)S(1)}, bf16[5,128,128]{2,1,0:T(8,128)(2,1)S(1)}, u32[]{:S(2)}, u32[]{:S(2)}) collective-permute-start(bf16[5,128,128]{2,1,0:T(8,128)(2,1)S(1)} %get-tuple-element.24.mine_ref), channel_id=1, source_target_pairs={{0,1},{1,0},{2,3},{3,2},{4,5},{5,4},{6,7},{7,6},{8,9},{9,8},{10,11... | collective-permute-start | bytes 491528 | tf_op jit(solution)/shard_map/ppermute | solution.py:242
  63.4 6.7 %collective-permute-start.11 = (bf16[5,128,128]{2,1,0:T(8,128)(2,1)S(1)}, bf16[5,128,128]{2,1,0:T(8,128)(2,1)S(1)}, u32[]{:S(2)}, u32[]{:S(2)}) collective-permute-start(bf16[5,128,128]{2,1,0:T(8,128)(2,1)S(1)} %second_layer.3.mine_ref), channel_id=1, source_target_pairs={{0,1},{1,0},{2,3},{3,2},{4,5},{5,4},{6,7},{7,6},{8,9},{9,8},{10,11... | collective-permute-start | bytes 491528 | tf_op jit(solution)/shard_map/ppermute | solution.py:242

commit v15 on v13

--- a/solution.py
+++ b/solution.py
@@ -44,8 +44,12 @@
         fetch(b, part).wait()
         for slot in part:
             col = jnp.where(slot < counts_ref[b], cols_ref[b, slot], groups)
-            block = held_ref[b, slot].astype(jnp.float32)
-            acc_ref[col] += jnp.sum(block.reshape(size // 8, 8, size), axis=0)
+            block = held_ref[b, slot]
+            for _ in range(2):
+                middle = block.shape[0] // 2
+                block = block[:middle] + block[middle:]
+            block = block.astype(jnp.float32).reshape(block.shape[0] // 8, 8, size)
+            acc_ref[col] += jnp.sum(block, axis=0)
 
     for b in range(rows):
         add(b, first)
@@ -115,21 +119,28 @@
     return scale
 
 
-GATHERED = (
-    ((0, 0, 0), (1, 0, 0), (1, 1, 0), (0, 1, 0)),
-    ((0, 0, 1), (0, 1, 1), (1, 0, 1), (1, 1, 1)),
-)
+HOME = ((0, 0, 0), (0, 1, 0), (1, 0, 0), (1, 1, 0))
+AWAY = ((0, 0, 1), (0, 1, 1), (1, 0, 1), (1, 1, 1))
+
+
+def collect(array, places, core, source_ref):
+    part = array.shape[0] // len(places)
+    for i, (z, y, away) in enumerate(places):
+        at = ((z * 4 + y * 2 + core) * 2 + away) * part
+        source_ref[at : at + part] = array[i * part : (i + 1) * part]
+
+
+def collect_kernel(home_ref, away_ref, home_core_ref, source_ref):
+    collect(home_ref, HOME, 0, source_ref)
+    collect(away_ref, AWAY, 0, source_ref)
+    collect(home_core_ref, HOME, 1, source_ref)
 
 
 def second_part_kernel(which, cols_ref, counts_ref, coef_ref, own_ref, *rest):
     part = own_ref.shape[0]
     if which == 0:
-        pieces, (out_ref, source_ref, acc_ref) = rest[:-3], rest[-3:]
-        for number, array in enumerate(pieces):
-            core = number // len(GATHERED)
-            for i, (z, y, away) in enumerate(GATHERED[number % len(GATHERED)]):
-                at = ((z * 4 + y * 2 + core) * 2 + away) * part
-                source_ref[at : at + part] = array[i * part : (i + 1) * part]
+        _, away_core_ref, out_ref, source_ref, acc_ref = rest
+        collect(away_core_ref, AWAY, 1, source_ref)
     else:
         source_ref, out_ref, acc_ref = rest
     side = lax.axis_index("col")
@@ -275,7 +286,8 @@
         return pl.pallas_call(
             kernel,
             name="second_layer",
-            out_shape=(out, jax.ShapeDtypeStruct((groups, size, width), jnp.bfloat16)) if keep_sources else out,
+            out_shape=(out, pltpu.VMEM((groups, size, width), jnp.bfloat16)) if keep_sources else out,
+            input_output_aliases={4: 1} if keep_sources else {},
             in_specs=[SMEM, SMEM] + [VMEM] * (2 + len(sources)),
             out_specs=(VMEM, VMEM) if keep_sources else VMEM,
             scratch_shapes=[pltpu.VMEM((count, size, width), jnp.float32)],
@@ -318,14 +330,23 @@
         )(*pieces)
 
     away = swap(away)
-    near_home = join([home, flip(home, 4), flip(home, 6), flip(home, 2)])
-    near_away = join([away, flip(away, 2), flip(away, 4), flip(away, 6)])
-    gathered = [near_home, near_away]
-    pieces = gathered + [flip(part, 1) for part in gathered]
-
-    part_a, source = second_call(functools.partial(second_part_kernel, 0), half, coefs, own, pieces, True)
+    home, away = [join([part] + [flip(part, mask) for mask in (2, 4, 6)]) for part in (home, away)]
+    home_core, away_core = flip(home, 1), flip(away, 1)
+    source = pl.pallas_call(
+        collect_kernel,
+        name="own_collected",
+        out_shape=pltpu.VMEM((groups, size, width), jnp.bfloat16),
+        in_specs=[VMEM] * 3,
+        out_specs=VMEM,
+        compiler_params=PARAMS,
+        cost_estimate=cost(0, 2 * groups * size * width * 2),
+    )(home, away, home_core)
+
+    part_a, source = second_call(
+        functools.partial(second_part_kernel, 0), half, coefs, own, [in_vmem(source), away_core], True
+    )
     other_a = swap(part_a)
-    part_b = second_call(functools.partial(second_part_kernel, 1), half, coefs, own, [source], False)
+    part_b = second_call(functools.partial(second_part_kernel, 1), half, coefs, own, [in_vmem(source)], False)
     other_b = swap(part_b)
 
     def result(first_row, inputs):

time: 69.1 us -> 67.8 us (0.981)
  starting transfers between devices: 18.5 us -> 23.4 us
  waiting for transfers between devices: 35 us -> 31 us
  Pallas kernels: 15.4 us -> 13.2 us
    ppermute x15, starting transfers between devices: 13.8 us -> 19.2 us  [flip(): return lax.ppermute(array, 'row', [(i, i ^ mask) for i in range(n_row)])]
    ppermute x15, waiting for transfers between devices: 27.6 us -> 22.5 us  [flip(): return lax.ppermute(array, 'row', [(i, i ^ mask) for i in range(n_row)])]
    ppermute x4, waiting for transfers between devices: 7.38 us -> 8.48 us  [swap(): return lax.ppermute(array, 'col', [(0, 1), (1, 0)])]
    pallas_call x2, Pallas kernels: 5.44 us -> 4.39 us  [first_layer(): pl.pallas_call(functools.partial(first_kernel, sending), name='first_laye...]
    pallas_call x2 -> x3, Pallas kernels: 4.24 us -> 3.55 us  [the longest x2 3.42 us: second_call(): pl.pallas_call(kernel, name='second_layer', out_shape=(out, pltpu.VMEM((g...]
  transfers between devices with their start and end apart: 19 -> 19, of which waited for: 14 -> 14; matrix products, arithmetic and copies ran while one was open for 0% -> 0% of each run, Pallas kernels for 8% -> 7%
where the time goes in v15:
time: 67.8 us; the launch traced here: 68.1 us
  waiting for transfers between devices  31 us (46%)
  starting transfers between devices  23.4 us (35%)
  Pallas kernels  13.2 us (19%)
    ppermute x15, waiting for transfers between devices, flip(): return lax.ppermute(array, 'row', [(i, i ^ mask) for i in range(n_row)])  22.5 us
    ppermute x15, starting transfers between devices, flip(): return lax.ppermute(array, 'row', [(i, i ^ mask) for i in range(n_row)])  19.2 us
    ppermute x4, waiting for transfers between devices, swap(): return lax.ppermute(array, 'col', [(0, 1), (1, 0)])  8.48 us
    pallas_call x2, Pallas kernels, first_layer(): pl.pallas_call(functools.partial(first_kernel, sending), name='first_laye...  4.39 us
    ppermute x4, starting transfers between devices, swap(): return lax.ppermute(array, 'col', [(0, 1), (1, 0)])  4.21 us
    pallas_call x1, Pallas kernels, body(): pl.pallas_call(sums_kernel, name='column_sums', out_shape=(jax.ShapeDtype...  3.74 us
    pallas_call x2, Pallas kernels, second_call(): pl.pallas_call(kernel, name='second_layer', out_shape=(out, pltpu.VMEM((g...  3.42 us
    pallas_call x2, Pallas kernels, result(): pl.pallas_call(functools.partial(result_kernel, first_row), name='result'...  1.43 us
  transfers between devices with their start and end apart: 19, of which 14 were waited for; matrix products, arithmetic and copies ran while one was open for 0% of the time, Pallas kernels for 7%

profile of v15, /device:TPU:0, one launch (start us, length us, event | category | flops | bytes accessed | tf_op | source)
XLA Modules:
  0.0 68.1 jit_solution(4811788602724798090)
XLA Ops:
  0.0 0.0 copy-start.1
  0.0 0.0 copy-start.3
  0.0 0.0 copy-start.2
  0.0 0.0 copy-start
  0.0 3.7 %column_sums.1 = (f32[80,128]{1,0:T(8,128)S(1)}, bf16[10,36,128,128]{3,2,1,0:T(8,128)(2,1)S(1)}) custom-call(s32[10,36]{1,0:T(8,128)} %cols_ref.7, s32[10]{0:T(128)} %bitcast.8, bf16[10,36,128,128]{3,2,1,0:T(8,128)(2,1)} %blocks_ref.1), custom_call_target="tpu_custom_call" | custom-call | bytes 23592960 | tf_op jit(solution)/shard_map/column_sums/pallas_call | solution.py:220
  3.8 3.3 %collective-permute-start.1 = (bf16[80,128]{1,0:T(8,128)(2,1)S(1)}, bf16[80,128]{1,0:T(8,128)(2,1)S(1)}, u32[]{:S(2)}, u32[]{:S(2)}) collective-permute-start(bf16[80,128]{1,0:T(8,128)(2,1)S(1)} %convert_element_type.36), channel_id=1, source_target_pairs={{0,4},{2,6},{4,0},{6,2},{8,12},{10,14},{12,8},{14,10},{16,20},{18,... | collective-permute-start | bytes 61448 | tf_op jit(solution)/shard_map/ppermute | solution.py:241
  7.1 0.0 collective-permute-start
  7.1 0.2 collective-permute-start.2
  7.3 1.6 %collective-permute-done.1 = bf16[80,128]{1,0:T(8,128)(2,1)S(1)} collective-permute-done((bf16[80,128]{1,0:T(8,128)(2,1)S(1)}, bf16[80,128]{1,0:T(8,128)(2,1)S(1)}, u32[]{:S(2)}, u32[]{:S(2)}) %collective-permute-start.1) | collective-permute-done | bytes 20512 | tf_op jit(solution)/shard_map/ppermute | solution.py:241
  8.8 0.0 collective-permute-done
  8.8 1.4 %collective-permute-done.2 = bf16[80,128]{1,0:T(8,128)(2,1)S(1)} collective-permute-done((bf16[80,128]{1,0:T(8,128)(2,1)S(1)}, bf16[80,128]{1,0:T(8,128)(2,1)S(1)}, u32[]{:S(2)}, u32[]{:S(2)}) %collective-permute-start.2) | collective-permute-done | bytes 20512 | tf_op jit(solution)/shard_map/ppermute | solution.py:241
  10.3 3.6 %collective-permute-start.5 = (bf16[80,128]{1,0:T(8,128)(2,1)S(1)}, bf16[80,128]{1,0:T(8,128)(2,1)S(1)}, u32[]{:S(2)}, u32[]{:S(2)}) collective-permute-start(bf16[80,128]{1,0:T(8,128)(2,1)S(1)} %add_convert_fusion.1), channel_id=1, source_target_pairs={{0,24},{2,26},{4,28},{6,30},{8,16},{10,18},{12,20},{14,22},{16,8},... | collective-permute-start | bytes 61448 | tf_op jit(solution)/shard_map/ppermute | solution.py:241
  13.9 0.0 collective-permute-start.4
  13.9 0.8 %collective-permute-start.3 = (bf16[80,128]{1,0:T(8,128)(2,1)S(1)}, bf16[80,128]{1,0:T(8,128)(2,1)S(1)}, u32[]{:S(2)}, u32[]{:S(2)}) collective-permute-start(bf16[80,128]{1,0:T(8,128)(2,1)S(1)} %add_convert_fusion.1), channel_id=1, source_target_pairs={{0,8},{2,10},{4,12},{6,14},{8,0},{10,2},{12,4},{14,6},{16,24},{18,... | collective-permute-start | bytes 61448 | tf_op jit(solution)/shard_map/ppermute | solution.py:241
  14.8 1.2 %collective-permute-done.5 = bf16[80,128]{1,0:T(8,128)(2,1)S(1)} collective-permute-done((bf16[80,128]{1,0:T(8,128)(2,1)S(1)}, bf16[80,128]{1,0:T(8,128)(2,1)S(1)}, u32[]{:S(2)}, u32[]{:S(2)}) %collective-permute-start.5) | collective-permute-done | bytes 20512 | tf_op jit(solution)/shard_map/ppermute | solution.py:241
  15.9 2.6 %collective-permute-done.4 = bf16[80,128]{1,0:T(8,128)(2,1)S(1)} collective-permute-done((bf16[80,128]{1,0:T(8,128)(2,1)S(1)}, bf16[80,128]{1,0:T(8,128)(2,1)S(1)}, u32[]{:S(2)}, u32[]{:S(2)}) %collective-permute-start.4) | collective-permute-done | bytes 20512 | tf_op jit(solution)/shard_map/ppermute | solution.py:241
  18.6 0.0 collective-permute-done.3
  18.6 0.0 copy-done.1
  18.6 0.0 copy-done.3
  18.6 0.0 copy-done.2
  18.6 0.0 copy-done
  18.7 2.5 %first_layer.2 = (bf16[5,128,128]{2,1,0:T(8,128)(2,1)S(1)}, bf16[10,36,128,128]{3,2,1,0:T(8,128)(2,1)S(1)}) custom-call(s32[10,36]{1,0:T(8,128)S(1)} %copy-done.1, s32[10]{0:T(128)S(1)} %bitcast.9, f32[80,128]{1,0:T(8,128)S(1)} %convert_add_fusion.sums_ref, f32[80,128]{1,0:T(8,128)S(1)} %bitcast.6, ...), custom_call_target="tpu_custom_call", output_to_operand_aliasing={{1}: (5, {})} | custom-call | flops 754974720 | bytes 5898240 | tf_op jit(solution)/shard_map/first_layer/pallas_call | solution.py:258
  21.1 1.0 %collective-permute-start.6 = (bf16[5,128,128]{2,1,0:T(8,128)(2,1)S(1)}, bf16[5,128,128]{2,1,0:T(8,128)(2,1)S(1)}, u32[]{:S(2)}, u32[]{:S(2)}) collective-permute-start(bf16[5,128,128]{2,1,0:T(8,128)(2,1)S(1)} %get-tuple-element.20), channel_id=1, source_target_pairs={{0,1},{1,0},{2,3},{3,2},{4,5},{5,4},{6,7},{7,6},{8,9},{9,8},{10,11... | collective-permute-start | bytes 491528 | tf_op jit(solution)/shard_map/ppermute | solution.py:244
  22.2 1.9 %first_layer.3 = (f32[5,128,128]{2,1,0:T(8,128)S(1)}, bf16[10,36,128,128]{3,2,1,0:T(8,128)(2,1)S(1)}) custom-call(s32[10,36]{1,0:T(8,128)S(1)} %copy-done.1, s32[10]{0:T(128)S(1)} %bitcast.10, f32[80,128]{1,0:T(8,128)S(1)} %convert_add_fusion.sums_ref, f32[80,128]{1,0:T(8,128)S(1)} %bitcast.7, ...), custom_call_target="tpu_custom_call", output_to_operand_aliasing={{1}: (5, {})} | custom-call | flops 754974720 | bytes 5898240 | tf_op jit(solution)/shard_map/first_layer/pallas_call | solution.py:258
  24.1 2.5 %collective-permute-done.6 = bf16[5,128,128]{2,1,0:T(8,128)(2,1)S(1)} collective-permute-done((bf16[5,128,128]{2,1,0:T(8,128)(2,1)S(1)}, bf16[5,128,128]{2,1,0:T(8,128)(2,1)S(1)}, u32[]{:S(2)}, u32[]{:S(2)}) %collective-permute-start.6) | collective-permute-done | bytes 163872 | tf_op jit(solution)/shard_map/ppermute | solution.py:244
  26.6 2.6 %collective-permute-start.7 = (bf16[5,128,128]{2,1,0:T(8,128)(2,1)S(1)}, bf16[5,128,128]{2,1,0:T(8,128)(2,1)S(1)}, u32[]{:S(2)}, u32[]{:S(2)}) collective-permute-start(bf16[5,128,128]{2,1,0:T(8,128)(2,1)S(1)} %add_convert_fusion.own_ref), channel_id=1, source_target_pairs={{0,16},{2,18},{4,20},{6,22},{8,24},{10,26},{12,28},{14,30},{16,0},... | collective-permute-start | bytes 491528 | tf_op jit(solution)/shard_map/ppermute | solution.py:241
  29.2 6.1 %collective-permute-done.7.crossed_ref = bf16[5,128,128]{2,1,0:T(8,128)(2,1)S(1)} collective-permute-done((bf16[5,128,128]{2,1,0:T(8,128)(2,1)S(1)}, bf16[5,128,128]{2,1,0:T(8,128)(2,1)S(1)}, u32[]{:S(2)}, u32[]{:S(2)}) %collective-permute-start.7) | collective-permute-done | bytes 163872 | tf_op jit(solution)/shard_map/ppermute | solution.py:241
  35.3 1.0 %collective-permute-start.11 = (bf16[5,128,128]{2,1,0:T(8,128)(2,1)S(1)}, bf16[5,128,128]{2,1,0:T(8,128)(2,1)S(1)}, u32[]{:S(2)}, u32[]{:S(2)}) collective-permute-start(bf16[5,128,128]{2,1,0:T(8,128)(2,1)S(1)} %get-tuple-element.22), channel_id=1, source_target_pairs={{0,1},{1,0},{2,3},{3,2},{4,5},{5,4},{6,7},{7,6},{8,9},{9,8},{10,11... | collective-permute-start | bytes 491528 | tf_op jit(solution)/shard_map/ppermute | solution.py:244
  36.3 0.6 collective-permute-start.10
  36.9 2.3 %collective-permute-start.9 = (bf16[5,128,128]{2,1,0:T(8,128)(2,1)S(1)}, bf16[5,128,128]{2,1,0:T(8,128)(2,1)S(1)}, u32[]{:S(2)}, u32[]{:S(2)}) collective-permute-start(bf16[5,128,128]{2,1,0:T(8,128)(2,1)S(1)} %get-tuple-element.21.refs_0_), channel_id=1, source_target_pairs={{0,8},{2,10},{4,12},{6,14},{8,0},{10,2},{12,4},{14,6},{16,24},{18,... | collective-permute-start | bytes 491528 | tf_op jit(solution)/shard_map/ppermute | solution.py:241
  39.2 0.6 collective-permute-start.8
  39.8 0.9 %collective-permute-done.11.refs_0_ = bf16[5,128,128]{2,1,0:T(8,128)(2,1)S(1)} collective-permute-done((bf16[5,128,128]{2,1,0:T(8,128)(2,1)S(1)}, bf16[5,128,128]{2,1,0:T(8,128)(2,1)S(1)}, u32[]{:S(2)}, u32[]{:S(2)}) %collective-permute-start.11) | collective-permute-done | bytes 163872 | tf_op jit(solution)/shard_map/ppermute | solution.py:244
  40.7 0.0 collective-permute-start.14
  40.7 4.2 %collective-permute-start.13 = (bf16[5,128,128]{2,1,0:T(8,128)(2,1)S(1)}, bf16[5,128,128]{2,1,0:T(8,128)(2,1)S(1)}, u32[]{:S(2)}, u32[]{:S(2)}) collective-permute-start(bf16[5,128,128]{2,1,0:T(8,128)(2,1)S(1)} %collective-permute-done.11.refs_0_), channel_id=1, source_target_pairs={{0,8},{2,10},{4,12},{6,14},{8,0},{10,2},{12,4},{14,6},{16,24},{18,... | collective-permute-start | bytes 491528 | tf_op jit(solution)/shard_map/ppermute | solution.py:241
  44.9 0.0 collective-permute-done.10.refs_3_
  44.9 0.9 %collective-permute-start.12 = (bf16[5,128,128]{2,1,0:T(8,128)(2,1)S(1)}, bf16[5,128,128]{2,1,0:T(8,128)(2,1)S(1)}, u32[]{:S(2)}, u32[]{:S(2)}) collective-permute-start(bf16[5,128,128]{2,1,0:T(8,128)(2,1)S(1)} %collective-permute-done.11.refs_0_), channel_id=1, source_target_pairs={{0,4},{2,6},{4,0},{6,2},{8,12},{10,14},{12,8},{14,10},{16,20},{18,... | collective-permute-start | bytes 491528 | tf_op jit(solution)/shard_map/ppermute | solution.py:241
  45.8 2.0 %collective-permute-done.9.refs_2_ = bf16[5,128,128]{2,1,0:T(8,128)(2,1)S(1)} collective-permute-done((bf16[5,128,128]{2,1,0:T(8,128)(2,1)S(1)}, bf16[5,128,128]{2,1,0:T(8,128)(2,1)S(1)}, u32[]{:S(2)}, u32[]{:S(2)}) %collective-permute-start.9) | collective-permute-done | bytes 163872 | tf_op jit(solution)/shard_map/ppermute | solution.py:241
  47.8 2.1 %collective-permute-done.8.refs_1_ = bf16[5,128,128]{2,1,0:T(8,128)(2,1)S(1)} collective-permute-done((bf16[5,128,128]{2,1,0:T(8,128)(2,1)S(1)}, bf16[5,128,128]{2,1,0:T(8,128)(2,1)S(1)}, u32[]{:S(2)}, u32[]{:S(2)}) %collective-permute-start.8) | collective-permute-done | bytes 163872 | tf_op jit(solution)/shard_map/ppermute | solution.py:241
  49.9 0.1 collective-permute-start.15
  50.0 1.1 %collective-permute-done.14.refs_3_ = bf16[5,128,128]{2,1,0:T(8,128)(2,1)S(1)} collective-permute-done((bf16[5,128,128]{2,1,0:T(8,128)(2,1)S(1)}, bf16[5,128,128]{2,1,0:T(8,128)(2,1)S(1)}, u32[]{:S(2)}, u32[]{:S(2)}) %collective-permute-start.14) | collective-permute-done | bytes 163872 | tf_op jit(solution)/shard_map/ppermute | solution.py:241
  51.1 2.4 %collective-permute-done.13.refs_2_ = bf16[5,128,128]{2,1,0:T(8,128)(2,1)S(1)} collective-permute-done((bf16[5,128,128]{2,1,0:T(8,128)(2,1)S(1)}, bf16[5,128,128]{2,1,0:T(8,128)(2,1)S(1)}, u32[]{:S(2)}, u32[]{:S(2)}) %collective-permute-start.13) | collective-permute-done | bytes 163872 | tf_op jit(solution)/shard_map/ppermute | solution.py:241
  53.5 0.0 collective-permute-done.12.refs_1_
  53.5 0.1 collective-permute-start.16
  53.6 0.0 collective-permute-done.15.home_core_ref
  53.6 0.1 own_collected.1.rest_0_
  53.8 1.9 %collective-permute-done.16.rest_1_ = bf16[20,128,128]{2,1,0:T(8,128)(2,1)S(1)} collective-permute-done((bf16[20,128,128]{2,1,0:T(8,128)(2,1)S(1)}, bf16[20,128,128]{2,1,0:T(8,128)(2,1)S(1)}, u32[]{:S(2)}, u32[]{:S(2)}) %collective-permute-start.16) | collective-permute-done | bytes 655392 | tf_op jit(solution)/shard_map/ppermute | solution.py:241
  55.7 1.6 %second_layer.2 = (bf16[5,128,128]{2,1,0:T(8,128)(2,1)S(1)}, bf16[80,128,128]{2,1,0:T(8,128)(2,1)S(1)}) custom-call(s32[10,36]{1,0:T(8,128)S(1)} %copy-done.1, s32[10]{0:T(128)S(1)} %bitcast.11, bf16[10,36,128,128]{3,2,1,0:T(8,128)(2,1)S(1)} %get-tuple-element.18.coef_ref, ...), custom_call_target="tpu_custom_call", output_to_operand_aliasing={{1}: (4, {})} | custom-call | flops 754974720 | bytes 5898240 | tf_op jit(solution)/shard_map/second_layer/pallas_call | solution.py:286
  57.4 1.8 %collective-permute-start.18 = (bf16[5,128,128]{2,1,0:T(8,128)(2,1)S(1)}, bf16[5,128,128]{2,1,0:T(8,128)(2,1)S(1)}, u32[]{:S(2)}, u32[]{:S(2)}) collective-permute-start(bf16[5,128,128]{2,1,0:T(8,128)(2,1)S(1)} %get-tuple-element.24.mine_ref), channel_id=1, source_target_pairs={{0,1},{1,0},{2,3},{3,2},{4,5},{5,4},{6,7},{7,6},{8,9},{9,8},{10,11... | collective-permute-start | bytes 491528 | tf_op jit(solution)/shard_map/ppermute | solution.py:244
  59.1 1.8 %second_layer.3.mine_ref = bf16[5,128,128]{2,1,0:T(8,128)(2,1)S(1)} custom-call(s32[10,36]{1,0:T(8,128)S(1)} %copy-done.1, s32[10]{0:T(128)S(1)} %bitcast.12, bf16[10,36,128,128]{3,2,1,0:T(8,128)(2,1)S(1)} %get-tuple-element.18.coef_ref, bf16[5,128,128]{2,1,0:T(8,128)(2,1)S(1)} %add_convert_fusion.own_ref, bf16[80,128,128]{2,1,0:T(8,128)(2,1)S(1)} %get-tuple-element.23.rest_0_), custom_call_target="tpu_custom_call" | custom-call | flops 754974720 | bytes 5898240 | tf_op jit(solution)/shard_map/second_layer/pallas_call | solution.py:286
  60.9 0.4 collective-permute-start.17
  61.3 2.5 %collective-permute-done.18.other_ref = bf16[5,128,128]{2,1,0:T(8,128)(2,1)S(1)} collective-permute-done((bf16[5,128,128]{2,1,0:T(8,128)(2,1)S(1)}, bf16[5,128,128]{2,1,0:T(8,128)(2,1)S(1)}, u32[]{:S(2)}, u32[]{:S(2)}) %collective-permute-start.18) | collective-permute-done | bytes 163872 | tf_op jit(solution)/shard_map/ppermute | solution.py:244
  63.8 0.7 %result.2.rest_0_ = bf16[10,128,128]{2,1,0:T(8,128)(2,1)} custom-call(bf16[5,128,128]{2,1,0:T(8,128)(2,1)S(1)} %get-tuple-element.24.mine_ref, bf16[5,128,128]{2,1,0:T(8,128)(2,1)S(1)} %collective-permute-done.18.other_ref), custom_call_target="tpu_custom_call" | custom-call | tf_op jit(solution)/shard_map/result/pallas_call | solution.py:353
  64.5 2.6 %collective-permute-done.17.other_ref = bf16[5,128,128]{2,1,0:T(8,128)(2,1)S(1)} collective-permute-done((bf16[5,128,128]{2,1,0:T(8,128)(2,1)S(1)}, bf16[5,128,128]{2,1,0:T(8,128)(2,1)S(1)}, u32[]{:S(2)}, u32[]{:S(2)}) %collective-permute-start.17) | collective-permute-done | bytes 163872 | tf_op jit(solution)/shard_map/ppermute | solution.py:244
  67.2 0.7 %result.3 = bf16[10,128,128]{2,1,0:T(8,128)(2,1)} custom-call(bf16[5,128,128]{2,1,0:T(8,128)(2,1)S(1)} %second_layer.3.mine_ref, bf16[5,128,128]{2,1,0:T(8,128)(2,1)S(1)} %collective-permute-done.17.other_ref, bf16[10,128,128]{2,1,0:T(8,128)(2,1)} %result.2.rest_0_), custom_call_target="tpu_custom_call", output_to_operand_aliasing={{}: (2, {})} | custom-call | tf_op jit(solution)/shard_map/result/pallas_call | solution.py:353
  (7 shorter events, 0.2 us)
Async XLA Ops:
  0.0 18.6 %copy-start.1 = (s32[10,36]{1,0:T(8,128)S(1)}, s32[10,36]{1,0:T(8,128)}, u32[]{:S(2)}) copy-start(s32[10,36]{1,0:T(8,128)} %cols_ref.7) | copy-start | bytes 4324
  0.0 18.6 %copy-start.3 = (s32[10,1]{0,1:T(1,128)S(1)}, s32[10,1]{0,1:T(1,128)}, u32[]{:S(2)}) copy-start(s32[10,1]{0,1:T(1,128)} %param.7) | copy-start | bytes 124
  0.0 18.6 %copy-start.2 = (f32[10240]{0:T(1024)S(1)}, f32[10240]{0:T(1024)}, u32[]{:S(2)}) copy-start(f32[10240]{0:T(1024)} %param.9) | copy-start | bytes 122884
  0.0 18.6 %copy-start = (bf16[10240,128]{1,0:T(8,128)(2,1)S(1)}, bf16[10240,128]{1,0:T(8,128)(2,1)}, u32[]{:S(2)}) copy-start(bf16[10240,128]{1,0:T(8,128)(2,1)} %param.8) | copy-start | bytes 7864324
  3.8 5.1 %collective-permute-start.1 = (bf16[80,128]{1,0:T(8,128)(2,1)S(1)}, bf16[80,128]{1,0:T(8,128)(2,1)S(1)}, u32[]{:S(2)}, u32[]{:S(2)}) collective-permute-start(bf16[80,128]{1,0:T(8,128)(2,1)S(1)} %convert_element_type.36), channel_id=1, source_target_pairs={{0,4},{2,6},{4,0},{6,2},{8,12},{10,14},{12,8},{14,10},{16,20},{18,... | collective-permute-start | bytes 61448 | tf_op jit(solution)/shard_map/ppermute | solution.py:241
  7.1 1.8 %collective-permute-start = (bf16[80,128]{1,0:T(8,128)(2,1)S(1)}, bf16[80,128]{1,0:T(8,128)(2,1)S(1)}, u32[]{:S(2)}, u32[]{:S(2)}) collective-permute-start(bf16[80,128]{1,0:T(8,128)(2,1)S(1)} %convert_element_type.36), channel_id=1, source_target_pairs={{0,2},{2,0},{4,6},{6,4},{8,10},{10,8},{12,14},{14,12},{16,18},{18,... | collective-permute-start | bytes 61448 | tf_op jit(solution)/shard_map/ppermute | solution.py:241
  7.1 3.2 %collective-permute-start.2 = (bf16[80,128]{1,0:T(8,128)(2,1)S(1)}, bf16[80,128]{1,0:T(8,128)(2,1)S(1)}, u32[]{:S(2)}, u32[]{:S(2)}) collective-permute-start(bf16[80,128]{1,0:T(8,128)(2,1)S(1)} %convert_element_type.36), channel_id=1, source_target_pairs={{0,6},{2,4},{4,2},{6,0},{8,14},{10,12},{12,10},{14,8},{16,22},{18,... | collective-permute-start | bytes 61448 | tf_op jit(solution)/shard_map/ppermute | solution.py:241
  10.3 5.6 %collective-permute-start.5 = (bf16[80,128]{1,0:T(8,128)(2,1)S(1)}, bf16[80,128]{1,0:T(8,128)(2,1)S(1)}, u32[]{:S(2)}, u32[]{:S(2)}) collective-permute-start(bf16[80,128]{1,0:T(8,128)(2,1)S(1)} %add_convert_fusion.1), channel_id=1, source_target_pairs={{0,24},{2,26},{4,28},{6,30},{8,16},{10,18},{12,20},{14,22},{16,8},... | collective-permute-start | bytes 61448 | tf_op jit(solution)/shard_map/ppermute | solution.py:241
  13.9 4.7 %collective-permute-start.4 = (bf16[80,128]{1,0:T(8,128)(2,1)S(1)}, bf16[80,128]{1,0:T(8,128)(2,1)S(1)}, u32[]{:S(2)}, u32[]{:S(2)}) collective-permute-start(bf16[80,128]{1,0:T(8,128)(2,1)S(1)} %add_convert_fusion.1), channel_id=1, source_target_pairs={{0,16},{2,18},{4,20},{6,22},{8,24},{10,26},{12,28},{14,30},{16,0},... | collective-permute-start | bytes 61448 | tf_op jit(solution)/shard_map/ppermute | solution.py:241
  13.9 4.7 %collective-permute-start.3 = (bf16[80,128]{1,0:T(8,128)(2,1)S(1)}, bf16[80,128]{1,0:T(8,128)(2,1)S(1)}, u32[]{:S(2)}, u32[]{:S(2)}) collective-permute-start(bf16[80,128]{1,0:T(8,128)(2,1)S(1)} %add_convert_fusion.1), channel_id=1, source_target_pairs={{0,8},{2,10},{4,12},{6,14},{8,0},{10,2},{12,4},{14,6},{16,24},{18,... | collective-permute-start | bytes 61448 | tf_op jit(solution)/shard_map/ppermute | solution.py:241
  21.1 5.4 %collective-permute-start.6 = (bf16[5,128,128]{2,1,0:T(8,128)(2,1)S(1)}, bf16[5,128,128]{2,1,0:T(8,128)(2,1)S(1)}, u32[]{:S(2)}, u32[]{:S(2)}) collective-permute-start(bf16[5,128,128]{2,1,0:T(8,128)(2,1)S(1)} %get-tuple-element.20), channel_id=1, source_target_pairs={{0,1},{1,0},{2,3},{3,2},{4,5},{5,4},{6,7},{7,6},{8,9},{9,8},{10,11... | collective-permute-start | bytes 491528 | tf_op jit(solution)/shard_map/ppermute | solution.py:244
  26.6 8.6 %collective-permute-start.7 = (bf16[5,128,128]{2,1,0:T(8,128)(2,1)S(1)}, bf16[5,128,128]{2,1,0:T(8,128)(2,1)S(1)}, u32[]{:S(2)}, u32[]{:S(2)}) collective-permute-start(bf16[5,128,128]{2,1,0:T(8,128)(2,1)S(1)} %add_convert_fusion.own_ref), channel_id=1, source_target_pairs={{0,16},{2,18},{4,20},{6,22},{8,24},{10,26},{12,28},{14,30},{16,0},... | collective-permute-start | bytes 491528 | tf_op jit(solution)/shard_map/ppermute | solution.py:241
  35.3 5.4 %collective-permute-start.11 = (bf16[5,128,128]{2,1,0:T(8,128)(2,1)S(1)}, bf16[5,128,128]{2,1,0:T(8,128)(2,1)S(1)}, u32[]{:S(2)}, u32[]{:S(2)}) collective-permute-start(bf16[5,128,128]{2,1,0:T(8,128)(2,1)S(1)} %get-tuple-element.22), channel_id=1, source_target_pairs={{0,1},{1,0},{2,3},{3,2},{4,5},{5,4},{6,7},{7,6},{8,9},{9,8},{10,11... | collective-permute-start | bytes 491528 | tf_op jit(solution)/shard_map/ppermute | solution.py:244
  36.3 8.6 %collective-permute-start.10 = (bf16[5,128,128]{2,1,0:T(8,128)(2,1)S(1)}, bf16[5,128,128]{2,1,0:T(8,128)(2,1)S(1)}, u32[]{:S(2)}, u32[]{:S(2)}) collective-permute-start(bf16[5,128,128]{2,1,0:T(8,128)(2,1)S(1)} %get-tuple-element.21.refs_0_), channel_id=1, source_target_pairs={{0,12},{2,14},{4,8},{6,10},{8,4},{10,6},{12,0},{14,2},{16,28},{18,... | collective-permute-start | bytes 491528 | tf_op jit(solution)/shard_map/ppermute | solution.py:241
  36.9 10.9 %collective-permute-start.9 = (bf16[5,128,128]{2,1,0:T(8,128)(2,1)S(1)}, bf16[5,128,128]{2,1,0:T(8,128)(2,1)S(1)}, u32[]{:S(2)}, u32[]{:S(2)}) collective-permute-start(bf16[5,128,128]{2,1,0:T(8,128)(2,1)S(1)} %get-tuple-element.21.refs_0_), channel_id=1, source_target_pairs={{0,8},{2,10},{4,12},{6,14},{8,0},{10,2},{12,4},{14,6},{16,24},{18,... | collective-permute-start | bytes 491528 | tf_op jit(solution)/shard_map/ppermute | solution.py:241
  39.2 10.7 %collective-permute-start.8 = (bf16[5,128,128]{2,1,0:T(8,128)(2,1)S(1)}, bf16[5,128,128]{2,1,0:T(8,128)(2,1)S(1)}, u32[]{:S(2)}, u32[]{:S(2)}) collective-permute-start(bf16[5,128,128]{2,1,0:T(8,128)(2,1)S(1)} %get-tuple-element.21.refs_0_), channel_id=1, source_target_pairs={{0,4},{2,6},{4,0},{6,2},{8,12},{10,14},{12,8},{14,10},{16,20},{18,... | collective-permute-start | bytes 491528 | tf_op jit(solution)/shard_map/ppermute | solution.py:241
  40.7 10.4 %collective-permute-start.14 = (bf16[5,128,128]{2,1,0:T(8,128)(2,1)S(1)}, bf16[5,128,128]{2,1,0:T(8,128)(2,1)S(1)}, u32[]{:S(2)}, u32[]{:S(2)}) collective-permute-start(bf16[5,128,128]{2,1,0:T(8,128)(2,1)S(1)} %collective-permute-done.11.refs_0_), channel_id=1, source_target_pairs={{0,12},{2,14},{4,8},{6,10},{8,4},{10,6},{12,0},{14,2},{16,28},{18,... | collective-permute-start | bytes 491528 | tf_op jit(solution)/shard_map/ppermute | solution.py:241
  40.7 12.8 %collective-permute-start.13 = (bf16[5,128,128]{2,1,0:T(8,128)(2,1)S(1)}, bf16[5,128,128]{2,1,0:T(8,128)(2,1)S(1)}, u32[]{:S(2)}, u32[]{:S(2)}) collective-permute-start(bf16[5,128,128]{2,1,0:T(8,128)(2,1)S(1)} %collective-permute-done.11.refs_0_), channel_id=1, source_target_pairs={{0,8},{2,10},{4,12},{6,14},{8,0},{10,2},{12,4},{14,6},{16,24},{18,... | collective-permute-start | bytes 491528 | tf_op jit(solution)/shard_map/ppermute | solution.py:241
  44.9 8.6 %collective-permute-start.12 = (bf16[5,128,128]{2,1,0:T(8,128)(2,1)S(1)}, bf16[5,128,128]{2,1,0:T(8,128)(2,1)S(1)}, u32[]{:S(2)}, u32[]{:S(2)}) collective-permute-start(bf16[5,128,128]{2,1,0:T(8,128)(2,1)S(1)} %collective-permute-done.11.refs_0_), channel_id=1, source_target_pairs={{0,4},{2,6},{4,0},{6,2},{8,12},{10,14},{12,8},{14,10},{16,20},{18,... | collective-permute-start | bytes 491528 | tf_op jit(solution)/shard_map/ppermute | solution.py:241
  49.9 3.7 %collective-permute-start.15 = (bf16[20,128,128]{2,1,0:T(8,128)(2,1)S(1)}, bf16[20,128,128]{2,1,0:T(8,128)(2,1)S(1)}, u32[]{:S(2)}, u32[]{:S(2)}) collective-permute-start(bf16[20,128,128]{2,1,0:T(8,128)(2,1)S(1)} %own_joined.2.home_ref), channel_id=1, source_target_pairs={{0,2},{2,0},{4,6},{6,4},{8,10},{10,8},{12,14},{14,12},{16,18},{18,... | collective-permute-start | bytes 1966088 | tf_op jit(solution)/shard_map/ppermute | solution.py:241
  53.5 2.2 %collective-permute-start.16 = (bf16[20,128,128]{2,1,0:T(8,128)(2,1)S(1)}, bf16[20,128,128]{2,1,0:T(8,128)(2,1)S(1)}, u32[]{:S(2)}, u32[]{:S(2)}) collective-permute-start(bf16[20,128,128]{2,1,0:T(8,128)(2,1)S(1)} %own_joined.3.away_ref), channel_id=1, source_target_pairs={{0,2},{2,0},{4,6},{6,4},{8,10},{10,8},{12,14},{14,12},{16,18},{18,... | collective-permute-start | bytes 1966088 | tf_op jit(solution)/shard_map/ppermute | solution.py:241
  57.4 6.5 %collective-permute-start.18 = (bf16[5,128,128]{2,1,0:T(8,128)(2,1)S(1)}, bf16[5,128,128]{2,1,0:T(8,128)(2,1)S(1)}, u32[]{:S(2)}, u32[]{:S(2)}) collective-permute-start(bf16[5,128,128]{2,1,0:T(8,128)(2,1)S(1)} %get-tuple-element.24.mine_ref), channel_id=1, source_target_pairs={{0,1},{1,0},{2,3},{3,2},{4,5},{5,4},{6,7},{7,6},{8,9},{9,8},{10,11... | collective-permute-start | bytes 491528 | tf_op jit(solution)/shard_map/ppermute | solution.py:244
  60.9 6.3 %collective-permute-start.17 = (bf16[5,128,128]{2,1,0:T(8,128)(2,1)S(1)}, bf16[5,128,128]{2,1,0:T(8,128)(2,1)S(1)}, u32[]{:S(2)}, u32[]{:S(2)}) collective-permute-start(bf16[5,128,128]{2,1,0:T(8,128)(2,1)S(1)} %second_layer.3.mine_ref), channel_id=1, source_target_pairs={{0,1},{1,0},{2,3},{3,2},{4,5},{5,4},{6,7},{7,6},{8,9},{9,8},{10,11... | collective-permute-start | bytes 491528 | tf_op jit(solution)/shard_map/ppermute | solution.py:244

commit v16 on v15

--- a/solution.py
+++ b/solution.py
@@ -15,9 +15,9 @@
     return [range(first)] + ([range(first, slots)] if slots > first else [])
 
 
-def sums_kernel(cols_hbm, counts_hbm, blocks_ref, sums_ref, held_ref, acc_ref, cols_ref, counts_ref, list_sems, sems):
+def sums_kernel(cols_hbm, counts_hbm, blocks_ref, sums_ref, held_ref, cols_ref, counts_ref, list_sems, sems, *acc_refs):
     rows, slots, size, _ = blocks_ref.shape
-    groups = acc_ref.shape[0] - 1
+    groups = acc_refs[0].shape[0] - 1
     first, *others = slot_ranges(slots)
 
     def fetch(b, part):
@@ -30,7 +30,8 @@
     cols_copy.start()
     for b in range(rows):
         fetch(b, first).start()
-    acc_ref[...] = jnp.zeros_like(acc_ref)
+    for acc_ref in acc_refs:
+        acc_ref[...] = jnp.zeros_like(acc_ref)
     counts_copy.wait()
     cols_copy.wait()
     for b in range(rows):
@@ -49,7 +50,7 @@
                 middle = block.shape[0] // 2
                 block = block[:middle] + block[middle:]
             block = block.astype(jnp.float32).reshape(block.shape[0] // 8, 8, size)
-            acc_ref[col] += jnp.sum(block, axis=0)
+            acc_refs[slot % len(acc_refs)][col] += jnp.sum(block, axis=0)
 
     for b in range(rows):
         add(b, first)
@@ -60,7 +61,7 @@
             def _(b=b, part=part):
                 add(b, part)
 
-    sums_ref[...] = jnp.sum(acc_ref[:groups], axis=1)
+    sums_ref[...] = jnp.sum(functools.reduce(jnp.add, [acc_ref[:groups] for acc_ref in acc_refs]), axis=1)
 
 
 def multiply_rows(rows, counts_ref, slots, start, gather, acc_ref):
@@ -227,12 +228,12 @@
         in_specs=[pl.BlockSpec(memory_space=pltpu.HBM)] * 3,
         out_specs=(VMEM, VMEM),
         scratch_shapes=[
-            pltpu.VMEM((groups + 1, 8, size), jnp.float32),
             pltpu.SMEM(slot_cols.shape, jnp.int32),
             pltpu.SMEM(counts.shape, jnp.int32),
             pltpu.SemaphoreType.DMA((2,)),
             pltpu.SemaphoreType.DMA((rows, 2)),
-        ],
+        ]
+        + [pltpu.VMEM((groups + 1, 8, size), jnp.float32)] * 4,
         compiler_params=PARAMS,
         cost_estimate=cost(0, 4 * rows * size * size * slots),
     )(*[pltpu.with_memory_space_constraint(array, pltpu.HBM) for array in (slot_cols, counts, blocks)])
@@ -244,10 +245,13 @@
         return lax.ppermute(array, "col", [(0, 1), (1, 0)])
 
     if paired:
-        for masks in ((1, 2, 3), (4, 8, 12)):
-            sums = sums.astype(jnp.bfloat16)
-            parts = [sums] + [flip(sums, m) for m in masks]
-            sums = functools.reduce(jnp.add, [part.astype(jnp.float32) for part in parts])
+        sums = sums + flip(sums.astype(jnp.bfloat16), 1).astype(jnp.float32)
+        shared = sums.astype(jnp.bfloat16)
+        parts = []
+        for masks in ((0, 8), (2, 10), (4, 12), (6, 14)):
+            parts.append(lax.ppermute(shared, "row", [(i, i ^ masks[i % 2]) for i in range(n_row)]))
+        sums = functools.reduce(jnp.add, [part.astype(jnp.float32) for part in parts])
+        sums = sums + flip(sums.astype(jnp.bfloat16), 1).astype(jnp.float32)
     else:
         sums = lax.psum(sums, "row")
 

time: 67.8 us -> 69.9 us (1.031)
  starting transfers between devices: 23.4 us -> 25.1 us
    ppermute x0 -> x4, starting transfers between devices: none -> 5.43 us  [body(): lax.ppermute(shared, 'row', [(i, i ^ masks[i % 2]) for i in range(n_row)])]
    ppermute x15 -> x11, starting transfers between devices: 19.2 us -> 14 us  [flip(): return lax.ppermute(array, 'row', [(i, i ^ mask) for i in range(n_row)])]
    ppermute x0 -> x4, waiting for transfers between devices: none -> 2.75 us  [body(): lax.ppermute(shared, 'row', [(i, i ^ masks[i % 2]) for i in range(n_row)])]
    ppermute x15 -> x11, waiting for transfers between devices: 22.5 us -> 20.2 us  [flip(): return lax.ppermute(array, 'row', [(i, i ^ mask) for i in range(n_row)])]
    ppermute x4, starting transfers between devices: 4.21 us -> 5.73 us  [swap(): return lax.ppermute(array, 'col', [(0, 1), (1, 0)])]
  transfers between devices with their start and end apart: 19 -> 19, of which waited for: 14 -> 17; matrix products, arithmetic and copies ran while one was open for 0% -> 0% of each run, Pallas kernels for 7% -> 7%
where the time goes in v16:
time: 69.9 us
  waiting for transfers between devices  31.1 us (44%)
  starting transfers between devices  25.1 us (36%)
  Pallas kernels  13.3 us (19%)
    ppermute x11, waiting for transfers between devices, flip(): return lax.ppermute(array, 'row', [(i, i ^ mask) for i in range(n_row)])  20.2 us
    ppermute x11, starting transfers between devices, flip(): return lax.ppermute(array, 'row', [(i, i ^ mask) for i in range(n_row)])  14 us
    ppermute x4, waiting for transfers between devices, swap(): return lax.ppermute(array, 'col', [(0, 1), (1, 0)])  8.17 us
    ppermute x4, starting transfers between devices, swap(): return lax.ppermute(array, 'col', [(0, 1), (1, 0)])  5.73 us
    ppermute x4, starting transfers between devices, body(): lax.ppermute(shared, 'row', [(i, i ^ masks[i % 2]) for i in range(n_row)])  5.43 us
    pallas_call x2, Pallas kernels, first_layer(): pl.pallas_call(functools.partial(first_kernel, sending), name='first_laye...  4.39 us
    pallas_call x1, Pallas kernels, body(): pl.pallas_call(sums_kernel, name='column_sums', out_shape=(jax.ShapeDtype...  3.8 us
    pallas_call x2, Pallas kernels, second_call(): pl.pallas_call(kernel, name='second_layer', out_shape=(out, pltpu.VMEM((g...  3.41 us
  transfers between devices with their start and end apart: 19, of which 17 were waited for; matrix products, arithmetic and copies ran while one was open for 0% of the time, Pallas kernels for 7%

profile of v16, /device:TPU:0, one launch (start us, length us, event | category | flops | bytes accessed | tf_op | source)
XLA Modules:
  0.0 69.9 jit_solution(14548734654446229929)
XLA Ops:
  0.0 0.0 copy-start.1
  0.0 0.0 copy-start.3
  0.0 0.0 copy-start.2
  0.0 0.0 copy-start
  0.0 3.8 %column_sums.1 = (f32[80,128]{1,0:T(8,128)S(1)}, bf16[10,36,128,128]{3,2,1,0:T(8,128)(2,1)S(1)}) custom-call(s32[10,36]{1,0:T(8,128)} %cols_ref.7, s32[10]{0:T(128)} %bitcast.8, bf16[10,36,128,128]{3,2,1,0:T(8,128)(2,1)} %blocks_ref.1), custom_call_target="tpu_custom_call" | custom-call | bytes 23592960 | tf_op jit(solution)/shard_map/column_sums/pallas_call | solution.py:221
  3.8 0.5 collective-permute-start
  4.3 0.8 %collective-permute-done = bf16[80,128]{1,0:T(8,128)(2,1)S(1)} collective-permute-done((bf16[80,128]{1,0:T(8,128)(2,1)S(1)}, bf16[80,128]{1,0:T(8,128)(2,1)S(1)}, u32[]{:S(2)}, u32[]{:S(2)}) %collective-permute-start) | collective-permute-done | bytes 20512 | tf_op jit(solution)/shard_map/ppermute | solution.py:242
  5.2 4.1 %collective-permute-start.4 = (bf16[80,128]{1,0:T(8,128)(2,1)S(1)}, bf16[80,128]{1,0:T(8,128)(2,1)S(1)}, u32[]{:S(2)}, u32[]{:S(2)}) collective-permute-start(bf16[80,128]{1,0:T(8,128)(2,1)S(1)} %add_convert_fusion.1), channel_id=1, source_target_pairs={{0,12},{2,30},{4,8},{6,26},{8,4},{10,22},{12,0},{14,18},{16,28},{1... | collective-permute-start | bytes 61448 | tf_op jit(solution)/shard_map/ppermute | solution.py:252
  9.3 0.3 collective-permute-start.3
  9.6 0.4 collective-permute-start.2
  10.0 0.7 collective-permute-start.1
  10.6 0.5 collective-permute-done.4
  11.1 2.0 %collective-permute-done.3 = bf16[80,128]{1,0:T(8,128)(2,1)S(1)} collective-permute-done((bf16[80,128]{1,0:T(8,128)(2,1)S(1)}, bf16[80,128]{1,0:T(8,128)(2,1)S(1)}, u32[]{:S(2)}, u32[]{:S(2)}) %collective-permute-start.3) | collective-permute-done | bytes 20512 | tf_op jit(solution)/shard_map/ppermute | solution.py:252
  13.1 0.3 collective-permute-done.2
  13.4 0.0 collective-permute-done.1
  13.4 4.0 %collective-permute-start.5 = (bf16[80,128]{1,0:T(8,128)(2,1)S(1)}, bf16[80,128]{1,0:T(8,128)(2,1)S(1)}, u32[]{:S(2)}, u32[]{:S(2)}) collective-permute-start(bf16[80,128]{1,0:T(8,128)(2,1)S(1)} %fusion), channel_id=1, source_target_pairs={{0,2},{2,0},{4,6},{6,4},{8,10},{10,8},{12,14},{14,12},{16,18},{18,... | collective-permute-start | bytes 61448 | tf_op jit(solution)/shard_map/ppermute | solution.py:242
  17.4 0.8 %collective-permute-done.5 = bf16[80,128]{1,0:T(8,128)(2,1)S(1)} collective-permute-done((bf16[80,128]{1,0:T(8,128)(2,1)S(1)}, bf16[80,128]{1,0:T(8,128)(2,1)S(1)}, u32[]{:S(2)}, u32[]{:S(2)}) %collective-permute-start.5) | collective-permute-done | bytes 20512 | tf_op jit(solution)/shard_map/ppermute | solution.py:242
  18.2 0.0 copy-done.1
  18.2 0.0 copy-done.3
  18.2 0.0 copy-done.2
  18.2 0.0 copy-done
  18.3 1.9 %first_layer.2 = (bf16[5,128,128]{2,1,0:T(8,128)(2,1)S(1)}, bf16[10,36,128,128]{3,2,1,0:T(8,128)(2,1)S(1)}) custom-call(s32[10,36]{1,0:T(8,128)S(1)} %copy-done.1, s32[10]{0:T(128)S(1)} %bitcast.9, f32[80,128]{1,0:T(8,128)S(1)} %convert_add_fusion.sums_ref, f32[80,128]{1,0:T(8,128)S(1)} %bitcast.6, ...), custom_call_target="tpu_custom_call", output_to_operand_aliasing={{1}: (5, {})} | custom-call | flops 754974720 | bytes 5898240 | tf_op jit(solution)/shard_map/first_layer/pallas_call | solution.py:262
  20.2 2.1 %collective-permute-start.6 = (bf16[5,128,128]{2,1,0:T(8,128)(2,1)S(1)}, bf16[5,128,128]{2,1,0:T(8,128)(2,1)S(1)}, u32[]{:S(2)}, u32[]{:S(2)}) collective-permute-start(bf16[5,128,128]{2,1,0:T(8,128)(2,1)S(1)} %get-tuple-element.20), channel_id=1, source_target_pairs={{0,1},{1,0},{2,3},{3,2},{4,5},{5,4},{6,7},{7,6},{8,9},{9,8},{10,11... | collective-permute-start | bytes 491528 | tf_op jit(solution)/shard_map/ppermute | solution.py:245
  22.3 2.5 %first_layer.3 = (f32[5,128,128]{2,1,0:T(8,128)S(1)}, bf16[10,36,128,128]{3,2,1,0:T(8,128)(2,1)S(1)}) custom-call(s32[10,36]{1,0:T(8,128)S(1)} %copy-done.1, s32[10]{0:T(128)S(1)} %bitcast.10, f32[80,128]{1,0:T(8,128)S(1)} %convert_add_fusion.sums_ref, f32[80,128]{1,0:T(8,128)S(1)} %bitcast.7, ...), custom_call_target="tpu_custom_call", output_to_operand_aliasing={{1}: (5, {})} | custom-call | flops 754974720 | bytes 5898240 | tf_op jit(solution)/shard_map/first_layer/pallas_call | solution.py:262
  24.7 2.2 %collective-permute-done.6 = bf16[5,128,128]{2,1,0:T(8,128)(2,1)S(1)} collective-permute-done((bf16[5,128,128]{2,1,0:T(8,128)(2,1)S(1)}, bf16[5,128,128]{2,1,0:T(8,128)(2,1)S(1)}, u32[]{:S(2)}, u32[]{:S(2)}) %collective-permute-start.6) | collective-permute-done | bytes 163872 | tf_op jit(solution)/shard_map/ppermute | solution.py:245
  27.0 2.1 %collective-permute-start.7 = (bf16[5,128,128]{2,1,0:T(8,128)(2,1)S(1)}, bf16[5,128,128]{2,1,0:T(8,128)(2,1)S(1)}, u32[]{:S(2)}, u32[]{:S(2)}) collective-permute-start(bf16[5,128,128]{2,1,0:T(8,128)(2,1)S(1)} %add_convert_fusion.own_ref), channel_id=1, source_target_pairs={{0,16},{2,18},{4,20},{6,22},{8,24},{10,26},{12,28},{14,30},{16,0},... | collective-permute-start | bytes 491528 | tf_op jit(solution)/shard_map/ppermute | solution.py:242
  29.1 8.4 %collective-permute-done.7.crossed_ref = bf16[5,128,128]{2,1,0:T(8,128)(2,1)S(1)} collective-permute-done((bf16[5,128,128]{2,1,0:T(8,128)(2,1)S(1)}, bf16[5,128,128]{2,1,0:T(8,128)(2,1)S(1)}, u32[]{:S(2)}, u32[]{:S(2)}) %collective-permute-start.7) | collective-permute-done | bytes 163872 | tf_op jit(solution)/shard_map/ppermute | solution.py:242
  37.5 1.5 %collective-permute-start.11 = (bf16[5,128,128]{2,1,0:T(8,128)(2,1)S(1)}, bf16[5,128,128]{2,1,0:T(8,128)(2,1)S(1)}, u32[]{:S(2)}, u32[]{:S(2)}) collective-permute-start(bf16[5,128,128]{2,1,0:T(8,128)(2,1)S(1)} %get-tuple-element.22), channel_id=1, source_target_pairs={{0,1},{1,0},{2,3},{3,2},{4,5},{5,4},{6,7},{7,6},{8,9},{9,8},{10,11... | collective-permute-start | bytes 491528 | tf_op jit(solution)/shard_map/ppermute | solution.py:245
  39.0 1.4 %collective-permute-start.10 = (bf16[5,128,128]{2,1,0:T(8,128)(2,1)S(1)}, bf16[5,128,128]{2,1,0:T(8,128)(2,1)S(1)}, u32[]{:S(2)}, u32[]{:S(2)}) collective-permute-start(bf16[5,128,128]{2,1,0:T(8,128)(2,1)S(1)} %get-tuple-element.21.refs_0_), channel_id=1, source_target_pairs={{0,12},{2,14},{4,8},{6,10},{8,4},{10,6},{12,0},{14,2},{16,28},{18,... | collective-permute-start | bytes 491528 | tf_op jit(solution)/shard_map/ppermute | solution.py:242
  40.4 0.6 collective-permute-start.9
  41.0 1.5 %collective-permute-start.8 = (bf16[5,128,128]{2,1,0:T(8,128)(2,1)S(1)}, bf16[5,128,128]{2,1,0:T(8,128)(2,1)S(1)}, u32[]{:S(2)}, u32[]{:S(2)}) collective-permute-start(bf16[5,128,128]{2,1,0:T(8,128)(2,1)S(1)} %get-tuple-element.21.refs_0_), channel_id=1, source_target_pairs={{0,4},{2,6},{4,0},{6,2},{8,12},{10,14},{12,8},{14,10},{16,20},{18,... | collective-permute-start | bytes 491528 | tf_op jit(solution)/shard_map/ppermute | solution.py:242
  42.5 0.4 collective-permute-done.11.refs_0_
  42.9 1.0 %collective-permute-start.14 = (bf16[5,128,128]{2,1,0:T(8,128)(2,1)S(1)}, bf16[5,128,128]{2,1,0:T(8,128)(2,1)S(1)}, u32[]{:S(2)}, u32[]{:S(2)}) collective-permute-start(bf16[5,128,128]{2,1,0:T(8,128)(2,1)S(1)} %collective-permute-done.11.refs_0_), channel_id=1, source_target_pairs={{0,12},{2,14},{4,8},{6,10},{8,4},{10,6},{12,0},{14,2},{16,28},{18,... | collective-permute-start | bytes 491528 | tf_op jit(solution)/shard_map/ppermute | solution.py:242
  43.9 2.4 %collective-permute-start.13 = (bf16[5,128,128]{2,1,0:T(8,128)(2,1)S(1)}, bf16[5,128,128]{2,1,0:T(8,128)(2,1)S(1)}, u32[]{:S(2)}, u32[]{:S(2)}) collective-permute-start(bf16[5,128,128]{2,1,0:T(8,128)(2,1)S(1)} %collective-permute-done.11.refs_0_), channel_id=1, source_target_pairs={{0,8},{2,10},{4,12},{6,14},{8,0},{10,2},{12,4},{14,6},{16,24},{18,... | collective-permute-start | bytes 491528 | tf_op jit(solution)/shard_map/ppermute | solution.py:242
  46.3 0.8 %collective-permute-done.10.refs_3_ = bf16[5,128,128]{2,1,0:T(8,128)(2,1)S(1)} collective-permute-done((bf16[5,128,128]{2,1,0:T(8,128)(2,1)S(1)}, bf16[5,128,128]{2,1,0:T(8,128)(2,1)S(1)}, u32[]{:S(2)}, u32[]{:S(2)}) %collective-permute-start.10) | collective-permute-done | bytes 163872 | tf_op jit(solution)/shard_map/ppermute | solution.py:242
  47.1 0.4 collective-permute-start.12
  47.5 2.0 %collective-permute-done.9.refs_2_ = bf16[5,128,128]{2,1,0:T(8,128)(2,1)S(1)} collective-permute-done((bf16[5,128,128]{2,1,0:T(8,128)(2,1)S(1)}, bf16[5,128,128]{2,1,0:T(8,128)(2,1)S(1)}, u32[]{:S(2)}, u32[]{:S(2)}) %collective-permute-start.9) | collective-permute-done | bytes 163872 | tf_op jit(solution)/shard_map/ppermute | solution.py:242
  49.6 2.0 %collective-permute-done.8.refs_1_ = bf16[5,128,128]{2,1,0:T(8,128)(2,1)S(1)} collective-permute-done((bf16[5,128,128]{2,1,0:T(8,128)(2,1)S(1)}, bf16[5,128,128]{2,1,0:T(8,128)(2,1)S(1)}, u32[]{:S(2)}, u32[]{:S(2)}) %collective-permute-start.8) | collective-permute-done | bytes 163872 | tf_op jit(solution)/shard_map/ppermute | solution.py:242
  51.7 0.1 collective-permute-start.15
  51.8 1.6 %collective-permute-done.14.refs_3_ = bf16[5,128,128]{2,1,0:T(8,128)(2,1)S(1)} collective-permute-done((bf16[5,128,128]{2,1,0:T(8,128)(2,1)S(1)}, bf16[5,128,128]{2,1,0:T(8,128)(2,1)S(1)}, u32[]{:S(2)}, u32[]{:S(2)}) %collective-permute-start.14) | collective-permute-done | bytes 163872 | tf_op jit(solution)/shard_map/ppermute | solution.py:242
  53.4 1.5 %collective-permute-done.13.refs_2_ = bf16[5,128,128]{2,1,0:T(8,128)(2,1)S(1)} collective-permute-done((bf16[5,128,128]{2,1,0:T(8,128)(2,1)S(1)}, bf16[5,128,128]{2,1,0:T(8,128)(2,1)S(1)}, u32[]{:S(2)}, u32[]{:S(2)}) %collective-permute-start.13) | collective-permute-done | bytes 163872 | tf_op jit(solution)/shard_map/ppermute | solution.py:242
  54.9 0.1 collective-permute-done.12.refs_1_
  55.0 0.1 collective-permute-start.16
  55.1 0.0 collective-permute-done.15.home_core_ref
  55.1 0.1 own_collected.1.rest_0_
  55.3 1.9 %collective-permute-done.16.rest_1_ = bf16[20,128,128]{2,1,0:T(8,128)(2,1)S(1)} collective-permute-done((bf16[20,128,128]{2,1,0:T(8,128)(2,1)S(1)}, bf16[20,128,128]{2,1,0:T(8,128)(2,1)S(1)}, u32[]{:S(2)}, u32[]{:S(2)}) %collective-permute-start.16) | collective-permute-done | bytes 655392 | tf_op jit(solution)/shard_map/ppermute | solution.py:242
  57.2 2.0 %second_layer.2 = (bf16[5,128,128]{2,1,0:T(8,128)(2,1)S(1)}, bf16[80,128,128]{2,1,0:T(8,128)(2,1)S(1)}) custom-call(s32[10,36]{1,0:T(8,128)S(1)} %copy-done.1, s32[10]{0:T(128)S(1)} %bitcast.11, bf16[10,36,128,128]{3,2,1,0:T(8,128)(2,1)S(1)} %get-tuple-element.18.coef_ref, ...), custom_call_target="tpu_custom_call", output_to_operand_aliasing={{1}: (4, {})} | custom-call | flops 754974720 | bytes 5898240 | tf_op jit(solution)/shard_map/second_layer/pallas_call | solution.py:290
  59.2 1.6 %collective-permute-start.18 = (bf16[5,128,128]{2,1,0:T(8,128)(2,1)S(1)}, bf16[5,128,128]{2,1,0:T(8,128)(2,1)S(1)}, u32[]{:S(2)}, u32[]{:S(2)}) collective-permute-start(bf16[5,128,128]{2,1,0:T(8,128)(2,1)S(1)} %get-tuple-element.24.mine_ref), channel_id=1, source_target_pairs={{0,1},{1,0},{2,3},{3,2},{4,5},{5,4},{6,7},{7,6},{8,9},{9,8},{10,11... | collective-permute-start | bytes 491528 | tf_op jit(solution)/shard_map/ppermute | solution.py:245
  60.9 1.4 %second_layer.3.mine_ref = bf16[5,128,128]{2,1,0:T(8,128)(2,1)S(1)} custom-call(s32[10,36]{1,0:T(8,128)S(1)} %copy-done.1, s32[10]{0:T(128)S(1)} %bitcast.12, bf16[10,36,128,128]{3,2,1,0:T(8,128)(2,1)S(1)} %get-tuple-element.18.coef_ref, bf16[5,128,128]{2,1,0:T(8,128)(2,1)S(1)} %add_convert_fusion.own_ref, bf16[80,128,128]{2,1,0:T(8,128)(2,1)S(1)} %get-tuple-element.23.rest_0_), custom_call_target="tpu_custom_call" | custom-call | flops 754974720 | bytes 5898240 | tf_op jit(solution)/shard_map/second_layer/pallas_call | solution.py:290
  62.3 0.5 collective-permute-start.17
  62.8 3.4 %collective-permute-done.18.other_ref = bf16[5,128,128]{2,1,0:T(8,128)(2,1)S(1)} collective-permute-done((bf16[5,128,128]{2,1,0:T(8,128)(2,1)S(1)}, bf16[5,128,128]{2,1,0:T(8,128)(2,1)S(1)}, u32[]{:S(2)}, u32[]{:S(2)}) %collective-permute-start.18) | collective-permute-done | bytes 163872 | tf_op jit(solution)/shard_map/ppermute | solution.py:245
  66.2 0.7 %result.2.rest_0_ = bf16[10,128,128]{2,1,0:T(8,128)(2,1)} custom-call(bf16[5,128,128]{2,1,0:T(8,128)(2,1)S(1)} %get-tuple-element.24.mine_ref, bf16[5,128,128]{2,1,0:T(8,128)(2,1)S(1)} %collective-permute-done.18.other_ref), custom_call_target="tpu_custom_call" | custom-call | tf_op jit(solution)/shard_map/result/pallas_call | solution.py:357
  66.9 2.1 %collective-permute-done.17.other_ref = bf16[5,128,128]{2,1,0:T(8,128)(2,1)S(1)} collective-permute-done((bf16[5,128,128]{2,1,0:T(8,128)(2,1)S(1)}, bf16[5,128,128]{2,1,0:T(8,128)(2,1)S(1)}, u32[]{:S(2)}, u32[]{:S(2)}) %collective-permute-start.17) | collective-permute-done | bytes 163872 | tf_op jit(solution)/shard_map/ppermute | solution.py:245
  69.0 0.7 %result.3 = bf16[10,128,128]{2,1,0:T(8,128)(2,1)} custom-call(bf16[5,128,128]{2,1,0:T(8,128)(2,1)S(1)} %second_layer.3.mine_ref, bf16[5,128,128]{2,1,0:T(8,128)(2,1)S(1)} %collective-permute-done.17.other_ref, bf16[10,128,128]{2,1,0:T(8,128)(2,1)} %result.2.rest_0_), custom_call_target="tpu_custom_call", output_to_operand_aliasing={{}: (2, {})} | custom-call | tf_op jit(solution)/shard_map/result/pallas_call | solution.py:357
  (8 shorter events, 0.2 us)
Async XLA Ops:
  0.0 18.2 %copy-start.1 = (s32[10,36]{1,0:T(8,128)S(1)}, s32[10,36]{1,0:T(8,128)}, u32[]{:S(2)}) copy-start(s32[10,36]{1,0:T(8,128)} %cols_ref.7) | copy-start | bytes 4324
  0.0 18.2 %copy-start.3 = (s32[10,1]{0,1:T(1,128)S(1)}, s32[10,1]{0,1:T(1,128)}, u32[]{:S(2)}) copy-start(s32[10,1]{0,1:T(1,128)} %param.7) | copy-start | bytes 124
  0.0 18.2 %copy-start.2 = (f32[10240]{0:T(1024)S(1)}, f32[10240]{0:T(1024)}, u32[]{:S(2)}) copy-start(f32[10240]{0:T(1024)} %param.9) | copy-start | bytes 122884
  0.0 18.2 %copy-start = (bf16[10240,128]{1,0:T(8,128)(2,1)S(1)}, bf16[10240,128]{1,0:T(8,128)(2,1)}, u32[]{:S(2)}) copy-start(bf16[10240,128]{1,0:T(8,128)(2,1)} %param.8) | copy-start | bytes 7864324
  3.8 1.3 %collective-permute-start = (bf16[80,128]{1,0:T(8,128)(2,1)S(1)}, bf16[80,128]{1,0:T(8,128)(2,1)S(1)}, u32[]{:S(2)}, u32[]{:S(2)}) collective-permute-start(bf16[80,128]{1,0:T(8,128)(2,1)S(1)} %convert_element_type.33), channel_id=1, source_target_pairs={{0,2},{2,0},{4,6},{6,4},{8,10},{10,8},{12,14},{14,12},{16,18},{18,... | collective-permute-start | bytes 61448 | tf_op jit(solution)/shard_map/ppermute | solution.py:242
  5.2 5.9 %collective-permute-start.4 = (bf16[80,128]{1,0:T(8,128)(2,1)S(1)}, bf16[80,128]{1,0:T(8,128)(2,1)S(1)}, u32[]{:S(2)}, u32[]{:S(2)}) collective-permute-start(bf16[80,128]{1,0:T(8,128)(2,1)S(1)} %add_convert_fusion.1), channel_id=1, source_target_pairs={{0,12},{2,30},{4,8},{6,26},{8,4},{10,22},{12,0},{14,18},{16,28},{1... | collective-permute-start | bytes 61448 | tf_op jit(solution)/shard_map/ppermute | solution.py:252
  9.3 3.8 %collective-permute-start.3 = (bf16[80,128]{1,0:T(8,128)(2,1)S(1)}, bf16[80,128]{1,0:T(8,128)(2,1)S(1)}, u32[]{:S(2)}, u32[]{:S(2)}) collective-permute-start(bf16[80,128]{1,0:T(8,128)(2,1)S(1)} %add_convert_fusion.1), channel_id=1, source_target_pairs={{0,8},{2,26},{4,12},{6,30},{8,0},{10,18},{12,4},{14,22},{16,24},{1... | collective-permute-start | bytes 61448 | tf_op jit(solution)/shard_map/ppermute | solution.py:252
  9.6 3.8 %collective-permute-start.2 = (bf16[80,128]{1,0:T(8,128)(2,1)S(1)}, bf16[80,128]{1,0:T(8,128)(2,1)S(1)}, u32[]{:S(2)}, u32[]{:S(2)}) collective-permute-start(bf16[80,128]{1,0:T(8,128)(2,1)S(1)} %add_convert_fusion.1), channel_id=1, source_target_pairs={{0,4},{2,22},{4,0},{6,18},{8,12},{10,30},{12,8},{14,26},{16,20},{1... | collective-permute-start | bytes 61448 | tf_op jit(solution)/shard_map/ppermute | solution.py:252
  10.0 3.4 %collective-permute-start.1 = (bf16[80,128]{1,0:T(8,128)(2,1)S(1)}, bf16[80,128]{1,0:T(8,128)(2,1)S(1)}, u32[]{:S(2)}, u32[]{:S(2)}) collective-permute-start(bf16[80,128]{1,0:T(8,128)(2,1)S(1)} %add_convert_fusion.1), channel_id=1, source_target_pairs={{0,0},{2,18},{4,4},{6,22},{8,8},{10,26},{12,12},{14,30},{16,16},{1... | collective-permute-start | bytes 61448 | tf_op jit(solution)/shard_map/ppermute | solution.py:252
  13.4 4.8 %collective-permute-start.5 = (bf16[80,128]{1,0:T(8,128)(2,1)S(1)}, bf16[80,128]{1,0:T(8,128)(2,1)S(1)}, u32[]{:S(2)}, u32[]{:S(2)}) collective-permute-start(bf16[80,128]{1,0:T(8,128)(2,1)S(1)} %fusion), channel_id=1, source_target_pairs={{0,2},{2,0},{4,6},{6,4},{8,10},{10,8},{12,14},{14,12},{16,18},{18,... | collective-permute-start | bytes 61448 | tf_op jit(solution)/shard_map/ppermute | solution.py:242
  20.2 6.8 %collective-permute-start.6 = (bf16[5,128,128]{2,1,0:T(8,128)(2,1)S(1)}, bf16[5,128,128]{2,1,0:T(8,128)(2,1)S(1)}, u32[]{:S(2)}, u32[]{:S(2)}) collective-permute-start(bf16[5,128,128]{2,1,0:T(8,128)(2,1)S(1)} %get-tuple-element.20), channel_id=1, source_target_pairs={{0,1},{1,0},{2,3},{3,2},{4,5},{5,4},{6,7},{7,6},{8,9},{9,8},{10,11... | collective-permute-start | bytes 491528 | tf_op jit(solution)/shard_map/ppermute | solution.py:245
  27.0 10.4 %collective-permute-start.7 = (bf16[5,128,128]{2,1,0:T(8,128)(2,1)S(1)}, bf16[5,128,128]{2,1,0:T(8,128)(2,1)S(1)}, u32[]{:S(2)}, u32[]{:S(2)}) collective-permute-start(bf16[5,128,128]{2,1,0:T(8,128)(2,1)S(1)} %add_convert_fusion.own_ref), channel_id=1, source_target_pairs={{0,16},{2,18},{4,20},{6,22},{8,24},{10,26},{12,28},{14,30},{16,0},... | collective-permute-start | bytes 491528 | tf_op jit(solution)/shard_map/ppermute | solution.py:242
  37.5 5.4 %collective-permute-start.11 = (bf16[5,128,128]{2,1,0:T(8,128)(2,1)S(1)}, bf16[5,128,128]{2,1,0:T(8,128)(2,1)S(1)}, u32[]{:S(2)}, u32[]{:S(2)}) collective-permute-start(bf16[5,128,128]{2,1,0:T(8,128)(2,1)S(1)} %get-tuple-element.22), channel_id=1, source_target_pairs={{0,1},{1,0},{2,3},{3,2},{4,5},{5,4},{6,7},{7,6},{8,9},{9,8},{10,11... | collective-permute-start | bytes 491528 | tf_op jit(solution)/shard_map/ppermute | solution.py:245
  39.0 8.1 %collective-permute-start.10 = (bf16[5,128,128]{2,1,0:T(8,128)(2,1)S(1)}, bf16[5,128,128]{2,1,0:T(8,128)(2,1)S(1)}, u32[]{:S(2)}, u32[]{:S(2)}) collective-permute-start(bf16[5,128,128]{2,1,0:T(8,128)(2,1)S(1)} %get-tuple-element.21.refs_0_), channel_id=1, source_target_pairs={{0,12},{2,14},{4,8},{6,10},{8,4},{10,6},{12,0},{14,2},{16,28},{18,... | collective-permute-start | bytes 491528 | tf_op jit(solution)/shard_map/ppermute | solution.py:242
  40.4 9.2 %collective-permute-start.9 = (bf16[5,128,128]{2,1,0:T(8,128)(2,1)S(1)}, bf16[5,128,128]{2,1,0:T(8,128)(2,1)S(1)}, u32[]{:S(2)}, u32[]{:S(2)}) collective-permute-start(bf16[5,128,128]{2,1,0:T(8,128)(2,1)S(1)} %get-tuple-element.21.refs_0_), channel_id=1, source_target_pairs={{0,8},{2,10},{4,12},{6,14},{8,0},{10,2},{12,4},{14,6},{16,24},{18,... | collective-permute-start | bytes 491528 | tf_op jit(solution)/shard_map/ppermute | solution.py:242
  41.0 10.7 %collective-permute-start.8 = (bf16[5,128,128]{2,1,0:T(8,128)(2,1)S(1)}, bf16[5,128,128]{2,1,0:T(8,128)(2,1)S(1)}, u32[]{:S(2)}, u32[]{:S(2)}) collective-permute-start(bf16[5,128,128]{2,1,0:T(8,128)(2,1)S(1)} %get-tuple-element.21.refs_0_), channel_id=1, source_target_pairs={{0,4},{2,6},{4,0},{6,2},{8,12},{10,14},{12,8},{14,10},{16,20},{18,... | collective-permute-start | bytes 491528 | tf_op jit(solution)/shard_map/ppermute | solution.py:242
  42.9 10.5 %collective-permute-start.14 = (bf16[5,128,128]{2,1,0:T(8,128)(2,1)S(1)}, bf16[5,128,128]{2,1,0:T(8,128)(2,1)S(1)}, u32[]{:S(2)}, u32[]{:S(2)}) collective-permute-start(bf16[5,128,128]{2,1,0:T(8,128)(2,1)S(1)} %collective-permute-done.11.refs_0_), channel_id=1, source_target_pairs={{0,12},{2,14},{4,8},{6,10},{8,4},{10,6},{12,0},{14,2},{16,28},{18,... | collective-permute-start | bytes 491528 | tf_op jit(solution)/shard_map/ppermute | solution.py:242
  43.9 11.0 %collective-permute-start.13 = (bf16[5,128,128]{2,1,0:T(8,128)(2,1)S(1)}, bf16[5,128,128]{2,1,0:T(8,128)(2,1)S(1)}, u32[]{:S(2)}, u32[]{:S(2)}) collective-permute-start(bf16[5,128,128]{2,1,0:T(8,128)(2,1)S(1)} %collective-permute-done.11.refs_0_), channel_id=1, source_target_pairs={{0,8},{2,10},{4,12},{6,14},{8,0},{10,2},{12,4},{14,6},{16,24},{18,... | collective-permute-start | bytes 491528 | tf_op jit(solution)/shard_map/ppermute | solution.py:242
  47.1 7.9 %collective-permute-start.12 = (bf16[5,128,128]{2,1,0:T(8,128)(2,1)S(1)}, bf16[5,128,128]{2,1,0:T(8,128)(2,1)S(1)}, u32[]{:S(2)}, u32[]{:S(2)}) collective-permute-start(bf16[5,128,128]{2,1,0:T(8,128)(2,1)S(1)} %collective-permute-done.11.refs_0_), channel_id=1, source_target_pairs={{0,4},{2,6},{4,0},{6,2},{8,12},{10,14},{12,8},{14,10},{16,20},{18,... | collective-permute-start | bytes 491528 | tf_op jit(solution)/shard_map/ppermute | solution.py:242
  51.7 3.4 %collective-permute-start.15 = (bf16[20,128,128]{2,1,0:T(8,128)(2,1)S(1)}, bf16[20,128,128]{2,1,0:T(8,128)(2,1)S(1)}, u32[]{:S(2)}, u32[]{:S(2)}) collective-permute-start(bf16[20,128,128]{2,1,0:T(8,128)(2,1)S(1)} %own_joined.2.home_ref), channel_id=1, source_target_pairs={{0,2},{2,0},{4,6},{6,4},{8,10},{10,8},{12,14},{14,12},{16,18},{18,... | collective-permute-start | bytes 1966088 | tf_op jit(solution)/shard_map/ppermute | solution.py:242
  55.0 2.2 %collective-permute-start.16 = (bf16[20,128,128]{2,1,0:T(8,128)(2,1)S(1)}, bf16[20,128,128]{2,1,0:T(8,128)(2,1)S(1)}, u32[]{:S(2)}, u32[]{:S(2)}) collective-permute-start(bf16[20,128,128]{2,1,0:T(8,128)(2,1)S(1)} %own_joined.3.away_ref), channel_id=1, source_target_pairs={{0,2},{2,0},{4,6},{6,4},{8,10},{10,8},{12,14},{14,12},{16,18},{18,... | collective-permute-start | bytes 1966088 | tf_op jit(solution)/shard_map/ppermute | solution.py:242
  59.2 7.0 %collective-permute-start.18 = (bf16[5,128,128]{2,1,0:T(8,128)(2,1)S(1)}, bf16[5,128,128]{2,1,0:T(8,128)(2,1)S(1)}, u32[]{:S(2)}, u32[]{:S(2)}) collective-permute-start(bf16[5,128,128]{2,1,0:T(8,128)(2,1)S(1)} %get-tuple-element.24.mine_ref), channel_id=1, source_target_pairs={{0,1},{1,0},{2,3},{3,2},{4,5},{5,4},{6,7},{7,6},{8,9},{9,8},{10,11... | collective-permute-start | bytes 491528 | tf_op jit(solution)/shard_map/ppermute | solution.py:245
  62.3 6.8 %collective-permute-start.17 = (bf16[5,128,128]{2,1,0:T(8,128)(2,1)S(1)}, bf16[5,128,128]{2,1,0:T(8,128)(2,1)S(1)}, u32[]{:S(2)}, u32[]{:S(2)}) collective-permute-start(bf16[5,128,128]{2,1,0:T(8,128)(2,1)S(1)} %second_layer.3.mine_ref), channel_id=1, source_target_pairs={{0,1},{1,0},{2,3},{3,2},{4,5},{5,4},{6,7},{7,6},{8,9},{9,8},{10,11... | collective-permute-start | bytes 491528 | tf_op jit(solution)/shard_map/ppermute | solution.py:245

commit v17 on v15

--- a/solution.py
+++ b/solution.py
@@ -19,46 +19,49 @@
     rows, slots, size, _ = blocks_ref.shape
     groups = acc_ref.shape[0] - 1
     first, *others = slot_ranges(slots)
-
-    def fetch(b, part):
-        span = pl.ds(part.start, len(part))
-        return pltpu.make_async_copy(blocks_ref.at[b, span], held_ref.at[b, span], sems.at[b, min(part.start, 1)])
+    spans = [range(start, min(start + 4, len(first))) for start in range(0, len(first), 4)] + others
+
+    def fetch(b, i):
+        span = pl.ds(spans[i].start, len(spans[i]))
+        return pltpu.make_async_copy(blocks_ref.at[b, span], held_ref.at[b, span], sems.at[b, i])
+
+    def when_live(b, i, action):
+        if i == 0:
+            action()
+        else:
+            pl.when(counts_ref[b] > spans[i].start)(action)
 
     counts_copy = pltpu.make_async_copy(counts_hbm, counts_ref, list_sems.at[0])
     cols_copy = pltpu.make_async_copy(cols_hbm, cols_ref, list_sems.at[1])
     counts_copy.start()
     cols_copy.start()
     for b in range(rows):
-        fetch(b, first).start()
+        fetch(b, 0).start()
     acc_ref[...] = jnp.zeros_like(acc_ref)
     counts_copy.wait()
     cols_copy.wait()
     for b in range(rows):
-        for part in others:
-
-            @pl.when(counts_ref[b] > part.start)
-            def _(b=b, part=part):
-                fetch(b, part).start()
+        for i in range(1, len(spans)):
+            when_live(b, i, lambda b=b, i=i: fetch(b, i).start())
 
     def add(b, part):
-        fetch(b, part).wait()
         for slot in part:
             col = jnp.where(slot < counts_ref[b], cols_ref[b, slot], groups)
-            block = held_ref[b, slot]
-            for _ in range(2):
-                middle = block.shape[0] // 2
-                block = block[:middle] + block[middle:]
-            block = block.astype(jnp.float32).reshape(block.shape[0] // 8, 8, size)
-            acc_ref[col] += jnp.sum(block, axis=0)
+            block = held_ref[b, slot].astype(jnp.float32)
+            acc_ref[col] += jnp.sum(block.reshape(size // 8, 8, size), axis=0)
 
     for b in range(rows):
+        for i in range(len(spans) - len(others)):
+            when_live(b, i, lambda b=b, i=i: fetch(b, i).wait())
         add(b, first)
     for b in range(rows):
-        for part in others:
-
-            @pl.when(counts_ref[b] > part.start)
-            def _(b=b, part=part):
-                add(b, part)
+        for i in range(len(spans) - len(others), len(spans)):
+
+            def finish(b=b, i=i):
+                fetch(b, i).wait()
+                add(b, spans[i])
+
+            when_live(b, i, finish)
 
     sums_ref[...] = jnp.sum(acc_ref[:groups], axis=1)
 
@@ -91,9 +94,10 @@
 
     def gather(row, slot):
         col = cols_ref[row, slot]
-        scale = jnp.where(slot < counts_ref[row], inverse_ref[col], 0.0)
+        live = slot < counts_ref[row]
+        scale = jnp.where(live, inverse_ref[col], 0.0)
         scale = jnp.broadcast_to(scale, (16, size)).astype(jnp.bfloat16)
-        coef = (blocks_ref[row, slot].reshape(size // 16, 16, size) * scale).reshape(size, size)
+        coef = (blocks_ref[row, jnp.where(live, slot, 0)].reshape(size // 16, 16, size) * scale).reshape(size, size)
         coef_ref[row, slot] = coef
         return coef, demand_ref[col]
 
@@ -231,7 +235,7 @@
             pltpu.SMEM(slot_cols.shape, jnp.int32),
             pltpu.SMEM(counts.shape, jnp.int32),
             pltpu.SemaphoreType.DMA((2,)),
-            pltpu.SemaphoreType.DMA((rows, 2)),
+            pltpu.SemaphoreType.DMA((rows, 4)),
         ],
         compiler_params=PARAMS,
         cost_estimate=cost(0, 4 * rows * size * size * slots),

time: 67.8 us -> 69 us (1.018)
  waiting for transfers between devices: 31 us -> 35.7 us
  starting transfers between devices: 23.4 us -> 18.9 us
  Pallas kernels: 13.2 us -> 14.9 us
    ppermute x15, starting transfers between devices: 19.2 us -> 14.9 us  [flip(): return lax.ppermute(array, 'row', [(i, i ^ mask) for i in range(n_row)])]
    ppermute x15, waiting for transfers between devices: 22.5 us -> 26.5 us  [flip(): return lax.ppermute(array, 'row', [(i, i ^ mask) for i in range(n_row)])]
    pallas_call x2, Pallas kernels: 4.39 us -> 5.44 us  [first_layer(): pl.pallas_call(functools.partial(first_kernel, sending), name='first_laye...]
    ppermute x4, waiting for transfers between devices: 8.48 us -> 9.2 us  [swap(): return lax.ppermute(array, 'col', [(0, 1), (1, 0)])]
  transfers between devices with their start and end apart: 19 -> 19, of which waited for: 14 -> 15; matrix products, arithmetic and copies ran while one was open for 0% -> 0% of each run, Pallas kernels for 7% -> 8%
where the time goes in v17:
time: 69 us; the launch traced here: 69.9 us
  waiting for transfers between devices  35.7 us (52%)
  starting transfers between devices  18.9 us (27%)
  Pallas kernels  14.9 us (22%)
    ppermute x15, waiting for transfers between devices, flip(): return lax.ppermute(array, 'row', [(i, i ^ mask) for i in range(n_row)])  26.5 us
    ppermute x15, starting transfers between devices, flip(): return lax.ppermute(array, 'row', [(i, i ^ mask) for i in range(n_row)])  14.9 us
    ppermute x4, waiting for transfers between devices, swap(): return lax.ppermute(array, 'col', [(0, 1), (1, 0)])  9.2 us
    pallas_call x2, Pallas kernels, first_layer(): pl.pallas_call(functools.partial(first_kernel, sending), name='first_laye...  5.44 us
    pallas_call x1, Pallas kernels, body(): pl.pallas_call(sums_kernel, name='column_sums', out_shape=(jax.ShapeDtype...  4.03 us
    ppermute x4, starting transfers between devices, swap(): return lax.ppermute(array, 'col', [(0, 1), (1, 0)])  4 us
    pallas_call x2, Pallas kernels, second_call(): pl.pallas_call(kernel, name='second_layer', out_shape=(out, pltpu.VMEM((g...  3.61 us
    pallas_call x2, Pallas kernels, result(): pl.pallas_call(functools.partial(result_kernel, first_row), name='result'...  1.43 us
  transfers between devices with their start and end apart: 19, of which 15 were waited for; matrix products, arithmetic and copies ran while one was open for 0% of the time, Pallas kernels for 8%

profile of v17, /device:TPU:0, one launch (start us, length us, event | category | flops | bytes accessed | tf_op | source)
XLA Modules:
  0.0 69.9 jit_solution(9417603772478016336)
XLA Ops:
  0.0 0.0 copy-start.1
  0.0 0.0 copy-start.3
  0.0 0.0 copy-start.2
  0.0 0.0 copy-start
  0.0 4.0 %column_sums.1 = (f32[80,128]{1,0:T(8,128)S(1)}, bf16[10,36,128,128]{3,2,1,0:T(8,128)(2,1)S(1)}) custom-call(s32[10,36]{1,0:T(8,128)} %cols_ref.7, s32[10]{0:T(128)} %bitcast.8, bf16[10,36,128,128]{3,2,1,0:T(8,128)(2,1)} %blocks_ref.1), custom_call_target="tpu_custom_call" | custom-call | bytes 23592960 | tf_op jit(solution)/shard_map/column_sums/pallas_call | solution.py:224
  4.1 3.1 %collective-permute-start.1 = (bf16[80,128]{1,0:T(8,128)(2,1)S(1)}, bf16[80,128]{1,0:T(8,128)(2,1)S(1)}, u32[]{:S(2)}, u32[]{:S(2)}) collective-permute-start(bf16[80,128]{1,0:T(8,128)(2,1)S(1)} %convert_element_type.36), channel_id=1, source_target_pairs={{0,4},{2,6},{4,0},{6,2},{8,12},{10,14},{12,8},{14,10},{16,20},{18,... | collective-permute-start | bytes 61448 | tf_op jit(solution)/shard_map/ppermute | solution.py:245
  7.2 0.0 collective-permute-start
  7.2 0.2 collective-permute-start.2
  7.4 1.6 %collective-permute-done.1 = bf16[80,128]{1,0:T(8,128)(2,1)S(1)} collective-permute-done((bf16[80,128]{1,0:T(8,128)(2,1)S(1)}, bf16[80,128]{1,0:T(8,128)(2,1)S(1)}, u32[]{:S(2)}, u32[]{:S(2)}) %collective-permute-start.1) | collective-permute-done | bytes 20512 | tf_op jit(solution)/shard_map/ppermute | solution.py:245
  8.9 0.0 collective-permute-done
  8.9 1.4 %collective-permute-done.2 = bf16[80,128]{1,0:T(8,128)(2,1)S(1)} collective-permute-done((bf16[80,128]{1,0:T(8,128)(2,1)S(1)}, bf16[80,128]{1,0:T(8,128)(2,1)S(1)}, u32[]{:S(2)}, u32[]{:S(2)}) %collective-permute-start.2) | collective-permute-done | bytes 20512 | tf_op jit(solution)/shard_map/ppermute | solution.py:245
  10.4 4.1 %collective-permute-start.5 = (bf16[80,128]{1,0:T(8,128)(2,1)S(1)}, bf16[80,128]{1,0:T(8,128)(2,1)S(1)}, u32[]{:S(2)}, u32[]{:S(2)}) collective-permute-start(bf16[80,128]{1,0:T(8,128)(2,1)S(1)} %add_convert_fusion.1), channel_id=1, source_target_pairs={{0,24},{2,26},{4,28},{6,30},{8,16},{10,18},{12,20},{14,22},{16,8},... | collective-permute-start | bytes 61448 | tf_op jit(solution)/shard_map/ppermute | solution.py:245
  14.5 0.0 collective-permute-start.4
  14.5 0.6 collective-permute-start.3
  15.2 1.2 %collective-permute-done.5 = bf16[80,128]{1,0:T(8,128)(2,1)S(1)} collective-permute-done((bf16[80,128]{1,0:T(8,128)(2,1)S(1)}, bf16[80,128]{1,0:T(8,128)(2,1)S(1)}, u32[]{:S(2)}, u32[]{:S(2)}) %collective-permute-start.5) | collective-permute-done | bytes 20512 | tf_op jit(solution)/shard_map/ppermute | solution.py:245
  16.3 2.9 %collective-permute-done.4 = bf16[80,128]{1,0:T(8,128)(2,1)S(1)} collective-permute-done((bf16[80,128]{1,0:T(8,128)(2,1)S(1)}, bf16[80,128]{1,0:T(8,128)(2,1)S(1)}, u32[]{:S(2)}, u32[]{:S(2)}) %collective-permute-start.4) | collective-permute-done | bytes 20512 | tf_op jit(solution)/shard_map/ppermute | solution.py:245
  19.2 0.0 collective-permute-done.3
  19.2 0.0 copy-done.1
  19.2 0.0 copy-done.3
  19.2 0.0 copy-done.2
  19.3 0.0 copy-done
  19.3 2.7 %first_layer.2 = (bf16[5,128,128]{2,1,0:T(8,128)(2,1)S(1)}, bf16[10,36,128,128]{3,2,1,0:T(8,128)(2,1)S(1)}) custom-call(s32[10,36]{1,0:T(8,128)S(1)} %copy-done.1, s32[10]{0:T(128)S(1)} %bitcast.9, f32[80,128]{1,0:T(8,128)S(1)} %convert_add_fusion.sums_ref, f32[80,128]{1,0:T(8,128)S(1)} %bitcast.6, ...), custom_call_target="tpu_custom_call", output_to_operand_aliasing={{1}: (5, {})} | custom-call | flops 754974720 | bytes 5898240 | tf_op jit(solution)/shard_map/first_layer/pallas_call | solution.py:262
  22.0 1.6 %collective-permute-start.6 = (bf16[5,128,128]{2,1,0:T(8,128)(2,1)S(1)}, bf16[5,128,128]{2,1,0:T(8,128)(2,1)S(1)}, u32[]{:S(2)}, u32[]{:S(2)}) collective-permute-start(bf16[5,128,128]{2,1,0:T(8,128)(2,1)S(1)} %get-tuple-element.20), channel_id=1, source_target_pairs={{0,1},{1,0},{2,3},{3,2},{4,5},{5,4},{6,7},{7,6},{8,9},{9,8},{10,11... | collective-permute-start | bytes 491528 | tf_op jit(solution)/shard_map/ppermute | solution.py:248
  23.6 2.7 %first_layer.3 = (f32[5,128,128]{2,1,0:T(8,128)S(1)}, bf16[10,36,128,128]{3,2,1,0:T(8,128)(2,1)S(1)}) custom-call(s32[10,36]{1,0:T(8,128)S(1)} %copy-done.1, s32[10]{0:T(128)S(1)} %bitcast.10, f32[80,128]{1,0:T(8,128)S(1)} %convert_add_fusion.sums_ref, f32[80,128]{1,0:T(8,128)S(1)} %bitcast.7, ...), custom_call_target="tpu_custom_call", output_to_operand_aliasing={{1}: (5, {})} | custom-call | flops 754974720 | bytes 5898240 | tf_op jit(solution)/shard_map/first_layer/pallas_call | solution.py:262
  26.4 1.4 %collective-permute-done.6 = bf16[5,128,128]{2,1,0:T(8,128)(2,1)S(1)} collective-permute-done((bf16[5,128,128]{2,1,0:T(8,128)(2,1)S(1)}, bf16[5,128,128]{2,1,0:T(8,128)(2,1)S(1)}, u32[]{:S(2)}, u32[]{:S(2)}) %collective-permute-start.6) | collective-permute-done | bytes 163872 | tf_op jit(solution)/shard_map/ppermute | solution.py:248
  27.8 1.9 %collective-permute-start.7 = (bf16[5,128,128]{2,1,0:T(8,128)(2,1)S(1)}, bf16[5,128,128]{2,1,0:T(8,128)(2,1)S(1)}, u32[]{:S(2)}, u32[]{:S(2)}) collective-permute-start(bf16[5,128,128]{2,1,0:T(8,128)(2,1)S(1)} %add_convert_fusion.own_ref), channel_id=1, source_target_pairs={{0,16},{2,18},{4,20},{6,22},{8,24},{10,26},{12,28},{14,30},{16,0},... | collective-permute-start | bytes 491528 | tf_op jit(solution)/shard_map/ppermute | solution.py:245
  29.7 7.4 %collective-permute-done.7.crossed_ref = bf16[5,128,128]{2,1,0:T(8,128)(2,1)S(1)} collective-permute-done((bf16[5,128,128]{2,1,0:T(8,128)(2,1)S(1)}, bf16[5,128,128]{2,1,0:T(8,128)(2,1)S(1)}, u32[]{:S(2)}, u32[]{:S(2)}) %collective-permute-start.7) | collective-permute-done | bytes 163872 | tf_op jit(solution)/shard_map/ppermute | solution.py:245
  37.1 0.2 home_and_away.1
  37.3 0.2 collective-permute-start.11
  37.5 0.0 collective-permute-start.10
  37.5 1.5 %collective-permute-start.9 = (bf16[5,128,128]{2,1,0:T(8,128)(2,1)S(1)}, bf16[5,128,128]{2,1,0:T(8,128)(2,1)S(1)}, u32[]{:S(2)}, u32[]{:S(2)}) collective-permute-start(bf16[5,128,128]{2,1,0:T(8,128)(2,1)S(1)} %get-tuple-element.21.refs_0_), channel_id=1, source_target_pairs={{0,8},{2,10},{4,12},{6,14},{8,0},{10,2},{12,4},{14,6},{16,24},{18,... | collective-permute-start | bytes 491528 | tf_op jit(solution)/shard_map/ppermute | solution.py:245
  39.0 2.0 %collective-permute-start.8 = (bf16[5,128,128]{2,1,0:T(8,128)(2,1)S(1)}, bf16[5,128,128]{2,1,0:T(8,128)(2,1)S(1)}, u32[]{:S(2)}, u32[]{:S(2)}) collective-permute-start(bf16[5,128,128]{2,1,0:T(8,128)(2,1)S(1)} %get-tuple-element.21.refs_0_), channel_id=1, source_target_pairs={{0,4},{2,6},{4,0},{6,2},{8,12},{10,14},{12,8},{14,10},{16,20},{18,... | collective-permute-start | bytes 491528 | tf_op jit(solution)/shard_map/ppermute | solution.py:245
  41.0 2.3 %collective-permute-done.11.refs_0_ = bf16[5,128,128]{2,1,0:T(8,128)(2,1)S(1)} collective-permute-done((bf16[5,128,128]{2,1,0:T(8,128)(2,1)S(1)}, bf16[5,128,128]{2,1,0:T(8,128)(2,1)S(1)}, u32[]{:S(2)}, u32[]{:S(2)}) %collective-permute-start.11) | collective-permute-done | bytes 163872 | tf_op jit(solution)/shard_map/ppermute | solution.py:248
  43.3 0.0 collective-permute-start.14
  43.3 0.0 collective-permute-start.13
  43.3 2.2 %collective-permute-done.10.refs_3_ = bf16[5,128,128]{2,1,0:T(8,128)(2,1)S(1)} collective-permute-done((bf16[5,128,128]{2,1,0:T(8,128)(2,1)S(1)}, bf16[5,128,128]{2,1,0:T(8,128)(2,1)S(1)}, u32[]{:S(2)}, u32[]{:S(2)}) %collective-permute-start.10) | collective-permute-done | bytes 163872 | tf_op jit(solution)/shard_map/ppermute | solution.py:245
  45.5 1.3 %collective-permute-start.12 = (bf16[5,128,128]{2,1,0:T(8,128)(2,1)S(1)}, bf16[5,128,128]{2,1,0:T(8,128)(2,1)S(1)}, u32[]{:S(2)}, u32[]{:S(2)}) collective-permute-start(bf16[5,128,128]{2,1,0:T(8,128)(2,1)S(1)} %collective-permute-done.11.refs_0_), channel_id=1, source_target_pairs={{0,4},{2,6},{4,0},{6,2},{8,12},{10,14},{12,8},{14,10},{16,20},{18,... | collective-permute-start | bytes 491528 | tf_op jit(solution)/shard_map/ppermute | solution.py:245
  46.8 0.3 collective-permute-done.9.refs_2_
  47.1 2.0 %collective-permute-done.8.refs_1_ = bf16[5,128,128]{2,1,0:T(8,128)(2,1)S(1)} collective-permute-done((bf16[5,128,128]{2,1,0:T(8,128)(2,1)S(1)}, bf16[5,128,128]{2,1,0:T(8,128)(2,1)S(1)}, u32[]{:S(2)}, u32[]{:S(2)}) %collective-permute-start.8) | collective-permute-done | bytes 163872 | tf_op jit(solution)/shard_map/ppermute | solution.py:245
  49.2 0.1 collective-permute-start.15
  49.3 3.3 %collective-permute-done.14.refs_3_ = bf16[5,128,128]{2,1,0:T(8,128)(2,1)S(1)} collective-permute-done((bf16[5,128,128]{2,1,0:T(8,128)(2,1)S(1)}, bf16[5,128,128]{2,1,0:T(8,128)(2,1)S(1)}, u32[]{:S(2)}, u32[]{:S(2)}) %collective-permute-start.14) | collective-permute-done | bytes 163872 | tf_op jit(solution)/shard_map/ppermute | solution.py:245
  52.6 0.0 collective-permute-done.13.refs_2_
  52.6 2.2 %collective-permute-done.12.refs_1_ = bf16[5,128,128]{2,1,0:T(8,128)(2,1)S(1)} collective-permute-done((bf16[5,128,128]{2,1,0:T(8,128)(2,1)S(1)}, bf16[5,128,128]{2,1,0:T(8,128)(2,1)S(1)}, u32[]{:S(2)}, u32[]{:S(2)}) %collective-permute-start.12) | collective-permute-done | bytes 163872 | tf_op jit(solution)/shard_map/ppermute | solution.py:245
  54.9 0.1 collective-permute-start.16
  55.0 0.0 collective-permute-done.15.home_core_ref
  55.0 0.1 own_collected.1.rest_0_
  55.1 1.9 %collective-permute-done.16.rest_1_ = bf16[20,128,128]{2,1,0:T(8,128)(2,1)S(1)} collective-permute-done((bf16[20,128,128]{2,1,0:T(8,128)(2,1)S(1)}, bf16[20,128,128]{2,1,0:T(8,128)(2,1)S(1)}, u32[]{:S(2)}, u32[]{:S(2)}) %collective-permute-start.16) | collective-permute-done | bytes 655392 | tf_op jit(solution)/shard_map/ppermute | solution.py:245
  57.0 1.8 %second_layer.2 = (bf16[5,128,128]{2,1,0:T(8,128)(2,1)S(1)}, bf16[80,128,128]{2,1,0:T(8,128)(2,1)S(1)}) custom-call(s32[10,36]{1,0:T(8,128)S(1)} %copy-done.1, s32[10]{0:T(128)S(1)} %bitcast.11, bf16[10,36,128,128]{3,2,1,0:T(8,128)(2,1)S(1)} %get-tuple-element.18.coef_ref, ...), custom_call_target="tpu_custom_call", output_to_operand_aliasing={{1}: (4, {})} | custom-call | flops 754974720 | bytes 5898240 | tf_op jit(solution)/shard_map/second_layer/pallas_call | solution.py:290
  58.9 1.7 %collective-permute-start.18 = (bf16[5,128,128]{2,1,0:T(8,128)(2,1)S(1)}, bf16[5,128,128]{2,1,0:T(8,128)(2,1)S(1)}, u32[]{:S(2)}, u32[]{:S(2)}) collective-permute-start(bf16[5,128,128]{2,1,0:T(8,128)(2,1)S(1)} %get-tuple-element.24.mine_ref), channel_id=1, source_target_pairs={{0,1},{1,0},{2,3},{3,2},{4,5},{5,4},{6,7},{7,6},{8,9},{9,8},{10,11... | collective-permute-start | bytes 491528 | tf_op jit(solution)/shard_map/ppermute | solution.py:248
  60.6 1.8 %second_layer.3.mine_ref = bf16[5,128,128]{2,1,0:T(8,128)(2,1)S(1)} custom-call(s32[10,36]{1,0:T(8,128)S(1)} %copy-done.1, s32[10]{0:T(128)S(1)} %bitcast.12, bf16[10,36,128,128]{3,2,1,0:T(8,128)(2,1)S(1)} %get-tuple-element.18.coef_ref, bf16[5,128,128]{2,1,0:T(8,128)(2,1)S(1)} %add_convert_fusion.own_ref, bf16[80,128,128]{2,1,0:T(8,128)(2,1)S(1)} %get-tuple-element.23.rest_0_), custom_call_target="tpu_custom_call" | custom-call | flops 754974720 | bytes 5898240 | tf_op jit(solution)/shard_map/second_layer/pallas_call | solution.py:290
  62.4 0.4 collective-permute-start.17
  62.8 2.9 %collective-permute-done.18.other_ref = bf16[5,128,128]{2,1,0:T(8,128)(2,1)S(1)} collective-permute-done((bf16[5,128,128]{2,1,0:T(8,128)(2,1)S(1)}, bf16[5,128,128]{2,1,0:T(8,128)(2,1)S(1)}, u32[]{:S(2)}, u32[]{:S(2)}) %collective-permute-start.18) | collective-permute-done | bytes 163872 | tf_op jit(solution)/shard_map/ppermute | solution.py:248
  65.7 0.7 %result.2.rest_0_ = bf16[10,128,128]{2,1,0:T(8,128)(2,1)} custom-call(bf16[5,128,128]{2,1,0:T(8,128)(2,1)S(1)} %get-tuple-element.24.mine_ref, bf16[5,128,128]{2,1,0:T(8,128)(2,1)S(1)} %collective-permute-done.18.other_ref), custom_call_target="tpu_custom_call" | custom-call | tf_op jit(solution)/shard_map/result/pallas_call | solution.py:357
  66.5 2.6 %collective-permute-done.17.other_ref = bf16[5,128,128]{2,1,0:T(8,128)(2,1)S(1)} collective-permute-done((bf16[5,128,128]{2,1,0:T(8,128)(2,1)S(1)}, bf16[5,128,128]{2,1,0:T(8,128)(2,1)S(1)}, u32[]{:S(2)}, u32[]{:S(2)}) %collective-permute-start.17) | collective-permute-done | bytes 163872 | tf_op jit(solution)/shard_map/ppermute | solution.py:248
  69.0 0.7 %result.3 = bf16[10,128,128]{2,1,0:T(8,128)(2,1)} custom-call(bf16[5,128,128]{2,1,0:T(8,128)(2,1)S(1)} %second_layer.3.mine_ref, bf16[5,128,128]{2,1,0:T(8,128)(2,1)S(1)} %collective-permute-done.17.other_ref, bf16[10,128,128]{2,1,0:T(8,128)(2,1)} %result.2.rest_0_), custom_call_target="tpu_custom_call", output_to_operand_aliasing={{}: (2, {})} | custom-call | tf_op jit(solution)/shard_map/result/pallas_call | solution.py:357
  (6 shorter events, 0.2 us)
Async XLA Ops:
  0.0 19.2 %copy-start.1 = (s32[10,36]{1,0:T(8,128)S(1)}, s32[10,36]{1,0:T(8,128)}, u32[]{:S(2)}) copy-start(s32[10,36]{1,0:T(8,128)} %cols_ref.7) | copy-start | bytes 4324
  0.0 19.2 %copy-start.3 = (s32[10,1]{0,1:T(1,128)S(1)}, s32[10,1]{0,1:T(1,128)}, u32[]{:S(2)}) copy-start(s32[10,1]{0,1:T(1,128)} %param.7) | copy-start | bytes 124
  0.0 19.2 %copy-start.2 = (f32[10240]{0:T(1024)S(1)}, f32[10240]{0:T(1024)}, u32[]{:S(2)}) copy-start(f32[10240]{0:T(1024)} %param.9) | copy-start | bytes 122884
  0.0 19.3 %copy-start = (bf16[10240,128]{1,0:T(8,128)(2,1)S(1)}, bf16[10240,128]{1,0:T(8,128)(2,1)}, u32[]{:S(2)}) copy-start(bf16[10240,128]{1,0:T(8,128)(2,1)} %param.8) | copy-start | bytes 7864324
  4.1 4.9 %collective-permute-start.1 = (bf16[80,128]{1,0:T(8,128)(2,1)S(1)}, bf16[80,128]{1,0:T(8,128)(2,1)S(1)}, u32[]{:S(2)}, u32[]{:S(2)}) collective-permute-start(bf16[80,128]{1,0:T(8,128)(2,1)S(1)} %convert_element_type.36), channel_id=1, source_target_pairs={{0,4},{2,6},{4,0},{6,2},{8,12},{10,14},{12,8},{14,10},{16,20},{18,... | collective-permute-start | bytes 61448 | tf_op jit(solution)/shard_map/ppermute | solution.py:245
  7.2 1.8 %collective-permute-start = (bf16[80,128]{1,0:T(8,128)(2,1)S(1)}, bf16[80,128]{1,0:T(8,128)(2,1)S(1)}, u32[]{:S(2)}, u32[]{:S(2)}) collective-permute-start(bf16[80,128]{1,0:T(8,128)(2,1)S(1)} %convert_element_type.36), channel_id=1, source_target_pairs={{0,2},{2,0},{4,6},{6,4},{8,10},{10,8},{12,14},{14,12},{16,18},{18,... | collective-permute-start | bytes 61448 | tf_op jit(solution)/shard_map/ppermute | solution.py:245
  7.2 3.2 %collective-permute-start.2 = (bf16[80,128]{1,0:T(8,128)(2,1)S(1)}, bf16[80,128]{1,0:T(8,128)(2,1)S(1)}, u32[]{:S(2)}, u32[]{:S(2)}) collective-permute-start(bf16[80,128]{1,0:T(8,128)(2,1)S(1)} %convert_element_type.36), channel_id=1, source_target_pairs={{0,6},{2,4},{4,2},{6,0},{8,14},{10,12},{12,10},{14,8},{16,22},{18,... | collective-permute-start | bytes 61448 | tf_op jit(solution)/shard_map/ppermute | solution.py:245
  10.4 5.9 %collective-permute-start.5 = (bf16[80,128]{1,0:T(8,128)(2,1)S(1)}, bf16[80,128]{1,0:T(8,128)(2,1)S(1)}, u32[]{:S(2)}, u32[]{:S(2)}) collective-permute-start(bf16[80,128]{1,0:T(8,128)(2,1)S(1)} %add_convert_fusion.1), channel_id=1, source_target_pairs={{0,24},{2,26},{4,28},{6,30},{8,16},{10,18},{12,20},{14,22},{16,8},... | collective-permute-start | bytes 61448 | tf_op jit(solution)/shard_map/ppermute | solution.py:245
  14.5 4.7 %collective-permute-start.4 = (bf16[80,128]{1,0:T(8,128)(2,1)S(1)}, bf16[80,128]{1,0:T(8,128)(2,1)S(1)}, u32[]{:S(2)}, u32[]{:S(2)}) collective-permute-start(bf16[80,128]{1,0:T(8,128)(2,1)S(1)} %add_convert_fusion.1), channel_id=1, source_target_pairs={{0,16},{2,18},{4,20},{6,22},{8,24},{10,26},{12,28},{14,30},{16,0},... | collective-permute-start | bytes 61448 | tf_op jit(solution)/shard_map/ppermute | solution.py:245
  14.5 4.7 %collective-permute-start.3 = (bf16[80,128]{1,0:T(8,128)(2,1)S(1)}, bf16[80,128]{1,0:T(8,128)(2,1)S(1)}, u32[]{:S(2)}, u32[]{:S(2)}) collective-permute-start(bf16[80,128]{1,0:T(8,128)(2,1)S(1)} %add_convert_fusion.1), channel_id=1, source_target_pairs={{0,8},{2,10},{4,12},{6,14},{8,0},{10,2},{12,4},{14,6},{16,24},{18,... | collective-permute-start | bytes 61448 | tf_op jit(solution)/shard_map/ppermute | solution.py:245
  22.0 5.8 %collective-permute-start.6 = (bf16[5,128,128]{2,1,0:T(8,128)(2,1)S(1)}, bf16[5,128,128]{2,1,0:T(8,128)(2,1)S(1)}, u32[]{:S(2)}, u32[]{:S(2)}) collective-permute-start(bf16[5,128,128]{2,1,0:T(8,128)(2,1)S(1)} %get-tuple-element.20), channel_id=1, source_target_pairs={{0,1},{1,0},{2,3},{3,2},{4,5},{5,4},{6,7},{7,6},{8,9},{9,8},{10,11... | collective-permute-start | bytes 491528 | tf_op jit(solution)/shard_map/ppermute | solution.py:248
  27.8 9.3 %collective-permute-start.7 = (bf16[5,128,128]{2,1,0:T(8,128)(2,1)S(1)}, bf16[5,128,128]{2,1,0:T(8,128)(2,1)S(1)}, u32[]{:S(2)}, u32[]{:S(2)}) collective-permute-start(bf16[5,128,128]{2,1,0:T(8,128)(2,1)S(1)} %add_convert_fusion.own_ref), channel_id=1, source_target_pairs={{0,16},{2,18},{4,20},{6,22},{8,24},{10,26},{12,28},{14,30},{16,0},... | collective-permute-start | bytes 491528 | tf_op jit(solution)/shard_map/ppermute | solution.py:245
  37.3 6.0 %collective-permute-start.11 = (bf16[5,128,128]{2,1,0:T(8,128)(2,1)S(1)}, bf16[5,128,128]{2,1,0:T(8,128)(2,1)S(1)}, u32[]{:S(2)}, u32[]{:S(2)}) collective-permute-start(bf16[5,128,128]{2,1,0:T(8,128)(2,1)S(1)} %get-tuple-element.22), channel_id=1, source_target_pairs={{0,1},{1,0},{2,3},{3,2},{4,5},{5,4},{6,7},{7,6},{8,9},{9,8},{10,11... | collective-permute-start | bytes 491528 | tf_op jit(solution)/shard_map/ppermute | solution.py:248
  37.5 8.0 %collective-permute-start.10 = (bf16[5,128,128]{2,1,0:T(8,128)(2,1)S(1)}, bf16[5,128,128]{2,1,0:T(8,128)(2,1)S(1)}, u32[]{:S(2)}, u32[]{:S(2)}) collective-permute-start(bf16[5,128,128]{2,1,0:T(8,128)(2,1)S(1)} %get-tuple-element.21.refs_0_), channel_id=1, source_target_pairs={{0,12},{2,14},{4,8},{6,10},{8,4},{10,6},{12,0},{14,2},{16,28},{18,... | collective-permute-start | bytes 491528 | tf_op jit(solution)/shard_map/ppermute | solution.py:245
  37.5 9.6 %collective-permute-start.9 = (bf16[5,128,128]{2,1,0:T(8,128)(2,1)S(1)}, bf16[5,128,128]{2,1,0:T(8,128)(2,1)S(1)}, u32[]{:S(2)}, u32[]{:S(2)}) collective-permute-start(bf16[5,128,128]{2,1,0:T(8,128)(2,1)S(1)} %get-tuple-element.21.refs_0_), channel_id=1, source_target_pairs={{0,8},{2,10},{4,12},{6,14},{8,0},{10,2},{12,4},{14,6},{16,24},{18,... | collective-permute-start | bytes 491528 | tf_op jit(solution)/shard_map/ppermute | solution.py:245
  39.0 10.1 %collective-permute-start.8 = (bf16[5,128,128]{2,1,0:T(8,128)(2,1)S(1)}, bf16[5,128,128]{2,1,0:T(8,128)(2,1)S(1)}, u32[]{:S(2)}, u32[]{:S(2)}) collective-permute-start(bf16[5,128,128]{2,1,0:T(8,128)(2,1)S(1)} %get-tuple-element.21.refs_0_), channel_id=1, source_target_pairs={{0,4},{2,6},{4,0},{6,2},{8,12},{10,14},{12,8},{14,10},{16,20},{18,... | collective-permute-start | bytes 491528 | tf_op jit(solution)/shard_map/ppermute | solution.py:245
  43.3 9.3 %collective-permute-start.14 = (bf16[5,128,128]{2,1,0:T(8,128)(2,1)S(1)}, bf16[5,128,128]{2,1,0:T(8,128)(2,1)S(1)}, u32[]{:S(2)}, u32[]{:S(2)}) collective-permute-start(bf16[5,128,128]{2,1,0:T(8,128)(2,1)S(1)} %collective-permute-done.11.refs_0_), channel_id=1, source_target_pairs={{0,12},{2,14},{4,8},{6,10},{8,4},{10,6},{12,0},{14,2},{16,28},{18,... | collective-permute-start | bytes 491528 | tf_op jit(solution)/shard_map/ppermute | solution.py:245
  43.3 9.3 %collective-permute-start.13 = (bf16[5,128,128]{2,1,0:T(8,128)(2,1)S(1)}, bf16[5,128,128]{2,1,0:T(8,128)(2,1)S(1)}, u32[]{:S(2)}, u32[]{:S(2)}) collective-permute-start(bf16[5,128,128]{2,1,0:T(8,128)(2,1)S(1)} %collective-permute-done.11.refs_0_), channel_id=1, source_target_pairs={{0,8},{2,10},{4,12},{6,14},{8,0},{10,2},{12,4},{14,6},{16,24},{18,... | collective-permute-start | bytes 491528 | tf_op jit(solution)/shard_map/ppermute | solution.py:245
  45.5 9.3 %collective-permute-start.12 = (bf16[5,128,128]{2,1,0:T(8,128)(2,1)S(1)}, bf16[5,128,128]{2,1,0:T(8,128)(2,1)S(1)}, u32[]{:S(2)}, u32[]{:S(2)}) collective-permute-start(bf16[5,128,128]{2,1,0:T(8,128)(2,1)S(1)} %collective-permute-done.11.refs_0_), channel_id=1, source_target_pairs={{0,4},{2,6},{4,0},{6,2},{8,12},{10,14},{12,8},{14,10},{16,20},{18,... | collective-permute-start | bytes 491528 | tf_op jit(solution)/shard_map/ppermute | solution.py:245
  49.2 5.8 %collective-permute-start.15 = (bf16[20,128,128]{2,1,0:T(8,128)(2,1)S(1)}, bf16[20,128,128]{2,1,0:T(8,128)(2,1)S(1)}, u32[]{:S(2)}, u32[]{:S(2)}) collective-permute-start(bf16[20,128,128]{2,1,0:T(8,128)(2,1)S(1)} %own_joined.2.home_ref), channel_id=1, source_target_pairs={{0,2},{2,0},{4,6},{6,4},{8,10},{10,8},{12,14},{14,12},{16,18},{18,... | collective-permute-start | bytes 1966088 | tf_op jit(solution)/shard_map/ppermute | solution.py:245
  54.9 2.2 %collective-permute-start.16 = (bf16[20,128,128]{2,1,0:T(8,128)(2,1)S(1)}, bf16[20,128,128]{2,1,0:T(8,128)(2,1)S(1)}, u32[]{:S(2)}, u32[]{:S(2)}) collective-permute-start(bf16[20,128,128]{2,1,0:T(8,128)(2,1)S(1)} %own_joined.3.away_ref), channel_id=1, source_target_pairs={{0,2},{2,0},{4,6},{6,4},{8,10},{10,8},{12,14},{14,12},{16,18},{18,... | collective-permute-start | bytes 1966088 | tf_op jit(solution)/shard_map/ppermute | solution.py:245
  58.9 6.9 %collective-permute-start.18 = (bf16[5,128,128]{2,1,0:T(8,128)(2,1)S(1)}, bf16[5,128,128]{2,1,0:T(8,128)(2,1)S(1)}, u32[]{:S(2)}, u32[]{:S(2)}) collective-permute-start(bf16[5,128,128]{2,1,0:T(8,128)(2,1)S(1)} %get-tuple-element.24.mine_ref), channel_id=1, source_target_pairs={{0,1},{1,0},{2,3},{3,2},{4,5},{5,4},{6,7},{7,6},{8,9},{9,8},{10,11... | collective-permute-start | bytes 491528 | tf_op jit(solution)/shard_map/ppermute | solution.py:248
  62.4 6.7 %collective-permute-start.17 = (bf16[5,128,128]{2,1,0:T(8,128)(2,1)S(1)}, bf16[5,128,128]{2,1,0:T(8,128)(2,1)S(1)}, u32[]{:S(2)}, u32[]{:S(2)}) collective-permute-start(bf16[5,128,128]{2,1,0:T(8,128)(2,1)S(1)} %second_layer.3.mine_ref), channel_id=1, source_target_pairs={{0,1},{1,0},{2,3},{3,2},{4,5},{5,4},{6,7},{7,6},{8,9},{9,8},{10,11... | collective-permute-start | bytes 491528 | tf_op jit(solution)/shard_map/ppermute | solution.py:248

commit v18 on v15

--- a/solution.py
+++ b/solution.py
@@ -44,12 +44,8 @@
         fetch(b, part).wait()
         for slot in part:
             col = jnp.where(slot < counts_ref[b], cols_ref[b, slot], groups)
-            block = held_ref[b, slot]
-            for _ in range(2):
-                middle = block.shape[0] // 2
-                block = block[:middle] + block[middle:]
-            block = block.astype(jnp.float32).reshape(block.shape[0] // 8, 8, size)
-            acc_ref[col] += jnp.sum(block, axis=0)
+            block = held_ref[b, slot].astype(jnp.float32)
+            acc_ref[col] += jnp.sum(block.reshape(size // 8, 8, size), axis=0)
 
     for b in range(rows):
         add(b, first)
@@ -80,26 +76,64 @@
                 acc_ref[b] += product(row, part)
 
 
-def first_kernel(sending, cols_ref, counts_ref, sums_ref, added_ref, demand_ref, blocks_ref, out_ref, coef_ref, inverse_ref, acc_ref):
-    slots, size = blocks_ref.shape[1:3]
+def scaled_block(row, slot, cols_ref, counts_ref, inverse_ref, blocks_ref):
+    size = blocks_ref.shape[2]
+    scale = jnp.where(slot < counts_ref[row], inverse_ref[pl.ds(cols_ref[row, slot], 1), :], 0.0)
+    scale = jnp.broadcast_to(scale, (16, size)).astype(jnp.bfloat16)
+    return (blocks_ref[row, slot].reshape(size // 16, 16, size) * scale).reshape(size, size)
+
+
+def first_row(sending, count):
+    if sending is None:
+        return 0
+    side = lax.axis_index("col")
+    return (1 - side if sending else side) * count
+
+
+def first_kernel(sending, cols_ref, counts_ref, sums_ref, added_ref, demand_ref, blocks_ref, *rest):
+    inverse_ref, acc_ref = rest[-2:]
+    if sending:
+        out_ref, coef_ref = rest[-3], None
+    else:
+        out_ref, coef_ref = rest[-4:-2]
+    slots = blocks_ref.shape[1]
     count = out_ref.shape[0]
-    base = 0
-    if sending is not None:
-        side = lax.axis_index("col")
-        base = (1 - side if sending else side) * count
-    inverse_ref[...] = (1.0 / (sums_ref[...] + added_ref[...]))[:, None, :]
+    inverse_ref[...] = 1.0 / (sums_ref[...] + added_ref[...])
 
     def gather(row, slot):
-        col = cols_ref[row, slot]
-        scale = jnp.where(slot < counts_ref[row], inverse_ref[col], 0.0)
-        scale = jnp.broadcast_to(scale, (16, size)).astype(jnp.bfloat16)
-        coef = (blocks_ref[row, slot].reshape(size // 16, 16, size) * scale).reshape(size, size)
-        coef_ref[row, slot] = coef
-        return coef, demand_ref[col]
-
-    rows = [base + b for b in range(count)]
+        coef = scaled_block(row, slot, cols_ref, counts_ref, inverse_ref, blocks_ref)
+        if coef_ref is not None:
+            coef_ref[row, slot] = coef
+        return coef, demand_ref[cols_ref[row, slot]]
+
+    rows = [first_row(sending, count) + b for b in range(count)]
     multiply_rows(rows, counts_ref, slots, lambda b: 0.0, gather, acc_ref)
     out_ref[...] = acc_ref[...].astype(out_ref.dtype)
+
+
+def scale_kernel(count, cols_ref, counts_ref, sums_ref, added_ref, blocks_ref, coef_ref, inverse_ref):
+    first, *others = slot_ranges(blocks_ref.shape[1])
+    inverse_ref[...] = 1.0 / (sums_ref[...] + added_ref[...])
+
+    def scale(row, part):
+        for slot in part:
+            coef_ref[row, slot] = scaled_block(row, slot, cols_ref, counts_ref, inverse_ref, blocks_ref)
+
+    rows = [first_row(True, count) + b for b in range(count)]
+    for row in rows:
+        scale(row, first)
+    for row in rows:
+        for part in others:
+
+            @pl.when(counts_ref[row] > part.start)
+            def _(row=row, part=part):
+                scale(row, part)
+
+
+def fetch_kernel(demand_hbm, _, demand_ref, sem):
+    copy = pltpu.make_async_copy(demand_hbm, demand_ref, sem)
+    copy.start()
+    copy.wait()
 
 
 def second_rows(first_row, place, cols_ref, counts_ref, coef_ref, source_ref, start, out_ref, acc_ref):
@@ -166,7 +200,7 @@
     second_rows(0, lambda col: col, cols_ref, counts_ref, coef_ref, source_ref, start, out_ref, acc_ref)
 
 
-def choose_kernel(own_ref, crossed_ref, home_ref, away_ref):
+def choose_kernel(own_ref, crossed_ref, _, home_ref, away_ref):
     owner = lax.div(lax.axis_index("row"), 8) == lax.axis_index("col")
 
     @pl.when(owner)
@@ -247,6 +281,17 @@
         for masks in ((1, 2, 3), (4, 8, 12)):
             sums = sums.astype(jnp.bfloat16)
             parts = [sums] + [flip(sums, m) for m in masks]
+            if masks[0] == 4:
+                demand = pl.pallas_call(
+                    fetch_kernel,
+                    name="own_demand",
+                    out_shape=pltpu.VMEM(demand.shape, demand.dtype),
+                    in_specs=[pl.BlockSpec(memory_space=pltpu.HBM), pl.BlockSpec(memory_space=pl.ANY)],
+                    out_specs=VMEM,
+                    scratch_shapes=[pltpu.SemaphoreType.DMA],
+                    compiler_params=PARAMS,
+                    cost_estimate=cost(0, 3 * demand.size * 2),
+                )(pltpu.with_memory_space_constraint(demand, pltpu.HBM), sums)
             sums = functools.reduce(jnp.add, [part.astype(jnp.float32) for part in parts])
     else:
         sums = lax.psum(sums, "row")
@@ -254,21 +299,19 @@
     def layer_cost(count):
         return cost(2 * count * slots * size * size * width, count * slots * size * size * 2)
 
-    def first_layer(sending, count, dtype, held):
+    def first_layer(sending, count, dtype, held, earlier=()):
+        out = jax.ShapeDtypeStruct((count, size, width), dtype)
         return pl.pallas_call(
             functools.partial(first_kernel, sending),
             name="first_layer",
-            out_shape=(
-                jax.ShapeDtypeStruct((count, size, width), dtype),
-                pltpu.VMEM(blocks.shape, blocks.dtype),
-            ),
-            in_specs=[SMEM, SMEM, VMEM, VMEM, VMEM, VMEM],
-            out_specs=(VMEM, VMEM),
+            out_shape=out if sending else (out, pltpu.VMEM(blocks.shape, blocks.dtype)),
+            in_specs=[SMEM, SMEM, VMEM, VMEM, VMEM, VMEM] + [pl.BlockSpec(memory_space=pl.ANY)] * len(earlier),
+            out_specs=VMEM if sending else (VMEM, VMEM),
             scratch_shapes=[
-                pltpu.VMEM((groups, 1, size), jnp.float32),
+                pltpu.VMEM((groups, size), jnp.float32),
                 pltpu.VMEM((count, size, width), jnp.float32),
             ],
-            input_output_aliases={5: 1},
+            input_output_aliases={} if sending else {5: 1},
             compiler_params=PARAMS,
             cost_estimate=layer_cost(count),
         )(
@@ -278,6 +321,7 @@
             value_added.reshape(groups, size),
             demand.reshape(groups, size, width),
             in_vmem(held),
+            *earlier,
         )
 
     def second_call(kernel, count, coefs, own, sources, keep_sources):
@@ -304,9 +348,20 @@
         partial = second_call(second_kernel, rows, coefs, layer_one, [source], False)
         return lax.psum(partial, "col").astype(jnp.bfloat16).reshape(rows * size, width)
 
-    sent, coefs = first_layer(True, half, jnp.bfloat16, held)
+    sent = first_layer(True, half, jnp.bfloat16, held)
     arrived = swap(sent)
-    kept, coefs = first_layer(False, half, jnp.float32, coefs)
+    kept, coefs = first_layer(False, half, jnp.float32, held, [sent])
+    coefs = pl.pallas_call(
+        functools.partial(scale_kernel, half),
+        name="own_coefficients",
+        out_shape=pltpu.VMEM(blocks.shape, blocks.dtype),
+        in_specs=[SMEM, SMEM, VMEM, VMEM, VMEM],
+        out_specs=VMEM,
+        scratch_shapes=[pltpu.VMEM((groups, size), jnp.float32)],
+        input_output_aliases={4: 0},
+        compiler_params=PARAMS,
+        cost_estimate=layer_cost(half),
+    )(slot_cols, counts, sums, value_added.reshape(groups, size), in_vmem(coefs))
     own = (kept + arrived.astype(jnp.float32)).astype(jnp.bfloat16)
 
     piece = jax.ShapeDtypeStruct(own.shape, own.dtype)
@@ -314,10 +369,10 @@
         choose_kernel,
         name="home_and_away",
         out_shape=(piece, piece),
-        in_specs=[VMEM] * 2,
+        in_specs=[VMEM] * 2 + [pl.BlockSpec(memory_space=pl.ANY)],
         out_specs=(VMEM, VMEM),
         compiler_params=PARAMS,
-    )(own, flip(own, group_devices))
+    )(own, flip(own, group_devices), in_vmem(coefs))
 
     def join(pieces):
         return pl.pallas_call(

time: 67.8 us -> 67.5 us (level); the launches traced: 68.1 us -> 68.8 us
  waiting for transfers between devices: 31 us -> 35.1 us
  starting transfers between devices: 23.4 us -> 19.7 us
    ppermute x15, starting transfers between devices: 19.2 us -> 14.4 us  [flip(): return lax.ppermute(array, 'row', [(i, i ^ mask) for i in range(n_row)])]
    pallas_call x0 -> x2, Pallas kernels: none -> 2.96 us  [the longest x1 1.75 us: body(): pl.pallas_call(fetch_kernel, name='own_demand', out_shape=pltpu.VMEM(dema...]
    ppermute x15, waiting for transfers between devices: 22.5 us -> 25.2 us  [flip(): return lax.ppermute(array, 'row', [(i, i ^ mask) for i in range(n_row)])]
    ppermute x4, waiting for transfers between devices: 8.48 us -> 9.82 us  [swap(): return lax.ppermute(array, 'col', [(0, 1), (1, 0)])]
    pallas_call x1, Pallas kernels: 3.74 us -> 2.49 us  [body(): pl.pallas_call(sums_kernel, name='column_sums', out_shape=(jax.ShapeDtype...]
    ppermute x4, starting transfers between devices: 4.21 us -> 5.37 us  [swap(): return lax.ppermute(array, 'col', [(0, 1), (1, 0)])]
    pallas_call x2, Pallas kernels: 4.39 us -> 3.4 us  [first_layer(): pl.pallas_call(functools.partial(first_kernel, sending), name='first_laye...]
  transfers between devices with their start and end apart: 19 -> 19, of which waited for: 14 -> 13; matrix products, arithmetic and copies ran while one was open for 0% -> 0% of each run, Pallas kernels for 7% -> 11%
where the time goes in v18:
time: 67.5 us; the launch traced here: 68.8 us
  waiting for transfers between devices  35.1 us (52%)
  starting transfers between devices  19.7 us (29%)
  Pallas kernels  13.6 us (20%)
    ppermute x15, waiting for transfers between devices, flip(): return lax.ppermute(array, 'row', [(i, i ^ mask) for i in range(n_row)])  25.2 us
    ppermute x15, starting transfers between devices, flip(): return lax.ppermute(array, 'row', [(i, i ^ mask) for i in range(n_row)])  14.4 us
    ppermute x4, waiting for transfers between devices, swap(): return lax.ppermute(array, 'col', [(0, 1), (1, 0)])  9.82 us
    ppermute x4, starting transfers between devices, swap(): return lax.ppermute(array, 'col', [(0, 1), (1, 0)])  5.37 us
    pallas_call x2, Pallas kernels, first_layer(): pl.pallas_call(functools.partial(first_kernel, sending), name='first_laye...  3.4 us
    pallas_call x2, Pallas kernels, second_call(): pl.pallas_call(kernel, name='second_layer', out_shape=(out, pltpu.VMEM((g...  2.88 us
    pallas_call x1, Pallas kernels, body(): pl.pallas_call(sums_kernel, name='column_sums', out_shape=(jax.ShapeDtype...  2.49 us
    pallas_call x1, Pallas kernels, body(): pl.pallas_call(fetch_kernel, name='own_demand', out_shape=pltpu.VMEM(dema...  1.75 us
  transfers between devices with their start and end apart: 19, of which 13 were waited for; matrix products, arithmetic and copies ran while one was open for 0% of the time, Pallas kernels for 11%

profile of v18, /device:TPU:0, one launch (start us, length us, event | category | flops | bytes accessed | tf_op | source)
XLA Modules:
  0.0 68.8 jit_solution(13520509971575378724)
XLA Ops:
  0.0 0.0 copy-start.1
  0.0 0.0 copy-start.2
  0.0 0.0 copy-start
  0.0 2.5 %column_sums.1 = (f32[80,128]{1,0:T(8,128)S(1)}, bf16[10,36,128,128]{3,2,1,0:T(8,128)(2,1)S(1)}) custom-call(s32[10,36]{1,0:T(8,128)} %cols_ref.9, s32[10]{0:T(128)} %bitcast.9, bf16[10,36,128,128]{3,2,1,0:T(8,128)(2,1)} %blocks_ref.1), custom_call_target="tpu_custom_call" | custom-call | bytes 23592960 | tf_op jit(solution)/shard_map/column_sums/pallas_call | solution.py:254
  2.5 4.0 %collective-permute-start.1 = (bf16[80,128]{1,0:T(8,128)(2,1)S(1)}, bf16[80,128]{1,0:T(8,128)(2,1)S(1)}, u32[]{:S(2)}, u32[]{:S(2)}) collective-permute-start(bf16[80,128]{1,0:T(8,128)(2,1)S(1)} %convert_element_type.36), channel_id=1, source_target_pairs={{0,4},{2,6},{4,0},{6,2},{8,12},{10,14},{12,8},{14,10},{16,20},{18,... | collective-permute-start | bytes 61448 | tf_op jit(solution)/shard_map/ppermute | solution.py:275
  6.5 0.0 collective-permute-start
  6.5 0.2 collective-permute-start.2
  6.7 1.6 %collective-permute-done.1 = bf16[80,128]{1,0:T(8,128)(2,1)S(1)} collective-permute-done((bf16[80,128]{1,0:T(8,128)(2,1)S(1)}, bf16[80,128]{1,0:T(8,128)(2,1)S(1)}, u32[]{:S(2)}, u32[]{:S(2)}) %collective-permute-start.1) | collective-permute-done | bytes 20512 | tf_op jit(solution)/shard_map/ppermute | solution.py:275
  8.3 0.0 collective-permute-done
  8.3 1.4 %collective-permute-done.2 = bf16[80,128]{1,0:T(8,128)(2,1)S(1)} collective-permute-done((bf16[80,128]{1,0:T(8,128)(2,1)S(1)}, bf16[80,128]{1,0:T(8,128)(2,1)S(1)}, u32[]{:S(2)}, u32[]{:S(2)}) %collective-permute-start.2) | collective-permute-done | bytes 20512 | tf_op jit(solution)/shard_map/ppermute | solution.py:275
  9.7 3.5 %collective-permute-start.5 = (bf16[80,128]{1,0:T(8,128)(2,1)S(1)}, bf16[80,128]{1,0:T(8,128)(2,1)S(1)}, u32[]{:S(2)}, u32[]{:S(2)}) collective-permute-start(bf16[80,128]{1,0:T(8,128)(2,1)S(1)} %add_convert_fusion.1._), channel_id=1, source_target_pairs={{0,24},{2,26},{4,28},{6,30},{8,16},{10,18},{12,20},{14,22},{16,8},... | collective-permute-start | bytes 61448 | tf_op jit(solution)/shard_map/ppermute | solution.py:275
  13.2 0.0 collective-permute-start.4
  13.2 1.0 %collective-permute-start.3 = (bf16[80,128]{1,0:T(8,128)(2,1)S(1)}, bf16[80,128]{1,0:T(8,128)(2,1)S(1)}, u32[]{:S(2)}, u32[]{:S(2)}) collective-permute-start(bf16[80,128]{1,0:T(8,128)(2,1)S(1)} %add_convert_fusion.1._), channel_id=1, source_target_pairs={{0,8},{2,10},{4,12},{6,14},{8,0},{10,2},{12,4},{14,6},{16,24},{18,... | collective-permute-start | bytes 61448 | tf_op jit(solution)/shard_map/ppermute | solution.py:275
  14.2 1.7 %own_demand.1 = bf16[10240,128]{1,0:T(8,128)(2,1)S(1)} custom-call(bf16[10240,128]{1,0:T(8,128)(2,1)} %demand_hbm.1, bf16[80,128]{1,0:T(8,128)(2,1)S(1)} %add_convert_fusion.1._), custom_call_target="tpu_custom_call" | custom-call | bytes 7864320 | tf_op jit(solution)/shard_map/own_demand/pallas_call | solution.py:285
  16.0 0.0 collective-permute-done.5
  16.0 1.9 %collective-permute-done.4 = bf16[80,128]{1,0:T(8,128)(2,1)S(1)} collective-permute-done((bf16[80,128]{1,0:T(8,128)(2,1)S(1)}, bf16[80,128]{1,0:T(8,128)(2,1)S(1)}, u32[]{:S(2)}, u32[]{:S(2)}) %collective-permute-start.4) | collective-permute-done | bytes 20512 | tf_op jit(solution)/shard_map/ppermute | solution.py:275
  17.9 0.0 collective-permute-done.3
  17.9 0.0 copy-done.1
  17.9 0.0 copy-done.2
  17.9 0.0 copy-done
  17.9 1.5 %first_layer.2.rest_0_ = bf16[5,128,128]{2,1,0:T(8,128)(2,1)S(1)} custom-call(s32[10,36]{1,0:T(8,128)S(1)} %copy-done.1, s32[10]{0:T(128)S(1)} %bitcast.10, f32[80,128]{1,0:T(8,128)S(1)} %convert_add_fusion.sums_ref, f32[80,128]{1,0:T(8,128)S(1)} %bitcast.6, bf16[80,128,128]{2,1,0:T(8,128)(2,1)S(1)} %bitcast.4, ...), custom_call_target="tpu_custom_call" | custom-call | flops 754974720 | bytes 5898240 | tf_op jit(solution)/shard_map/first_layer/pallas_call | solution.py:304
  19.4 1.6 %collective-permute-start.6 = (bf16[5,128,128]{2,1,0:T(8,128)(2,1)S(1)}, bf16[5,128,128]{2,1,0:T(8,128)(2,1)S(1)}, u32[]{:S(2)}, u32[]{:S(2)}) collective-permute-start(bf16[5,128,128]{2,1,0:T(8,128)(2,1)S(1)} %first_layer.2.rest_0_), channel_id=1, source_target_pairs={{0,1},{1,0},{2,3},{3,2},{4,5},{5,4},{6,7},{7,6},{8,9},{9,8},{10,11... | collective-permute-start | bytes 491528 | tf_op jit(solution)/shard_map/ppermute | solution.py:278
  21.0 1.9 %first_layer.3 = (f32[5,128,128]{2,1,0:T(8,128)S(1)}, bf16[10,36,128,128]{3,2,1,0:T(8,128)(2,1)S(1)}) custom-call(s32[10,36]{1,0:T(8,128)S(1)} %copy-done.1, s32[10]{0:T(128)S(1)} %bitcast.11, f32[80,128]{1,0:T(8,128)S(1)} %convert_add_fusion.sums_ref, f32[80,128]{1,0:T(8,128)S(1)} %bitcast.7, ...), custom_call_target="tpu_custom_call", output_to_operand_aliasing={{1}: (5, {})} | custom-call | flops 754974720 | bytes 5898240 | tf_op jit(solution)/shard_map/first_layer/pallas_call | solution.py:304
  22.9 2.5 %collective-permute-done.6 = bf16[5,128,128]{2,1,0:T(8,128)(2,1)S(1)} collective-permute-done((bf16[5,128,128]{2,1,0:T(8,128)(2,1)S(1)}, bf16[5,128,128]{2,1,0:T(8,128)(2,1)S(1)}, u32[]{:S(2)}, u32[]{:S(2)}) %collective-permute-start.6) | collective-permute-done | bytes 163872 | tf_op jit(solution)/shard_map/ppermute | solution.py:278
  25.5 1.4 %collective-permute-start.7 = (bf16[5,128,128]{2,1,0:T(8,128)(2,1)S(1)}, bf16[5,128,128]{2,1,0:T(8,128)(2,1)S(1)}, u32[]{:S(2)}, u32[]{:S(2)}) collective-permute-start(bf16[5,128,128]{2,1,0:T(8,128)(2,1)S(1)} %add_convert_fusion.own_ref), channel_id=1, source_target_pairs={{0,16},{2,18},{4,20},{6,22},{8,24},{10,26},{12,28},{14,30},{16,0},... | collective-permute-start | bytes 491528 | tf_op jit(solution)/shard_map/ppermute | solution.py:275
  26.9 1.2 %own_coefficients.1._.coef_ref = bf16[10,36,128,128]{3,2,1,0:T(8,128)(2,1)S(1)} custom-call(s32[10,36]{1,0:T(8,128)S(1)} %copy-done.1, s32[10]{0:T(128)S(1)} %bitcast.12, f32[80,128]{1,0:T(8,128)S(1)} %convert_add_fusion.sums_ref, f32[80,128]{1,0:T(8,128)S(1)} %bitcast.8, ...), custom_call_target="tpu_custom_call", output_to_operand_aliasing={{}: (4, {})} | custom-call | flops 754974720 | bytes 5898240 | tf_op jit(solution)/shard_map/own_coefficients/pallas_call | solution.py:354
  28.1 6.4 %collective-permute-done.7.crossed_ref = bf16[5,128,128]{2,1,0:T(8,128)(2,1)S(1)} collective-permute-done((bf16[5,128,128]{2,1,0:T(8,128)(2,1)S(1)}, bf16[5,128,128]{2,1,0:T(8,128)(2,1)S(1)}, u32[]{:S(2)}, u32[]{:S(2)}) %collective-permute-start.7) | collective-permute-done | bytes 163872 | tf_op jit(solution)/shard_map/ppermute | solution.py:275
  34.6 0.2 home_and_away.1
  34.8 1.7 %collective-permute-start.11 = (bf16[5,128,128]{2,1,0:T(8,128)(2,1)S(1)}, bf16[5,128,128]{2,1,0:T(8,128)(2,1)S(1)}, u32[]{:S(2)}, u32[]{:S(2)}) collective-permute-start(bf16[5,128,128]{2,1,0:T(8,128)(2,1)S(1)} %get-tuple-element.18), channel_id=1, source_target_pairs={{0,1},{1,0},{2,3},{3,2},{4,5},{5,4},{6,7},{7,6},{8,9},{9,8},{10,11... | collective-permute-start | bytes 491528 | tf_op jit(solution)/shard_map/ppermute | solution.py:278
  36.4 0.0 collective-permute-start.10
  36.4 0.0 collective-permute-start.9
  36.4 3.5 %collective-permute-start.8 = (bf16[5,128,128]{2,1,0:T(8,128)(2,1)S(1)}, bf16[5,128,128]{2,1,0:T(8,128)(2,1)S(1)}, u32[]{:S(2)}, u32[]{:S(2)}) collective-permute-start(bf16[5,128,128]{2,1,0:T(8,128)(2,1)S(1)} %get-tuple-element.17.refs_0_), channel_id=1, source_target_pairs={{0,4},{2,6},{4,0},{6,2},{8,12},{10,14},{12,8},{14,10},{16,20},{18,... | collective-permute-start | bytes 491528 | tf_op jit(solution)/shard_map/ppermute | solution.py:275
  39.9 1.0 %collective-permute-done.11.refs_0_ = bf16[5,128,128]{2,1,0:T(8,128)(2,1)S(1)} collective-permute-done((bf16[5,128,128]{2,1,0:T(8,128)(2,1)S(1)}, bf16[5,128,128]{2,1,0:T(8,128)(2,1)S(1)}, u32[]{:S(2)}, u32[]{:S(2)}) %collective-permute-start.11) | collective-permute-done | bytes 163872 | tf_op jit(solution)/shard_map/ppermute | solution.py:278
  40.9 0.0 collective-permute-start.14
  40.9 0.7 collective-permute-start.13
  41.6 2.9 %collective-permute-done.10.refs_3_ = bf16[5,128,128]{2,1,0:T(8,128)(2,1)S(1)} collective-permute-done((bf16[5,128,128]{2,1,0:T(8,128)(2,1)S(1)}, bf16[5,128,128]{2,1,0:T(8,128)(2,1)S(1)}, u32[]{:S(2)}, u32[]{:S(2)}) %collective-permute-start.10) | collective-permute-done | bytes 163872 | tf_op jit(solution)/shard_map/ppermute | solution.py:275
  44.5 0.0 collective-permute-start.12
  44.5 0.0 collective-permute-done.9.refs_2_
  44.5 3.5 %collective-permute-done.8.refs_1_ = bf16[5,128,128]{2,1,0:T(8,128)(2,1)S(1)} collective-permute-done((bf16[5,128,128]{2,1,0:T(8,128)(2,1)S(1)}, bf16[5,128,128]{2,1,0:T(8,128)(2,1)S(1)}, u32[]{:S(2)}, u32[]{:S(2)}) %collective-permute-start.8) | collective-permute-done | bytes 163872 | tf_op jit(solution)/shard_map/ppermute | solution.py:275
  48.1 0.1 collective-permute-start.15
  48.2 3.4 %collective-permute-done.14.refs_3_ = bf16[5,128,128]{2,1,0:T(8,128)(2,1)S(1)} collective-permute-done((bf16[5,128,128]{2,1,0:T(8,128)(2,1)S(1)}, bf16[5,128,128]{2,1,0:T(8,128)(2,1)S(1)}, u32[]{:S(2)}, u32[]{:S(2)}) %collective-permute-start.14) | collective-permute-done | bytes 163872 | tf_op jit(solution)/shard_map/ppermute | solution.py:275
  51.5 0.0 collective-permute-done.13.refs_2_
  51.5 2.2 %collective-permute-done.12.refs_1_ = bf16[5,128,128]{2,1,0:T(8,128)(2,1)S(1)} collective-permute-done((bf16[5,128,128]{2,1,0:T(8,128)(2,1)S(1)}, bf16[5,128,128]{2,1,0:T(8,128)(2,1)S(1)}, u32[]{:S(2)}, u32[]{:S(2)}) %collective-permute-start.12) | collective-permute-done | bytes 163872 | tf_op jit(solution)/shard_map/ppermute | solution.py:275
  53.7 0.1 collective-permute-start.16
  53.8 0.0 collective-permute-done.15.home_core_ref
  53.8 0.1 own_collected.1.rest_0_
  54.0 1.9 %collective-permute-done.16.rest_1_ = bf16[20,128,128]{2,1,0:T(8,128)(2,1)S(1)} collective-permute-done((bf16[20,128,128]{2,1,0:T(8,128)(2,1)S(1)}, bf16[20,128,128]{2,1,0:T(8,128)(2,1)S(1)}, u32[]{:S(2)}, u32[]{:S(2)}) %collective-permute-start.16) | collective-permute-done | bytes 655392 | tf_op jit(solution)/shard_map/ppermute | solution.py:275
  55.9 1.5 %second_layer.2 = (bf16[5,128,128]{2,1,0:T(8,128)(2,1)S(1)}, bf16[80,128,128]{2,1,0:T(8,128)(2,1)S(1)}) custom-call(s32[10,36]{1,0:T(8,128)S(1)} %copy-done.1, s32[10]{0:T(128)S(1)} %bitcast.13, bf16[10,36,128,128]{3,2,1,0:T(8,128)(2,1)S(1)} %own_coefficients.1._.coef_ref, ...), custom_call_target="tpu_custom_call", output_to_operand_aliasing={{1}: (4, {})} | custom-call | flops 754974720 | bytes 5898240 | tf_op jit(solution)/shard_map/second_layer/pallas_call | solution.py:330
  57.4 0.5 collective-permute-start.18
  57.9 1.4 %second_layer.3.mine_ref = bf16[5,128,128]{2,1,0:T(8,128)(2,1)S(1)} custom-call(s32[10,36]{1,0:T(8,128)S(1)} %copy-done.1, s32[10]{0:T(128)S(1)} %bitcast.14, bf16[10,36,128,128]{3,2,1,0:T(8,128)(2,1)S(1)} %own_coefficients.1._.coef_ref, bf16[5,128,128]{2,1,0:T(8,128)(2,1)S(1)} %add_convert_fusion.own_ref, bf16[80,128,128]{2,1,0:T(8,128)(2,1)S(1)} %get-tuple-element.19.rest_0_), custom_call_target="tpu_custom_call" | custom-call | flops 754974720 | bytes 5898240 | tf_op jit(solution)/shard_map/second_layer/pallas_call | solution.py:330
  59.3 1.7 %collective-permute-start.17 = (bf16[5,128,128]{2,1,0:T(8,128)(2,1)S(1)}, bf16[5,128,128]{2,1,0:T(8,128)(2,1)S(1)}, u32[]{:S(2)}, u32[]{:S(2)}) collective-permute-start(bf16[5,128,128]{2,1,0:T(8,128)(2,1)S(1)} %second_layer.3.mine_ref), channel_id=1, source_target_pairs={{0,1},{1,0},{2,3},{3,2},{4,5},{5,4},{6,7},{7,6},{8,9},{9,8},{10,11... | collective-permute-start | bytes 491528 | tf_op jit(solution)/shard_map/ppermute | solution.py:278
  61.0 3.6 %collective-permute-done.18.other_ref = bf16[5,128,128]{2,1,0:T(8,128)(2,1)S(1)} collective-permute-done((bf16[5,128,128]{2,1,0:T(8,128)(2,1)S(1)}, bf16[5,128,128]{2,1,0:T(8,128)(2,1)S(1)}, u32[]{:S(2)}, u32[]{:S(2)}) %collective-permute-start.18) | collective-permute-done | bytes 163872 | tf_op jit(solution)/shard_map/ppermute | solution.py:278
  64.5 0.7 %result.2.rest_0_ = bf16[10,128,128]{2,1,0:T(8,128)(2,1)} custom-call(bf16[5,128,128]{2,1,0:T(8,128)(2,1)S(1)} %get-tuple-element.20.mine_ref, bf16[5,128,128]{2,1,0:T(8,128)(2,1)S(1)} %collective-permute-done.18.other_ref), custom_call_target="tpu_custom_call" | custom-call | tf_op jit(solution)/shard_map/result/pallas_call | solution.py:408
  65.2 2.7 %collective-permute-done.17.other_ref = bf16[5,128,128]{2,1,0:T(8,128)(2,1)S(1)} collective-permute-done((bf16[5,128,128]{2,1,0:T(8,128)(2,1)S(1)}, bf16[5,128,128]{2,1,0:T(8,128)(2,1)S(1)}, u32[]{:S(2)}, u32[]{:S(2)}) %collective-permute-start.17) | collective-permute-done | bytes 163872 | tf_op jit(solution)/shard_map/ppermute | solution.py:278
  67.9 0.7 %result.3 = bf16[10,128,128]{2,1,0:T(8,128)(2,1)} custom-call(bf16[5,128,128]{2,1,0:T(8,128)(2,1)S(1)} %second_layer.3.mine_ref, bf16[5,128,128]{2,1,0:T(8,128)(2,1)S(1)} %collective-permute-done.17.other_ref, bf16[10,128,128]{2,1,0:T(8,128)(2,1)} %result.2.rest_0_), custom_call_target="tpu_custom_call", output_to_operand_aliasing={{}: (2, {})} | custom-call | tf_op jit(solution)/shard_map/result/pallas_call | solution.py:408
  (6 shorter events, 0.2 us)
Async XLA Ops:
  0.0 17.9 %copy-start.1 = (s32[10,36]{1,0:T(8,128)S(1)}, s32[10,36]{1,0:T(8,128)}, u32[]{:S(2)}) copy-start(s32[10,36]{1,0:T(8,128)} %cols_ref.9) | copy-start | bytes 4324
  0.0 17.9 %copy-start.2 = (s32[10,1]{0,1:T(1,128)S(1)}, s32[10,1]{0,1:T(1,128)}, u32[]{:S(2)}) copy-start(s32[10,1]{0,1:T(1,128)} %param.7) | copy-start | bytes 124
  0.0 17.9 %copy-start = (f32[10240]{0:T(1024)S(1)}, f32[10240]{0:T(1024)}, u32[]{:S(2)}) copy-start(f32[10240]{0:T(1024)} %param.9) | copy-start | bytes 122884
  2.5 5.8 %collective-permute-start.1 = (bf16[80,128]{1,0:T(8,128)(2,1)S(1)}, bf16[80,128]{1,0:T(8,128)(2,1)S(1)}, u32[]{:S(2)}, u32[]{:S(2)}) collective-permute-start(bf16[80,128]{1,0:T(8,128)(2,1)S(1)} %convert_element_type.36), channel_id=1, source_target_pairs={{0,4},{2,6},{4,0},{6,2},{8,12},{10,14},{12,8},{14,10},{16,20},{18,... | collective-permute-start | bytes 61448 | tf_op jit(solution)/shard_map/ppermute | solution.py:275
  6.5 1.8 %collective-permute-start = (bf16[80,128]{1,0:T(8,128)(2,1)S(1)}, bf16[80,128]{1,0:T(8,128)(2,1)S(1)}, u32[]{:S(2)}, u32[]{:S(2)}) collective-permute-start(bf16[80,128]{1,0:T(8,128)(2,1)S(1)} %convert_element_type.36), channel_id=1, source_target_pairs={{0,2},{2,0},{4,6},{6,4},{8,10},{10,8},{12,14},{14,12},{16,18},{18,... | collective-permute-start | bytes 61448 | tf_op jit(solution)/shard_map/ppermute | solution.py:275
  6.5 3.2 %collective-permute-start.2 = (bf16[80,128]{1,0:T(8,128)(2,1)S(1)}, bf16[80,128]{1,0:T(8,128)(2,1)S(1)}, u32[]{:S(2)}, u32[]{:S(2)}) collective-permute-start(bf16[80,128]{1,0:T(8,128)(2,1)S(1)} %convert_element_type.36), channel_id=1, source_target_pairs={{0,6},{2,4},{4,2},{6,0},{8,14},{10,12},{12,10},{14,8},{16,22},{18,... | collective-permute-start | bytes 61448 | tf_op jit(solution)/shard_map/ppermute | solution.py:275
  9.7 6.2 %collective-permute-start.5 = (bf16[80,128]{1,0:T(8,128)(2,1)S(1)}, bf16[80,128]{1,0:T(8,128)(2,1)S(1)}, u32[]{:S(2)}, u32[]{:S(2)}) collective-permute-start(bf16[80,128]{1,0:T(8,128)(2,1)S(1)} %add_convert_fusion.1._), channel_id=1, source_target_pairs={{0,24},{2,26},{4,28},{6,30},{8,16},{10,18},{12,20},{14,22},{16,8},... | collective-permute-start | bytes 61448 | tf_op jit(solution)/shard_map/ppermute | solution.py:275
  13.2 4.7 %collective-permute-start.4 = (bf16[80,128]{1,0:T(8,128)(2,1)S(1)}, bf16[80,128]{1,0:T(8,128)(2,1)S(1)}, u32[]{:S(2)}, u32[]{:S(2)}) collective-permute-start(bf16[80,128]{1,0:T(8,128)(2,1)S(1)} %add_convert_fusion.1._), channel_id=1, source_target_pairs={{0,16},{2,18},{4,20},{6,22},{8,24},{10,26},{12,28},{14,30},{16,0},... | collective-permute-start | bytes 61448 | tf_op jit(solution)/shard_map/ppermute | solution.py:275
  13.2 4.7 %collective-permute-start.3 = (bf16[80,128]{1,0:T(8,128)(2,1)S(1)}, bf16[80,128]{1,0:T(8,128)(2,1)S(1)}, u32[]{:S(2)}, u32[]{:S(2)}) collective-permute-start(bf16[80,128]{1,0:T(8,128)(2,1)S(1)} %add_convert_fusion.1._), channel_id=1, source_target_pairs={{0,8},{2,10},{4,12},{6,14},{8,0},{10,2},{12,4},{14,6},{16,24},{18,... | collective-permute-start | bytes 61448 | tf_op jit(solution)/shard_map/ppermute | solution.py:275
  19.4 6.1 %collective-permute-start.6 = (bf16[5,128,128]{2,1,0:T(8,128)(2,1)S(1)}, bf16[5,128,128]{2,1,0:T(8,128)(2,1)S(1)}, u32[]{:S(2)}, u32[]{:S(2)}) collective-permute-start(bf16[5,128,128]{2,1,0:T(8,128)(2,1)S(1)} %first_layer.2.rest_0_), channel_id=1, source_target_pairs={{0,1},{1,0},{2,3},{3,2},{4,5},{5,4},{6,7},{7,6},{8,9},{9,8},{10,11... | collective-permute-start | bytes 491528 | tf_op jit(solution)/shard_map/ppermute | solution.py:278
  25.5 9.1 %collective-permute-start.7 = (bf16[5,128,128]{2,1,0:T(8,128)(2,1)S(1)}, bf16[5,128,128]{2,1,0:T(8,128)(2,1)S(1)}, u32[]{:S(2)}, u32[]{:S(2)}) collective-permute-start(bf16[5,128,128]{2,1,0:T(8,128)(2,1)S(1)} %add_convert_fusion.own_ref), channel_id=1, source_target_pairs={{0,16},{2,18},{4,20},{6,22},{8,24},{10,26},{12,28},{14,30},{16,0},... | collective-permute-start | bytes 491528 | tf_op jit(solution)/shard_map/ppermute | solution.py:275
  34.8 6.2 %collective-permute-start.11 = (bf16[5,128,128]{2,1,0:T(8,128)(2,1)S(1)}, bf16[5,128,128]{2,1,0:T(8,128)(2,1)S(1)}, u32[]{:S(2)}, u32[]{:S(2)}) collective-permute-start(bf16[5,128,128]{2,1,0:T(8,128)(2,1)S(1)} %get-tuple-element.18), channel_id=1, source_target_pairs={{0,1},{1,0},{2,3},{3,2},{4,5},{5,4},{6,7},{7,6},{8,9},{9,8},{10,11... | collective-permute-start | bytes 491528 | tf_op jit(solution)/shard_map/ppermute | solution.py:278
  36.4 8.0 %collective-permute-start.10 = (bf16[5,128,128]{2,1,0:T(8,128)(2,1)S(1)}, bf16[5,128,128]{2,1,0:T(8,128)(2,1)S(1)}, u32[]{:S(2)}, u32[]{:S(2)}) collective-permute-start(bf16[5,128,128]{2,1,0:T(8,128)(2,1)S(1)} %get-tuple-element.17.refs_0_), channel_id=1, source_target_pairs={{0,12},{2,14},{4,8},{6,10},{8,4},{10,6},{12,0},{14,2},{16,28},{18,... | collective-permute-start | bytes 491528 | tf_op jit(solution)/shard_map/ppermute | solution.py:275
  36.4 8.1 %collective-permute-start.9 = (bf16[5,128,128]{2,1,0:T(8,128)(2,1)S(1)}, bf16[5,128,128]{2,1,0:T(8,128)(2,1)S(1)}, u32[]{:S(2)}, u32[]{:S(2)}) collective-permute-start(bf16[5,128,128]{2,1,0:T(8,128)(2,1)S(1)} %get-tuple-element.17.refs_0_), channel_id=1, source_target_pairs={{0,8},{2,10},{4,12},{6,14},{8,0},{10,2},{12,4},{14,6},{16,24},{18,... | collective-permute-start | bytes 491528 | tf_op jit(solution)/shard_map/ppermute | solution.py:275
  36.4 11.6 %collective-permute-start.8 = (bf16[5,128,128]{2,1,0:T(8,128)(2,1)S(1)}, bf16[5,128,128]{2,1,0:T(8,128)(2,1)S(1)}, u32[]{:S(2)}, u32[]{:S(2)}) collective-permute-start(bf16[5,128,128]{2,1,0:T(8,128)(2,1)S(1)} %get-tuple-element.17.refs_0_), channel_id=1, source_target_pairs={{0,4},{2,6},{4,0},{6,2},{8,12},{10,14},{12,8},{14,10},{16,20},{18,... | collective-permute-start | bytes 491528 | tf_op jit(solution)/shard_map/ppermute | solution.py:275
  40.9 10.6 %collective-permute-start.14 = (bf16[5,128,128]{2,1,0:T(8,128)(2,1)S(1)}, bf16[5,128,128]{2,1,0:T(8,128)(2,1)S(1)}, u32[]{:S(2)}, u32[]{:S(2)}) collective-permute-start(bf16[5,128,128]{2,1,0:T(8,128)(2,1)S(1)} %collective-permute-done.11.refs_0_), channel_id=1, source_target_pairs={{0,12},{2,14},{4,8},{6,10},{8,4},{10,6},{12,0},{14,2},{16,28},{18,... | collective-permute-start | bytes 491528 | tf_op jit(solution)/shard_map/ppermute | solution.py:275
  40.9 10.6 %collective-permute-start.13 = (bf16[5,128,128]{2,1,0:T(8,128)(2,1)S(1)}, bf16[5,128,128]{2,1,0:T(8,128)(2,1)S(1)}, u32[]{:S(2)}, u32[]{:S(2)}) collective-permute-start(bf16[5,128,128]{2,1,0:T(8,128)(2,1)S(1)} %collective-permute-done.11.refs_0_), channel_id=1, source_target_pairs={{0,8},{2,10},{4,12},{6,14},{8,0},{10,2},{12,4},{14,6},{16,24},{18,... | collective-permute-start | bytes 491528 | tf_op jit(solution)/shard_map/ppermute | solution.py:275
  44.5 9.2 %collective-permute-start.12 = (bf16[5,128,128]{2,1,0:T(8,128)(2,1)S(1)}, bf16[5,128,128]{2,1,0:T(8,128)(2,1)S(1)}, u32[]{:S(2)}, u32[]{:S(2)}) collective-permute-start(bf16[5,128,128]{2,1,0:T(8,128)(2,1)S(1)} %collective-permute-done.11.refs_0_), channel_id=1, source_target_pairs={{0,4},{2,6},{4,0},{6,2},{8,12},{10,14},{12,8},{14,10},{16,20},{18,... | collective-permute-start | bytes 491528 | tf_op jit(solution)/shard_map/ppermute | solution.py:275
  48.1 5.7 %collective-permute-start.15 = (bf16[20,128,128]{2,1,0:T(8,128)(2,1)S(1)}, bf16[20,128,128]{2,1,0:T(8,128)(2,1)S(1)}, u32[]{:S(2)}, u32[]{:S(2)}) collective-permute-start(bf16[20,128,128]{2,1,0:T(8,128)(2,1)S(1)} %own_joined.2.home_ref), channel_id=1, source_target_pairs={{0,2},{2,0},{4,6},{6,4},{8,10},{10,8},{12,14},{14,12},{16,18},{18,... | collective-permute-start | bytes 1966088 | tf_op jit(solution)/shard_map/ppermute | solution.py:275
  53.7 2.2 %collective-permute-start.16 = (bf16[20,128,128]{2,1,0:T(8,128)(2,1)S(1)}, bf16[20,128,128]{2,1,0:T(8,128)(2,1)S(1)}, u32[]{:S(2)}, u32[]{:S(2)}) collective-permute-start(bf16[20,128,128]{2,1,0:T(8,128)(2,1)S(1)} %own_joined.3.away_ref), channel_id=1, source_target_pairs={{0,2},{2,0},{4,6},{6,4},{8,10},{10,8},{12,14},{14,12},{16,18},{18,... | collective-permute-start | bytes 1966088 | tf_op jit(solution)/shard_map/ppermute | solution.py:275
  57.4 7.1 %collective-permute-start.18 = (bf16[5,128,128]{2,1,0:T(8,128)(2,1)S(1)}, bf16[5,128,128]{2,1,0:T(8,128)(2,1)S(1)}, u32[]{:S(2)}, u32[]{:S(2)}) collective-permute-start(bf16[5,128,128]{2,1,0:T(8,128)(2,1)S(1)} %get-tuple-element.20.mine_ref), channel_id=1, source_target_pairs={{0,1},{1,0},{2,3},{3,2},{4,5},{5,4},{6,7},{7,6},{8,9},{9,8},{10,11... | collective-permute-start | bytes 491528 | tf_op jit(solution)/shard_map/ppermute | solution.py:278
  59.3 8.6 %collective-permute-start.17 = (bf16[5,128,128]{2,1,0:T(8,128)(2,1)S(1)}, bf16[5,128,128]{2,1,0:T(8,128)(2,1)S(1)}, u32[]{:S(2)}, u32[]{:S(2)}) collective-permute-start(bf16[5,128,128]{2,1,0:T(8,128)(2,1)S(1)} %second_layer.3.mine_ref), channel_id=1, source_target_pairs={{0,1},{1,0},{2,3},{3,2},{4,5},{5,4},{6,7},{7,6},{8,9},{9,8},{10,11... | collective-permute-start | bytes 491528 | tf_op jit(solution)/shard_map/ppermute | solution.py:278
